TPU v7x, 128 devices: a whole 4x4x4 slice. The times are simulated.
128 devices in a mesh: db: 16 (over x, z), head: 8 (over y, core).
Axes of the slice: x: 4, y: 4, z: 4, core: 2. Of those that a mesh axis runs over, the one named last changes fastest.
Arguments:
- queries: bfloat16 [2048, 4096], P('db', 'head'), may hold values from -6 to 6
- w_key: bfloat16 [896, 4096], P(None, 'head'), may hold values from -0.1875 to 0.1875
- w_value: bfloat16 [896, 4096], P(None, 'head'), may hold values from -0.1875 to 0.1875
- w_out: bfloat16 [4096, 4096], P('head'), may hold values from -0.375 to 0.375
- encodings: bfloat16 [1024, 128, 896], P('db', 'head'), may hold values from -6 to 6
- nbr_row: int32 [32, 8], P('db'), may hold values from 0 to 63
- nbr_owner: int32 [32, 8], P('db'), may hold values from 0 to 15, all different within a row; in each aligned block of 2 rows (0 to 1, 2 to 3, ...) at most 2 rows name the same one
- nbr_count: int32 [32], P('db'), may hold values from 2 to 8
- grad_out: bfloat16 [2048, 4096], P('db', 'head'), may hold values from -6 to 6
Outputs:
- attended: bfloat16 [2048, 4096], P('db', 'head')
- grad_queries: bfloat16 [2048, 4096], P('db', 'head')
- grad_wk: float32 [896, 4096], P('db', 'head')
- grad_wv: float32 [896, 4096], P('db', 'head')
- grad_wo: float32 [4096, 4096], P('head', 'db')
Inputs may be any that keep to these rules, and one draw needn't show every extreme that they name: `nbr_owner`: the 8 owners named by one group are all different.
All inputs are finite; a program needn't handle non-finite values.
Results may differ from a plain program's by a relative error of at most 0.023.
Values may be sent and summed in bfloat16 or wider, within the bound.
No kernel may reach another device: no remote copies, remote signals or barrier semaphores. Data moves between devices by JAX's collectives and lax.ppermute only.
A program may use at most 128 MiB of HBM per device.

v0:
```python
import math

import jax
import jax.numpy as jnp
from jax import lax
from jax.sharding import PartitionSpec as P

HD = 128


def shards(queries, w_key, w_value, w_out, encodings, nbr_row, nbr_owner, nbr_count, grad_out):
    db_count = lax.axis_size("db")
    head_count = lax.axis_size("head")
    groups, slot_count = nbr_row.shape
    tok_rows, local_width = queries.shape
    group_len = tok_rows // groups
    enc_width = encodings.shape[2]
    slice_len = encodings.shape[1]
    local_heads = local_width // HD
    factor = 1.0 / math.sqrt(HD)
    owner_ids = lax.broadcasted_iota(jnp.int32, (1, 1, db_count), 2)
    chosen = nbr_owner[:, :, None] == owner_ids
    wanted = jnp.sum(jnp.where(chosen, nbr_row[:, :, None], 0), axis=1)
    incoming = lax.all_to_all(wanted, "db", split_axis=1, concat_axis=1, tiled=True)
    table = jnp.take(encodings, incoming, axis=0)
    selector = chosen.astype(jnp.bfloat16)
    spread = jnp.broadcast_to(
        table[:, :, None], (groups, db_count, head_count, slice_len, enc_width)
    )
    spread = spread.reshape(groups, db_count * head_count * slice_len, enc_width)
    received = lax.all_to_all(spread, ("db", "head"), split_axis=1, concat_axis=1, tiled=True)
    received = received.reshape(groups, db_count, head_count * slice_len, enc_width)
    slots = jnp.einsum(
        "ckn,cnte->ckte", selector, received, preferred_element_type=jnp.float32
    ).astype(jnp.bfloat16)
    keys = jnp.einsum("cste,ef->cstf", slots, w_key, preferred_element_type=jnp.float32).astype(
        jnp.bfloat16
    )
    values = jnp.einsum("cste,ef->cstf", slots, w_value, preferred_element_type=jnp.float32).astype(
        jnp.bfloat16
    )
    keys, values = (keys, values)
    key_len = slot_count * keys.shape[2]
    query_heads = queries.reshape(groups, group_len, local_heads, HD)
    key_heads = keys.reshape(groups, key_len, local_heads, HD)
    value_heads = values.reshape(groups, key_len, local_heads, HD)
    scores = (
        jnp.einsum("cqhd,ckhd->chqk", query_heads, key_heads, preferred_element_type=jnp.float32)
        * factor
    )
    key_slot = lax.broadcasted_iota(jnp.int32, (1, key_len), 1) // keys.shape[2]
    live = key_slot < nbr_count[:, None]
    expo = jnp.where(live[:, None, None, :], jnp.exp(scores), jnp.float32(0.0))
    probs = expo / jnp.sum(expo, axis=-1, keepdims=True)
    probs_b = probs.astype(jnp.bfloat16)
    mixed = jnp.einsum("chqk,ckhd->cqhd", probs_b, value_heads, preferred_element_type=jnp.float32)
    mixed = mixed.astype(jnp.bfloat16).reshape(tok_rows, local_width)
    out_term = jnp.dot(mixed, w_out, preferred_element_type=jnp.float32)
    attended = lax.psum_scatter(
        out_term.astype(jnp.bfloat16), "head", scatter_dimension=1, tiled=True
    )
    piece = lax.all_gather(grad_out, "head", axis=1, tiled=True)
    acc_mixed = lax.dot_general(
        piece, w_out, (((1,), (1,)), ((), ())), preferred_element_type=jnp.float32
    )
    block = lax.dot_general(
        mixed, piece, (((0,), (0,)), ((), ())), preferred_element_type=jnp.float32
    )
    out_grad = block
    acc_mixed, out_grad = (acc_mixed, out_grad)
    grad_wo = lax.psum_scatter(
        out_grad.astype(jnp.bfloat16), "db", scatter_dimension=1, tiled=True
    ).astype(jnp.float32)
    d_mixed = acc_mixed.astype(jnp.bfloat16).reshape(groups, group_len, local_heads, HD)
    d_probs = jnp.einsum(
        "cqhd,ckhd->chqk", d_mixed, value_heads, preferred_element_type=jnp.float32
    )
    inner = jnp.sum(probs * d_probs, axis=-1, keepdims=True)
    d_scores = (probs * (d_probs - inner) * factor).astype(jnp.bfloat16)
    grad_queries = jnp.einsum(
        "chqk,ckhd->cqhd", d_scores, key_heads, preferred_element_type=jnp.float32
    )
    grad_queries = grad_queries.astype(jnp.bfloat16).reshape(tok_rows, local_width)
    d_keys = jnp.einsum(
        "chqk,cqhd->ckhd", d_scores, query_heads, preferred_element_type=jnp.float32
    ).astype(jnp.bfloat16)
    d_values = jnp.einsum(
        "chqk,cqhd->ckhd", probs_b, d_mixed, preferred_element_type=jnp.float32
    ).astype(jnp.bfloat16)
    d_keys = d_keys.reshape(keys.shape)
    d_values = d_values.reshape(values.shape)
    key_term = jnp.einsum("cste,cstf->ef", slots, d_keys, preferred_element_type=jnp.float32)
    value_term = jnp.einsum("cste,cstf->ef", slots, d_values, preferred_element_type=jnp.float32)
    grad_wk, grad_wv = (
        lax.psum_scatter(
            key_term.astype(jnp.bfloat16), "db", scatter_dimension=0, tiled=True
        ).astype(jnp.float32),
        lax.psum_scatter(
            value_term.astype(jnp.bfloat16), "db", scatter_dimension=0, tiled=True
        ).astype(jnp.float32),
    )
    return (attended, grad_queries, grad_wk, grad_wv, grad_wo)


def solution(mesh):
    placed = (
        P("db", "head"),
        P(None, "head"),
        P(None, "head"),
        P("head", None),
        P("db", "head", None),
        P("db", None),
        P("db", None),
        P("db"),
        P("db", "head"),
    )
    return jax.shard_map(
        shards,
        mesh=mesh,
        in_specs=placed,
        out_specs=(
            P("db", "head"),
            P("db", "head"),
            P("db", "head"),
            P("db", "head"),
            P("head", "db"),
        ),
        check_vma=False,
    )
```

profile of v0, /device:TPU:0, one launch (start us, length us, event | category | flops | bytes accessed | tf_op | source)
XLA Modules:
  0.0 467.3 jit_solution(7181345065615964185)
XLA Ops:
  8.2 15.3 %all_to_all.14 = s32[2,16,1]{0,2,1:T(1,128)S(1)} all-to-all(s32[2,16,1]{0,2,1:T(1,128)S(1)} %copy.45), channel_id=1, replica_groups=mesh['db'=16,'head'=8] {'db'}, dimensions={1} | all-to-all | bytes 256 | tf_op jit(solution)/shard_map/all_to_all | solution.py:24
  25.6 5.6 %broadcast_in_dim.50 = bf16[2,16,8,16,896]{4,0,3,2,1:T(2,128)(2,1)} broadcast(bf16[2,16,16,896]{3,0,2,1:T(2,128)(2,1)S(1)} %copy.48), dimensions={0,1,3,4} | broadcast | bytes 8257536 | tf_op jit(solution)/shard_map/broadcast_in_dim | solution.py:27
  31.2 6.8 %all-to-all-start.1 = ((bf16[2,2048,896]{2,0,1:T(2,128)(2,1)}), bf16[2,2048,896]{2,0,1:T(2,128)(2,1)}, u32[]{:S(2)}, u32[]{:S(2)}) async-start(bf16[2,2048,896]{2,0,1:T(2,128)(2,1)} %bitcast.101), calls=%async_computation.1 | async-start | bytes 14680064 | tf_op jit(solution)/shard_map/all_to_all | solution.py:31
  39.2 82.6 %all-gather.2.cloned.1.call-done = bf16[128,4096]{1,0:T(8,128)(2,1)} async-done(((bf16[128,512]{1,0:T(8,128)(2,1)}), bf16[128,4096]{1,0:T(8,128)(2,1)}) %all-gather.2.cloned.1.call-update) | async-done | bytes 1048592 | tf_op jit(solution)/shard_map/all_gather | solution.py:62
  121.8 4.0 convolution_convert_fusion.3
  125.9 6.2 %all-to-all-done.1 = bf16[2,2048,896]{2,0,1:T(2,128)(2,1)} async-done(((bf16[2,2048,896]{2,0,1:T(2,128)(2,1)}), bf16[2,2048,896]{2,0,1:T(2,128)(2,1)}, u32[]{:S(2)}, u32[]{:S(2)}) %all-to-all-start.1) | async-done | bytes 7340064 | tf_op jit(solution)/shard_map/all_to_all | solution.py:31
  132.2 11.2 %fusion.7 = bf16[2,8,128,896]{3,1,2,0:T(8,128)(2,1)S(1)} fusion(bf16[2,16,128,896]{3,0,2,1:T(2,128)(2,1)} %bitcast.6, s32[2,8]{1,0:T(2,128)S(1)} %copy-done.5), kind=kOutput, calls=%fused_computation.10 | convolution fusion | flops 60555520 | bytes 11010112 | tf_op jit(solution)/shard_map/ckn,cnte->ckte/dot_general | solution.py:33
  145.1 3.7 fusion.13
  148.8 4.0 reshape.115
  152.8 6.0 %fusion.16 = bf16[2,8,128,512]{3,2,1,0:T(8,128)(2,1)} fusion(bf16[2,8,128,896]{3,1,2,0:T(8,128)(2,1)} %copy-done.2, bf16[896,512]{1,0:T(8,128)(2,1)} %param.10), kind=kOutput, calls=%fused_computation.19 | convolution fusion | flops 1880096768 | bytes 6684672 | tf_op jit(solution)/shard_map/cste,ef->cstf/dot_general | solution.py:36
  158.7 4.0 reshape.116
  162.7 3.9 fusion.19
  171.1 8.5 %convert_bitcast_fusion = bf16[2,1024,4,128]{3,1,2,0:T(8,128)(2,1)} fusion(f32[2,4,64,1024]{3,2,1,0:T(8,128)} %fusion.19, bf16[2,64,4,128]{3,2,1,0:T(4,128)(2,1)S(1)} %reshape.117, f32[2,4,1024,64]{2,3,1,0:T(8,128)} %copy-done.8, f32[2,4,64]{2,1,0:T(4,128)S(1)} %get-tuple-element.7, pred[2,1024]{1,0:T(4,128)(4,1)S(1)} %broadcast_compare_fusion), kind=kOutput, calls=%fused_computation.13 | convolution fusion | flops 141035008 | bytes 6426624 | tf_op jit(solution)/shard_map/chqk,cqhd->ckhd/dot_general | solution.py:84
  179.7 4.0 copy.62
  187.2 4.9 %copy.63 = bf16[2,8,128,512]{3,1,2,0:T(8,128)(2,1)} copy(bf16[2,8,128,512]{2,1,3,0:T(8,128)(2,1)} %bitcast.103) | data formatting | bytes 4194304 | tf_op jit(solution)/shard_map/reshape | solution.py:90
  192.0 5.7 %bitcast_convert_fusion.1 = bf16[896,512]{1,0:T(8,128)(2,1)} fusion(bf16[2,8,128,896]{3,1,2,0:T(8,128)(2,1)} %copy-done.2, bf16[2,8,128,512]{3,1,2,0:T(8,128)(2,1)} %copy.63), kind=kOutput, calls=%fused_computation.30 | convolution fusion | flops 1879506944 | bytes 6684672 | tf_op jit(solution)/shard_map/cste,cstf->ef/dot_general | solution.py:92
  201.4 4.9 %copy.65 = bf16[2,8,128,512]{3,1,2,0:T(8,128)(2,1)} copy(bf16[2,8,128,512]{2,1,3,0:T(8,128)(2,1)} %bitcast.104) | data formatting | bytes 4194304 | tf_op jit(solution)/shard_map/reshape | solution.py:91
  206.3 5.8 %bitcast_convert_fusion = bf16[896,512]{1,0:T(8,128)(2,1)} fusion(bf16[2,8,128,896]{3,1,2,0:T(8,128)(2,1)} %copy-done.2, bf16[2,8,128,512]{3,1,2,0:T(8,128)(2,1)} %copy.65), kind=kOutput, calls=%fused_computation.29 | convolution fusion | flops 1879506944 | bytes 6684672 | tf_op jit(solution)/shard_map/cste,cstf->ef/dot_general | solution.py:93
  218.7 3.9 convolution_convert_fusion.1
  222.7 6.8 %fusion.39 = bf16[2,64,4,128]{3,1,2,0:T(8,128)(2,1)S(1)} fusion(bf16[2,1024,4,128]{3,2,1,0:T(4,128)(2,1)} %reshape.116, f32[2,4,64,1024]{3,2,1,0:T(8,128)} %fusion.19, f32[2,4,1024,64]{2,3,1,0:T(8,128)} %copy-done.8, f32[2,4,64]{2,1,0:T(4,128)S(1)} %get-tuple-element.7, pred[2,1024]{1,0:T(4,128)(4,1)S(1)} %broadcast_compare_fusion), kind=kOutput, calls=%fused_computation.34 | convolution fusion | flops 140051968 | bytes 6426624 | tf_op jit(solution)/shard_map/chqk,ckhd->cqhd/dot_general | solution.py:80
  230.2 40.4 %reduce-scatter.13.cloned.1.call-done = bf16[56,512]{1,0:T(8,128)(2,1)} async-done(((bf16[896,512]{1,0:T(8,128)(2,1)}), bf16[56,512]{1,0:T(8,128)(2,1)}) %reduce-scatter.13.cloned.1.call-update) | async-done | bytes 57360
  272.1 74.4 %reduce-scatter.15.cloned.1.call-done = bf16[56,512]{1,0:T(8,128)(2,1)} async-done(((bf16[896,512]{1,0:T(8,128)(2,1)}), bf16[56,512]{1,0:T(8,128)(2,1)}) %reduce-scatter.15.cloned.1.call-update) | async-done | bytes 57360
  347.9 78.8 %reduce-scatter.11.cloned.1.call-done = bf16[512,256]{1,0:T(8,128)(2,1)} async-done(((bf16[512,4096]{1,0:T(8,128)(2,1)}), bf16[512,256]{1,0:T(8,128)(2,1)}) %reduce-scatter.11.cloned.1.call-update) | async-done | bytes 262160 | tf_op jit(solution)/shard_map/reduce_scatter | solution.py:71
  428.5 32.3 %reduce-scatter.9.cloned.1.call-done = bf16[128,512]{1,0:T(8,128)(2,1)} async-done(((bf16[128,4096]{1,0:T(8,128)(2,1)}), bf16[128,512]{1,0:T(8,128)(2,1)}) %reduce-scatter.9.cloned.1.call-update) | async-done | bytes 131088 | tf_op jit(solution)/shard_map/reduce_scatter | solution.py:59
  (54 shorter events, 29.7 us)
Async XLA Ops:
  7.2 16.6 %copy-start = (bf16[64,16,896]{2,1,0:T(8,128)(2,1)S(1)}, bf16[64,16,896]{2,1,0:T(8,128)(2,1)}, u32[]{:S(2)}) copy-start(bf16[64,16,896]{2,1,0:T(8,128)(2,1)} %param.13) | copy-start | bytes 5505028
  31.2 7.8 %copy-start.4 = (bf16[128,512]{1,0:T(8,128)(2,1)S(1)}, bf16[128,512]{1,0:T(8,128)(2,1)}, u32[]{:S(2)}) copy-start(bf16[128,512]{1,0:T(8,128)(2,1)} %param.9) | copy-start | bytes 393220
  31.2 7.9 %copy-start.6 = (s32[2]{0:T(128)S(1)}, s32[2]{0:T(128)}, u32[]{:S(2)}) copy-start(s32[2]{0:T(128)} %param.16) | copy-start | bytes 28
  31.2 100.9 %all-to-all-start.1 = ((bf16[2,2048,896]{2,0,1:T(2,128)(2,1)}), bf16[2,2048,896]{2,0,1:T(2,128)(2,1)}, u32[]{:S(2)}, u32[]{:S(2)}) async-start(bf16[2,2048,896]{2,0,1:T(2,128)(2,1)} %bitcast.101), calls=%async_computation.1 | async-start | bytes 14680064 | tf_op jit(solution)/shard_map/all_to_all | solution.py:31
  38.1 83.8 %all-gather.2.cloned.1.call-start = ((), (), s32[]{:S(2)}) async-start(), calls=%async_computation.7 | async-start | bytes 1179648 | tf_op jit(solution)/shard_map/all_gather | solution.py:62
  38.8 231.8 %reduce-scatter.13.cloned.1.call-start = ((), (), s32[]{:S(2)}) async-start(), calls=%async_computation.9 | async-start | bytes 974848
  39.2 93.0 %copy-start.5 = (s32[2,8]{1,0:T(2,128)S(1)}, s32[2,8]{1,0:T(2,128)}, u32[]{:S(2)}) copy-start(s32[2,8]{1,0:T(2,128)} %param.15) | copy-start | bytes 196
  132.2 13.0 %copy-start.7 = (bf16[896,512]{1,0:T(8,128)(2,1)S(1)}, bf16[896,512]{1,0:T(8,128)(2,1)}, u32[]{:S(2)}) copy-start(bf16[896,512]{1,0:T(8,128)(2,1)} %param.11) | copy-start | bytes 2752516
  143.3 1.8 copy-start.2
  162.7 3.9 copy-start.3
  167.7 1.3 copy-start.8
  197.8 148.7 %reduce-scatter.15.cloned.1.call-start = ((), (), s32[]{:S(2)}) async-start(), calls=%async_computation.10 | async-start | bytes 974848
  212.1 3.3 copy-start.1
  212.1 214.6 %reduce-scatter.11.cloned.1.call-start = ((), (), s32[]{:S(2)}) async-start(), calls=%async_computation.8 | async-start | bytes 4456448 | tf_op jit(solution)/shard_map/reduce_scatter | solution.py:71
  218.6 242.2 %reduce-scatter.9.cloned.1.call-start = ((), (), s32[]{:S(2)}) async-start(), calls=%async_computation.6 | async-start | bytes 1179648 | tf_op jit(solution)/shard_map/reduce_scatter | solution.py:59
Sparse Core Ops, SparseCore 0:
  40.6 81.1 all-gather.1
  197.9 72.6 reduce-scatter.12
  274.2 72.2 reduce-scatter.14
  349.7 77.0 reduce-scatter.10
  429.7 31.0 reduce-scatter.8
where the time goes:
time: 468 us; the launch traced here: 467 us
  waiting for transfers between devices  315 us (67%)
  matrix products  69 us (15%)
  local copies, waits for them, and re-layouts  40.5 us (9%)
  blocking collectives  15.3 us (3%)
  between operations  13.9 us (3%)
  starting transfers between devices  7.22 us (2%)
  other arithmetic  5.91 us (1%)
    unnamed x7, waiting for transfers between devices  116 us
    all_gather x1, waiting for transfers between devices, shards(): piece = lax.all_gather(grad_out, 'head', axis=1, tiled=True)  82.6 us
    reduce_scatter x1, waiting for transfers between devices, shards(): lax.psum_scatter(out_grad.astype(jnp.bfloat16), 'db', scatter_dimension=1...  78.8 us
    reduce_scatter x1, waiting for transfers between devices, shards(): lax.psum_scatter(out_term.astype(jnp.bfloat16), 'head', scatter_dimension...  32.3 us
    all_to_all x1, blocking collectives, shards(): lax.all_to_all(wanted, 'db', split_axis=1, concat_axis=1, tiled=True)  15.3 us
    dot_general x1, matrix products, shards(): jnp.einsum('ckn,cnte->ckte', selector, received, preferred_element_type=j...  11.2 us
    unnamed x21, local copies, waits for them, and re-layouts  10.9 us
  transfers between devices with their start and end apart: 6, of which 6 were waited for; matrix products, arithmetic and copies ran while one was open for 9% of the time, Pallas kernels for 0%

commit v1 on v0

v1 whole, which is shorter than its diff:
```python
import functools
import math

import jax
import jax.numpy as jnp
from jax import lax
from jax.experimental import pallas as pl
from jax.experimental.pallas import tpu as pltpu
from jax.sharding import PartitionSpec as P

HD = 128
BF = jnp.bfloat16
F32 = jnp.float32
VMEM_LIMIT = 40 * 1024 * 1024


def mm(a, b, ca, cb):
    return lax.dot_general(a, b, (((ca,), (cb,)), ((), ())), preferred_element_type=F32)


def params():
    return pltpu.CompilerParams(vmem_limit_bytes=VMEM_LIMIT)


ANY = pl.BlockSpec(memory_space=pl.ANY)
VM = pl.BlockSpec(memory_space=pltpu.VMEM)
SM = pl.BlockSpec(memory_space=pltpu.SMEM)


def pick_kernel(rows_ref, src_ref, *rest, counts):
    outs, sem = rest[: len(counts)], rest[-1]
    copies, k = [], 0
    for out, count in zip(outs, counts):
        for n in range(count):
            copies.append(pltpu.make_async_copy(src_ref.at[rows_ref[k]], out.at[n], sem.at[k]))
            k += 1
    for copy in copies:
        copy.start()
    for copy in copies:
        copy.wait()


def pick(rows, src, counts):
    item = src.shape[1:]
    return pl.pallas_call(
        functools.partial(pick_kernel, counts=counts),
        out_shape=[jax.ShapeDtypeStruct((n, *item), src.dtype) for n in counts],
        in_specs=[SM, ANY],
        out_specs=[ANY] * len(counts),
        scratch_shapes=[pltpu.SemaphoreType.DMA((sum(counts),))],
        compiler_params=params(),
    )(rows, src)


def prep_kernel(g_ref, wo_ref, q_ref, wk_ref, wv_ref, dm_ref, qt_ref, dt_ref, gc_ref):
    blocks, rows, width = g_ref.shape
    groups = qt_ref.shape[0]
    part = rows // groups
    acc = jnp.zeros((rows, width), F32)
    for j in range(blocks):
        acc += mm(g_ref[j], wo_ref[:, j * width : (j + 1) * width], 1, 1)
        half = width * blocks // gc_ref.shape[0]
        for p in range(width // half):
            gc_ref[j * (width // half) + p] = g_ref[j, :, p * half : (p + 1) * half]
    dm = acc.astype(BF)
    dm_ref[...] = dm
    for h in range(width // HD):
        cols = slice(h * HD, (h + 1) * HD)
        back_q = mm(q_ref[:, cols], wk_ref[:, cols], 1, 1).astype(BF)
        back_d = mm(dm[:, cols], wv_ref[:, cols], 1, 1).astype(BF)
        for c in range(groups):
            qt_ref[c, h * part : (h + 1) * part] = back_q[c * part : (c + 1) * part]
            dt_ref[c, h * part : (h + 1) * part] = back_d[c * part : (c + 1) * part]


def prep(g, wo, q, wk, wv, groups, db_count):
    blocks, rows, width = g.shape
    heads = width // HD
    enc = wk.shape[0]
    tall = (groups, heads * rows // groups, enc)
    return pl.pallas_call(
        prep_kernel,
        out_shape=[
            jax.ShapeDtypeStruct((rows, width), BF),
            jax.ShapeDtypeStruct(tall, BF),
            jax.ShapeDtypeStruct(tall, BF),
            jax.ShapeDtypeStruct((db_count, rows, width * blocks // db_count), BF),
        ],
        in_specs=[VM] * 5,
        out_specs=[VM] * 4,
        compiler_params=params(),
        cost_estimate=pl.CostEstimate(flops=1_000_000_000, bytes_accessed=10_000_000, transcendentals=0),
    )(g, wo, q, wk, wv)


def attn_kernel(count_ref, *refs, c, pieces, last):
    x_refs, refs = refs[:pieces], refs[pieces:]
    qt_ref, dt_ref, wk_ref, wv_ref, wo_ref = refs[:5]
    refs = refs[5:]
    if last:
        q_ref, dm_ref, t0_ref, u0_ref, mixed_ref, out_ref, gq_ref, gw_ref, x_ref, sem = refs
    else:
        mixed_ref, out_ref, gq_ref, t_ref, u_ref, x_ref, sem = refs
    slots, sub, enc = x_refs[0].shape
    copies = [
        pltpu.make_async_copy(x_refs[p], x_ref.at[pl.ds(p * slots, slots)], sem.at[p])
        for p in range(pieces)
    ]
    for copy in copies:
        copy.start()
    for copy in copies:
        copy.wait()
    factor = 1.0 / math.sqrt(HD)
    x = x_ref[...].reshape(pieces * slots * sub, enc)
    keys = x.shape[0]
    s = mm(qt_ref[c], x, 1, 1) * factor
    slot = (lax.broadcasted_iota(jnp.int32, (1, keys), 1) // sub) % slots
    expo = jnp.where(slot < count_ref[c], jnp.exp(s), 0.0)
    probs = expo / jnp.sum(expo, axis=-1, keepdims=True)
    t = mm(probs.astype(BF), x, 1, 0).astype(BF)
    width = wk_ref.shape[1]
    heads = width // HD
    part = t.shape[0] // heads
    for h in range(heads):
        cols = slice(h * HD, (h + 1) * HD)
        mixed_ref[:, cols] = mm(t[h * part : (h + 1) * part], wv_ref[:, cols], 1, 0).astype(BF)
    mixed = mixed_ref[...]
    for j in range(out_ref.shape[0]):
        out_ref[j] = mm(mixed, wo_ref[:, j * width : (j + 1) * width], 1, 0).astype(BF)
    d = mm(dt_ref[c], x, 1, 1)
    inner = jnp.sum(probs * d, axis=-1, keepdims=True)
    ds = (probs * (d - inner) * factor).astype(BF)
    u = mm(ds, x, 1, 0).astype(BF)
    for h in range(heads):
        cols = slice(h * HD, (h + 1) * HD)
        gq_ref[:, cols] = mm(u[h * part : (h + 1) * part], wk_ref[:, cols], 1, 0).astype(BF)
    if not last:
        t_ref[...] = t
        u_ref[...] = u
        return
    for h in range(heads):
        rows = slice(h * part, (h + 1) * part)
        cols = slice(h * HD, (h + 1) * HD)
        u_all = jnp.concatenate([u0_ref[rows], u[rows]], axis=0)
        t_all = jnp.concatenate([t0_ref[rows], t[rows]], axis=0)
        gw_ref[:, cols] = mm(u_all, q_ref[:, cols], 0, 0).astype(BF)
        gw_ref[:, width + h * HD : width + (h + 1) * HD] = mm(t_all, dm_ref[:, cols], 0, 0).astype(BF)


def attn(count, xs, qt, dt, wk, wv, wo, c, head_count, extra=None):
    slots, sub, enc = xs[0].shape
    width = wk.shape[1]
    heads = width // HD
    part = qt.shape[1] // heads
    last = extra is not None
    out_shape = [
        jax.ShapeDtypeStruct((part, width), BF),
        jax.ShapeDtypeStruct((head_count, part, width), BF),
        jax.ShapeDtypeStruct((part, width), BF),
    ]
    if last:
        out_shape += [jax.ShapeDtypeStruct((enc, 2 * width), BF)]
    else:
        out_shape += [jax.ShapeDtypeStruct(qt.shape[1:], BF)] * 2
    more = list(extra) if last else []
    return pl.pallas_call(
        functools.partial(attn_kernel, c=c, pieces=len(xs), last=last),
        out_shape=out_shape,
        in_specs=[SM] + [ANY] * len(xs) + [VM] * (5 + len(more)),
        out_specs=[VM] * len(out_shape),
        scratch_shapes=[
            pltpu.VMEM((len(xs) * slots, sub, enc), BF),
            pltpu.SemaphoreType.DMA((len(xs),)),
        ],
        compiler_params=params(),
        cost_estimate=pl.CostEstimate(flops=4_000_000_000, bytes_accessed=12_000_000, transcendentals=262144),
    )(count, *xs, qt, dt, wk, wv, wo, *more)


def spread_head(x, head_count):
    chips = head_count // 2

    def along(v, step):
        return lax.ppermute(
            v, "head", [(i, ((i // 2 + step) % chips) * 2 + i % 2) for i in range(head_count)]
        )

    steps = sorted(range(1, chips), key=lambda s: min(s, chips - s))
    mine = [x] + [along(x, s) for s in steps]
    other = [lax.ppermute(v, "head", [(i, i ^ 1) for i in range(head_count)]) for v in mine]
    return mine + other


def exchange(x, axis):
    return lax.all_to_all(x, axis, split_axis=0, concat_axis=0, tiled=True)


def shards(queries, w_key, w_value, w_out, encodings, nbr_row, nbr_owner, nbr_count, grad_out):
    db_count = lax.axis_size("db")
    head_count = lax.axis_size("head")
    groups, slot_count = nbr_row.shape
    tok_rows, width = queries.shape
    part = tok_rows // groups
    enc = encodings.shape[2]
    owner_ids = lax.broadcasted_iota(jnp.int32, (db_count, 1, 1), 0)
    wanted = jnp.sum(jnp.where(nbr_owner[None] == owner_ids, nbr_row[None], 0), axis=2)
    incoming = exchange(wanted, "db")
    grad_all = exchange(jnp.broadcast_to(grad_out[None], (head_count, *grad_out.shape)), "head")
    tables = pick(incoming.T.reshape(-1), encodings, (db_count,) * groups)
    received = [exchange(t, "db") for t in tables]
    dm, qt, dt, grad_cols = prep(grad_all, w_out, queries, w_key, w_value, groups, db_count)
    spread = []
    for c in range(groups):
        (mine,) = pick(nbr_owner[c], received[c], (slot_count,))
        spread.append(spread_head(mine, head_count))
    grad_tok = exchange(grad_cols, "db")
    mixed, outs, grad_q, kept = [], [], [], []
    for c in range(groups):
        last = c == groups - 1
        extra = (queries, dm, *kept) if last else None
        m, o, gq, *kept = attn(nbr_count, spread[c], qt, dt, w_key, w_value, w_out, c, head_count, extra)
        mixed.append(exchange(jnp.broadcast_to(m[None], (db_count, *m.shape)), "db"))
        outs.append(exchange(o, "head"))
        grad_q.append(gq)
    (grad_w,) = kept
    grad_w = exchange(grad_w.reshape(db_count, enc // db_count, 2 * width), "db")
    attended = jnp.concatenate(
        [jnp.sum(o.astype(F32), axis=0).astype(BF) for o in outs], axis=0
    )
    summed = jnp.sum(grad_w.astype(F32), axis=0)
    grad_tok = grad_tok.reshape(db_count, groups, part, -1)
    grad_wo = sum(
        lax.dot_general(
            mixed[c], grad_tok[:, c], (((0, 1), (0, 1)), ((), ())), preferred_element_type=F32
        )
        for c in range(groups)
    )
    return (
        attended,
        jnp.concatenate(grad_q, axis=0),
        summed[:, :width],
        summed[:, width:],
        grad_wo,
    )


def solution(mesh):
    placed = (
        P("db", "head"),
        P(None, "head"),
        P(None, "head"),
        P("head", None),
        P("db", "head", None),
        P("db", None),
        P("db", None),
        P("db"),
        P("db", "head"),
    )
    return jax.shard_map(
        shards,
        mesh=mesh,
        in_specs=placed,
        out_specs=(
            P("db", "head"),
            P("db", "head"),
            P("db", "head"),
            P("db", "head"),
            P("head", "db"),
        ),
        check_vma=False,
    )
```

time: 468 us -> 223 us (0.48)
  waiting for transfers between devices: 315 us -> 42 us
  blocking collectives: 15.3 us -> 126 us
  matrix products: 69 us -> 3.25 us
  local copies, waits for them, and re-layouts: 40.5 us -> 7.16 us
  Pallas kernels: 0 us -> 21.5 us
  between operations: 13.9 us -> 0.85 us
  starting transfers between devices: 7.22 us -> 18.8 us
    unnamed x7 -> x0, waiting for transfers between devices: 116 us -> none
    reduce_scatter x2 -> x0, waiting for transfers between devices: 111 us -> none  [the longest x1 78.8 us: shards(): lax.psum_scatter(out_grad.astype(jnp.bfloat16), 'db', scatter_dimension=1...]
    all_to_all x1 -> x8, blocking collectives: 15.3 us -> 126 us  [exchange(): return lax.all_to_all(x, axis, split_axis=0, concat_axis=0, tiled=True)]
    all_gather x1 -> x0, waiting for transfers between devices: 82.6 us -> none  [shards(): piece = lax.all_gather(grad_out, 'head', axis=1, tiled=True)]
    dot_general x14 -> x2, matrix products: 69 us -> 3.25 us  [shards(): lax.dot_general(mixed[c], grad_tok[:, c], (((0, 1), (0, 1)), ((), ())), p...]
    ppermute x0 -> x14, waiting for transfers between devices: none -> 23.5 us  [the longest x6 23.5 us: along(): lax.ppermute(v, 'head', [(i, (i // 2 + step) % chips * 2 + i % 2) for i i...]
    pallas_call x0 -> x6, Pallas kernels: none -> 21.5 us  [the longest x2 15.2 us: attn(): pl.pallas_call(functools.partial(attn_kernel, c=c, pieces=len(xs), last=l...]
    reshape x6 -> x1, local copies, waits for them, and re-layouts: 17.8 us -> 0.08 us  [shards(): tables = pick(incoming.T.reshape(-1), encodings, (db_count,) * groups)]
  transfers between devices with their start and end apart: 6 -> 16, of which waited for: 6 -> 5; matrix products, arithmetic and copies ran while one was open for 9% -> 2% of each run, Pallas kernels for 0% -> 5%
where the time goes in v1:
time: 223 us; the launch traced here: 222 us
  blocking collectives  126 us (57%)
  waiting for transfers between devices  42 us (19%)
  Pallas kernels  21.5 us (10%)
  starting transfers between devices  18.8 us (8%)
  local copies, waits for them, and re-layouts  7.16 us (3%)
  matrix products  3.25 us (1%)
  other arithmetic  2.6 us (1%)
    all_to_all x8, blocking collectives, exchange(): return lax.all_to_all(x, axis, split_axis=0, concat_axis=0, tiled=True)  126 us
    ppermute x6, waiting for transfers between devices, along(): lax.ppermute(v, 'head', [(i, (i // 2 + step) % chips * 2 + i % 2) for i i...  23.5 us
    all_to_all x2, waiting for transfers between devices, exchange(): return lax.all_to_all(x, axis, split_axis=0, concat_axis=0, tiled=True)  18.4 us
    pallas_call x2, Pallas kernels, attn(): pl.pallas_call(functools.partial(attn_kernel, c=c, pieces=len(xs), last=l...  15.2 us
    ppermute x6, starting transfers between devices, along(): lax.ppermute(v, 'head', [(i, (i // 2 + step) % chips * 2 + i % 2) for i i...  8.89 us
    all_to_all x2, starting transfers between devices, exchange(): return lax.all_to_all(x, axis, split_axis=0, concat_axis=0, tiled=True)  8.32 us
    unnamed x30, local copies, waits for them, and re-layouts  4.92 us
  transfers between devices with their start and end apart: 16, of which 5 were waited for; matrix products, arithmetic and copies ran while one was open for 2% of the time, Pallas kernels for 5%

profile of v1, /device:TPU:0, one launch (start us, length us, event | category | flops | bytes accessed | tf_op | source)
XLA Modules:
  0.0 221.9 jit_solution(10761269153180431019)
XLA Ops:
  1.5 15.3 %all_to_all.57 = s32[16,1,2]{2,1,0:T(1,128)S(1)} all-to-all(s32[16,1,2]{2,1,0:T(1,128)S(1)} %copy.20), channel_id=1, replica_groups=mesh['db'=16,'head'=8] {'db'}, dimensions={0} | all-to-all | bytes 256 | tf_op jit(solution)/shard_map/all_to_all | solution.py:195
  18.5 2.3 %shard_map.128 = (bf16[16,16,896]{2,1,0:T(8,128)(2,1)S(1)}, bf16[16,16,896]{2,1,0:T(8,128)(2,1)S(1)}) custom-call(s32[32]{0:T(128)S(1)} %reshape.26.rows_ref, bf16[64,16,896]{2,1,0:T(8,128)(2,1)S(1)} %copy-done.2), custom_call_target="tpu_custom_call" | custom-call | tf_op jit(solution)/shard_map/pallas_call | solution.py:45
  20.8 12.7 %all_to_all.58.src_ref = bf16[16,16,896]{2,1,0:T(8,128)(2,1)S(1)} all-to-all(bf16[16,16,896]{2,1,0:T(8,128)(2,1)S(1)} %get-tuple-element.20), channel_id=1, replica_groups=mesh['db'=16,'head'=8] {'db'}, dimensions={0} | all-to-all | bytes 917504 | tf_op jit(solution)/shard_map/all_to_all | solution.py:195
  33.5 13.0 %all_to_all.59.src_ref = bf16[16,16,896]{2,1,0:T(8,128)(2,1)S(1)} all-to-all(bf16[16,16,896]{2,1,0:T(8,128)(2,1)S(1)} %get-tuple-element.24), channel_id=1, replica_groups=mesh['db'=16,'head'=8] {'db'}, dimensions={0} | all-to-all | bytes 917504 | tf_op jit(solution)/shard_map/all_to_all | solution.py:195
  47.6 4.6 %all-to-all-start.2 = ((bf16[8,128,512]{2,1,0:T(8,128)(2,1)}), bf16[8,128,512]{2,1,0:T(8,128)(2,1)S(1)}, u32[]{:S(2)}, u32[]{:S(2)}) async-start(bf16[8,128,512]{2,1,0:T(8,128)(2,1)} %broadcast_in_dim.20), calls=%async_computation.2 | async-start | bytes 2097152 | tf_op jit(solution)/shard_map/all_to_all | solution.py:195
  53.2 3.6 %collective-permute-start.9 = (bf16[8,16,896]{2,1,0:T(8,128)(2,1)S(1)}, bf16[8,16,896]{2,1,0:T(8,128)(2,1)S(1)}, u32[]{:S(2)}, u32[]{:S(2)}) collective-permute-start(bf16[8,16,896]{2,1,0:T(8,128)(2,1)S(1)} %shard_map.132.refs_0_), channel_id=1, source_target_pairs={{0,4},{1,5},{2,6},{3,7},{4,0},{5,1},{6,2},{7,3},{8,12},{9,13},{10,... | collective-permute-start | bytes 688136 | tf_op jit(solution)/shard_map/ppermute | solution.py:184
  58.9 1.5 collective-permute-start.2
  60.4 2.1 collective-permute-start.1
  62.5 11.2 %collective-permute-done.9.refs_3_ = bf16[8,16,896]{2,1,0:T(8,128)(2,1)S(1)} collective-permute-done((bf16[8,16,896]{2,1,0:T(8,128)(2,1)S(1)}, bf16[8,16,896]{2,1,0:T(8,128)(2,1)S(1)}, u32[]{:S(2)}, u32[]{:S(2)}) %collective-permute-start.9) | collective-permute-done | bytes 229408 | tf_op jit(solution)/shard_map/ppermute | solution.py:184
  74.2 2.8 %collective-permute-done.8.refs_2_ = bf16[8,16,896]{2,1,0:T(8,128)(2,1)S(1)} collective-permute-done((bf16[8,16,896]{2,1,0:T(8,128)(2,1)S(1)}, bf16[8,16,896]{2,1,0:T(8,128)(2,1)S(1)}, u32[]{:S(2)}, u32[]{:S(2)}) %collective-permute-start.8) | collective-permute-done | bytes 229408 | tf_op jit(solution)/shard_map/ppermute | solution.py:184
  77.0 1.6 collective-permute-done.2.refs_3_
  78.6 7.9 %collective-permute-done.1.refs_2_ = bf16[8,16,896]{2,1,0:T(8,128)(2,1)} collective-permute-done((bf16[8,16,896]{2,1,0:T(8,128)(2,1)S(1)}, bf16[8,16,896]{2,1,0:T(8,128)(2,1)}, u32[]{:S(2)}, u32[]{:S(2)}) %collective-permute-start.1) | collective-permute-done | bytes 229408 | tf_op jit(solution)/shard_map/ppermute | solution.py:184
  87.1 2.2 copy-done
  90.4 2.1 shard_map.130
  93.7 6.5 %shard_map.131 = (bf16[64,512]{1,0:T(8,128)(2,1)S(1)}, bf16[8,64,512]{2,1,0:T(8,128)(2,1)S(1)}, bf16[64,512]{1,0:T(8,128)(2,1)S(1)}, bf16[256,896]{1,0:T(8,128)(2,1)S(1)}, bf16[256,896]{1,0:T(8,128)(2,1)S(1)}) custom-call(s32[2]{0:T(128)S(1)} %copy-done.10, bf16[8,16,896]{2,1,0:T(8,128)(2,1)S(1)} %shard_map.129.refs_0_, ...), custom_call_target="tpu_custom_call" | custom-call | flops 4000000000 | bytes 12000000 | tf_op jit(solution)/shard_map/pallas_call | solution.py:166
  100.2 8.7 %shard_map.133 = (bf16[64,512]{1,0:T(8,128)(2,1)S(1)}, bf16[8,64,512]{2,1,0:T(8,128)(2,1)S(1)}, bf16[64,512]{1,0:T(8,128)(2,1)S(1)}, bf16[896,1024]{1,0:T(8,128)(2,1)}) custom-call(s32[2]{0:T(128)S(1)} %copy-done.10, bf16[8,16,896]{2,1,0:T(8,128)(2,1)S(1)} %shard_map.132.refs_0_, bf16[8,16,896]{2,1,0:T(8,128)(2,1)} %collective-permute-done.7.refs_1_, ...), custom_call_target="tpu_custom_call" | custom-call | flops 4000000000 | bytes 12000000 | tf_op jit(solution)/shard_map/pallas_call | solution.py:166
  109.0 14.1 %all_to_all.60 = bf16[8,64,512]{2,1,0:T(8,128)(2,1)S(1)} all-to-all(bf16[8,64,512]{2,1,0:T(8,128)(2,1)S(1)} %get-tuple-element.28), channel_id=1, replica_groups=mesh['db'=16,'head'=8] {'head'}, dimensions={0} | all-to-all | bytes 1048576 | tf_op jit(solution)/shard_map/all_to_all | solution.py:195
  123.1 12.8 %all_to_all.61 = bf16[8,64,512]{2,1,0:T(8,128)(2,1)S(1)} all-to-all(bf16[8,64,512]{2,1,0:T(8,128)(2,1)S(1)} %get-tuple-element.23), channel_id=1, replica_groups=mesh['db'=16,'head'=8] {'head'}, dimensions={0} | all-to-all | bytes 1048576 | tf_op jit(solution)/shard_map/all_to_all | solution.py:195
  135.9 20.3 %all_to_all.62 = bf16[16,128,256]{2,1,0:T(8,128)(2,1)} all-to-all(bf16[16,128,256]{2,1,0:T(8,128)(2,1)S(1)} %get-tuple-element.33), channel_id=1, replica_groups=mesh['db'=16,'head'=8] {'db'}, dimensions={0} | all-to-all | bytes 2097152 | tf_op jit(solution)/shard_map/all_to_all | solution.py:195
  156.3 19.2 %all_to_all.63 = bf16[16,64,512]{2,1,0:T(8,128)(2,1)} all-to-all(bf16[16,64,512]{2,1,0:T(8,128)(2,1)S(1)} %broadcast_in_dim.36), channel_id=1, replica_groups=mesh['db'=16,'head'=8] {'db'}, dimensions={0} | all-to-all | bytes 2097152 | tf_op jit(solution)/shard_map/all_to_all | solution.py:195
  175.6 18.3 %all_to_all.64 = bf16[16,64,512]{2,1,0:T(8,128)(2,1)} all-to-all(bf16[16,64,512]{2,1,0:T(8,128)(2,1)S(1)} %broadcast_in_dim.21), channel_id=1, replica_groups=mesh['db'=16,'head'=8] {'db'}, dimensions={0} | all-to-all | bytes 2097152 | tf_op jit(solution)/shard_map/all_to_all | solution.py:195
  193.9 3.7 %all-to-all-start.6 = ((bf16[16,56,1024]{2,1,0:T(8,128)(2,1)}), bf16[16,56,1024]{2,1,0:T(8,128)(2,1)S(1)}, u32[]{:S(2)}, u32[]{:S(2)}) async-start(bf16[16,56,1024]{2,1,0:T(8,128)(2,1)} %bitcast.5), calls=%async_computation.6 | async-start | bytes 3670016 | tf_op jit(solution)/shard_map/all_to_all | solution.py:195
  199.1 2.0 convolution_bitcast_fusion
  202.4 18.4 %all-to-all-done.6 = bf16[16,56,1024]{2,1,0:T(8,128)(2,1)S(1)} async-done(((bf16[16,56,1024]{2,1,0:T(8,128)(2,1)}), bf16[16,56,1024]{2,1,0:T(8,128)(2,1)S(1)}, u32[]{:S(2)}, u32[]{:S(2)}) %all-to-all-start.6) | async-done | bytes 1835040 | tf_op jit(solution)/shard_map/all_to_all | solution.py:195
  (68 shorter events, 14.0 us)
Async XLA Ops:
  18.5 28.0 %copy-start.13 = (bf16[128,512]{1,0:T(8,128)(2,1)S(1)}, bf16[128,512]{1,0:T(8,128)(2,1)}, u32[]{:S(2)}) copy-start(bf16[128,512]{1,0:T(8,128)(2,1)} %param.17) | copy-start | bytes 393220
  46.5 5.7 %copy-start.14 = (s32[2,8]{1,0:T(2,128)S(1)}, s32[2,8]{1,0:T(2,128)}, u32[]{:S(2)}) copy-start(s32[2,8]{1,0:T(2,128)} %param.15) | copy-start | bytes 196
  47.6 39.5 %copy-start.3 = (bf16[896,512]{1,0:T(8,128)(2,1)S(1)}, bf16[896,512]{1,0:T(8,128)(2,1)}, u32[]{:S(2)}) copy-start(bf16[896,512]{1,0:T(8,128)(2,1)} %refs_10_.3) | copy-start | bytes 2752516
  47.6 39.5 %copy-start.5 = (bf16[128,512]{1,0:T(8,128)(2,1)S(1)}, bf16[128,512]{1,0:T(8,128)(2,1)}, u32[]{:S(2)}) copy-start(bf16[128,512]{1,0:T(8,128)(2,1)} %refs_13_.1) | copy-start | bytes 393220
  47.6 39.4 %all-to-all-start.2 = ((bf16[8,128,512]{2,1,0:T(8,128)(2,1)}), bf16[8,128,512]{2,1,0:T(8,128)(2,1)S(1)}, u32[]{:S(2)}, u32[]{:S(2)}) async-start(bf16[8,128,512]{2,1,0:T(8,128)(2,1)} %broadcast_in_dim.20), calls=%async_computation.2 | async-start | bytes 2097152 | tf_op jit(solution)/shard_map/all_to_all | solution.py:195
  53.2 20.5 %collective-permute-start.9 = (bf16[8,16,896]{2,1,0:T(8,128)(2,1)S(1)}, bf16[8,16,896]{2,1,0:T(8,128)(2,1)S(1)}, u32[]{:S(2)}, u32[]{:S(2)}) collective-permute-start(bf16[8,16,896]{2,1,0:T(8,128)(2,1)S(1)} %shard_map.132.refs_0_), channel_id=1, source_target_pairs={{0,4},{1,5},{2,6},{3,7},{4,0},{5,1},{6,2},{7,3},{8,12},{9,13},{10,... | collective-permute-start | bytes 688136 | tf_op jit(solution)/shard_map/ppermute | solution.py:184
  56.8 20.3 %collective-permute-start.8 = (bf16[8,16,896]{2,1,0:T(8,128)(2,1)S(1)}, bf16[8,16,896]{2,1,0:T(8,128)(2,1)S(1)}, u32[]{:S(2)}, u32[]{:S(2)}) collective-permute-start(bf16[8,16,896]{2,1,0:T(8,128)(2,1)S(1)} %shard_map.132.refs_0_), channel_id=1, source_target_pairs={{0,6},{1,7},{2,0},{3,1},{4,2},{5,3},{6,4},{7,5},{8,14},{9,15},{10,... | collective-permute-start | bytes 688136 | tf_op jit(solution)/shard_map/ppermute | solution.py:184
  57.9 35.8 %copy-start.10 = (s32[2]{0:T(128)S(1)}, s32[2]{0:T(128)}, u32[]{:S(2)}) copy-start(s32[2]{0:T(128)} %count_ref.3) | copy-start | bytes 28
  58.9 19.8 %collective-permute-start.2 = (bf16[8,16,896]{2,1,0:T(8,128)(2,1)S(1)}, bf16[8,16,896]{2,1,0:T(8,128)(2,1)}, u32[]{:S(2)}, u32[]{:S(2)}) collective-permute-start(bf16[8,16,896]{2,1,0:T(8,128)(2,1)S(1)} %shard_map.129.refs_0_), channel_id=1, source_target_pairs={{0,4},{1,5},{2,6},{3,7},{4,0},{5,1},{6,2},{7,3},{8,12},{9,13},{10,... | collective-permute-start | bytes 688136 | tf_op jit(solution)/shard_map/ppermute | solution.py:184
  60.4 26.1 %collective-permute-start.1 = (bf16[8,16,896]{2,1,0:T(8,128)(2,1)S(1)}, bf16[8,16,896]{2,1,0:T(8,128)(2,1)}, u32[]{:S(2)}, u32[]{:S(2)}) collective-permute-start(bf16[8,16,896]{2,1,0:T(8,128)(2,1)S(1)} %shard_map.129.refs_0_), channel_id=1, source_target_pairs={{0,6},{1,7},{2,0},{3,1},{4,2},{5,3},{6,4},{7,5},{8,14},{9,15},{10,... | collective-permute-start | bytes 688136 | tf_op jit(solution)/shard_map/ppermute | solution.py:184
  62.5 24.0 %collective-permute-start = (bf16[8,16,896]{2,1,0:T(8,128)(2,1)S(1)}, bf16[8,16,896]{2,1,0:T(8,128)(2,1)}, u32[]{:S(2)}, u32[]{:S(2)}) collective-permute-start(bf16[8,16,896]{2,1,0:T(8,128)(2,1)S(1)} %shard_map.129.refs_0_), channel_id=1, source_target_pairs={{0,2},{1,3},{2,4},{3,5},{4,6},{5,7},{6,0},{7,1},{8,10},{9,11},{10,... | collective-permute-start | bytes 688136 | tf_op jit(solution)/shard_map/ppermute | solution.py:184
  73.7 13.4 %copy-start.6 = (bf16[8,16,896]{2,1,0:T(8,128)(2,1)}, bf16[8,16,896]{2,1,0:T(8,128)(2,1)S(1)}, u32[]{:S(2)}) copy-start(bf16[8,16,896]{2,1,0:T(8,128)(2,1)S(1)} %collective-permute-done.9.refs_3_) | copy-start | bytes 688132
  73.7 18.9 %collective-permute-start.7 = (bf16[8,16,896]{2,1,0:T(8,128)(2,1)S(1)}, bf16[8,16,896]{2,1,0:T(8,128)(2,1)}, u32[]{:S(2)}, u32[]{:S(2)}) collective-permute-start(bf16[8,16,896]{2,1,0:T(8,128)(2,1)S(1)} %shard_map.132.refs_0_), channel_id=1, source_target_pairs={{0,2},{1,3},{2,4},{3,5},{4,6},{5,7},{6,0},{7,1},{8,10},{9,11},{10,... | collective-permute-start | bytes 688136 | tf_op jit(solution)/shard_map/ppermute | solution.py:184
  77.0 10.0 %copy-start.8 = (bf16[8,16,896]{2,1,0:T(8,128)(2,1)}, bf16[8,16,896]{2,1,0:T(8,128)(2,1)S(1)}, u32[]{:S(2)}) copy-start(bf16[8,16,896]{2,1,0:T(8,128)(2,1)S(1)} %collective-permute-done.8.refs_2_) | copy-start | bytes 688132
  77.0 15.7 %collective-permute-start.3 = (bf16[8,16,896]{2,1,0:T(8,128)(2,1)S(1)}, bf16[8,16,896]{2,1,0:T(8,128)(2,1)}, u32[]{:S(2)}, u32[]{:S(2)}) collective-permute-start(bf16[8,16,896]{2,1,0:T(8,128)(2,1)S(1)} %shard_map.129.refs_0_), channel_id=1, source_target_pairs={{0,1},{1,0},{2,3},{3,2},{4,5},{5,4},{6,7},{7,6},{8,9},{9,8},{10,11... | collective-permute-start | bytes 688136 | tf_op jit(solution)/shard_map/ppermute | solution.py:190
  78.6 14.6 %collective-permute-start.6 = (bf16[8,16,896]{2,1,0:T(8,128)(2,1)}, bf16[8,16,896]{2,1,0:T(8,128)(2,1)}, u32[]{:S(2)}, u32[]{:S(2)}) collective-permute-start(bf16[8,16,896]{2,1,0:T(8,128)(2,1)} %collective-permute-done.2.refs_3_), channel_id=1, source_target_pairs={{0,1},{1,0},{2,3},{3,2},{4,5},{5,4},{6,7},{7,6},{8,9},{9,8},{10,11... | collective-permute-start | bytes 688136 | tf_op jit(solution)/shard_map/ppermute | solution.py:190
  86.5 6.8 %collective-permute-start.5 = (bf16[8,16,896]{2,1,0:T(8,128)(2,1)}, bf16[8,16,896]{2,1,0:T(8,128)(2,1)}, u32[]{:S(2)}, u32[]{:S(2)}) collective-permute-start(bf16[8,16,896]{2,1,0:T(8,128)(2,1)} %collective-permute-done.1.refs_2_), channel_id=1, source_target_pairs={{0,1},{1,0},{2,3},{3,2},{4,5},{5,4},{6,7},{7,6},{8,9},{9,8},{10,11... | collective-permute-start | bytes 688136 | tf_op jit(solution)/shard_map/ppermute | solution.py:190
  86.5 7.2 %collective-permute-start.4 = (bf16[8,16,896]{2,1,0:T(8,128)(2,1)}, bf16[8,16,896]{2,1,0:T(8,128)(2,1)}, u32[]{:S(2)}, u32[]{:S(2)}) collective-permute-start(bf16[8,16,896]{2,1,0:T(8,128)(2,1)} %collective-permute-done.refs_1_), channel_id=1, source_target_pairs={{0,1},{1,0},{2,3},{3,2},{4,5},{5,4},{6,7},{7,6},{8,9},{9,8},{10,11... | collective-permute-start | bytes 688136 | tf_op jit(solution)/shard_map/ppermute | solution.py:190
  90.4 3.3 %copy-start.1 = (bf16[512,4096]{1,0:T(8,128)(2,1)S(1)}, bf16[512,4096]{1,0:T(8,128)(2,1)}, u32[]{:S(2)}) copy-start(bf16[512,4096]{1,0:T(8,128)(2,1)} %refs_12_.3) | copy-start | bytes 12582916
  92.6 7.6 %collective-permute-start.10 = (bf16[8,16,896]{2,1,0:T(8,128)(2,1)S(1)}, bf16[8,16,896]{2,1,0:T(8,128)(2,1)S(1)}, u32[]{:S(2)}, u32[]{:S(2)}) collective-permute-start(bf16[8,16,896]{2,1,0:T(8,128)(2,1)S(1)} %shard_map.132.refs_0_), channel_id=1, source_target_pairs={{0,1},{1,0},{2,3},{3,2},{4,5},{5,4},{6,7},{7,6},{8,9},{9,8},{10,11... | collective-permute-start | bytes 688136 | tf_op jit(solution)/shard_map/ppermute | solution.py:190
  92.7 7.5 %collective-permute-start.13 = (bf16[8,16,896]{2,1,0:T(8,128)(2,1)S(1)}, bf16[8,16,896]{2,1,0:T(8,128)(2,1)S(1)}, u32[]{:S(2)}, u32[]{:S(2)}) collective-permute-start(bf16[8,16,896]{2,1,0:T(8,128)(2,1)S(1)} %copy-done.7), channel_id=1, source_target_pairs={{0,1},{1,0},{2,3},{3,2},{4,5},{5,4},{6,7},{7,6},{8,9},{9,8},{10,11... | collective-permute-start | bytes 688136 | tf_op jit(solution)/shard_map/ppermute | solution.py:190
  93.2 7.0 %collective-permute-start.12 = (bf16[8,16,896]{2,1,0:T(8,128)(2,1)S(1)}, bf16[8,16,896]{2,1,0:T(8,128)(2,1)S(1)}, u32[]{:S(2)}, u32[]{:S(2)}) collective-permute-start(bf16[8,16,896]{2,1,0:T(8,128)(2,1)S(1)} %copy-done.9), channel_id=1, source_target_pairs={{0,1},{1,0},{2,3},{3,2},{4,5},{5,4},{6,7},{7,6},{8,9},{9,8},{10,11... | collective-permute-start | bytes 688136 | tf_op jit(solution)/shard_map/ppermute | solution.py:190
  93.3 6.9 %collective-permute-start.11 = (bf16[8,16,896]{2,1,0:T(8,128)(2,1)}, bf16[8,16,896]{2,1,0:T(8,128)(2,1)S(1)}, u32[]{:S(2)}, u32[]{:S(2)}) collective-permute-start(bf16[8,16,896]{2,1,0:T(8,128)(2,1)} %collective-permute-done.7.refs_1_), channel_id=1, source_target_pairs={{0,1},{1,0},{2,3},{3,2},{4,5},{5,4},{6,7},{7,6},{8,9},{9,8},{10,11... | collective-permute-start | bytes 688136 | tf_op jit(solution)/shard_map/ppermute | solution.py:190
  193.9 26.9 %all-to-all-start.6 = ((bf16[16,56,1024]{2,1,0:T(8,128)(2,1)}), bf16[16,56,1024]{2,1,0:T(8,128)(2,1)S(1)}, u32[]{:S(2)}, u32[]{:S(2)}) async-start(bf16[16,56,1024]{2,1,0:T(8,128)(2,1)} %bitcast.5), calls=%async_computation.6 | async-start | bytes 3670016 | tf_op jit(solution)/shard_map/all_to_all | solution.py:195
  (7 other events, 13.9 us)

commit v2 on v1

v2 whole, which is shorter than its diff:
```python
import functools
import math

import jax
import jax.numpy as jnp
from jax import lax
from jax.experimental import pallas as pl
from jax.experimental.pallas import tpu as pltpu
from jax.sharding import PartitionSpec as P

HD = 128
BF = jnp.bfloat16
F32 = jnp.float32
VMEM_LIMIT = 40 * 1024 * 1024


def mm(a, b, ca, cb):
    return lax.dot_general(a, b, (((ca,), (cb,)), ((), ())), preferred_element_type=F32)


def params():
    return pltpu.CompilerParams(vmem_limit_bytes=VMEM_LIMIT)


ANY = pl.BlockSpec(memory_space=pl.ANY)
VM = pl.BlockSpec(memory_space=pltpu.VMEM)
SM = pl.BlockSpec(memory_space=pltpu.SMEM)


def pick_kernel(rows_ref, src_ref, *rest, counts):
    outs, sem = rest[: len(counts)], rest[-1]
    copies, k = [], 0
    for out, count in zip(outs, counts):
        for n in range(count):
            copies.append(pltpu.make_async_copy(src_ref.at[rows_ref[k]], out.at[n], sem.at[k]))
            k += 1
    for copy in copies:
        copy.start()
    for copy in copies:
        copy.wait()


def pick(rows, src, counts):
    item = src.shape[1:]
    return pl.pallas_call(
        functools.partial(pick_kernel, counts=counts),
        out_shape=[jax.ShapeDtypeStruct((n, *item), src.dtype) for n in counts],
        in_specs=[SM, ANY],
        out_specs=[ANY] * len(counts),
        scratch_shapes=[pltpu.SemaphoreType.DMA((sum(counts),))],
        compiler_params=params(),
    )(rows, src)


def prep_kernel(at_ref, near_ref, far_ref, wo_ref, q_ref, wk_ref, wv_ref, dm_ref, qt_ref, dt_ref, gc_ref):
    chips, rows, width = near_ref.shape
    groups = qt_ref.shape[0]
    part = rows // groups
    cuts = gc_ref.shape[0] // (2 * chips)
    piece = width // cuts
    acc = jnp.zeros((rows, width), F32)
    for core, g_ref in enumerate((near_ref, far_ref)):
        for s in range(chips):
            j = lax.rem(at_ref[0] + chips - s, chips) * 2 + lax.rem(at_ref[1] + core, 2)
            cols = pl.ds(pl.multiple_of(j * width, width), width)
            acc += mm(g_ref[s], wo_ref[:, cols], 1, 1)
            for p in range(cuts):
                gc_ref[j * cuts + p] = g_ref[s, :, p * piece : (p + 1) * piece]
    dm = acc.astype(BF)
    dm_ref[...] = dm
    for h in range(width // HD):
        cols = slice(h * HD, (h + 1) * HD)
        back_q = mm(q_ref[:, cols], wk_ref[:, cols], 1, 1).astype(BF)
        back_d = mm(dm[:, cols], wv_ref[:, cols], 1, 1).astype(BF)
        for c in range(groups):
            qt_ref[c, h * part : (h + 1) * part] = back_q[c * part : (c + 1) * part]
            dt_ref[c, h * part : (h + 1) * part] = back_d[c * part : (c + 1) * part]


def prep(at, near, far, wo, q, wk, wv, groups, db_count):
    chips, rows, width = near.shape
    heads = width // HD
    enc = wk.shape[0]
    tall = (groups, heads * rows // groups, enc)
    return pl.pallas_call(
        prep_kernel,
        out_shape=[
            jax.ShapeDtypeStruct((rows, width), BF),
            jax.ShapeDtypeStruct(tall, BF),
            jax.ShapeDtypeStruct(tall, BF),
            jax.ShapeDtypeStruct((db_count, rows, 2 * chips * width // db_count), BF),
        ],
        in_specs=[SM] + [VM] * 6,
        out_specs=[VM] * 4,
        compiler_params=params(),
        cost_estimate=pl.CostEstimate(flops=1_000_000_000, bytes_accessed=10_000_000, transcendentals=0),
    )(at, near, far, wo, q, wk, wv)


def attn_kernel(at_ref, count_ref, *refs, c, pieces, last):
    x_refs, refs = refs[:pieces], refs[pieces:]
    qt_ref, dt_ref, wk_ref, wv_ref, wo_ref = refs[:5]
    refs = refs[5:]
    if last:
        q_ref, dm_ref, t0_ref, u0_ref, send_ref, keep_ref, give_ref, gq_ref, x_ref, sem = refs
    else:
        send_ref, keep_ref, give_ref, gq_ref, t_ref, u_ref, x_ref, sem = refs
    slots, sub, enc = x_refs[0].shape
    copies = [
        pltpu.make_async_copy(x_refs[p], x_ref.at[pl.ds(p * slots, slots)], sem.at[p])
        for p in range(pieces)
    ]
    for copy in copies:
        copy.start()
    for copy in copies:
        copy.wait()
    factor = 1.0 / math.sqrt(HD)
    x = x_ref[...].reshape(pieces * slots * sub, enc)
    keys = x.shape[0]
    s = mm(qt_ref[c], x, 1, 1) * factor
    slot = (lax.broadcasted_iota(jnp.int32, (1, keys), 1) // sub) % slots
    expo = jnp.where(slot < count_ref[c], jnp.exp(s), 0.0)
    probs = expo / jnp.sum(expo, axis=-1, keepdims=True)
    t = mm(probs.astype(BF), x, 1, 0).astype(BF)
    width = wk_ref.shape[1]
    heads = width // HD
    part = t.shape[0] // heads
    mixed = jnp.concatenate(
        [
            mm(t[h * part : (h + 1) * part], wv_ref[:, h * HD : (h + 1) * HD], 1, 0).astype(BF)
            for h in range(heads)
        ],
        axis=1,
    )
    db_count = send_ref.shape[0]
    for i in range(db_count):
        send_ref[i, :part] = mixed
    chips = keep_ref.shape[0]
    for core, block_ref in enumerate((keep_ref, give_ref)):
        for step in range(chips):
            j = lax.rem(at_ref[0] + step, chips) * 2 + lax.rem(at_ref[1] + core, 2)
            cols = pl.ds(pl.multiple_of(j * width, width), width)
            block_ref[step] = mm(mixed, wo_ref[:, cols], 1, 0).astype(BF)
    d = mm(dt_ref[c], x, 1, 1)
    inner = jnp.sum(probs * d, axis=-1, keepdims=True)
    ds = (probs * (d - inner) * factor).astype(BF)
    u = mm(ds, x, 1, 0).astype(BF)
    for h in range(heads):
        cols = slice(h * HD, (h + 1) * HD)
        gq_ref[:, cols] = mm(u[h * part : (h + 1) * part], wk_ref[:, cols], 1, 0).astype(BF)
    if not last:
        t_ref[...] = t
        u_ref[...] = u
        return
    for h in range(heads):
        rows = slice(h * part, (h + 1) * part)
        cols = slice(h * HD, (h + 1) * HD)
        u_all = jnp.concatenate([u0_ref[rows], u[rows]], axis=0)
        t_all = jnp.concatenate([t0_ref[rows], t[rows]], axis=0)
        sums = (mm(u_all, q_ref[:, cols], 0, 0), mm(t_all, dm_ref[:, cols], 0, 0))
        share = enc // db_count
        for k, total in enumerate(sums):
            for i in range(db_count):
                at = part + k * share
                send_ref[i, at : at + share, cols] = total[i * share : (i + 1) * share].astype(BF)


def attn(at, count, xs, qt, dt, wk, wv, wo, c, db_count, head_count, extra=None):
    slots, sub, enc = xs[0].shape
    width = wk.shape[1]
    heads = width // HD
    part = qt.shape[1] // heads
    last = extra is not None
    half = jax.ShapeDtypeStruct((head_count // 2, part, width), BF)
    sent = part + (2 * enc // db_count if last else 0)
    out_shape = [
        jax.ShapeDtypeStruct((db_count, sent, width), BF),
        half,
        half,
        jax.ShapeDtypeStruct((part, width), BF),
    ]
    if not last:
        out_shape += [jax.ShapeDtypeStruct(qt.shape[1:], BF)] * 2
    more = list(extra) if last else []
    return pl.pallas_call(
        functools.partial(attn_kernel, c=c, pieces=len(xs), last=last),
        out_shape=out_shape,
        in_specs=[SM, SM] + [ANY] * len(xs) + [VM] * (5 + len(more)),
        out_specs=[VM] * len(out_shape),
        scratch_shapes=[
            pltpu.VMEM((len(xs) * slots, sub, enc), BF),
            pltpu.SemaphoreType.DMA((len(xs),)),
        ],
        compiler_params=params(),
        cost_estimate=pl.CostEstimate(flops=4_000_000_000, bytes_accessed=12_000_000, transcendentals=262144),
    )(at, count, *xs, qt, dt, wk, wv, wo, *more)


def along(v, step, count):
    chips = count // 2
    return lax.ppermute(v, "head", [(i, ((i // 2 + step) % chips) * 2 + i % 2) for i in range(count)])


def swap(v, count):
    return lax.ppermute(v, "head", [(i, i ^ 1) for i in range(count)])


def ring_steps(count):
    chips = count // 2
    return sorted(range(1, chips), key=lambda s: min(s, chips - s))


def exchange(x, axis):
    return lax.all_to_all(x, axis, split_axis=0, concat_axis=0, tiled=True)


def after(x, *others):
    return lax.optimization_barrier((x, *others))[0]


def shards(queries, w_key, w_value, w_out, encodings, nbr_row, nbr_owner, nbr_count, grad_out):
    db_count = lax.axis_size("db")
    head_count = lax.axis_size("head")
    chips = head_count // 2
    groups, slot_count = nbr_row.shape
    tok_rows, width = queries.shape
    part = tok_rows // groups
    enc = encodings.shape[2]
    head_at = lax.axis_index("head")
    at = jnp.stack([head_at // 2, head_at % 2]).astype(jnp.int32)
    owner_ids = lax.broadcasted_iota(jnp.int32, (db_count, 1, 1), 0)
    wanted = jnp.sum(jnp.where(nbr_owner[None] == owner_ids, nbr_row[None], 0), axis=2)
    incoming = exchange(wanted, "db")
    steps = ring_steps(head_count)
    near = [grad_out] + [along(grad_out, s, head_count) for s in steps]
    near = jnp.stack([near[([0] + steps).index(s)] for s in range(chips)])
    far = swap(near, head_count)
    tables = pick(incoming.T.reshape(-1), encodings, (db_count,) * groups)
    dm, qt, dt, grad_cols = prep(at, near, far, w_out, queries, w_key, w_value, groups, db_count)
    spread, token = [], None
    for c in range(groups):
        table = tables[c] if c == 0 else after(tables[c], token, dm)
        received = exchange(table, "db")
        (mine,) = pick(nbr_owner[c], received, (slot_count,))
        token = mine
        pieces = [mine] + [along(mine, s, head_count) for s in steps]
        spread.append(pieces + [swap(v, head_count) for v in pieces])
    grad_tok = exchange(after(grad_cols, token), "db")
    sent, keep, give, grad_q, kept = [], [], [], [], []
    for c in range(groups):
        last = c == groups - 1
        extra = (queries, dm, *kept) if last else None
        m, k, g, gq, *kept = attn(
            at, nbr_count, spread[c], qt, dt, w_key, w_value, w_out, c, db_count, head_count, extra
        )
        sent.append(exchange(m, "db"))
        keep.append(k)
        give.append(g)
        grad_q.append(gq)
    keep = jnp.concatenate(keep, axis=1)
    other = swap(jnp.concatenate(give, axis=1), head_count)
    pair = (keep.astype(F32) + other.astype(F32)).astype(BF)
    terms = [pair[0]] + [along(pair[s], s, head_count) for s in steps]
    attended = sum(t.astype(F32) for t in terms).astype(BF)
    share = enc // db_count
    grad_tok = grad_tok.reshape(db_count, groups, part, -1)
    grad_wo = sum(
        lax.dot_general(
            sent[c][:, :part], grad_tok[:, c], (((0, 1), (0, 1)), ((), ())), preferred_element_type=F32
        )
        for c in range(groups)
    )
    grad_w = [
        jnp.sum(sent[-1][:, part + k * share : part + (k + 1) * share].astype(F32), axis=0)
        for k in range(2)
    ]
    return (attended, jnp.concatenate(grad_q, axis=0), *grad_w, grad_wo)


def solution(mesh):
    placed = (
        P("db", "head"),
        P(None, "head"),
        P(None, "head"),
        P("head", None),
        P("db", "head", None),
        P("db", None),
        P("db", None),
        P("db"),
        P("db", "head"),
    )
    return jax.shard_map(
        shards,
        mesh=mesh,
        in_specs=placed,
        out_specs=(
            P("db", "head"),
            P("db", "head"),
            P("db", "head"),
            P("db", "head"),
            P("head", "db"),
        ),
        check_vma=False,
    )
```

time: 223 us -> 187 us (0.84)
  blocking collectives: 126 us -> 15.2 us
  waiting for transfers between devices: 42 us -> 76.3 us
  starting transfers between devices: 18.8 us -> 46.8 us
  local copies, waits for them, and re-layouts: 7.16 us -> 12.2 us
  Pallas kernels: 21.5 us -> 24.7 us
  other arithmetic: 2.6 us -> 5.79 us
    all_to_all x8 -> x1, blocking collectives: 126 us -> 15.2 us  [exchange(): return lax.all_to_all(x, axis, split_axis=0, concat_axis=0, tiled=True)]
    all_to_all x2 -> x5, waiting for transfers between devices: 18.4 us -> 55.8 us  [exchange(): return lax.all_to_all(x, axis, split_axis=0, concat_axis=0, tiled=True)]
    all_to_all x2 -> x5, starting transfers between devices: 8.32 us -> 26.4 us  [exchange(): return lax.all_to_all(x, axis, split_axis=0, concat_axis=0, tiled=True)]
    ppermute x6 -> x12, starting transfers between devices: 8.89 us -> 18.6 us  [along(): lax.ppermute(v, 'head', [(i, (i // 2 + step) % chips * 2 + i % 2) for i i...]
    unnamed x30 -> x40, local copies, waits for them, and re-layouts: 4.92 us -> 11.9 us
    ppermute x6 -> x12, waiting for transfers between devices: 23.5 us -> 18.6 us  [along(): lax.ppermute(v, 'head', [(i, (i // 2 + step) % chips * 2 + i % 2) for i i...]
  transfers between devices with their start and end apart: 16 -> 27, of which waited for: 5 -> 13; matrix products, arithmetic and copies ran while one was open for 2% -> 4% of each run, Pallas kernels for 5% -> 13%
where the time goes in v2:
time: 187 us; the launch traced here: 186 us
  waiting for transfers between devices  76.3 us (41%)
  starting transfers between devices  46.8 us (25%)
  Pallas kernels  24.7 us (13%)
  blocking collectives  15.2 us (8%)
  local copies, waits for them, and re-layouts  12.2 us (7%)
  other arithmetic  5.79 us (3%)
  matrix products  4.15 us (2%)
    all_to_all x5, waiting for transfers between devices, exchange(): return lax.all_to_all(x, axis, split_axis=0, concat_axis=0, tiled=True)  55.8 us
    all_to_all x5, starting transfers between devices, exchange(): return lax.all_to_all(x, axis, split_axis=0, concat_axis=0, tiled=True)  26.4 us
    ppermute x12, starting transfers between devices, along(): lax.ppermute(v, 'head', [(i, (i // 2 + step) % chips * 2 + i % 2) for i i...  18.6 us
    ppermute x12, waiting for transfers between devices, along(): lax.ppermute(v, 'head', [(i, (i // 2 + step) % chips * 2 + i % 2) for i i...  18.6 us
    pallas_call x2, Pallas kernels, attn(): pl.pallas_call(functools.partial(attn_kernel, c=c, pieces=len(xs), last=l...  16.6 us
    all_to_all x1, blocking collectives, exchange(): return lax.all_to_all(x, axis, split_axis=0, concat_axis=0, tiled=True)  15.2 us
    unnamed x40, local copies, waits for them, and re-layouts  11.9 us
    pallas_call x3, Pallas kernels, pick(): pl.pallas_call(functools.partial(pick_kernel, counts=counts), out_shape=[...  4.45 us
  transfers between devices with their start and end apart: 27, of which 13 were waited for; matrix products, arithmetic and copies ran while one was open for 4% of the time, Pallas kernels for 13%

profile of v2, /device:TPU:0, one launch (start us, length us, event | category | flops | bytes accessed | tf_op | source)
XLA Modules:
  0.0 186.1 jit_solution(6464500576208244963)
XLA Ops:
  4.0 2.1 %collective-permute-start.8 = (bf16[128,512]{1,0:T(8,128)(2,1)}, bf16[128,512]{1,0:T(8,128)(2,1)S(1)}, u32[]{:S(2)}, u32[]{:S(2)}) collective-permute-start(bf16[128,512]{1,0:T(8,128)(2,1)} %param.17), channel_id=1, source_target_pairs={{0,4},{1,5},{2,6},{3,7},{4,0},{5,1},{6,2},{7,3},{8,12},{9,13},{10,... | collective-permute-start | bytes 393224 | tf_op jit(solution)/shard_map/ppermute | solution.py:201
  7.5 2.3 %collective-permute-done.9 = bf16[128,512]{1,0:T(8,128)(2,1)S(1)} collective-permute-done((bf16[128,512]{1,0:T(8,128)(2,1)}, bf16[128,512]{1,0:T(8,128)(2,1)S(1)}, u32[]{:S(2)}, u32[]{:S(2)}) %collective-permute-start.9) | collective-permute-done | bytes 131104 | tf_op jit(solution)/shard_map/ppermute | solution.py:201
  13.5 15.2 %all_to_all.37 = s32[16,1,2]{2,1,0:T(1,128)S(1)} all-to-all(s32[16,1,2]{2,1,0:T(1,128)S(1)} %copy.20), channel_id=1, replica_groups=mesh['db'=16,'head'=8] {'db'}, dimensions={0} | all-to-all | bytes 256 | tf_op jit(solution)/shard_map/all_to_all | solution.py:214
  30.4 2.2 %shard_map.128 = (bf16[16,16,896]{2,1,0:T(8,128)(2,1)S(1)}, bf16[16,16,896]{2,1,0:T(8,128)(2,1)}) custom-call(s32[32]{0:T(128)S(1)} %reshape.22.rows_ref, bf16[64,16,896]{2,1,0:T(8,128)(2,1)S(1)} %copy-done.3), custom_call_target="tpu_custom_call" | custom-call | tf_op jit(solution)/shard_map/pallas_call | solution.py:45
  33.3 3.6 %all-to-all-start.1 = ((bf16[16,16,896]{2,1,0:T(8,128)(2,1)}), bf16[16,16,896]{2,1,0:T(8,128)(2,1)S(1)}, u32[]{:S(2)}, u32[]{:S(2)}) async-start(bf16[16,16,896]{2,1,0:T(8,128)(2,1)} %copy-done.6), calls=%async_computation.1 | async-start | bytes 917504 | tf_op jit(solution)/shard_map/all_to_all | solution.py:214
  37.0 10.2 %all-to-all-done.1.src_ref = bf16[16,16,896]{2,1,0:T(8,128)(2,1)S(1)} async-done(((bf16[16,16,896]{2,1,0:T(8,128)(2,1)}), bf16[16,16,896]{2,1,0:T(8,128)(2,1)S(1)}, u32[]{:S(2)}, u32[]{:S(2)}) %all-to-all-start.1) | async-done | bytes 458784 | tf_op jit(solution)/shard_map/all_to_all | solution.py:214
  49.8 2.2 %copy-done = bf16[512,4096]{1,0:T(8,128)(2,1)S(1)} copy-done((bf16[512,4096]{1,0:T(8,128)(2,1)S(1)}, bf16[512,4096]{1,0:T(8,128)(2,1)}, u32[]{:S(2)}) %copy-start) | copy-done | bytes 4194328
  52.0 3.6 %shard_map.130 = (bf16[128,512]{1,0:T(8,128)(2,1)S(1)}, bf16[2,256,896]{2,1,0:T(8,128)(2,1)S(1)}, bf16[2,256,896]{2,1,0:T(8,128)(2,1)S(1)}, bf16[16,128,256]{2,1,0:T(8,128)(2,1)}) custom-call(s32[2]{0:T(128)S(1)} %pad_add_fusion.at_ref, bf16[4,128,512]{2,1,0:T(8,128)(2,1)S(1)} %pad_maximum_fusion.near_ref, ...), custom_call_target="tpu_custom_call" | custom-call | flops 1000000000 | bytes 10000000 | tf_op jit(solution)/shard_map/pallas_call | solution.py:85
  57.5 3.7 %all-to-all-start.2 = ((bf16[16,16,896]{2,1,0:T(8,128)(2,1)}), bf16[16,16,896]{2,1,0:T(8,128)(2,1)S(1)}, u32[]{:S(2)}, u32[]{:S(2)}) async-start(bf16[16,16,896]{2,1,0:T(8,128)(2,1)} %get-tuple-element.29), calls=%async_computation.2 | async-start | bytes 917504 | tf_op jit(solution)/shard_map/all_to_all | solution.py:214
  61.2 2.7 %collective-permute-start.1 = (bf16[8,16,896]{2,1,0:T(8,128)(2,1)}, bf16[8,16,896]{2,1,0:T(8,128)(2,1)S(1)}, u32[]{:S(2)}, u32[]{:S(2)}) collective-permute-start(bf16[8,16,896]{2,1,0:T(8,128)(2,1)} %shard_map.129.refs_0_), channel_id=1, source_target_pairs={{0,6},{1,7},{2,0},{3,1},{4,2},{5,3},{6,4},{7,5},{8,14},{9,15},{10,... | collective-permute-start | bytes 688136 | tf_op jit(solution)/shard_map/ppermute | solution.py:201
  64.5 6.4 %all-to-all-done.2.src_ref = bf16[16,16,896]{2,1,0:T(8,128)(2,1)S(1)} async-done(((bf16[16,16,896]{2,1,0:T(8,128)(2,1)}), bf16[16,16,896]{2,1,0:T(8,128)(2,1)S(1)}, u32[]{:S(2)}, u32[]{:S(2)}) %all-to-all-start.2) | async-done | bytes 458784 | tf_op jit(solution)/shard_map/all_to_all | solution.py:214
  71.9 4.4 %all-to-all-start.5 = ((bf16[16,128,256]{2,1,0:T(8,128)(2,1)}), bf16[16,128,256]{2,1,0:T(8,128)(2,1)}, u32[]{:S(2)}, u32[]{:S(2)}) async-start(bf16[16,128,256]{2,1,0:T(8,128)(2,1)} %get-tuple-element.40), calls=%async_computation.5 | async-start | bytes 2097152 | tf_op jit(solution)/shard_map/all_to_all | solution.py:214
  76.3 2.4 %collective-permute-start.13 = (bf16[8,16,896]{2,1,0:T(8,128)(2,1)S(1)}, bf16[8,16,896]{2,1,0:T(8,128)(2,1)S(1)}, u32[]{:S(2)}, u32[]{:S(2)}) collective-permute-start(bf16[8,16,896]{2,1,0:T(8,128)(2,1)S(1)} %shard_map.132.refs_0_), channel_id=1, source_target_pairs={{0,4},{1,5},{2,6},{3,7},{4,0},{5,1},{6,2},{7,3},{8,12},{9,13},{10,... | collective-permute-start | bytes 688136 | tf_op jit(solution)/shard_map/ppermute | solution.py:201
  81.3 5.0 %collective-permute-done.13.refs_3_ = bf16[8,16,896]{2,1,0:T(8,128)(2,1)S(1)} collective-permute-done((bf16[8,16,896]{2,1,0:T(8,128)(2,1)S(1)}, bf16[8,16,896]{2,1,0:T(8,128)(2,1)S(1)}, u32[]{:S(2)}, u32[]{:S(2)}) %collective-permute-start.13) | collective-permute-done | bytes 229408 | tf_op jit(solution)/shard_map/ppermute | solution.py:201
  86.3 4.4 %collective-permute-done.12.refs_2_ = bf16[8,16,896]{2,1,0:T(8,128)(2,1)S(1)} collective-permute-done((bf16[8,16,896]{2,1,0:T(8,128)(2,1)S(1)}, bf16[8,16,896]{2,1,0:T(8,128)(2,1)S(1)}, u32[]{:S(2)}, u32[]{:S(2)}) %collective-permute-start.12) | collective-permute-done | bytes 229408 | tf_op jit(solution)/shard_map/ppermute | solution.py:201
  91.3 2.2 %copy-done.1 = bf16[512,4096]{1,0:T(8,128)(2,1)S(1)} copy-done((bf16[512,4096]{1,0:T(8,128)(2,1)S(1)}, bf16[512,4096]{1,0:T(8,128)(2,1)}, u32[]{:S(2)}) %copy-start.1) | copy-done | bytes 4194328
  96.8 7.2 %shard_map.131 = (bf16[16,64,512]{2,1,0:T(8,128)(2,1)}, bf16[4,64,512]{2,1,0:T(8,128)(2,1)S(1)}, bf16[4,64,512]{2,1,0:T(8,128)(2,1)S(1)}, bf16[64,512]{1,0:T(8,1...) custom-call(s32[2]{0:T(128)S(1)} %pad_add_fusion.at_ref, s32[2]{0:T(128)S(1)} %copy-done.18, ...), custom_call_target="tpu_custom_call" | custom-call | flops 4000000000 | bytes 12000000 | tf_op jit(solution)/shard_map/pallas_call | solution.py:185
  104.0 9.4 %shard_map.133 = (bf16[16,176,512]{2,1,0:T(8,128)(2,1)}, bf16[4,64,512]{2,1,0:T(8,128)(2,1)S(1)}, bf16[4,64,512]{2,1,0:T(8,128)(2,1)S(1)}, bf16[64,512]{1,0:T(8,128)(2,1)S(1)}) custom-call(s32[2]{0:T(128)S(1)} %pad_add_fusion.at_ref, s32[2]{0:T(128)S(1)} %copy-done.18, bf16[8,16,896]{2,1,0:T(8,128)(2,1)S(1)} %shard_map.132.refs_0_, ...), custom_call_target="tpu_custom_call" | custom-call | flops 4000000000 | bytes 12000000 | tf_op jit(solution)/shard_map/pallas_call | solution.py:185
  113.5 7.1 %all-to-all-start.3 = ((bf16[16,176,512]{2,1,0:T(8,128)(2,1)}), bf16[16,176,512]{2,1,0:T(8,128)(2,1)}, u32[]{:S(2)}, u32[]{:S(2)}) async-start(bf16[16,176,512]{2,1,0:T(8,128)(2,1)} %get-tuple-element.37), calls=%async_computation.3 | async-start | bytes 5767168 | tf_op jit(solution)/shard_map/all_to_all | solution.py:214
  122.8 37.4 %all-to-all-done.3 = bf16[16,176,512]{2,1,0:T(8,128)(2,1)} async-done(((bf16[16,176,512]{2,1,0:T(8,128)(2,1)}), bf16[16,176,512]{2,1,0:T(8,128)(2,1)}, u32[]{:S(2)}, u32[]{:S(2)}) %all-to-all-start.3) | async-done | bytes 2883616 | tf_op jit(solution)/shard_map/all_to_all | solution.py:214
  160.2 7.6 %all-to-all-start.4 = ((bf16[16,64,512]{2,1,0:T(8,128)(2,1)}), bf16[16,64,512]{2,1,0:T(8,128)(2,1)S(1)}, u32[]{:S(2)}, u32[]{:S(2)}) async-start(bf16[16,64,512]{2,1,0:T(8,128)(2,1)} %get-tuple-element.38), calls=%async_computation.4 | async-start | bytes 2097152 | tf_op jit(solution)/shard_map/all_to_all | solution.py:214
  169.5 2.6 %collective-permute-start.21 = (bf16[128,512]{1,0:T(8,128)(2,1)S(1)}, bf16[128,512]{1,0:T(8,128)(2,1)S(1)}, u32[]{:S(2)}, u32[]{:S(2)}) collective-permute-start(bf16[128,512]{1,0:T(8,128)(2,1)S(1)} %get-tuple-element.44), channel_id=1, source_target_pairs={{0,4},{1,5},{2,6},{3,7},{4,0},{5,1},{6,2},{7,3},{8,12},{9,13},{10,... | collective-permute-start | bytes 393224 | tf_op jit(solution)/shard_map/ppermute | solution.py:201
  177.8 2.4 %convert_reduce_fusion = (f32[56,512]{1,0:T(8,128)}, f32[56,512]{1,0:T(8,128)}) fusion(bf16[16,176,512]{2,1,0:T(8,128)(2,1)} %all-to-all-done.3), kind=kLoop, calls=%fused_computation | loop fusion | flops 1777664 | bytes 2064384 | tf_op jit(solution)/shard_map/reduce_sum | solution.py:274
  183.8 2.3 %fusion = f32[512,256]{1,0:T(8,128)} fusion(f32[512,256]{1,0:T(8,128)S(1)} %convolution_bitcast_fusion, bf16[16,64,512]{2,1,0:T(8,128)(2,1)S(1)} %all-to-all-done.4, bf16[16,2,64,256]{3,2,1,0:T(8,128)(2,1)} %bitcast.15), kind=kOutput, calls=%fused_computation.4 | convolution fusion | flops 268566528 | bytes 2621440 | tf_op jit(solution)/shard_map/dot_general | solution.py:268
  (92 shorter events, 36.6 us)
Async XLA Ops:
  0.7 6.9 %collective-permute-start.7 = (bf16[128,512]{1,0:T(8,128)(2,1)}, bf16[128,512]{1,0:T(8,128)(2,1)S(1)}, u32[]{:S(2)}, u32[]{:S(2)}) collective-permute-start(bf16[128,512]{1,0:T(8,128)(2,1)} %param.17), channel_id=1, source_target_pairs={{0,2},{1,3},{2,4},{3,5},{4,6},{5,7},{6,0},{7,1},{8,10},{9,11},{10,... | collective-permute-start | bytes 393224 | tf_op jit(solution)/shard_map/ppermute | solution.py:201
  2.4 7.4 %collective-permute-start.9 = (bf16[128,512]{1,0:T(8,128)(2,1)}, bf16[128,512]{1,0:T(8,128)(2,1)S(1)}, u32[]{:S(2)}, u32[]{:S(2)}) collective-permute-start(bf16[128,512]{1,0:T(8,128)(2,1)} %param.17), channel_id=1, source_target_pairs={{0,6},{1,7},{2,0},{3,1},{4,2},{5,3},{6,4},{7,5},{8,14},{9,15},{10,... | collective-permute-start | bytes 393224 | tf_op jit(solution)/shard_map/ppermute | solution.py:201
  4.0 7.6 %collective-permute-start.8 = (bf16[128,512]{1,0:T(8,128)(2,1)}, bf16[128,512]{1,0:T(8,128)(2,1)S(1)}, u32[]{:S(2)}, u32[]{:S(2)}) collective-permute-start(bf16[128,512]{1,0:T(8,128)(2,1)} %param.17), channel_id=1, source_target_pairs={{0,4},{1,5},{2,6},{3,7},{4,0},{5,1},{6,2},{7,3},{8,12},{9,13},{10,... | collective-permute-start | bytes 393224 | tf_op jit(solution)/shard_map/ppermute | solution.py:201
  12.5 37.3 %collective-permute-start.10 = (bf16[4,128,512]{2,1,0:T(8,128)(2,1)S(1)}, bf16[4,128,512]{2,1,0:T(8,128)(2,1)S(1)}, u32[]{:S(2)}, u32[]{:S(2)}) collective-permute-start(bf16[4,128,512]{2,1,0:T(8,128)(2,1)S(1)} %pad_maximum_fusion.near_ref), channel_id=1, source_target_pairs={{0,1},{1,0},{2,3},{3,2},{4,5},{5,4},{6,7},{7,6},{8,9},{9,8},{10,11... | collective-permute-start | bytes 1572872 | tf_op jit(solution)/shard_map/ppermute | solution.py:205
  33.3 13.8 %all-to-all-start.1 = ((bf16[16,16,896]{2,1,0:T(8,128)(2,1)}), bf16[16,16,896]{2,1,0:T(8,128)(2,1)S(1)}, u32[]{:S(2)}, u32[]{:S(2)}) async-start(bf16[16,16,896]{2,1,0:T(8,128)(2,1)} %copy-done.6), calls=%async_computation.1 | async-start | bytes 917504 | tf_op jit(solution)/shard_map/all_to_all | solution.py:214
  48.5 15.4 %collective-permute-start.2 = (bf16[8,16,896]{2,1,0:T(8,128)(2,1)}, bf16[8,16,896]{2,1,0:T(8,128)(2,1)S(1)}, u32[]{:S(2)}, u32[]{:S(2)}) collective-permute-start(bf16[8,16,896]{2,1,0:T(8,128)(2,1)} %shard_map.129.refs_0_), channel_id=1, source_target_pairs={{0,4},{1,5},{2,6},{3,7},{4,0},{5,1},{6,2},{7,3},{8,12},{9,13},{10,... | collective-permute-start | bytes 688136 | tf_op jit(solution)/shard_map/ppermute | solution.py:201
  57.5 13.4 %all-to-all-start.2 = ((bf16[16,16,896]{2,1,0:T(8,128)(2,1)}), bf16[16,16,896]{2,1,0:T(8,128)(2,1)S(1)}, u32[]{:S(2)}, u32[]{:S(2)}) async-start(bf16[16,16,896]{2,1,0:T(8,128)(2,1)} %get-tuple-element.29), calls=%async_computation.2 | async-start | bytes 917504 | tf_op jit(solution)/shard_map/all_to_all | solution.py:214
  61.2 15.0 %collective-permute-start.1 = (bf16[8,16,896]{2,1,0:T(8,128)(2,1)}, bf16[8,16,896]{2,1,0:T(8,128)(2,1)S(1)}, u32[]{:S(2)}, u32[]{:S(2)}) collective-permute-start(bf16[8,16,896]{2,1,0:T(8,128)(2,1)} %shard_map.129.refs_0_), channel_id=1, source_target_pairs={{0,6},{1,7},{2,0},{3,1},{4,2},{5,3},{6,4},{7,5},{8,14},{9,15},{10,... | collective-permute-start | bytes 688136 | tf_op jit(solution)/shard_map/ppermute | solution.py:201
  63.9 14.8 %collective-permute-start.3 = (bf16[8,16,896]{2,1,0:T(8,128)(2,1)}, bf16[8,16,896]{2,1,0:T(8,128)(2,1)S(1)}, u32[]{:S(2)}, u32[]{:S(2)}) collective-permute-start(bf16[8,16,896]{2,1,0:T(8,128)(2,1)} %shard_map.129.refs_0_), channel_id=1, source_target_pairs={{0,1},{1,0},{2,3},{3,2},{4,5},{5,4},{6,7},{7,6},{8,9},{9,8},{10,11... | collective-permute-start | bytes 688136 | tf_op jit(solution)/shard_map/ppermute | solution.py:205
  63.9 16.7 %collective-permute-start = (bf16[8,16,896]{2,1,0:T(8,128)(2,1)}, bf16[8,16,896]{2,1,0:T(8,128)(2,1)}, u32[]{:S(2)}, u32[]{:S(2)}) collective-permute-start(bf16[8,16,896]{2,1,0:T(8,128)(2,1)} %shard_map.129.refs_0_), channel_id=1, source_target_pairs={{0,2},{1,3},{2,4},{3,5},{4,6},{5,7},{6,0},{7,1},{8,10},{9,11},{10,... | collective-permute-start | bytes 688136 | tf_op jit(solution)/shard_map/ppermute | solution.py:201
  63.9 16.9 %collective-permute-start.6 = (bf16[8,16,896]{2,1,0:T(8,128)(2,1)S(1)}, bf16[8,16,896]{2,1,0:T(8,128)(2,1)}, u32[]{:S(2)}, u32[]{:S(2)}) collective-permute-start(bf16[8,16,896]{2,1,0:T(8,128)(2,1)S(1)} %collective-permute-done.2.refs_3_), channel_id=1, source_target_pairs={{0,1},{1,0},{2,3},{3,2},{4,5},{5,4},{6,7},{7,6},{8,9},{9,8},{10,11... | collective-permute-start | bytes 688136 | tf_op jit(solution)/shard_map/ppermute | solution.py:205
  71.9 41.6 %all-to-all-start.5 = ((bf16[16,128,256]{2,1,0:T(8,128)(2,1)}), bf16[16,128,256]{2,1,0:T(8,128)(2,1)}, u32[]{:S(2)}, u32[]{:S(2)}) async-start(bf16[16,128,256]{2,1,0:T(8,128)(2,1)} %get-tuple-element.40), calls=%async_computation.5 | async-start | bytes 2097152 | tf_op jit(solution)/shard_map/all_to_all | solution.py:214
  76.3 10.0 %collective-permute-start.13 = (bf16[8,16,896]{2,1,0:T(8,128)(2,1)S(1)}, bf16[8,16,896]{2,1,0:T(8,128)(2,1)S(1)}, u32[]{:S(2)}, u32[]{:S(2)}) collective-permute-start(bf16[8,16,896]{2,1,0:T(8,128)(2,1)S(1)} %shard_map.132.refs_0_), channel_id=1, source_target_pairs={{0,4},{1,5},{2,6},{3,7},{4,0},{5,1},{6,2},{7,3},{8,12},{9,13},{10,... | collective-permute-start | bytes 688136 | tf_op jit(solution)/shard_map/ppermute | solution.py:201
  78.7 12.0 %collective-permute-start.12 = (bf16[8,16,896]{2,1,0:T(8,128)(2,1)S(1)}, bf16[8,16,896]{2,1,0:T(8,128)(2,1)S(1)}, u32[]{:S(2)}, u32[]{:S(2)}) collective-permute-start(bf16[8,16,896]{2,1,0:T(8,128)(2,1)S(1)} %shard_map.132.refs_0_), channel_id=1, source_target_pairs={{0,6},{1,7},{2,0},{3,1},{4,2},{5,3},{6,4},{7,5},{8,14},{9,15},{10,... | collective-permute-start | bytes 688136 | tf_op jit(solution)/shard_map/ppermute | solution.py:201
  80.6 10.2 %collective-permute-start.11 = (bf16[8,16,896]{2,1,0:T(8,128)(2,1)S(1)}, bf16[8,16,896]{2,1,0:T(8,128)(2,1)S(1)}, u32[]{:S(2)}, u32[]{:S(2)}) collective-permute-start(bf16[8,16,896]{2,1,0:T(8,128)(2,1)S(1)} %shard_map.132.refs_0_), channel_id=1, source_target_pairs={{0,2},{1,3},{2,4},{3,5},{4,6},{5,7},{6,0},{7,1},{8,10},{9,11},{10,... | collective-permute-start | bytes 688136 | tf_op jit(solution)/shard_map/ppermute | solution.py:201
  80.8 10.5 %collective-permute-start.4 = (bf16[8,16,896]{2,1,0:T(8,128)(2,1)}, bf16[8,16,896]{2,1,0:T(8,128)(2,1)S(1)}, u32[]{:S(2)}, u32[]{:S(2)}) collective-permute-start(bf16[8,16,896]{2,1,0:T(8,128)(2,1)} %collective-permute-done.refs_1_), channel_id=1, source_target_pairs={{0,1},{1,0},{2,3},{3,2},{4,5},{5,4},{6,7},{7,6},{8,9},{9,8},{10,11... | collective-permute-start | bytes 688136 | tf_op jit(solution)/shard_map/ppermute | solution.py:205
  80.8 23.2 %collective-permute-start.14 = (bf16[8,16,896]{2,1,0:T(8,128)(2,1)S(1)}, bf16[8,16,896]{2,1,0:T(8,128)(2,1)S(1)}, u32[]{:S(2)}, u32[]{:S(2)}) collective-permute-start(bf16[8,16,896]{2,1,0:T(8,128)(2,1)S(1)} %shard_map.132.refs_0_), channel_id=1, source_target_pairs={{0,1},{1,0},{2,3},{3,2},{4,5},{5,4},{6,7},{7,6},{8,9},{9,8},{10,11... | collective-permute-start | bytes 688136 | tf_op jit(solution)/shard_map/ppermute | solution.py:205
  86.3 17.6 %collective-permute-start.17 = (bf16[8,16,896]{2,1,0:T(8,128)(2,1)S(1)}, bf16[8,16,896]{2,1,0:T(8,128)(2,1)S(1)}, u32[]{:S(2)}, u32[]{:S(2)}) collective-permute-start(bf16[8,16,896]{2,1,0:T(8,128)(2,1)S(1)} %collective-permute-done.13.refs_3_), channel_id=1, source_target_pairs={{0,1},{1,0},{2,3},{3,2},{4,5},{5,4},{6,7},{7,6},{8,9},{9,8},{10,11... | collective-permute-start | bytes 688136 | tf_op jit(solution)/shard_map/ppermute | solution.py:205
  90.7 13.2 %collective-permute-start.16 = (bf16[8,16,896]{2,1,0:T(8,128)(2,1)S(1)}, bf16[8,16,896]{2,1,0:T(8,128)(2,1)S(1)}, u32[]{:S(2)}, u32[]{:S(2)}) collective-permute-start(bf16[8,16,896]{2,1,0:T(8,128)(2,1)S(1)} %collective-permute-done.12.refs_2_), channel_id=1, source_target_pairs={{0,1},{1,0},{2,3},{3,2},{4,5},{5,4},{6,7},{7,6},{8,9},{9,8},{10,11... | collective-permute-start | bytes 688136 | tf_op jit(solution)/shard_map/ppermute | solution.py:205
  90.8 13.2 %collective-permute-start.15 = (bf16[8,16,896]{2,1,0:T(8,128)(2,1)S(1)}, bf16[8,16,896]{2,1,0:T(8,128)(2,1)S(1)}, u32[]{:S(2)}, u32[]{:S(2)}) collective-permute-start(bf16[8,16,896]{2,1,0:T(8,128)(2,1)S(1)} %collective-permute-done.11.refs_1_), channel_id=1, source_target_pairs={{0,1},{1,0},{2,3},{3,2},{4,5},{5,4},{6,7},{7,6},{8,9},{9,8},{10,11... | collective-permute-start | bytes 688136 | tf_op jit(solution)/shard_map/ppermute | solution.py:205
  113.5 46.7 %all-to-all-start.3 = ((bf16[16,176,512]{2,1,0:T(8,128)(2,1)}), bf16[16,176,512]{2,1,0:T(8,128)(2,1)}, u32[]{:S(2)}, u32[]{:S(2)}) async-start(bf16[16,176,512]{2,1,0:T(8,128)(2,1)} %get-tuple-element.37), calls=%async_computation.3 | async-start | bytes 5767168 | tf_op jit(solution)/shard_map/all_to_all | solution.py:214
  160.2 23.6 %all-to-all-start.4 = ((bf16[16,64,512]{2,1,0:T(8,128)(2,1)}), bf16[16,64,512]{2,1,0:T(8,128)(2,1)S(1)}, u32[]{:S(2)}, u32[]{:S(2)}) async-start(bf16[16,64,512]{2,1,0:T(8,128)(2,1)} %get-tuple-element.38), calls=%async_computation.4 | async-start | bytes 2097152 | tf_op jit(solution)/shard_map/all_to_all | solution.py:214
  167.9 7.6 %collective-permute-start.19 = (bf16[128,512]{1,0:T(8,128)(2,1)S(1)}, bf16[128,512]{1,0:T(8,128)(2,1)S(1)}, u32[]{:S(2)}, u32[]{:S(2)}) collective-permute-start(bf16[128,512]{1,0:T(8,128)(2,1)S(1)} %get-tuple-element.43), channel_id=1, source_target_pairs={{0,2},{1,3},{2,4},{3,5},{4,6},{5,7},{6,0},{7,1},{8,10},{9,11},{10,... | collective-permute-start | bytes 393224 | tf_op jit(solution)/shard_map/ppermute | solution.py:201
  169.5 7.3 %collective-permute-start.21 = (bf16[128,512]{1,0:T(8,128)(2,1)S(1)}, bf16[128,512]{1,0:T(8,128)(2,1)S(1)}, u32[]{:S(2)}, u32[]{:S(2)}) collective-permute-start(bf16[128,512]{1,0:T(8,128)(2,1)S(1)} %get-tuple-element.44), channel_id=1, source_target_pairs={{0,4},{1,5},{2,6},{3,7},{4,0},{5,1},{6,2},{7,3},{8,12},{9,13},{10,... | collective-permute-start | bytes 393224 | tf_op jit(solution)/shard_map/ppermute | solution.py:201
  (23 other events, 281.0 us)

commit v3 on v2

--- a/solution.py
+++ b/solution.py
@@ -11,7 +11,7 @@
 HD = 128
 BF = jnp.bfloat16
 F32 = jnp.float32
-VMEM_LIMIT = 40 * 1024 * 1024
+VMEM_LIMIT = 60 * 1024 * 1024
 
 
 def mm(a, b, ca, cb):
@@ -23,6 +23,7 @@
 
 
 ANY = pl.BlockSpec(memory_space=pl.ANY)
+HBM = pl.BlockSpec(memory_space=pltpu.HBM)
 VM = pl.BlockSpec(memory_space=pltpu.VMEM)
 SM = pl.BlockSpec(memory_space=pltpu.SMEM)
 
@@ -45,25 +46,39 @@
     return pl.pallas_call(
         functools.partial(pick_kernel, counts=counts),
         out_shape=[jax.ShapeDtypeStruct((n, *item), src.dtype) for n in counts],
-        in_specs=[SM, ANY],
+        in_specs=[SM, HBM],
         out_specs=[ANY] * len(counts),
         scratch_shapes=[pltpu.SemaphoreType.DMA((sum(counts),))],
         compiler_params=params(),
     )(rows, src)
 
 
-def prep_kernel(at_ref, near_ref, far_ref, wo_ref, q_ref, wk_ref, wv_ref, dm_ref, qt_ref, dt_ref, gc_ref):
+def stream_out_weight(wo_ref, w_ref, sem):
+    step = wo_ref.shape[0] // sem.shape[0]
+    loads = [
+        pltpu.make_async_copy(wo_ref.at[pl.ds(k * step, step)], w_ref.at[pl.ds(k * step, step)], sem.at[k])
+        for k in range(sem.shape[0])
+    ]
+    for load in loads:
+        load.start()
+    return loads
+
+
+def prep_kernel(at_ref, near_ref, far_ref, wo_ref, q_ref, wk_ref, wv_ref, dm_ref, qt_ref, dt_ref, gc_ref, w_ref, sem):
     chips, rows, width = near_ref.shape
     groups = qt_ref.shape[0]
     part = rows // groups
     cuts = gc_ref.shape[0] // (2 * chips)
     piece = width // cuts
+    loads = stream_out_weight(wo_ref, w_ref, sem)
     acc = jnp.zeros((rows, width), F32)
+    for load in loads:
+        load.wait()
     for core, g_ref in enumerate((near_ref, far_ref)):
         for s in range(chips):
             j = lax.rem(at_ref[0] + chips - s, chips) * 2 + lax.rem(at_ref[1] + core, 2)
             cols = pl.ds(pl.multiple_of(j * width, width), width)
-            acc += mm(g_ref[s], wo_ref[:, cols], 1, 1)
+            acc += mm(g_ref[s], w_ref[:, cols], 1, 1)
             for p in range(cuts):
                 gc_ref[j * cuts + p] = g_ref[s, :, p * piece : (p + 1) * piece]
     dm = acc.astype(BF)
@@ -90,8 +105,9 @@
             jax.ShapeDtypeStruct(tall, BF),
             jax.ShapeDtypeStruct((db_count, rows, 2 * chips * width // db_count), BF),
         ],
-        in_specs=[SM] + [VM] * 6,
+        in_specs=[SM, VM, VM, HBM, VM, VM, VM],
         out_specs=[VM] * 4,
+        scratch_shapes=[pltpu.VMEM(wo.shape, BF), pltpu.SemaphoreType.DMA((4,))],
         compiler_params=params(),
         cost_estimate=pl.CostEstimate(flops=1_000_000_000, bytes_accessed=10_000_000, transcendentals=0),
     )(at, near, far, wo, q, wk, wv)
@@ -102,9 +118,9 @@
     qt_ref, dt_ref, wk_ref, wv_ref, wo_ref = refs[:5]
     refs = refs[5:]
     if last:
-        q_ref, dm_ref, t0_ref, u0_ref, send_ref, keep_ref, give_ref, gq_ref, x_ref, sem = refs
+        q_ref, dm_ref, t0_ref, u0_ref, send_ref, keep_ref, give_ref, gq_ref, x_ref, w_ref, sem, w_sem = refs
     else:
-        send_ref, keep_ref, give_ref, gq_ref, t_ref, u_ref, x_ref, sem = refs
+        send_ref, keep_ref, give_ref, gq_ref, t_ref, u_ref, x_ref, w_ref, sem, w_sem = refs
     slots, sub, enc = x_refs[0].shape
     copies = [
         pltpu.make_async_copy(x_refs[p], x_ref.at[pl.ds(p * slots, slots)], sem.at[p])
@@ -114,6 +130,7 @@
         copy.start()
     for copy in copies:
         copy.wait()
+    loads = stream_out_weight(wo_ref, w_ref, w_sem)
     factor = 1.0 / math.sqrt(HD)
     x = x_ref[...].reshape(pieces * slots * sub, enc)
     keys = x.shape[0]
@@ -132,6 +149,8 @@
         ],
         axis=1,
     )
+    for load in loads:
+        load.wait()
     db_count = send_ref.shape[0]
     for i in range(db_count):
         send_ref[i, :part] = mixed
@@ -140,7 +159,7 @@
         for step in range(chips):
             j = lax.rem(at_ref[0] + step, chips) * 2 + lax.rem(at_ref[1] + core, 2)
             cols = pl.ds(pl.multiple_of(j * width, width), width)
-            block_ref[step] = mm(mixed, wo_ref[:, cols], 1, 0).astype(BF)
+            block_ref[step] = mm(mixed, w_ref[:, cols], 1, 0).astype(BF)
     d = mm(dt_ref[c], x, 1, 1)
     inner = jnp.sum(probs * d, axis=-1, keepdims=True)
     ds = (probs * (d - inner) * factor).astype(BF)
@@ -185,11 +204,13 @@
     return pl.pallas_call(
         functools.partial(attn_kernel, c=c, pieces=len(xs), last=last),
         out_shape=out_shape,
-        in_specs=[SM, SM] + [ANY] * len(xs) + [VM] * (5 + len(more)),
+        in_specs=[SM, SM] + [ANY] * len(xs) + [VM] * 4 + [HBM] + [VM] * len(more),
         out_specs=[VM] * len(out_shape),
         scratch_shapes=[
             pltpu.VMEM((len(xs) * slots, sub, enc), BF),
+            pltpu.VMEM(wo.shape, BF),
             pltpu.SemaphoreType.DMA((len(xs),)),
+            pltpu.SemaphoreType.DMA((4,)),
         ],
         compiler_params=params(),
         cost_estimate=pl.CostEstimate(flops=4_000_000_000, bytes_accessed=12_000_000, transcendentals=262144),
@@ -232,19 +253,26 @@
     wanted = jnp.sum(jnp.where(nbr_owner[None] == owner_ids, nbr_row[None], 0), axis=2)
     incoming = exchange(wanted, "db")
     steps = ring_steps(head_count)
-    near = [grad_out] + [along(grad_out, s, head_count) for s in steps]
+    tables = pick(incoming.T.reshape(-1), encodings, (db_count,) * groups)
+    near = [grad_out] + [along(after(grad_out, wanted), s, head_count) for s in steps]
+    near = lax.optimization_barrier((*near, *tables))[: len(near)]
     near = jnp.stack([near[([0] + steps).index(s)] for s in range(chips)])
     far = swap(near, head_count)
-    tables = pick(incoming.T.reshape(-1), encodings, (db_count,) * groups)
     dm, qt, dt, grad_cols = prep(at, near, far, w_out, queries, w_key, w_value, groups, db_count)
-    spread, token = [], None
+    ring, tokens = [], []
     for c in range(groups):
-        table = tables[c] if c == 0 else after(tables[c], token, dm)
-        received = exchange(table, "db")
-        (mine,) = pick(nbr_owner[c], received, (slot_count,))
-        token = mine
-        pieces = [mine] + [along(mine, s, head_count) for s in steps]
-        spread.append(pieces + [swap(v, head_count) for v in pieces])
+        received = exchange(tables[c] if c == 0 else after(tables[c], *tokens), "db")
+        if c == 0:
+            received = after(received, dm)
+        else:
+            received, *ring[-1] = lax.optimization_barrier((received, *ring[-1]))
+        (token,) = pick(nbr_owner[c], received, (slot_count,))
+        tokens.append(token)
+        ring.append([token] + [along(token, s, head_count) for s in steps])
+    token = tokens[-1]
+    spread = []
+    for pieces in ring:
+        spread.append([*pieces, *(swap(v, head_count) for v in pieces)])
     grad_tok = exchange(after(grad_cols, token), "db")
     sent, keep, give, grad_q, kept = [], [], [], [], []
     for c in range(groups):
@@ -253,7 +281,8 @@
         m, k, g, gq, *kept = attn(
             at, nbr_count, spread[c], qt, dt, w_key, w_value, w_out, c, db_count, head_count, extra
         )
-        sent.append(exchange(m, "db"))
+        hold = (grad_tok, *ring[-1]) if c == 0 else sent
+        sent.append(exchange(after(m, *hold), "db"))
         keep.append(k)
         give.append(g)
         grad_q.append(gq)

time: 187 us -> 204 us (1.091)
  Pallas kernels: 24.7 us -> 75.3 us
  waiting for transfers between devices: 76.3 us -> 53.1 us
  local copies, waits for them, and re-layouts: 12.2 us -> 6.19 us
  starting transfers between devices: 46.8 us -> 43 us
    pallas_call x3, Pallas kernels: 4.45 us -> 47.4 us  [pick(): pl.pallas_call(functools.partial(pick_kernel, counts=counts), out_shape=[...]
    all_to_all x5, waiting for transfers between devices: 55.8 us -> 32.9 us  [exchange(): return lax.all_to_all(x, axis, split_axis=0, concat_axis=0, tiled=True)]
    unnamed x40 -> x58, local copies, waits for them, and re-layouts: 11.9 us -> 4.89 us
    pallas_call x1, Pallas kernels: 3.6 us -> 7.67 us  [prep(): pl.pallas_call(prep_kernel, out_shape=[jax.ShapeDtypeStruct((rows, width)...]
    pallas_call x2, Pallas kernels: 16.6 us -> 20.1 us  [attn(): pl.pallas_call(functools.partial(attn_kernel, c=c, pieces=len(xs), last=l...]
    ppermute x12, starting transfers between devices: 18.6 us -> 16.1 us  [along(): lax.ppermute(v, 'head', [(i, (i // 2 + step) % chips * 2 + i % 2) for i i...]
  transfers between devices with their start and end apart: 27 -> 27, of which waited for: 13 -> 17; matrix products, arithmetic and copies ran while one was open for 4% -> 3% of each run, Pallas kernels for 13% -> 28%
where the time goes in v3:
time: 204 us
  Pallas kernels  75.3 us (37%)
  waiting for transfers between devices  53.1 us (26%)
  starting transfers between devices  43 us (21%)
  blocking collectives  15.2 us (7%)
  other arithmetic  6.82 us (3%)
  local copies, waits for them, and re-layouts  6.19 us (3%)
  matrix products  2.79 us (1%)
    pallas_call x3, Pallas kernels, pick(): pl.pallas_call(functools.partial(pick_kernel, counts=counts), out_shape=[...  47.4 us
    all_to_all x5, waiting for transfers between devices, exchange(): return lax.all_to_all(x, axis, split_axis=0, concat_axis=0, tiled=True)  32.9 us
    all_to_all x5, starting transfers between devices, exchange(): return lax.all_to_all(x, axis, split_axis=0, concat_axis=0, tiled=True)  24.6 us
    pallas_call x2, Pallas kernels, attn(): pl.pallas_call(functools.partial(attn_kernel, c=c, pieces=len(xs), last=l...  20.1 us
    ppermute x12, waiting for transfers between devices, along(): lax.ppermute(v, 'head', [(i, (i // 2 + step) % chips * 2 + i % 2) for i i...  16.9 us
    ppermute x12, starting transfers between devices, along(): lax.ppermute(v, 'head', [(i, (i // 2 + step) % chips * 2 + i % 2) for i i...  16.1 us
    all_to_all x1, blocking collectives, exchange(): return lax.all_to_all(x, axis, split_axis=0, concat_axis=0, tiled=True)  15.2 us
    pallas_call x1, Pallas kernels, prep(): pl.pallas_call(prep_kernel, out_shape=[jax.ShapeDtypeStruct((rows, width)...  7.67 us
  transfers between devices with their start and end apart: 27, of which 17 were waited for; matrix products, arithmetic and copies ran while one was open for 3% of the time, Pallas kernels for 28%

profile of v3, /device:TPU:0, one launch (start us, length us, event | category | flops | bytes accessed | tf_op | source)
XLA Modules:
  0.0 203.5 jit_solution(858590486177145810)
XLA Ops:
  1.5 3.4 %collective-permute-start.2 = (bf16[128,512]{1,0:T(8,128)(2,1)}, bf16[128,512]{1,0:T(8,128)(2,1)S(1)}, u32[]{:S(2)}, u32[]{:S(2)}) collective-permute-start(bf16[128,512]{1,0:T(8,128)(2,1)} %param.17), channel_id=1, source_target_pairs={{0,4},{1,5},{2,6},{3,7},{4,0},{5,1},{6,2},{7,3},{8,12},{9,13},{10,... | collective-permute-start | bytes 393224 | tf_op jit(solution)/shard_map/ppermute | solution.py:222
  6.9 15.2 %all_to_all.37 = s32[16,1,2]{2,1,0:T(1,128)S(1)} all-to-all(s32[16,1,2]{2,1,0:T(1,128)S(1)} %copy.20), channel_id=1, replica_groups=mesh['db'=16,'head'=8] {'db'}, dimensions={0} | all-to-all | bytes 256 | tf_op jit(solution)/shard_map/all_to_all | solution.py:235
  22.8 29.9 %shard_map.128 = (bf16[16,16,896]{2,1,0:T(8,128)(2,1)}, bf16[16,16,896]{2,1,0:T(8,128)(2,1)}) custom-call(s32[32]{0:T(128)} %reshape.22.rows_ref, bf16[64,16,896]{2,1,0:T(8,128)(2,1)} %src_ref.1), custom_call_target="tpu_custom_call" | custom-call | tf_op jit(solution)/shard_map/pallas_call | solution.py:46
  53.8 3.6 %all-to-all-start.1 = ((bf16[16,16,896]{2,1,0:T(8,128)(2,1)}), bf16[16,16,896]{2,1,0:T(8,128)(2,1)S(1)}, u32[]{:S(2)}, u32[]{:S(2)}) async-start(bf16[16,16,896]{2,1,0:T(8,128)(2,1)} %get-tuple-element.37), calls=%async_computation.1 | async-start | bytes 917504 | tf_op jit(solution)/shard_map/all_to_all | solution.py:235
  59.3 7.7 %shard_map.129 = (bf16[128,512]{1,0:T(8,128)(2,1)}, bf16[2,256,896]{2,1,0:T(8,128)(2,1)}, bf16[2,256,896]{2,1,0:T(8,128)(2,1)}, bf16[16,128,256]{2,1,0:T(8,128)(2,1)}) custom-call(s32[2]{0:T(128)} %pad_add_fusion.at_ref, bf16[4,128,512]{2,1,0:T(8,128)(2,1)} %copy-done, bf16[4,128,512]{2,1,0:T(8,128)(2,1)} %copy-done.7, bf16[512,4096]{1,0:T(8,128)(2,1)} %refs_12_.3, ...), custom_call_target="tpu_custom_call" | custom-call | flops 1000000000 | bytes 10000000 | tf_op jit(solution)/shard_map/pallas_call | solution.py:100
  67.0 2.1 %all-to-all-done.1.src_ref = bf16[16,16,896]{2,1,0:T(8,128)(2,1)S(1)} async-done(((bf16[16,16,896]{2,1,0:T(8,128)(2,1)}), bf16[16,16,896]{2,1,0:T(8,128)(2,1)S(1)}, u32[]{:S(2)}, u32[]{:S(2)}) %all-to-all-start.1) | async-done | bytes 458784 | tf_op jit(solution)/shard_map/all_to_all | solution.py:235
  69.9 8.8 %shard_map.130.refs_0_ = bf16[8,16,896]{2,1,0:T(8,128)(2,1)} custom-call(s32[8]{0:T(128)} %get-tuple-element.72.rows_ref, bf16[16,16,896]{2,1,0:T(8,128)(2,1)} %copy-done.2), custom_call_target="tpu_custom_call" | custom-call | tf_op jit(solution)/shard_map/pallas_call | solution.py:46
  78.7 5.2 %all-to-all-start.2 = ((bf16[16,16,896]{2,1,0:T(8,128)(2,1)}), bf16[16,16,896]{2,1,0:T(8,128)(2,1)S(1)}, u32[]{:S(2)}, u32[]{:S(2)}) async-start(bf16[16,16,896]{2,1,0:T(8,128)(2,1)} %get-tuple-element.45), calls=%async_computation.2 | async-start | bytes 917504 | tf_op jit(solution)/shard_map/all_to_all | solution.py:235
  84.7 2.6 %collective-permute-start.5 = (bf16[8,16,896]{2,1,0:T(8,128)(2,1)}, bf16[8,16,896]{2,1,0:T(8,128)(2,1)S(1)}, u32[]{:S(2)}, u32[]{:S(2)}) collective-permute-start(bf16[8,16,896]{2,1,0:T(8,128)(2,1)} %shard_map.130.refs_0_), channel_id=1, source_target_pairs={{0,6},{1,7},{2,0},{3,1},{4,2},{5,3},{6,4},{7,5},{8,14},{9,15},{10,... | collective-permute-start | bytes 688136 | tf_op jit(solution)/shard_map/ppermute | solution.py:222
  87.3 6.8 %collective-permute-done.6.refs_3_ = bf16[8,16,896]{2,1,0:T(8,128)(2,1)S(1)} collective-permute-done((bf16[8,16,896]{2,1,0:T(8,128)(2,1)}, bf16[8,16,896]{2,1,0:T(8,128)(2,1)S(1)}, u32[]{:S(2)}, u32[]{:S(2)}) %collective-permute-start.6) | collective-permute-done | bytes 229408 | tf_op jit(solution)/shard_map/ppermute | solution.py:222
  94.2 3.5 %collective-permute-done.5.refs_2_ = bf16[8,16,896]{2,1,0:T(8,128)(2,1)S(1)} collective-permute-done((bf16[8,16,896]{2,1,0:T(8,128)(2,1)}, bf16[8,16,896]{2,1,0:T(8,128)(2,1)S(1)}, u32[]{:S(2)}, u32[]{:S(2)}) %collective-permute-start.5) | collective-permute-done | bytes 229408 | tf_op jit(solution)/shard_map/ppermute | solution.py:222
  98.8 8.8 %shard_map.132.refs_0_ = bf16[8,16,896]{2,1,0:T(8,128)(2,1)} custom-call(s32[8]{0:T(128)} %get-tuple-element.73.rows_ref, bf16[16,16,896]{2,1,0:T(8,128)(2,1)} %copy-done.1), custom_call_target="tpu_custom_call" | custom-call | tf_op jit(solution)/shard_map/pallas_call | solution.py:46
  107.6 6.9 %all-to-all-start.3 = ((bf16[16,128,256]{2,1,0:T(8,128)(2,1)}), bf16[16,128,256]{2,1,0:T(8,128)(2,1)S(1)}, u32[]{:S(2)}, u32[]{:S(2)}) async-start(bf16[16,128,256]{2,1,0:T(8,128)(2,1)} %get-tuple-element.64), calls=%async_computation.3 | async-start | bytes 2097152 | tf_op jit(solution)/shard_map/all_to_all | solution.py:235
  117.0 2.0 collective-permute-start.12
  119.9 9.5 %shard_map.131 = (bf16[16,64,512]{2,1,0:T(8,128)(2,1)}, bf16[4,64,512]{2,1,0:T(8,128)(2,1)}, bf16[4,64,512]{2,1,0:T(8,128)(2,1)}, bf16[64,512]{1,0:T(8,128)(2,1)...) custom-call(s32[2]{0:T(128)} %pad_add_fusion.at_ref, s32[2]{0:T(128)} %count_ref.3, ...), custom_call_target="tpu_custom_call" | custom-call | flops 4000000000 | bytes 12000000 | tf_op jit(solution)/shard_map/pallas_call | solution.py:204
  129.9 2.0 all-to-all-done.3
  131.9 5.2 %all-to-all-start.4 = ((bf16[16,64,512]{2,1,0:T(8,128)(2,1)}), bf16[16,64,512]{2,1,0:T(8,128)(2,1)S(1)}, u32[]{:S(2)}, u32[]{:S(2)}) async-start(bf16[16,64,512]{2,1,0:T(8,128)(2,1)} %get-tuple-element.65), calls=%async_computation.4 | async-start | bytes 2097152 | tf_op jit(solution)/shard_map/all_to_all | solution.py:235
  140.4 10.7 %shard_map.133 = (bf16[16,176,512]{2,1,0:T(8,128)(2,1)}, bf16[4,64,512]{2,1,0:T(8,128)(2,1)}, bf16[4,64,512]{2,1,0:T(8,128)(2,1)}, bf16[64,512]{1,0:T(8,128)(2,1)}) custom-call(s32[2]{0:T(128)} %pad_add_fusion.at_ref, s32[2]{0:T(128)} %count_ref.3, bf16[8,16,896]{2,1,0:T(8,128)(2,1)} %shard_map.132.refs_0_, bf16[8,16,896]{2,1,0:T(8,128)(2,1)} %copy-done.17, ...), custom_call_target="tpu_custom_call" | custom-call | flops 4000000000 | bytes 12000000 | tf_op jit(solution)/shard_map/pallas_call | solution.py:204
  151.1 4.0 %all-to-all-done.4 = bf16[16,64,512]{2,1,0:T(8,128)(2,1)S(1)} async-done(((bf16[16,64,512]{2,1,0:T(8,128)(2,1)}), bf16[16,64,512]{2,1,0:T(8,128)(2,1)S(1)}, u32[]{:S(2)}, u32[]{:S(2)}) %all-to-all-start.4) | async-done | bytes 1048608 | tf_op jit(solution)/shard_map/all_to_all | solution.py:235
  156.1 3.7 %all-to-all-start.5 = ((bf16[16,176,512]{2,1,0:T(8,128)(2,1)}), bf16[16,176,512]{2,1,0:T(8,128)(2,1)S(1)}, u32[]{:S(2)}, u32[]{:S(2)}) async-start(bf16[16,176,512]{2,1,0:T(8,128)(2,1)} %get-tuple-element.66), calls=%async_computation.5 | async-start | bytes 5767168 | tf_op jit(solution)/shard_map/all_to_all | solution.py:235
  164.8 2.9 %collective-permute-start.21 = (bf16[128,512]{1,0:T(8,128)(2,1)S(1)}, bf16[128,512]{1,0:T(8,128)(2,1)S(1)}, u32[]{:S(2)}, u32[]{:S(2)}) collective-permute-start(bf16[128,512]{1,0:T(8,128)(2,1)S(1)} %get-tuple-element.70), channel_id=1, source_target_pairs={{0,4},{1,5},{2,6},{3,7},{4,0},{5,1},{6,2},{7,3},{8,12},{9,13},{10,... | collective-permute-start | bytes 393224 | tf_op jit(solution)/shard_map/ppermute | solution.py:222
  168.5 2.6 %collective-permute-done.19 = bf16[128,512]{1,0:T(8,128)(2,1)S(1)} collective-permute-done((bf16[128,512]{1,0:T(8,128)(2,1)S(1)}, bf16[128,512]{1,0:T(8,128)(2,1)S(1)}, u32[]{:S(2)}, u32[]{:S(2)}) %collective-permute-start.19) | collective-permute-done | bytes 131104 | tf_op jit(solution)/shard_map/ppermute | solution.py:222
  171.2 2.9 %collective-permute-done.21 = bf16[128,512]{1,0:T(8,128)(2,1)S(1)} collective-permute-done((bf16[128,512]{1,0:T(8,128)(2,1)S(1)}, bf16[128,512]{1,0:T(8,128)(2,1)S(1)}, u32[]{:S(2)}, u32[]{:S(2)}) %collective-permute-start.21) | collective-permute-done | bytes 131104 | tf_op jit(solution)/shard_map/ppermute | solution.py:222
  174.9 24.8 %all-to-all-done.5 = bf16[16,176,512]{2,1,0:T(8,128)(2,1)S(1)} async-done(((bf16[16,176,512]{2,1,0:T(8,128)(2,1)}), bf16[16,176,512]{2,1,0:T(8,128)(2,1)S(1)}, u32[]{:S(2)}, u32[]{:S(2)}) %all-to-all-start.5) | async-done | bytes 2883616 | tf_op jit(solution)/shard_map/all_to_all | solution.py:235
  (110 shorter events, 27.7 us)
Async XLA Ops:
  1.5 51.2 %collective-permute-start.2 = (bf16[128,512]{1,0:T(8,128)(2,1)}, bf16[128,512]{1,0:T(8,128)(2,1)S(1)}, u32[]{:S(2)}, u32[]{:S(2)}) collective-permute-start(bf16[128,512]{1,0:T(8,128)(2,1)} %param.17), channel_id=1, source_target_pairs={{0,4},{1,5},{2,6},{3,7},{4,0},{5,1},{6,2},{7,3},{8,12},{9,13},{10,... | collective-permute-start | bytes 393224 | tf_op jit(solution)/shard_map/ppermute | solution.py:222
  4.8 47.9 %collective-permute-start.1 = (bf16[128,512]{1,0:T(8,128)(2,1)}, bf16[128,512]{1,0:T(8,128)(2,1)S(1)}, u32[]{:S(2)}, u32[]{:S(2)}) collective-permute-start(bf16[128,512]{1,0:T(8,128)(2,1)} %param.17), channel_id=1, source_target_pairs={{0,6},{1,7},{2,0},{3,1},{4,2},{5,3},{6,4},{7,5},{8,14},{9,15},{10,... | collective-permute-start | bytes 393224 | tf_op jit(solution)/shard_map/ppermute | solution.py:222
  5.9 46.9 %collective-permute-start = (bf16[128,512]{1,0:T(8,128)(2,1)}, bf16[128,512]{1,0:T(8,128)(2,1)S(1)}, u32[]{:S(2)}, u32[]{:S(2)}) collective-permute-start(bf16[128,512]{1,0:T(8,128)(2,1)} %param.17), channel_id=1, source_target_pairs={{0,2},{1,3},{2,4},{3,5},{4,6},{5,7},{6,0},{7,1},{8,10},{9,11},{10,... | collective-permute-start | bytes 393224 | tf_op jit(solution)/shard_map/ppermute | solution.py:222
  53.7 4.8 %collective-permute-start.3 = (bf16[4,128,512]{2,1,0:T(8,128)(2,1)S(1)}, bf16[4,128,512]{2,1,0:T(8,128)(2,1)S(1)}, u32[]{:S(2)}, u32[]{:S(2)}) collective-permute-start(bf16[4,128,512]{2,1,0:T(8,128)(2,1)S(1)} %pad_maximum_fusion.near_ref), channel_id=1, source_target_pairs={{0,1},{1,0},{2,3},{3,2},{4,5},{5,4},{6,7},{7,6},{8,9},{9,8},{10,11... | collective-permute-start | bytes 1572872 | tf_op jit(solution)/shard_map/ppermute | solution.py:226
  53.8 15.2 %all-to-all-start.1 = ((bf16[16,16,896]{2,1,0:T(8,128)(2,1)}), bf16[16,16,896]{2,1,0:T(8,128)(2,1)S(1)}, u32[]{:S(2)}, u32[]{:S(2)}) async-start(bf16[16,16,896]{2,1,0:T(8,128)(2,1)} %get-tuple-element.37), calls=%async_computation.1 | async-start | bytes 917504 | tf_op jit(solution)/shard_map/all_to_all | solution.py:235
  78.7 19.4 %all-to-all-start.2 = ((bf16[16,16,896]{2,1,0:T(8,128)(2,1)}), bf16[16,16,896]{2,1,0:T(8,128)(2,1)S(1)}, u32[]{:S(2)}, u32[]{:S(2)}) async-start(bf16[16,16,896]{2,1,0:T(8,128)(2,1)} %get-tuple-element.45), calls=%async_computation.2 | async-start | bytes 917504 | tf_op jit(solution)/shard_map/all_to_all | solution.py:235
  83.9 10.3 %collective-permute-start.6 = (bf16[8,16,896]{2,1,0:T(8,128)(2,1)}, bf16[8,16,896]{2,1,0:T(8,128)(2,1)S(1)}, u32[]{:S(2)}, u32[]{:S(2)}) collective-permute-start(bf16[8,16,896]{2,1,0:T(8,128)(2,1)} %shard_map.130.refs_0_), channel_id=1, source_target_pairs={{0,4},{1,5},{2,6},{3,7},{4,0},{5,1},{6,2},{7,3},{8,12},{9,13},{10,... | collective-permute-start | bytes 688136 | tf_op jit(solution)/shard_map/ppermute | solution.py:222
  84.7 13.0 %collective-permute-start.5 = (bf16[8,16,896]{2,1,0:T(8,128)(2,1)}, bf16[8,16,896]{2,1,0:T(8,128)(2,1)S(1)}, u32[]{:S(2)}, u32[]{:S(2)}) collective-permute-start(bf16[8,16,896]{2,1,0:T(8,128)(2,1)} %shard_map.130.refs_0_), channel_id=1, source_target_pairs={{0,6},{1,7},{2,0},{3,1},{4,2},{5,3},{6,4},{7,5},{8,14},{9,15},{10,... | collective-permute-start | bytes 688136 | tf_op jit(solution)/shard_map/ppermute | solution.py:222
  87.3 10.7 %collective-permute-start.4 = (bf16[8,16,896]{2,1,0:T(8,128)(2,1)}, bf16[8,16,896]{2,1,0:T(8,128)(2,1)S(1)}, u32[]{:S(2)}, u32[]{:S(2)}) collective-permute-start(bf16[8,16,896]{2,1,0:T(8,128)(2,1)} %shard_map.130.refs_0_), channel_id=1, source_target_pairs={{0,2},{1,3},{2,4},{3,5},{4,6},{5,7},{6,0},{7,1},{8,10},{9,11},{10,... | collective-permute-start | bytes 688136 | tf_op jit(solution)/shard_map/ppermute | solution.py:222
  107.6 24.2 %all-to-all-start.3 = ((bf16[16,128,256]{2,1,0:T(8,128)(2,1)}), bf16[16,128,256]{2,1,0:T(8,128)(2,1)S(1)}, u32[]{:S(2)}, u32[]{:S(2)}) async-start(bf16[16,128,256]{2,1,0:T(8,128)(2,1)} %get-tuple-element.64), calls=%async_computation.3 | async-start | bytes 2097152 | tf_op jit(solution)/shard_map/all_to_all | solution.py:235
  114.5 2.5 %collective-permute-start.7 = (bf16[8,16,896]{2,1,0:T(8,128)(2,1)S(1)}, bf16[8,16,896]{2,1,0:T(8,128)(2,1)S(1)}, u32[]{:S(2)}, u32[]{:S(2)}) collective-permute-start(bf16[8,16,896]{2,1,0:T(8,128)(2,1)S(1)} %copy-done.11), channel_id=1, source_target_pairs={{0,1},{1,0},{2,3},{3,2},{4,5},{5,4},{6,7},{7,6},{8,9},{9,8},{10,11... | collective-permute-start | bytes 688136 | tf_op jit(solution)/shard_map/ppermute | solution.py:226
  114.6 4.4 %collective-permute-start.8 = (bf16[8,16,896]{2,1,0:T(8,128)(2,1)S(1)}, bf16[8,16,896]{2,1,0:T(8,128)(2,1)S(1)}, u32[]{:S(2)}, u32[]{:S(2)}) collective-permute-start(bf16[8,16,896]{2,1,0:T(8,128)(2,1)S(1)} %collective-permute-done.4.refs_1_), channel_id=1, source_target_pairs={{0,1},{1,0},{2,3},{3,2},{4,5},{5,4},{6,7},{7,6},{8,9},{9,8},{10,11... | collective-permute-start | bytes 688136 | tf_op jit(solution)/shard_map/ppermute | solution.py:226
  115.1 3.9 %collective-permute-start.9 = (bf16[8,16,896]{2,1,0:T(8,128)(2,1)S(1)}, bf16[8,16,896]{2,1,0:T(8,128)(2,1)S(1)}, u32[]{:S(2)}, u32[]{:S(2)}) collective-permute-start(bf16[8,16,896]{2,1,0:T(8,128)(2,1)S(1)} %collective-permute-done.5.refs_2_), channel_id=1, source_target_pairs={{0,1},{1,0},{2,3},{3,2},{4,5},{5,4},{6,7},{7,6},{8,9},{9,8},{10,11... | collective-permute-start | bytes 688136 | tf_op jit(solution)/shard_map/ppermute | solution.py:226
  115.2 3.8 %collective-permute-start.10 = (bf16[8,16,896]{2,1,0:T(8,128)(2,1)S(1)}, bf16[8,16,896]{2,1,0:T(8,128)(2,1)S(1)}, u32[]{:S(2)}, u32[]{:S(2)}) collective-permute-start(bf16[8,16,896]{2,1,0:T(8,128)(2,1)S(1)} %collective-permute-done.6.refs_3_), channel_id=1, source_target_pairs={{0,1},{1,0},{2,3},{3,2},{4,5},{5,4},{6,7},{7,6},{8,9},{9,8},{10,11... | collective-permute-start | bytes 688136 | tf_op jit(solution)/shard_map/ppermute | solution.py:226
  115.6 13.7 %collective-permute-start.13 = (bf16[8,16,896]{2,1,0:T(8,128)(2,1)}, bf16[8,16,896]{2,1,0:T(8,128)(2,1)S(1)}, u32[]{:S(2)}, u32[]{:S(2)}) collective-permute-start(bf16[8,16,896]{2,1,0:T(8,128)(2,1)} %shard_map.132.refs_0_), channel_id=1, source_target_pairs={{0,4},{1,5},{2,6},{3,7},{4,0},{5,1},{6,2},{7,3},{8,12},{9,13},{10,... | collective-permute-start | bytes 688136 | tf_op jit(solution)/shard_map/ppermute | solution.py:222
  117.0 12.5 %collective-permute-start.12 = (bf16[8,16,896]{2,1,0:T(8,128)(2,1)}, bf16[8,16,896]{2,1,0:T(8,128)(2,1)S(1)}, u32[]{:S(2)}, u32[]{:S(2)}) collective-permute-start(bf16[8,16,896]{2,1,0:T(8,128)(2,1)} %shard_map.132.refs_0_), channel_id=1, source_target_pairs={{0,6},{1,7},{2,0},{3,1},{4,2},{5,3},{6,4},{7,5},{8,14},{9,15},{10,... | collective-permute-start | bytes 688136 | tf_op jit(solution)/shard_map/ppermute | solution.py:222
  119.0 10.8 %collective-permute-start.11 = (bf16[8,16,896]{2,1,0:T(8,128)(2,1)}, bf16[8,16,896]{2,1,0:T(8,128)(2,1)S(1)}, u32[]{:S(2)}, u32[]{:S(2)}) collective-permute-start(bf16[8,16,896]{2,1,0:T(8,128)(2,1)} %shard_map.132.refs_0_), channel_id=1, source_target_pairs={{0,2},{1,3},{2,4},{3,5},{4,6},{5,7},{6,0},{7,1},{8,10},{9,11},{10,... | collective-permute-start | bytes 688136 | tf_op jit(solution)/shard_map/ppermute | solution.py:222
  131.9 23.2 %all-to-all-start.4 = ((bf16[16,64,512]{2,1,0:T(8,128)(2,1)}), bf16[16,64,512]{2,1,0:T(8,128)(2,1)S(1)}, u32[]{:S(2)}, u32[]{:S(2)}) async-start(bf16[16,64,512]{2,1,0:T(8,128)(2,1)} %get-tuple-element.65), calls=%async_computation.4 | async-start | bytes 2097152 | tf_op jit(solution)/shard_map/all_to_all | solution.py:235
  137.8 1.9 collective-permute-start.15
  156.1 43.7 %all-to-all-start.5 = ((bf16[16,176,512]{2,1,0:T(8,128)(2,1)}), bf16[16,176,512]{2,1,0:T(8,128)(2,1)S(1)}, u32[]{:S(2)}, u32[]{:S(2)}) async-start(bf16[16,176,512]{2,1,0:T(8,128)(2,1)} %get-tuple-element.66), calls=%async_computation.5 | async-start | bytes 5767168 | tf_op jit(solution)/shard_map/all_to_all | solution.py:235
  160.9 2.0 collective-permute-start.18
  164.0 7.2 %collective-permute-start.19 = (bf16[128,512]{1,0:T(8,128)(2,1)S(1)}, bf16[128,512]{1,0:T(8,128)(2,1)S(1)}, u32[]{:S(2)}, u32[]{:S(2)}) collective-permute-start(bf16[128,512]{1,0:T(8,128)(2,1)S(1)} %get-tuple-element.69), channel_id=1, source_target_pairs={{0,2},{1,3},{2,4},{3,5},{4,6},{5,7},{6,0},{7,1},{8,10},{9,11},{10,... | collective-permute-start | bytes 393224 | tf_op jit(solution)/shard_map/ppermute | solution.py:222
  164.8 9.2 %collective-permute-start.21 = (bf16[128,512]{1,0:T(8,128)(2,1)S(1)}, bf16[128,512]{1,0:T(8,128)(2,1)S(1)}, u32[]{:S(2)}, u32[]{:S(2)}) collective-permute-start(bf16[128,512]{1,0:T(8,128)(2,1)S(1)} %get-tuple-element.70), channel_id=1, source_target_pairs={{0,4},{1,5},{2,6},{3,7},{4,0},{5,1},{6,2},{7,3},{8,12},{9,13},{10,... | collective-permute-start | bytes 393224 | tf_op jit(solution)/shard_map/ppermute | solution.py:222
  167.7 6.5 %collective-permute-start.20 = (bf16[128,512]{1,0:T(8,128)(2,1)S(1)}, bf16[128,512]{1,0:T(8,128)(2,1)S(1)}, u32[]{:S(2)}, u32[]{:S(2)}) collective-permute-start(bf16[128,512]{1,0:T(8,128)(2,1)S(1)} %get-tuple-element.71), channel_id=1, source_target_pairs={{0,6},{1,7},{2,0},{3,1},{4,2},{5,3},{6,4},{7,5},{8,14},{9,15},{10,... | collective-permute-start | bytes 393224 | tf_op jit(solution)/shard_map/ppermute | solution.py:222
  (32 other events, 281.5 us)

commit v4 on v2

v4 whole, which is shorter than its diff:
```python
import functools
import math

import jax
import jax.numpy as jnp
from jax import lax
from jax.experimental import pallas as pl
from jax.experimental.pallas import tpu as pltpu
from jax.sharding import PartitionSpec as P

HD = 128
BF = jnp.bfloat16
F32 = jnp.float32
VMEM_LIMIT = 60 * 1024 * 1024


def mm(a, b, ca, cb):
    return lax.dot_general(a, b, (((ca,), (cb,)), ((), ())), preferred_element_type=F32)


def params():
    return pltpu.CompilerParams(vmem_limit_bytes=VMEM_LIMIT)


ANY = pl.BlockSpec(memory_space=pl.ANY)
HBM = pl.BlockSpec(memory_space=pltpu.HBM)
VM = pl.BlockSpec(memory_space=pltpu.VMEM)
SM = pl.BlockSpec(memory_space=pltpu.SMEM)


def pick_kernel(rows_ref, src_ref, *rest, counts):
    outs, sem = rest[: len(counts)], rest[-1]
    copies, k = [], 0
    for out, count in zip(outs, counts):
        for n in range(count):
            copies.append(pltpu.make_async_copy(src_ref.at[rows_ref[k]], out.at[n], sem.at[k]))
            k += 1
    for copy in copies:
        copy.start()
    for copy in copies:
        copy.wait()


def pick(rows, src, counts, place):
    item = src.shape[1:]
    return pl.pallas_call(
        functools.partial(pick_kernel, counts=counts),
        out_shape=[jax.ShapeDtypeStruct((n, *item), src.dtype) for n in counts],
        in_specs=[SM, place],
        out_specs=[VM] * len(counts),
        scratch_shapes=[pltpu.SemaphoreType.DMA((sum(counts),))],
        compiler_params=params(),
    )(rows, src)


def start_loads(pairs, sem, first=0):
    loads = [pltpu.make_async_copy(src, dst, sem.at[first + k]) for k, (src, dst) in enumerate(pairs)]
    for load in loads:
        load.start()
    return loads


def wait_all(copies):
    for copy in copies:
        copy.wait()


def row_blocks(src, dst, count):
    step = src.shape[0] // count
    return [(src.at[pl.ds(k * step, step)], dst.at[pl.ds(k * step, step)]) for k in range(count)]


def prep_kernel(at_ref, *refs):
    near_in, far_in, wo_in, q_in, wk_in, wv_in = refs[:6]
    dm_ref, qt_ref, dt_ref, gc_ref = refs[6:10]
    near_ref, far_ref, wo_ref, q_ref, wk_ref, wv_ref, sem = refs[10:]
    chips, rows, width = near_ref.shape
    groups = qt_ref.shape[0]
    part = rows // groups
    heads = width // HD
    cuts = gc_ref.shape[0] // (2 * chips)
    piece = width // cuts
    first = start_loads([(q_in, q_ref), (wk_in, wk_ref), (near_in, near_ref), (far_in, far_ref)], sem)
    blocks = start_loads(row_blocks(wo_in, wo_ref, heads), sem, 4)
    late = start_loads([(wv_in, wv_ref)], sem, 4 + heads)

    def split(ref, h, value):
        for c in range(groups):
            ref[c, h * part : (h + 1) * part] = value[c * part : (c + 1) * part].astype(BF)

    wait_all(first[:2])
    for h in range(heads):
        cols = slice(h * HD, (h + 1) * HD)
        split(qt_ref, h, mm(q_ref[:, cols], wk_ref[:, cols], 1, 1))
    wait_all(first[2:])
    wait_all(blocks)
    acc = jnp.zeros((rows, width), F32)
    for core, g_ref in enumerate((near_ref, far_ref)):
        for s in range(chips):
            j = lax.rem(at_ref[0] + chips - s, chips) * 2 + lax.rem(at_ref[1] + core, 2)
            cols = pl.ds(pl.multiple_of(j * width, width), width)
            acc += mm(g_ref[s], wo_ref[:, cols], 1, 1)
            for p in range(cuts):
                gc_ref[j * cuts + p] = g_ref[s, :, p * piece : (p + 1) * piece]
    dm = acc.astype(BF)
    dm_ref[...] = dm
    wait_all(late)
    for h in range(heads):
        cols = slice(h * HD, (h + 1) * HD)
        split(dt_ref, h, mm(dm[:, cols], wv_ref[:, cols], 1, 1))


def prep(at, near, far, wo, q, wk, wv, groups, db_count):
    chips, rows, width = near.shape
    heads = width // HD
    enc = wk.shape[0]
    tall = (groups, heads * rows // groups, enc)
    operands = (near, far, wo, q, wk, wv)
    return pl.pallas_call(
        prep_kernel,
        out_shape=[
            jax.ShapeDtypeStruct((rows, width), BF),
            jax.ShapeDtypeStruct(tall, BF),
            jax.ShapeDtypeStruct(tall, BF),
            jax.ShapeDtypeStruct((db_count, rows, 2 * chips * width // db_count), BF),
        ],
        in_specs=[SM] + [HBM] * 6,
        out_specs=[VM] * 4,
        scratch_shapes=[pltpu.VMEM(v.shape, BF) for v in operands]
        + [pltpu.SemaphoreType.DMA((5 + heads,))],
        compiler_params=params(),
        cost_estimate=pl.CostEstimate(flops=1_000_000_000, bytes_accessed=10_000_000, transcendentals=0),
    )(at, *operands)


def attn_kernel(at_ref, count_ref, *refs, c, pieces, last):
    x_in, refs = refs[:pieces], refs[pieces:]
    more = 9 if last else 5
    ins, refs = refs[:more], refs[more:]
    outs = 4 if last else 6
    send_ref, keep_ref, give_ref, gq_ref, *tu_refs = refs[:outs]
    x_ref, mixed_ref, qt_ref, dt_ref, wk_ref, wv_ref, wo_ref, *refs = refs[outs:]
    sem = refs[-1]
    slots, sub, enc = x_in[0].shape
    qt_in, dt_in, wk_in, wv_in, wo_in = ins[:5]
    chips, part, width = keep_ref.shape
    heads = width // HD
    db_count = send_ref.shape[0]
    used = 0

    def start(pairs):
        nonlocal used
        loads = start_loads(pairs, sem, used)
        used += len(pairs)
        return loads

    x_loads = start(
        [(qt_in.at[c], qt_ref)]
        + [(x_in[p], x_ref.at[pl.ds(p * slots, slots)]) for p in range(pieces)]
    )
    wv_loads = start([(wv_in, wv_ref)])
    wo_loads = start(row_blocks(wo_in, wo_ref, 4))
    dt_loads = start([(dt_in.at[c], dt_ref)])
    wk_loads = start([(wk_in, wk_ref)])
    if last:
        q_ref, dm_ref, t0_ref, u0_ref, gw_ref = refs[:5]
        last_loads = start(list(zip(ins[5:], (q_ref, dm_ref, t0_ref, u0_ref))))
    factor = 1.0 / math.sqrt(HD)
    wait_all(x_loads)
    x = x_ref[...].reshape(pieces * slots * sub, enc)
    keys = x.shape[0]
    s = mm(qt_ref[...], x, 1, 1) * factor
    slot = (lax.broadcasted_iota(jnp.int32, (1, keys), 1) // sub) % slots
    expo = jnp.where(slot < count_ref[c], jnp.exp(s), 0.0)
    probs = expo / jnp.sum(expo, axis=-1, keepdims=True)
    t = mm(probs.astype(BF), x, 1, 0).astype(BF)
    wait_all(wv_loads)
    for h in range(heads):
        cols = slice(h * HD, (h + 1) * HD)
        mixed_ref[:, cols] = mm(t[h * part : (h + 1) * part], wv_ref[:, cols], 1, 0).astype(BF)
    stores = start([(mixed_ref, send_ref.at[i, pl.ds(0, part)]) for i in range(db_count)])
    wait_all(dt_loads)
    d = mm(dt_ref[...], x, 1, 1)
    inner = jnp.sum(probs * d, axis=-1, keepdims=True)
    ds = (probs * (d - inner) * factor).astype(BF)
    u = mm(ds, x, 1, 0).astype(BF)
    wait_all(wk_loads)
    if last:
        wait_all(last_loads)
        share = enc // db_count
        for h in range(heads):
            rows = slice(h * part, (h + 1) * part)
            cols = slice(h * HD, (h + 1) * HD)
            u_all = jnp.concatenate([u0_ref[rows], u[rows]], axis=0)
            t_all = jnp.concatenate([t0_ref[rows], t[rows]], axis=0)
            sums = (mm(u_all, q_ref[:, cols], 0, 0), mm(t_all, dm_ref[:, cols], 0, 0))
            for k, total in enumerate(sums):
                for i in range(db_count):
                    gw_ref[i, k * share : (k + 1) * share, cols] = total[
                        i * share : (i + 1) * share
                    ].astype(BF)
        stores += start(
            [(gw_ref.at[i], send_ref.at[i, pl.ds(part, 2 * share)]) for i in range(db_count)]
        )
    else:
        for ref, value in zip(tu_refs, (t, u)):
            ref[...] = value
    for h in range(heads):
        cols = slice(h * HD, (h + 1) * HD)
        gq_ref[:, cols] = mm(u[h * part : (h + 1) * part], wk_ref[:, cols], 1, 0).astype(BF)
    wait_all(wo_loads)
    mixed = mixed_ref[...]
    for core, block_ref in enumerate((keep_ref, give_ref)):
        for step in range(chips):
            j = lax.rem(at_ref[0] + step, chips) * 2 + lax.rem(at_ref[1] + core, 2)
            cols = pl.ds(pl.multiple_of(j * width, width), width)
            block_ref[step] = mm(mixed, wo_ref[:, cols], 1, 0).astype(BF)
    wait_all(stores)


def attn(at, count, xs, qt, dt, wk, wv, wo, c, db_count, head_count, extra=None):
    slots, sub, enc = xs[0].shape
    width = wk.shape[1]
    heads = width // HD
    part = qt.shape[1] // heads
    last = extra is not None
    half = jax.ShapeDtypeStruct((head_count // 2, part, width), BF)
    grown = 2 * enc // db_count
    out_shape = [
        jax.ShapeDtypeStruct((db_count, part + (grown if last else 0), width), BF),
        half,
        half,
        jax.ShapeDtypeStruct((part, width), BF),
    ]
    more = list(extra) if last else []
    held = [(len(xs) * slots, sub, enc), (part, width), qt.shape[1:], dt.shape[1:]]
    held += [v.shape for v in (wk, wv, wo, *more)]
    copies = len(xs) + 8 + len(more) + db_count
    if last:
        held += [(db_count, grown, width)]
        copies += db_count
    else:
        out_shape += [jax.ShapeDtypeStruct(qt.shape[1:], BF)] * 2
    return pl.pallas_call(
        functools.partial(attn_kernel, c=c, pieces=len(xs), last=last),
        out_shape=out_shape,
        in_specs=[SM, SM] + [HBM] * (len(xs) + 5 + len(more)),
        out_specs=[HBM] + [VM] * (len(out_shape) - 1),
        scratch_shapes=[pltpu.VMEM(shape, BF) for shape in held] + [pltpu.SemaphoreType.DMA((copies,))],
        compiler_params=params(),
        cost_estimate=pl.CostEstimate(flops=4_000_000_000, bytes_accessed=12_000_000, transcendentals=262144),
    )(at, count, *xs, qt, dt, wk, wv, wo, *more)


def along(v, step, count):
    chips = count // 2
    return lax.ppermute(v, "head", [(i, ((i // 2 + step) % chips) * 2 + i % 2) for i in range(count)])


def swap(v, count):
    return lax.ppermute(v, "head", [(i, i ^ 1) for i in range(count)])


def ring_steps(count):
    chips = count // 2
    return sorted(range(1, chips), key=lambda s: min(s, chips - s))


def exchange(x, axis):
    return lax.all_to_all(x, axis, split_axis=0, concat_axis=0, tiled=True)


def after(x, *others):
    return lax.optimization_barrier((x, *others))[0]


def shards(queries, w_key, w_value, w_out, encodings, nbr_row, nbr_owner, nbr_count, grad_out):
    db_count = lax.axis_size("db")
    head_count = lax.axis_size("head")
    chips = head_count // 2
    groups, slot_count = nbr_row.shape
    tok_rows, width = queries.shape
    part = tok_rows // groups
    enc = encodings.shape[2]
    head_at = lax.axis_index("head")
    at = jnp.stack([head_at // 2, head_at % 2]).astype(jnp.int32)
    owner_ids = lax.broadcasted_iota(jnp.int32, (db_count, 1, 1), 0)
    wanted = jnp.sum(jnp.where(nbr_owner[None] == owner_ids, nbr_row[None], 0), axis=2)
    incoming = exchange(wanted, "db")
    steps = ring_steps(head_count)
    (table,) = pick(incoming.reshape(-1), encodings, (db_count * groups,), HBM)
    near = [grad_out] + [along(after(grad_out, wanted), s, head_count) for s in steps]
    near = lax.optimization_barrier((*near, table))[:-1]
    near = jnp.stack([near[([0] + steps).index(s)] for s in range(chips)])
    far = swap(near, head_count)
    dm, qt, dt, grad_cols = prep(at, near, far, w_out, queries, w_key, w_value, groups, db_count)
    received = after(exchange(table, "db"), dm)
    rows = nbr_owner * groups + lax.broadcasted_iota(jnp.int32, nbr_owner.shape, 0)
    mine = pick(rows.reshape(-1), received, (slot_count,) * groups, ANY)
    token = mine[0]
    ring = []
    for c in range(groups):
        held = mine[c] if c == 0 else after(mine[c], *ring[-1])
        ring.append([held] + [along(held, s, head_count) for s in steps])
    spread = []
    for pieces in ring:
        spread.append([*pieces, *(swap(v, head_count) for v in pieces)])
    grad_tok = exchange(after(grad_cols, token), "db")
    sent, keep, give, grad_q, kept = [], [], [], [], []
    for c in range(groups):
        last = c == groups - 1
        extra = (queries, dm, *kept) if last else None
        m, k, g, gq, *kept = attn(
            at, nbr_count, spread[c], qt, dt, w_key, w_value, w_out, c, db_count, head_count, extra
        )
        hold = (grad_tok, *ring[-1]) if c == 0 else sent
        sent.append(exchange(after(m, *hold), "db"))
        keep.append(k)
        give.append(g)
        grad_q.append(gq)
    keep = jnp.concatenate(keep, axis=1)
    other = swap(jnp.concatenate(give, axis=1), head_count)
    pair = (keep.astype(F32) + other.astype(F32)).astype(BF)
    terms = [pair[0]] + [along(pair[s], s, head_count) for s in steps]
    attended = sum(t.astype(F32) for t in terms).astype(BF)
    share = enc // db_count
    grad_tok = grad_tok.reshape(db_count, groups, part, -1)
    grad_wo = sum(
        lax.dot_general(
            sent[c][:, :part], grad_tok[:, c], (((0, 1), (0, 1)), ((), ())), preferred_element_type=F32
        )
        for c in range(groups)
    )
    grad_w = [
        jnp.sum(sent[-1][:, part + k * share : part + (k + 1) * share].astype(F32), axis=0)
        for k in range(2)
    ]
    return (attended, jnp.concatenate(grad_q, axis=0), *grad_w, grad_wo)


def solution(mesh):
    placed = (
        P("db", "head"),
        P(None, "head"),
        P(None, "head"),
        P("head", None),
        P("db", "head", None),
        P("db", None),
        P("db", None),
        P("db"),
        P("db", "head"),
    )
    return jax.shard_map(
        shards,
        mesh=mesh,
        in_specs=placed,
        out_specs=(
            P("db", "head"),
            P("db", "head"),
            P("db", "head"),
            P("db", "head"),
            P("head", "db"),
        ),
        check_vma=False,
    )
```

time: 187 us -> 151 us (0.81)
  waiting for transfers between devices: 76.3 us -> 53.2 us
  starting transfers between devices: 46.8 us -> 36 us
  local copies, waits for them, and re-layouts: 12.2 us -> 6.05 us
  Pallas kernels: 24.7 us -> 29.7 us
    all_to_all x5 -> x4, waiting for transfers between devices: 55.8 us -> 32 us  [exchange(): return lax.all_to_all(x, axis, split_axis=0, concat_axis=0, tiled=True)]
    all_to_all x5 -> x4, starting transfers between devices: 26.4 us -> 17.9 us  [exchange(): return lax.all_to_all(x, axis, split_axis=0, concat_axis=0, tiled=True)]
    unnamed x40 -> x56, local copies, waits for them, and re-layouts: 11.9 us -> 4.27 us
    pallas_call x1, Pallas kernels: 3.6 us -> 6.72 us  [prep(): pl.pallas_call(prep_kernel, out_shape=[jax.ShapeDtypeStruct((rows, width)...]
    ppermute x10, waiting for transfers between devices: 1.92 us -> 4.06 us  [swap(): return lax.ppermute(v, 'head', [(i, i ^ 1) for i in range(count)])]
    ppermute x12, starting transfers between devices: 18.6 us -> 16.6 us  [along(): lax.ppermute(v, 'head', [(i, (i // 2 + step) % chips * 2 + i % 2) for i i...]
    pallas_call x3 -> x2, Pallas kernels: 4.45 us -> 5.94 us  [pick(): pl.pallas_call(functools.partial(pick_kernel, counts=counts), out_shape=[...]
  transfers between devices with their start and end apart: 27 -> 26, of which waited for: 13 -> 16; matrix products, arithmetic and copies ran while one was open for 4% -> 4% of each run, Pallas kernels for 13% -> 18%
where the time goes in v4:
time: 151 us
  waiting for transfers between devices  53.2 us (35%)
  starting transfers between devices  36 us (24%)
  Pallas kernels  29.7 us (20%)
  blocking collectives  15.2 us (10%)
  other arithmetic  6.57 us (4%)
  local copies, waits for them, and re-layouts  6.05 us (4%)
  matrix products  2.79 us (2%)
    all_to_all x4, waiting for transfers between devices, exchange(): return lax.all_to_all(x, axis, split_axis=0, concat_axis=0, tiled=True)  32 us
    all_to_all x4, starting transfers between devices, exchange(): return lax.all_to_all(x, axis, split_axis=0, concat_axis=0, tiled=True)  17.9 us
    ppermute x12, waiting for transfers between devices, along(): lax.ppermute(v, 'head', [(i, (i // 2 + step) % chips * 2 + i % 2) for i i...  17.1 us
    pallas_call x2, Pallas kernels, attn(): pl.pallas_call(functools.partial(attn_kernel, c=c, pieces=len(xs), last=l...  17 us
    ppermute x12, starting transfers between devices, along(): lax.ppermute(v, 'head', [(i, (i // 2 + step) % chips * 2 + i % 2) for i i...  16.6 us
    all_to_all x1, blocking collectives, exchange(): return lax.all_to_all(x, axis, split_axis=0, concat_axis=0, tiled=True)  15.2 us
    pallas_call x1, Pallas kernels, prep(): pl.pallas_call(prep_kernel, out_shape=[jax.ShapeDtypeStruct((rows, width)...  6.72 us
    pallas_call x2, Pallas kernels, pick(): pl.pallas_call(functools.partial(pick_kernel, counts=counts), out_shape=[...  5.94 us
  transfers between devices with their start and end apart: 26, of which 16 were waited for; matrix products, arithmetic and copies ran while one was open for 4% of the time, Pallas kernels for 18%

profile of v4, /device:TPU:0, one launch (start us, length us, event | category | flops | bytes accessed | tf_op | source)
XLA Modules:
  0.0 150.5 jit_solution(2370570009577737418)
XLA Ops:
  1.5 3.4 %collective-permute-start.2 = (bf16[128,512]{1,0:T(8,128)(2,1)}, bf16[128,512]{1,0:T(8,128)(2,1)S(1)}, u32[]{:S(2)}, u32[]{:S(2)}) collective-permute-start(bf16[128,512]{1,0:T(8,128)(2,1)} %param.17), channel_id=1, source_target_pairs={{0,4},{1,5},{2,6},{3,7},{4,0},{5,1},{6,2},{7,3},{8,12},{9,13},{10,... | collective-permute-start | bytes 393224 | tf_op jit(solution)/shard_map/ppermute | solution.py:257
  6.9 15.2 %all_to_all.29 = s32[16,1,2]{2,1,0:T(1,128)S(1)} all-to-all(s32[16,1,2]{2,1,0:T(1,128)S(1)} %copy.23), channel_id=1, replica_groups=mesh['db'=16,'head'=8] {'db'}, dimensions={0} | all-to-all | bytes 256 | tf_op jit(solution)/shard_map/all_to_all | solution.py:270
  23.9 3.4 %shard_map.128 = bf16[32,16,896]{2,1,0:T(8,128)(2,1)} custom-call(s32[32]{0:T(128)} %reshape.27.rows_ref, bf16[64,16,896]{2,1,0:T(8,128)(2,1)} %src_ref.1), custom_call_target="tpu_custom_call" | custom-call | tf_op jit(solution)/shard_map/pallas_call | solution.py:46
  27.3 3.6 %all-to-all-start.1 = ((bf16[32,16,896]{2,1,0:T(8,128)(2,1)}), bf16[32,16,896]{2,1,0:T(8,128)(2,1)S(1)}, u32[]{:S(2)}, u32[]{:S(2)}) async-start(bf16[32,16,896]{2,1,0:T(8,128)(2,1)} %shard_map.128), calls=%async_computation.1 | async-start | bytes 1835008 | tf_op jit(solution)/shard_map/all_to_all | solution.py:270
  33.9 6.7 %shard_map.129 = (bf16[128,512]{1,0:T(8,128)(2,1)}, bf16[2,256,896]{2,1,0:T(8,128)(2,1)}, bf16[2,256,896]{2,1,0:T(8,128)(2,1)}, bf16[16,128,256]{2,1,0:T(8,128)(2,1)}) custom-call(s32[2]{0:T(128)} %pad_add_fusion.at_ref, bf16[4,128,512]{2,1,0:T(8,128)(2,1)} %copy-done.1, bf16[4,128,512]{2,1,0:T(8,128)(2,1)} %copy-done.6, bf16[512,4096]{1,0:T(8,128)(2,1)} %refs_12_.3, ...), custom_call_target="tpu_custom_call" | custom-call | flops 1000000000 | bytes 10000000 | tf_op jit(solution)/shard_map/pallas_call | solution.py:119
  40.6 4.0 %all-to-all-done.1.src_ref = bf16[32,16,896]{2,1,0:T(8,128)(2,1)S(1)} async-done(((bf16[32,16,896]{2,1,0:T(8,128)(2,1)}), bf16[32,16,896]{2,1,0:T(8,128)(2,1)S(1)}, u32[]{:S(2)}, u32[]{:S(2)}) %all-to-all-start.1) | async-done | bytes 917536 | tf_op jit(solution)/shard_map/all_to_all | solution.py:270
  45.6 2.6 %shard_map.130 = (bf16[8,16,896]{2,1,0:T(8,128)(2,1)}, bf16[8,16,896]{2,1,0:T(8,128)(2,1)}) custom-call(s32[16]{0:T(128)} %reshape.26.rows_ref, bf16[32,16,896]{2,1,0:T(8,128)(2,1)} %copy-done), custom_call_target="tpu_custom_call" | custom-call | tf_op jit(solution)/shard_map/pallas_call | solution.py:46
  48.2 3.7 %all-to-all-start.2 = ((bf16[16,128,256]{2,1,0:T(8,128)(2,1)}), bf16[16,128,256]{2,1,0:T(8,128)(2,1)S(1)}, u32[]{:S(2)}, u32[]{:S(2)}) async-start(bf16[16,128,256]{2,1,0:T(8,128)(2,1)} %get-tuple-element.54), calls=%async_computation.2 | async-start | bytes 2097152 | tf_op jit(solution)/shard_map/all_to_all | solution.py:270
  52.9 2.3 %collective-permute-start.5 = (bf16[8,16,896]{2,1,0:T(8,128)(2,1)}, bf16[8,16,896]{2,1,0:T(8,128)(2,1)S(1)}, u32[]{:S(2)}, u32[]{:S(2)}) collective-permute-start(bf16[8,16,896]{2,1,0:T(8,128)(2,1)} %get-tuple-element.38.refs_0_), channel_id=1, source_target_pairs={{0,6},{1,7},{2,0},{3,1},{4,2},{5,3},{6,4},{7,5},{8,14},{9,15},{10,... | collective-permute-start | bytes 688136 | tf_op jit(solution)/shard_map/ppermute | solution.py:257
  55.3 6.9 %collective-permute-done.6.refs_3_ = bf16[8,16,896]{2,1,0:T(8,128)(2,1)S(1)} collective-permute-done((bf16[8,16,896]{2,1,0:T(8,128)(2,1)}, bf16[8,16,896]{2,1,0:T(8,128)(2,1)S(1)}, u32[]{:S(2)}, u32[]{:S(2)}) %collective-permute-start.6) | collective-permute-done | bytes 229408 | tf_op jit(solution)/shard_map/ppermute | solution.py:257
  62.2 2.9 %collective-permute-done.5.refs_2_ = bf16[8,16,896]{2,1,0:T(8,128)(2,1)S(1)} collective-permute-done((bf16[8,16,896]{2,1,0:T(8,128)(2,1)}, bf16[8,16,896]{2,1,0:T(8,128)(2,1)S(1)}, u32[]{:S(2)}, u32[]{:S(2)}) %collective-permute-start.5) | collective-permute-done | bytes 229408 | tf_op jit(solution)/shard_map/ppermute | solution.py:257
  65.6 1.7 %collective-permute-start.13 = (bf16[8,16,896]{2,1,0:T(8,128)(2,1)}, bf16[8,16,896]{2,1,0:T(8,128)(2,1)S(1)}, u32[]{:S(2)}, u32[]{:S(2)}) collective-permute-start(bf16[8,16,896]{2,1,0:T(8,128)(2,1)} %get-tuple-element.43.refs_0_), channel_id=1, source_target_pairs={{0,4},{1,5},{2,6},{3,7},{4,0},{5,1},{6,2},{7,3},{8,12},{9,13},{10,... | collective-permute-start | bytes 688136 | tf_op jit(solution)/shard_map/ppermute | solution.py:257
  67.3 2.0 %collective-permute-start.12 = (bf16[8,16,896]{2,1,0:T(8,128)(2,1)}, bf16[8,16,896]{2,1,0:T(8,128)(2,1)S(1)}, u32[]{:S(2)}, u32[]{:S(2)}) collective-permute-start(bf16[8,16,896]{2,1,0:T(8,128)(2,1)} %get-tuple-element.43.refs_0_), channel_id=1, source_target_pairs={{0,6},{1,7},{2,0},{3,1},{4,2},{5,3},{6,4},{7,5},{8,14},{9,15},{10,... | collective-permute-start | bytes 688136 | tf_op jit(solution)/shard_map/ppermute | solution.py:257
  70.2 8.3 %shard_map.131 = (bf16[16,64,512]{2,1,0:T(8,128)(2,1)}, bf16[4,64,512]{2,1,0:T(8,128)(2,1)}, bf16[4,64,512]{2,1,0:T(8,128)(2,1)}, bf16[64,512]{1,0:T(8,128)(2,1)...) custom-call(s32[2]{0:T(128)} %pad_add_fusion.at_ref, s32[2]{0:T(128)} %count_ref.3, ...), custom_call_target="tpu_custom_call" | custom-call | flops 4000000000 | bytes 12000000 | tf_op jit(solution)/shard_map/pallas_call | solution.py:244
  80.1 6.9 %all-to-all-start.3 = ((bf16[16,64,512]{2,1,0:T(8,128)(2,1)}), bf16[16,64,512]{2,1,0:T(8,128)(2,1)S(1)}, u32[]{:S(2)}, u32[]{:S(2)}) async-start(bf16[16,64,512]{2,1,0:T(8,128)(2,1)} %get-tuple-element.55), calls=%async_computation.3 | async-start | bytes 2097152 | tf_op jit(solution)/shard_map/all_to_all | solution.py:270
  90.2 8.7 %shard_map.132 = (bf16[16,176,512]{2,1,0:T(8,128)(2,1)}, bf16[4,64,512]{2,1,0:T(8,128)(2,1)}, bf16[4,64,512]{2,1,0:T(8,128)(2,1)}, bf16[64,512]{1,0:T(8,128)(2,1)}) custom-call(s32[2]{0:T(128)} %pad_add_fusion.at_ref, s32[2]{0:T(128)} %count_ref.3, bf16[8,16,896]{2,1,0:T(8,128)(2,1)} %get-tuple-element.43.refs_0_, bf16[8,16,896]{2,1,0:T(8,128)(2,1)} %copy-done.16, ...), custom_call_target="tpu_custom_call" | custom-call | flops 4000000000 | bytes 12000000 | tf_op jit(solution)/shard_map/pallas_call | solution.py:244
  98.9 6.0 %all-to-all-done.3 = bf16[16,64,512]{2,1,0:T(8,128)(2,1)S(1)} async-done(((bf16[16,64,512]{2,1,0:T(8,128)(2,1)}), bf16[16,64,512]{2,1,0:T(8,128)(2,1)S(1)}, u32[]{:S(2)}, u32[]{:S(2)}) %all-to-all-start.3) | async-done | bytes 1048608 | tf_op jit(solution)/shard_map/all_to_all | solution.py:270
  105.9 3.7 %all-to-all-start.4 = ((bf16[16,176,512]{2,1,0:T(8,128)(2,1)}), bf16[16,176,512]{2,1,0:T(8,128)(2,1)S(1)}, u32[]{:S(2)}, u32[]{:S(2)}) async-start(bf16[16,176,512]{2,1,0:T(8,128)(2,1)} %get-tuple-element.56), calls=%async_computation.4 | async-start | bytes 5767168 | tf_op jit(solution)/shard_map/all_to_all | solution.py:270
  110.8 1.9 %collective-permute-done.18 = bf16[4,128,512]{2,1,0:T(8,128)(2,1)S(1)} collective-permute-done((bf16[4,128,512]{2,1,0:T(8,128)(2,1)S(1)}, bf16[4,128,512]{2,1,0:T(8,128)(2,1)S(1)}, u32[]{:S(2)}, u32[]{:S(2)}) %collective-permute-start.18) | collective-permute-done | bytes 524320 | tf_op jit(solution)/shard_map/ppermute | solution.py:261
  114.7 3.0 %collective-permute-start.21 = (bf16[128,512]{1,0:T(8,128)(2,1)S(1)}, bf16[128,512]{1,0:T(8,128)(2,1)S(1)}, u32[]{:S(2)}, u32[]{:S(2)}) collective-permute-start(bf16[128,512]{1,0:T(8,128)(2,1)S(1)} %get-tuple-element.60), channel_id=1, source_target_pairs={{0,4},{1,5},{2,6},{3,7},{4,0},{5,1},{6,2},{7,3},{8,12},{9,13},{10,... | collective-permute-start | bytes 393224 | tf_op jit(solution)/shard_map/ppermute | solution.py:257
  118.6 2.2 %collective-permute-done.19 = bf16[128,512]{1,0:T(8,128)(2,1)S(1)} collective-permute-done((bf16[128,512]{1,0:T(8,128)(2,1)S(1)}, bf16[128,512]{1,0:T(8,128)(2,1)S(1)}, u32[]{:S(2)}, u32[]{:S(2)}) %collective-permute-start.19) | collective-permute-done | bytes 131104 | tf_op jit(solution)/shard_map/ppermute | solution.py:257
  120.8 3.2 %collective-permute-done.21 = bf16[128,512]{1,0:T(8,128)(2,1)S(1)} collective-permute-done((bf16[128,512]{1,0:T(8,128)(2,1)S(1)}, bf16[128,512]{1,0:T(8,128)(2,1)S(1)}, u32[]{:S(2)}, u32[]{:S(2)}) %collective-permute-start.21) | collective-permute-done | bytes 131104 | tf_op jit(solution)/shard_map/ppermute | solution.py:257
  124.8 22.0 %all-to-all-done.4 = bf16[16,176,512]{2,1,0:T(8,128)(2,1)S(1)} async-done(((bf16[16,176,512]{2,1,0:T(8,128)(2,1)}), bf16[16,176,512]{2,1,0:T(8,128)(2,1)S(1)}, u32[]{:S(2)}, u32[]{:S(2)}) %all-to-all-start.4) | async-done | bytes 2883616 | tf_op jit(solution)/shard_map/all_to_all | solution.py:270
  147.7 1.5 %convolution_bitcast_fusion = f32[512,256]{1,0:T(8,128)S(1)} fusion(bf16[16,176,512]{2,1,0:T(8,128)(2,1)S(1)} %all-to-all-done.4, bf16[16,2,64,256]{3,2,1,0:T(8,128)(2,1)} %bitcast.36), kind=kOutput, calls=%fused_computation.2 | convolution fusion | flops 268435456 | bytes 2097152 | tf_op jit(solution)/shard_map/dot_general | solution.py:329
  (107 shorter events, 23.6 us)
Async XLA Ops:
  1.5 29.5 %collective-permute-start.2 = (bf16[128,512]{1,0:T(8,128)(2,1)}, bf16[128,512]{1,0:T(8,128)(2,1)S(1)}, u32[]{:S(2)}, u32[]{:S(2)}) collective-permute-start(bf16[128,512]{1,0:T(8,128)(2,1)} %param.17), channel_id=1, source_target_pairs={{0,4},{1,5},{2,6},{3,7},{4,0},{5,1},{6,2},{7,3},{8,12},{9,13},{10,... | collective-permute-start | bytes 393224 | tf_op jit(solution)/shard_map/ppermute | solution.py:257
  4.8 26.1 %collective-permute-start.1 = (bf16[128,512]{1,0:T(8,128)(2,1)}, bf16[128,512]{1,0:T(8,128)(2,1)S(1)}, u32[]{:S(2)}, u32[]{:S(2)}) collective-permute-start(bf16[128,512]{1,0:T(8,128)(2,1)} %param.17), channel_id=1, source_target_pairs={{0,6},{1,7},{2,0},{3,1},{4,2},{5,3},{6,4},{7,5},{8,14},{9,15},{10,... | collective-permute-start | bytes 393224 | tf_op jit(solution)/shard_map/ppermute | solution.py:257
  5.9 25.1 %collective-permute-start = (bf16[128,512]{1,0:T(8,128)(2,1)}, bf16[128,512]{1,0:T(8,128)(2,1)S(1)}, u32[]{:S(2)}, u32[]{:S(2)}) collective-permute-start(bf16[128,512]{1,0:T(8,128)(2,1)} %param.17), channel_id=1, source_target_pairs={{0,2},{1,3},{2,4},{3,5},{4,6},{5,7},{6,0},{7,1},{8,10},{9,11},{10,... | collective-permute-start | bytes 393224 | tf_op jit(solution)/shard_map/ppermute | solution.py:257
  27.3 17.3 %all-to-all-start.1 = ((bf16[32,16,896]{2,1,0:T(8,128)(2,1)}), bf16[32,16,896]{2,1,0:T(8,128)(2,1)S(1)}, u32[]{:S(2)}, u32[]{:S(2)}) async-start(bf16[32,16,896]{2,1,0:T(8,128)(2,1)} %shard_map.128), calls=%async_computation.1 | async-start | bytes 1835008 | tf_op jit(solution)/shard_map/all_to_all | solution.py:270
  31.1 2.0 %collective-permute-start.3 = (bf16[4,128,512]{2,1,0:T(8,128)(2,1)S(1)}, bf16[4,128,512]{2,1,0:T(8,128)(2,1)S(1)}, u32[]{:S(2)}, u32[]{:S(2)}) collective-permute-start(bf16[4,128,512]{2,1,0:T(8,128)(2,1)S(1)} %pad_maximum_fusion.refs_0_), channel_id=1, source_target_pairs={{0,1},{1,0},{2,3},{3,2},{4,5},{5,4},{6,7},{7,6},{8,9},{9,8},{10,11... | collective-permute-start | bytes 1572872 | tf_op jit(solution)/shard_map/ppermute | solution.py:261
  48.2 31.9 %all-to-all-start.2 = ((bf16[16,128,256]{2,1,0:T(8,128)(2,1)}), bf16[16,128,256]{2,1,0:T(8,128)(2,1)S(1)}, u32[]{:S(2)}, u32[]{:S(2)}) async-start(bf16[16,128,256]{2,1,0:T(8,128)(2,1)} %get-tuple-element.54), calls=%async_computation.2 | async-start | bytes 2097152 | tf_op jit(solution)/shard_map/all_to_all | solution.py:270
  51.9 10.3 %collective-permute-start.6 = (bf16[8,16,896]{2,1,0:T(8,128)(2,1)}, bf16[8,16,896]{2,1,0:T(8,128)(2,1)S(1)}, u32[]{:S(2)}, u32[]{:S(2)}) collective-permute-start(bf16[8,16,896]{2,1,0:T(8,128)(2,1)} %get-tuple-element.38.refs_0_), channel_id=1, source_target_pairs={{0,4},{1,5},{2,6},{3,7},{4,0},{5,1},{6,2},{7,3},{8,12},{9,13},{10,... | collective-permute-start | bytes 688136 | tf_op jit(solution)/shard_map/ppermute | solution.py:257
  52.9 12.1 %collective-permute-start.5 = (bf16[8,16,896]{2,1,0:T(8,128)(2,1)}, bf16[8,16,896]{2,1,0:T(8,128)(2,1)S(1)}, u32[]{:S(2)}, u32[]{:S(2)}) collective-permute-start(bf16[8,16,896]{2,1,0:T(8,128)(2,1)} %get-tuple-element.38.refs_0_), channel_id=1, source_target_pairs={{0,6},{1,7},{2,0},{3,1},{4,2},{5,3},{6,4},{7,5},{8,14},{9,15},{10,... | collective-permute-start | bytes 688136 | tf_op jit(solution)/shard_map/ppermute | solution.py:257
  55.3 10.1 %collective-permute-start.4 = (bf16[8,16,896]{2,1,0:T(8,128)(2,1)}, bf16[8,16,896]{2,1,0:T(8,128)(2,1)S(1)}, u32[]{:S(2)}, u32[]{:S(2)}) collective-permute-start(bf16[8,16,896]{2,1,0:T(8,128)(2,1)} %get-tuple-element.38.refs_0_), channel_id=1, source_target_pairs={{0,2},{1,3},{2,4},{3,5},{4,6},{5,7},{6,0},{7,1},{8,10},{9,11},{10,... | collective-permute-start | bytes 688136 | tf_op jit(solution)/shard_map/ppermute | solution.py:257
  55.3 12.0 %collective-permute-start.7 = (bf16[8,16,896]{2,1,0:T(8,128)(2,1)}, bf16[8,16,896]{2,1,0:T(8,128)(2,1)S(1)}, u32[]{:S(2)}, u32[]{:S(2)}) collective-permute-start(bf16[8,16,896]{2,1,0:T(8,128)(2,1)} %get-tuple-element.38.refs_0_), channel_id=1, source_target_pairs={{0,1},{1,0},{2,3},{3,2},{4,5},{5,4},{6,7},{7,6},{8,9},{9,8},{10,11... | collective-permute-start | bytes 688136 | tf_op jit(solution)/shard_map/ppermute | solution.py:261
  62.2 7.1 %collective-permute-start.10 = (bf16[8,16,896]{2,1,0:T(8,128)(2,1)S(1)}, bf16[8,16,896]{2,1,0:T(8,128)(2,1)S(1)}, u32[]{:S(2)}, u32[]{:S(2)}) collective-permute-start(bf16[8,16,896]{2,1,0:T(8,128)(2,1)S(1)} %collective-permute-done.6.refs_3_), channel_id=1, source_target_pairs={{0,1},{1,0},{2,3},{3,2},{4,5},{5,4},{6,7},{7,6},{8,9},{9,8},{10,11... | collective-permute-start | bytes 688136 | tf_op jit(solution)/shard_map/ppermute | solution.py:261
  65.0 4.3 %collective-permute-start.9 = (bf16[8,16,896]{2,1,0:T(8,128)(2,1)S(1)}, bf16[8,16,896]{2,1,0:T(8,128)(2,1)S(1)}, u32[]{:S(2)}, u32[]{:S(2)}) collective-permute-start(bf16[8,16,896]{2,1,0:T(8,128)(2,1)S(1)} %collective-permute-done.5.refs_2_), channel_id=1, source_target_pairs={{0,1},{1,0},{2,3},{3,2},{4,5},{5,4},{6,7},{7,6},{8,9},{9,8},{10,11... | collective-permute-start | bytes 688136 | tf_op jit(solution)/shard_map/ppermute | solution.py:261
  65.4 3.9 %collective-permute-start.8 = (bf16[8,16,896]{2,1,0:T(8,128)(2,1)S(1)}, bf16[8,16,896]{2,1,0:T(8,128)(2,1)S(1)}, u32[]{:S(2)}, u32[]{:S(2)}) collective-permute-start(bf16[8,16,896]{2,1,0:T(8,128)(2,1)S(1)} %collective-permute-done.4.refs_1_), channel_id=1, source_target_pairs={{0,1},{1,0},{2,3},{3,2},{4,5},{5,4},{6,7},{7,6},{8,9},{9,8},{10,11... | collective-permute-start | bytes 688136 | tf_op jit(solution)/shard_map/ppermute | solution.py:261
  65.6 12.9 %collective-permute-start.13 = (bf16[8,16,896]{2,1,0:T(8,128)(2,1)}, bf16[8,16,896]{2,1,0:T(8,128)(2,1)S(1)}, u32[]{:S(2)}, u32[]{:S(2)}) collective-permute-start(bf16[8,16,896]{2,1,0:T(8,128)(2,1)} %get-tuple-element.43.refs_0_), channel_id=1, source_target_pairs={{0,4},{1,5},{2,6},{3,7},{4,0},{5,1},{6,2},{7,3},{8,12},{9,13},{10,... | collective-permute-start | bytes 688136 | tf_op jit(solution)/shard_map/ppermute | solution.py:257
  67.3 12.5 %collective-permute-start.12 = (bf16[8,16,896]{2,1,0:T(8,128)(2,1)}, bf16[8,16,896]{2,1,0:T(8,128)(2,1)S(1)}, u32[]{:S(2)}, u32[]{:S(2)}) collective-permute-start(bf16[8,16,896]{2,1,0:T(8,128)(2,1)} %get-tuple-element.43.refs_0_), channel_id=1, source_target_pairs={{0,6},{1,7},{2,0},{3,1},{4,2},{5,3},{6,4},{7,5},{8,14},{9,15},{10,... | collective-permute-start | bytes 688136 | tf_op jit(solution)/shard_map/ppermute | solution.py:257
  69.3 10.8 %collective-permute-start.11 = (bf16[8,16,896]{2,1,0:T(8,128)(2,1)}, bf16[8,16,896]{2,1,0:T(8,128)(2,1)S(1)}, u32[]{:S(2)}, u32[]{:S(2)}) collective-permute-start(bf16[8,16,896]{2,1,0:T(8,128)(2,1)} %get-tuple-element.43.refs_0_), channel_id=1, source_target_pairs={{0,2},{1,3},{2,4},{3,5},{4,6},{5,7},{6,0},{7,1},{8,10},{9,11},{10,... | collective-permute-start | bytes 688136 | tf_op jit(solution)/shard_map/ppermute | solution.py:257
  80.1 24.9 %all-to-all-start.3 = ((bf16[16,64,512]{2,1,0:T(8,128)(2,1)}), bf16[16,64,512]{2,1,0:T(8,128)(2,1)S(1)}, u32[]{:S(2)}, u32[]{:S(2)}) async-start(bf16[16,64,512]{2,1,0:T(8,128)(2,1)} %get-tuple-element.55), calls=%async_computation.3 | async-start | bytes 2097152 | tf_op jit(solution)/shard_map/all_to_all | solution.py:270
  87.1 1.8 %collective-permute-start.17 = (bf16[8,16,896]{2,1,0:T(8,128)(2,1)S(1)}, bf16[8,16,896]{2,1,0:T(8,128)(2,1)S(1)}, u32[]{:S(2)}, u32[]{:S(2)}) collective-permute-start(bf16[8,16,896]{2,1,0:T(8,128)(2,1)S(1)} %collective-permute-done.13.refs_3_), channel_id=1, source_target_pairs={{0,1},{1,0},{2,3},{3,2},{4,5},{5,4},{6,7},{7,6},{8,9},{9,8},{10,11... | collective-permute-start | bytes 688136 | tf_op jit(solution)/shard_map/ppermute | solution.py:261
  87.8 1.7 %collective-permute-start.15 = (bf16[8,16,896]{2,1,0:T(8,128)(2,1)S(1)}, bf16[8,16,896]{2,1,0:T(8,128)(2,1)S(1)}, u32[]{:S(2)}, u32[]{:S(2)}) collective-permute-start(bf16[8,16,896]{2,1,0:T(8,128)(2,1)S(1)} %collective-permute-done.11.refs_1_), channel_id=1, source_target_pairs={{0,1},{1,0},{2,3},{3,2},{4,5},{5,4},{6,7},{7,6},{8,9},{9,8},{10,11... | collective-permute-start | bytes 688136 | tf_op jit(solution)/shard_map/ppermute | solution.py:261
  105.9 40.8 %all-to-all-start.4 = ((bf16[16,176,512]{2,1,0:T(8,128)(2,1)}), bf16[16,176,512]{2,1,0:T(8,128)(2,1)S(1)}, u32[]{:S(2)}, u32[]{:S(2)}) async-start(bf16[16,176,512]{2,1,0:T(8,128)(2,1)} %get-tuple-element.56), calls=%async_computation.4 | async-start | bytes 5767168 | tf_op jit(solution)/shard_map/all_to_all | solution.py:270
  110.7 2.0 %collective-permute-start.18 = (bf16[4,128,512]{2,1,0:T(8,128)(2,1)S(1)}, bf16[4,128,512]{2,1,0:T(8,128)(2,1)S(1)}, u32[]{:S(2)}, u32[]{:S(2)}) collective-permute-start(bf16[4,128,512]{2,1,0:T(8,128)(2,1)S(1)} %pad_maximum_fusion.1), channel_id=1, source_target_pairs={{0,1},{1,0},{2,3},{3,2},{4,5},{5,4},{6,7},{7,6},{8,9},{9,8},{10,11... | collective-permute-start | bytes 1572872 | tf_op jit(solution)/shard_map/ppermute | solution.py:261
  113.8 7.0 %collective-permute-start.19 = (bf16[128,512]{1,0:T(8,128)(2,1)S(1)}, bf16[128,512]{1,0:T(8,128)(2,1)S(1)}, u32[]{:S(2)}, u32[]{:S(2)}) collective-permute-start(bf16[128,512]{1,0:T(8,128)(2,1)S(1)} %get-tuple-element.59), channel_id=1, source_target_pairs={{0,2},{1,3},{2,4},{3,5},{4,6},{5,7},{6,0},{7,1},{8,10},{9,11},{10,... | collective-permute-start | bytes 393224 | tf_op jit(solution)/shard_map/ppermute | solution.py:257
  114.7 9.4 %collective-permute-start.21 = (bf16[128,512]{1,0:T(8,128)(2,1)S(1)}, bf16[128,512]{1,0:T(8,128)(2,1)S(1)}, u32[]{:S(2)}, u32[]{:S(2)}) collective-permute-start(bf16[128,512]{1,0:T(8,128)(2,1)S(1)} %get-tuple-element.60), channel_id=1, source_target_pairs={{0,4},{1,5},{2,6},{3,7},{4,0},{5,1},{6,2},{7,3},{8,12},{9,13},{10,... | collective-permute-start | bytes 393224 | tf_op jit(solution)/shard_map/ppermute | solution.py:257
  117.7 6.3 %collective-permute-start.20 = (bf16[128,512]{1,0:T(8,128)(2,1)S(1)}, bf16[128,512]{1,0:T(8,128)(2,1)S(1)}, u32[]{:S(2)}, u32[]{:S(2)}) collective-permute-start(bf16[128,512]{1,0:T(8,128)(2,1)S(1)} %get-tuple-element.61), channel_id=1, source_target_pairs={{0,6},{1,7},{2,0},{3,1},{4,2},{5,3},{6,4},{7,5},{8,14},{9,15},{10,... | collective-permute-start | bytes 393224 | tf_op jit(solution)/shard_map/ppermute | solution.py:257
  (30 other events, 191.7 us)

commit v5 on v4

--- a/solution.py
+++ b/solution.py
@@ -12,6 +12,7 @@
 BF = jnp.bfloat16
 F32 = jnp.float32
 VMEM_LIMIT = 60 * 1024 * 1024
+SMALL_LIMIT = 8 * 1024 * 1024
 
 
 def mm(a, b, ca, cb):
@@ -28,28 +29,37 @@
 SM = pl.BlockSpec(memory_space=pltpu.SMEM)
 
 
-def pick_kernel(rows_ref, src_ref, *rest, counts):
-    outs, sem = rest[: len(counts)], rest[-1]
-    copies, k = [], 0
-    for out, count in zip(outs, counts):
-        for n in range(count):
-            copies.append(pltpu.make_async_copy(src_ref.at[rows_ref[k]], out.at[n], sem.at[k]))
-            k += 1
-    for copy in copies:
-        copy.start()
-    for copy in copies:
-        copy.wait()
-
-
-def pick(rows, src, counts, place):
+def pick_kernel(rows_ref, src_ref, *rest, row_of, count):
+    *outs, held, load_sem, store_sem = rest
+    places = [out.at[n] for out in outs for n in range(out.shape[0])]
+    loads = [
+        pltpu.make_async_copy(src_ref.at[row_of(rows_ref, k)], held.at[k], load_sem.at[k])
+        for k in range(count)
+    ]
+    stores = [pltpu.make_async_copy(held.at[k], places[k], store_sem.at[k]) for k in range(count)]
+    for load in loads:
+        load.start()
+    for load, store in zip(loads, stores):
+        load.wait()
+        store.start()
+    for store in stores:
+        store.wait()
+
+
+def pick(rows, row_of, src, counts, place, limit):
     item = src.shape[1:]
+    total = sum(counts)
     return pl.pallas_call(
-        functools.partial(pick_kernel, counts=counts),
+        functools.partial(pick_kernel, row_of=row_of, count=total),
         out_shape=[jax.ShapeDtypeStruct((n, *item), src.dtype) for n in counts],
         in_specs=[SM, place],
-        out_specs=[VM] * len(counts),
-        scratch_shapes=[pltpu.SemaphoreType.DMA((sum(counts),))],
-        compiler_params=params(),
+        out_specs=[ANY] * len(counts),
+        scratch_shapes=[
+            pltpu.VMEM((total, *item), src.dtype),
+            pltpu.SemaphoreType.DMA((total,)),
+            pltpu.SemaphoreType.DMA((total,)),
+        ],
+        compiler_params=pltpu.CompilerParams(vmem_limit_bytes=limit),
     )(rows, src)
 
 
@@ -158,15 +168,15 @@
         [(qt_in.at[c], qt_ref)]
         + [(x_in[p], x_ref.at[pl.ds(p * slots, slots)]) for p in range(pieces)]
     )
+    wait_all(x_loads)
     wv_loads = start([(wv_in, wv_ref)])
-    wo_loads = start(row_blocks(wo_in, wo_ref, 4))
     dt_loads = start([(dt_in.at[c], dt_ref)])
     wk_loads = start([(wk_in, wk_ref)])
     if last:
         q_ref, dm_ref, t0_ref, u0_ref, gw_ref = refs[:5]
         last_loads = start(list(zip(ins[5:], (q_ref, dm_ref, t0_ref, u0_ref))))
+    wo_loads = start(row_blocks(wo_in, wo_ref, 4))
     factor = 1.0 / math.sqrt(HD)
-    wait_all(x_loads)
     x = x_ref[...].reshape(pieces * slots * sub, enc)
     keys = x.shape[0]
     s = mm(qt_ref[...], x, 1, 1) * factor
@@ -284,20 +294,32 @@
     enc = encodings.shape[2]
     head_at = lax.axis_index("head")
     at = jnp.stack([head_at // 2, head_at % 2]).astype(jnp.int32)
-    owner_ids = lax.broadcasted_iota(jnp.int32, (db_count, 1, 1), 0)
-    wanted = jnp.sum(jnp.where(nbr_owner[None] == owner_ids, nbr_row[None], 0), axis=2)
+    owner_ids = lax.broadcasted_iota(jnp.int32, (db_count, 1, 1, 1), 0)
+    wanted = jnp.sum(jnp.where(nbr_owner[None, None] == owner_ids, nbr_row[None, None], 0), axis=3)
     incoming = exchange(wanted, "db")
     steps = ring_steps(head_count)
-    (table,) = pick(incoming.reshape(-1), encodings, (db_count * groups,), HBM)
-    near = [grad_out] + [along(after(grad_out, wanted), s, head_count) for s in steps]
-    near = lax.optimization_barrier((*near, table))[:-1]
+    (table,) = pick(
+        incoming,
+        lambda ref, k: ref[k // groups, 0, k % groups],
+        encodings,
+        (db_count * groups,),
+        HBM,
+        VMEM_LIMIT,
+    )
+    received = exchange(table, "db")
+    mine = pick(
+        nbr_owner,
+        lambda ref, k: ref[k // slot_count, k % slot_count] * groups + k // slot_count,
+        received,
+        (slot_count,) * groups,
+        ANY,
+        SMALL_LIMIT,
+    )
+    token = mine[0]
+    near = [grad_out] + [along(after(grad_out, table), s, head_count) for s in steps]
     near = jnp.stack([near[([0] + steps).index(s)] for s in range(chips)])
     far = swap(near, head_count)
     dm, qt, dt, grad_cols = prep(at, near, far, w_out, queries, w_key, w_value, groups, db_count)
-    received = after(exchange(table, "db"), dm)
-    rows = nbr_owner * groups + lax.broadcasted_iota(jnp.int32, nbr_owner.shape, 0)
-    mine = pick(rows.reshape(-1), received, (slot_count,) * groups, ANY)
-    token = mine[0]
     ring = []
     for c in range(groups):
         held = mine[c] if c == 0 else after(mine[c], *ring[-1])
@@ -325,12 +347,14 @@
     attended = sum(t.astype(F32) for t in terms).astype(BF)
     share = enc // db_count
     grad_tok = grad_tok.reshape(db_count, groups, part, -1)
-    grad_wo = sum(
-        lax.dot_general(
+    grad_wo = None
+    for c in range(groups):
+        term = lax.dot_general(
             sent[c][:, :part], grad_tok[:, c], (((0, 1), (0, 1)), ((), ())), preferred_element_type=F32
         )
-        for c in range(groups)
-    )
+        grad_wo = term if grad_wo is None else grad_wo + term
+        if c < groups - 1:
+            sent[-1], grad_wo = lax.optimization_barrier((sent[-1], grad_wo))
     grad_w = [
         jnp.sum(sent[-1][:, part + k * share : part + (k + 1) * share].astype(F32), axis=0)
         for k in range(2)

time: 151 us -> 148 us (0.980)
  local copies, waits for them, and re-layouts: 6.05 us -> 3.41 us
    all_to_all x4, waiting for transfers between devices: 32 us -> 28.4 us  [exchange(): return lax.all_to_all(x, axis, split_axis=0, concat_axis=0, tiled=True)]
    ppermute x12, waiting for transfers between devices: 17.1 us -> 19.9 us  [along(): lax.ppermute(v, 'head', [(i, (i // 2 + step) % chips * 2 + i % 2) for i i...]
  transfers between devices with their start and end apart: 26 -> 26, of which waited for: 16 -> 19; matrix products, arithmetic and copies ran while one was open for 4% -> 3% of each run, Pallas kernels for 18% -> 16%
where the time goes in v5:
time: 148 us; the launch traced here: 147 us
  waiting for transfers between devices  52.9 us (36%)
  starting transfers between devices  35.9 us (24%)
  Pallas kernels  29.4 us (20%)
  blocking collectives  15.3 us (10%)
  other arithmetic  6.02 us (4%)
  local copies, waits for them, and re-layouts  3.41 us (2%)
  matrix products  2.79 us (2%)
    all_to_all x4, waiting for transfers between devices, exchange(): return lax.all_to_all(x, axis, split_axis=0, concat_axis=0, tiled=True)  28.4 us
    ppermute x12, waiting for transfers between devices, along(): lax.ppermute(v, 'head', [(i, (i // 2 + step) % chips * 2 + i % 2) for i i...  19.9 us
    all_to_all x4, starting transfers between devices, exchange(): return lax.all_to_all(x, axis, split_axis=0, concat_axis=0, tiled=True)  17.9 us
    pallas_call x2, Pallas kernels, attn(): pl.pallas_call(functools.partial(attn_kernel, c=c, pieces=len(xs), last=l...  16.9 us
    ppermute x12, starting transfers between devices, along(): lax.ppermute(v, 'head', [(i, (i // 2 + step) % chips * 2 + i % 2) for i i...  16.6 us
    all_to_all x1, blocking collectives, exchange(): return lax.all_to_all(x, axis, split_axis=0, concat_axis=0, tiled=True)  15.3 us
    pallas_call x1, Pallas kernels, prep(): pl.pallas_call(prep_kernel, out_shape=[jax.ShapeDtypeStruct((rows, width)...  6.71 us
    pallas_call x2, Pallas kernels, pick(): pl.pallas_call(functools.partial(pick_kernel, row_of=row_of, count=total)...  5.77 us
  transfers between devices with their start and end apart: 26, of which 19 were waited for; matrix products, arithmetic and copies ran while one was open for 3% of the time, Pallas kernels for 16%

profile of v5, /device:TPU:0, one launch (start us, length us, event | category | flops | bytes accessed | tf_op | source)
XLA Modules:
  0.0 146.7 jit_solution(6176171613270884308)
XLA Ops:
  1.5 15.3 %all_to_all.25.rows_ref = s32[16,1,2]{2,1,0:T(1,128)} all-to-all(s32[16,1,2]{2,1,0:T(1,128)S(1)} %copy.17), channel_id=1, replica_groups=mesh['db'=16,'head'=8] {'db'}, dimensions={0} | all-to-all | bytes 256 | tf_op jit(solution)/shard_map/all_to_all | solution.py:280
  16.8 3.6 %shard_map.128 = bf16[32,16,896]{2,1,0:T(8,128)(2,1)} custom-call(s32[16,1,2]{2,1,0:T(1,128)} %all_to_all.25.rows_ref, bf16[64,16,896]{2,1,0:T(8,128)(2,1)} %src_ref.1), custom_call_target="tpu_custom_call" | custom-call | tf_op jit(solution)/shard_map/pallas_call | solution.py:52
  20.4 3.1 %collective-permute-start.9 = (bf16[128,512]{1,0:T(8,128)(2,1)}, bf16[128,512]{1,0:T(8,128)(2,1)S(1)}, u32[]{:S(2)}, u32[]{:S(2)}) collective-permute-start(bf16[128,512]{1,0:T(8,128)(2,1)} %param.17), channel_id=1, source_target_pairs={{0,6},{1,7},{2,0},{3,1},{4,2},{5,3},{6,4},{7,5},{8,14},{9,15},{10,... | collective-permute-start | bytes 393224 | tf_op jit(solution)/shard_map/ppermute | solution.py:267
  25.1 3.6 %all-to-all-start.1 = ((bf16[32,16,896]{2,1,0:T(8,128)(2,1)}), bf16[32,16,896]{2,1,0:T(8,128)(2,1)S(1)}, u32[]{:S(2)}, u32[]{:S(2)}) async-start(bf16[32,16,896]{2,1,0:T(8,128)(2,1)} %shard_map.128), calls=%async_computation.1 | async-start | bytes 1835008 | tf_op jit(solution)/shard_map/all_to_all | solution.py:280
  28.8 1.7 %collective-permute-done.8 = bf16[128,512]{1,0:T(8,128)(2,1)S(1)} collective-permute-done((bf16[128,512]{1,0:T(8,128)(2,1)}, bf16[128,512]{1,0:T(8,128)(2,1)S(1)}, u32[]{:S(2)}, u32[]{:S(2)}) %collective-permute-start.8) | collective-permute-done | bytes 131104 | tf_op jit(solution)/shard_map/ppermute | solution.py:267
  34.6 6.7 %shard_map.130 = (bf16[128,512]{1,0:T(8,128)(2,1)}, bf16[2,256,896]{2,1,0:T(8,128)(2,1)}, bf16[2,256,896]{2,1,0:T(8,128)(2,1)}, bf16[16,128,256]{2,1,0:T(8,128)(2,1)}) custom-call(s32[2]{0:T(128)} %pad_add_fusion.at_ref, bf16[4,128,512]{2,1,0:T(8,128)(2,1)} %copy-done.3, bf16[4,128,512]{2,1,0:T(8,128)(2,1)} %copy-done.8, bf16[512,4096]{1,0:T(8,128)(2,1)} %refs_12_.3, ...), custom_call_target="tpu_custom_call" | custom-call | flops 1000000000 | bytes 10000000 | tf_op jit(solution)/shard_map/pallas_call | solution.py:129
  42.6 2.2 %shard_map.129 = (bf16[8,16,896]{2,1,0:T(8,128)(2,1)S(1)}, bf16[8,16,896]{2,1,0:T(8,128)(2,1)S(1)}) custom-call(s32[2,8]{1,0:T(2,128)S(1)} %copy-done, bf16[32,16,896]{2,1,0:T(8,128)(2,1)S(1)} %all-to-all-done.1.src_ref), custom_call_target="tpu_custom_call" | custom-call | tf_op jit(solution)/shard_map/pallas_call | solution.py:52
  44.8 3.7 %all-to-all-start.2 = ((bf16[16,128,256]{2,1,0:T(8,128)(2,1)}), bf16[16,128,256]{2,1,0:T(8,128)(2,1)S(1)}, u32[]{:S(2)}, u32[]{:S(2)}) async-start(bf16[16,128,256]{2,1,0:T(8,128)(2,1)} %get-tuple-element.46), calls=%async_computation.2 | async-start | bytes 2097152 | tf_op jit(solution)/shard_map/all_to_all | solution.py:280
  48.4 2.0 %collective-permute-start = (bf16[8,16,896]{2,1,0:T(8,128)(2,1)S(1)}, bf16[8,16,896]{2,1,0:T(8,128)(2,1)S(1)}, u32[]{:S(2)}, u32[]{:S(2)}) collective-permute-start(bf16[8,16,896]{2,1,0:T(8,128)(2,1)S(1)} %get-tuple-element.28.refs_0_), channel_id=1, source_target_pairs={{0,2},{1,3},{2,4},{3,5},{4,6},{5,7},{6,0},{7,1},{8,10},{9,11},{10,... | collective-permute-start | bytes 688136 | tf_op jit(solution)/shard_map/ppermute | solution.py:267
  52.8 5.0 %collective-permute-done.refs_1_ = bf16[8,16,896]{2,1,0:T(8,128)(2,1)S(1)} collective-permute-done((bf16[8,16,896]{2,1,0:T(8,128)(2,1)S(1)}, bf16[8,16,896]{2,1,0:T(8,128)(2,1)S(1)}, u32[]{:S(2)}, u32[]{:S(2)}) %collective-permute-start) | collective-permute-done | bytes 229408 | tf_op jit(solution)/shard_map/ppermute | solution.py:267
  59.0 2.9 %collective-permute-done.2.refs_3_ = bf16[8,16,896]{2,1,0:T(8,128)(2,1)S(1)} collective-permute-done((bf16[8,16,896]{2,1,0:T(8,128)(2,1)S(1)}, bf16[8,16,896]{2,1,0:T(8,128)(2,1)S(1)}, u32[]{:S(2)}, u32[]{:S(2)}) %collective-permute-start.2) | collective-permute-done | bytes 229408 | tf_op jit(solution)/shard_map/ppermute | solution.py:267
  63.0 2.1 %collective-permute-start.12 = (bf16[8,16,896]{2,1,0:T(8,128)(2,1)S(1)}, bf16[8,16,896]{2,1,0:T(8,128)(2,1)S(1)}, u32[]{:S(2)}, u32[]{:S(2)}) collective-permute-start(bf16[8,16,896]{2,1,0:T(8,128)(2,1)S(1)} %get-tuple-element.34.refs_0_), channel_id=1, source_target_pairs={{0,6},{1,7},{2,0},{3,1},{4,2},{5,3},{6,4},{7,5},{8,14},{9,15},{10,... | collective-permute-start | bytes 688136 | tf_op jit(solution)/shard_map/ppermute | solution.py:267
  66.8 8.2 %shard_map.131 = (bf16[16,64,512]{2,1,0:T(8,128)(2,1)}, bf16[4,64,512]{2,1,0:T(8,128)(2,1)}, bf16[4,64,512]{2,1,0:T(8,128)(2,1)}, bf16[64,512]{1,0:T(8,128)(2,1)...) custom-call(s32[2]{0:T(128)} %pad_add_fusion.at_ref, s32[2]{0:T(128)} %count_ref.3, bf16[8,16,896]{2,1,0:T(8,128)(2,1)} %copy-done.2, ...), custom_call_target="tpu_custom_call" | custom-call | flops 4000000000 | bytes 12000000 | tf_op jit(solution)/shard_map/pallas_call | solution.py:254
  75.3 1.5 %collective-permute-done.13.refs_3_ = bf16[8,16,896]{2,1,0:T(8,128)(2,1)S(1)} collective-permute-done((bf16[8,16,896]{2,1,0:T(8,128)(2,1)S(1)}, bf16[8,16,896]{2,1,0:T(8,128)(2,1)S(1)}, u32[]{:S(2)}, u32[]{:S(2)}) %collective-permute-start.13) | collective-permute-done | bytes 229408 | tf_op jit(solution)/shard_map/ppermute | solution.py:267
  76.8 6.9 %all-to-all-start.3 = ((bf16[16,64,512]{2,1,0:T(8,128)(2,1)}), bf16[16,64,512]{2,1,0:T(8,128)(2,1)S(1)}, u32[]{:S(2)}, u32[]{:S(2)}) async-start(bf16[16,64,512]{2,1,0:T(8,128)(2,1)} %get-tuple-element.47), calls=%async_computation.3 | async-start | bytes 2097152 | tf_op jit(solution)/shard_map/all_to_all | solution.py:280
  87.1 8.8 %shard_map.132 = (bf16[16,176,512]{2,1,0:T(8,128)(2,1)}, bf16[4,64,512]{2,1,0:T(8,128)(2,1)}, bf16[4,64,512]{2,1,0:T(8,128)(2,1)}, bf16[64,512]{1,0:T(8,128)(2,1)}) custom-call(s32[2]{0:T(128)} %pad_add_fusion.at_ref, s32[2]{0:T(128)} %count_ref.3, bf16[8,16,896]{2,1,0:T(8,128)(2,1)} %copy-done.1, bf16[8,16,896]{2,1,0:T(8,128)(2,1)} %copy-done.14, ...), custom_call_target="tpu_custom_call" | custom-call | flops 4000000000 | bytes 12000000 | tf_op jit(solution)/shard_map/pallas_call | solution.py:254
  95.9 5.3 %all-to-all-done.3 = bf16[16,64,512]{2,1,0:T(8,128)(2,1)S(1)} async-done(((bf16[16,64,512]{2,1,0:T(8,128)(2,1)}), bf16[16,64,512]{2,1,0:T(8,128)(2,1)S(1)}, u32[]{:S(2)}, u32[]{:S(2)}) %all-to-all-start.3) | async-done | bytes 1048608 | tf_op jit(solution)/shard_map/all_to_all | solution.py:280
  102.2 3.7 %all-to-all-start.4 = ((bf16[16,176,512]{2,1,0:T(8,128)(2,1)}), bf16[16,176,512]{2,1,0:T(8,128)(2,1)S(1)}, u32[]{:S(2)}, u32[]{:S(2)}) async-start(bf16[16,176,512]{2,1,0:T(8,128)(2,1)} %get-tuple-element.48), calls=%async_computation.4 | async-start | bytes 5767168 | tf_op jit(solution)/shard_map/all_to_all | solution.py:280
  107.2 1.9 %collective-permute-done.18 = bf16[4,128,512]{2,1,0:T(8,128)(2,1)S(1)} collective-permute-done((bf16[4,128,512]{2,1,0:T(8,128)(2,1)S(1)}, bf16[4,128,512]{2,1,0:T(8,128)(2,1)S(1)}, u32[]{:S(2)}, u32[]{:S(2)}) %collective-permute-start.18) | collective-permute-done | bytes 524320 | tf_op jit(solution)/shard_map/ppermute | solution.py:271
  111.2 2.5 %collective-permute-start.20 = (bf16[128,512]{1,0:T(8,128)(2,1)S(1)}, bf16[128,512]{1,0:T(8,128)(2,1)S(1)}, u32[]{:S(2)}, u32[]{:S(2)}) collective-permute-start(bf16[128,512]{1,0:T(8,128)(2,1)S(1)} %get-tuple-element.55), channel_id=1, source_target_pairs={{0,6},{1,7},{2,0},{3,1},{4,2},{5,3},{6,4},{7,5},{8,14},{9,15},{10,... | collective-permute-start | bytes 393224 | tf_op jit(solution)/shard_map/ppermute | solution.py:267
  114.4 3.8 %collective-permute-done.21 = bf16[128,512]{1,0:T(8,128)(2,1)S(1)} collective-permute-done((bf16[128,512]{1,0:T(8,128)(2,1)S(1)}, bf16[128,512]{1,0:T(8,128)(2,1)S(1)}, u32[]{:S(2)}, u32[]{:S(2)}) %collective-permute-start.21) | collective-permute-done | bytes 131104 | tf_op jit(solution)/shard_map/ppermute | solution.py:267
  118.3 2.2 %collective-permute-done.19 = bf16[128,512]{1,0:T(8,128)(2,1)S(1)} collective-permute-done((bf16[128,512]{1,0:T(8,128)(2,1)S(1)}, bf16[128,512]{1,0:T(8,128)(2,1)S(1)}, u32[]{:S(2)}, u32[]{:S(2)}) %collective-permute-start.19) | collective-permute-done | bytes 131104 | tf_op jit(solution)/shard_map/ppermute | solution.py:267
  121.7 21.8 %all-to-all-done.4 = bf16[16,176,512]{2,1,0:T(8,128)(2,1)S(1)} async-done(((bf16[16,176,512]{2,1,0:T(8,128)(2,1)}), bf16[16,176,512]{2,1,0:T(8,128)(2,1)S(1)}, u32[]{:S(2)}, u32[]{:S(2)}) %all-to-all-start.4) | async-done | bytes 2883616 | tf_op jit(solution)/shard_map/all_to_all | solution.py:280
  144.4 2.3 %fusion = f32[512,256]{1,0:T(8,128)} fusion(f32[512,256]{1,0:T(8,128)S(1)} %convolution_bitcast_fusion.1, bf16[16,176,512]{2,1,0:T(8,128)(2,1)S(1)} %all-to-all-done.4, bf16[16,2,64,256]{3,2,1,0:T(8,128)(2,1)} %bitcast.36), kind=kOutput, calls=%fused_computation.4 | convolution fusion | flops 268566528 | bytes 2621440 | tf_op jit(solution)/shard_map/dot_general | solution.py:352
  (102 shorter events, 25.1 us)
Async XLA Ops:
  20.4 8.3 %collective-permute-start.9 = (bf16[128,512]{1,0:T(8,128)(2,1)}, bf16[128,512]{1,0:T(8,128)(2,1)S(1)}, u32[]{:S(2)}, u32[]{:S(2)}) collective-permute-start(bf16[128,512]{1,0:T(8,128)(2,1)} %param.17), channel_id=1, source_target_pairs={{0,6},{1,7},{2,0},{3,1},{4,2},{5,3},{6,4},{7,5},{8,14},{9,15},{10,... | collective-permute-start | bytes 393224 | tf_op jit(solution)/shard_map/ppermute | solution.py:267
  23.5 6.9 %collective-permute-start.8 = (bf16[128,512]{1,0:T(8,128)(2,1)}, bf16[128,512]{1,0:T(8,128)(2,1)S(1)}, u32[]{:S(2)}, u32[]{:S(2)}) collective-permute-start(bf16[128,512]{1,0:T(8,128)(2,1)} %param.17), channel_id=1, source_target_pairs={{0,4},{1,5},{2,6},{3,7},{4,0},{5,1},{6,2},{7,3},{8,12},{9,13},{10,... | collective-permute-start | bytes 393224 | tf_op jit(solution)/shard_map/ppermute | solution.py:267
  24.1 7.6 %collective-permute-start.7 = (bf16[128,512]{1,0:T(8,128)(2,1)}, bf16[128,512]{1,0:T(8,128)(2,1)S(1)}, u32[]{:S(2)}, u32[]{:S(2)}) collective-permute-start(bf16[128,512]{1,0:T(8,128)(2,1)} %param.17), channel_id=1, source_target_pairs={{0,2},{1,3},{2,4},{3,5},{4,6},{5,7},{6,0},{7,1},{8,10},{9,11},{10,... | collective-permute-start | bytes 393224 | tf_op jit(solution)/shard_map/ppermute | solution.py:267
  25.1 17.5 %all-to-all-start.1 = ((bf16[32,16,896]{2,1,0:T(8,128)(2,1)}), bf16[32,16,896]{2,1,0:T(8,128)(2,1)S(1)}, u32[]{:S(2)}, u32[]{:S(2)}) async-start(bf16[32,16,896]{2,1,0:T(8,128)(2,1)} %shard_map.128), calls=%async_computation.1 | async-start | bytes 1835008 | tf_op jit(solution)/shard_map/all_to_all | solution.py:280
  31.8 2.0 %collective-permute-start.10 = (bf16[4,128,512]{2,1,0:T(8,128)(2,1)S(1)}, bf16[4,128,512]{2,1,0:T(8,128)(2,1)S(1)}, u32[]{:S(2)}, u32[]{:S(2)}) collective-permute-start(bf16[4,128,512]{2,1,0:T(8,128)(2,1)S(1)} %pad_maximum_fusion.refs_0_), channel_id=1, source_target_pairs={{0,1},{1,0},{2,3},{3,2},{4,5},{5,4},{6,7},{7,6},{8,9},{9,8},{10,11... | collective-permute-start | bytes 1572872 | tf_op jit(solution)/shard_map/ppermute | solution.py:271
  44.8 32.0 %all-to-all-start.2 = ((bf16[16,128,256]{2,1,0:T(8,128)(2,1)}), bf16[16,128,256]{2,1,0:T(8,128)(2,1)S(1)}, u32[]{:S(2)}, u32[]{:S(2)}) async-start(bf16[16,128,256]{2,1,0:T(8,128)(2,1)} %get-tuple-element.46), calls=%async_computation.2 | async-start | bytes 2097152 | tf_op jit(solution)/shard_map/all_to_all | solution.py:280
  48.4 9.3 %collective-permute-start = (bf16[8,16,896]{2,1,0:T(8,128)(2,1)S(1)}, bf16[8,16,896]{2,1,0:T(8,128)(2,1)S(1)}, u32[]{:S(2)}, u32[]{:S(2)}) collective-permute-start(bf16[8,16,896]{2,1,0:T(8,128)(2,1)S(1)} %get-tuple-element.28.refs_0_), channel_id=1, source_target_pairs={{0,2},{1,3},{2,4},{3,5},{4,6},{5,7},{6,0},{7,1},{8,10},{9,11},{10,... | collective-permute-start | bytes 688136 | tf_op jit(solution)/shard_map/ppermute | solution.py:267
  50.4 8.5 %collective-permute-start.1 = (bf16[8,16,896]{2,1,0:T(8,128)(2,1)S(1)}, bf16[8,16,896]{2,1,0:T(8,128)(2,1)S(1)}, u32[]{:S(2)}, u32[]{:S(2)}) collective-permute-start(bf16[8,16,896]{2,1,0:T(8,128)(2,1)S(1)} %get-tuple-element.28.refs_0_), channel_id=1, source_target_pairs={{0,6},{1,7},{2,0},{3,1},{4,2},{5,3},{6,4},{7,5},{8,14},{9,15},{10,... | collective-permute-start | bytes 688136 | tf_op jit(solution)/shard_map/ppermute | solution.py:267
  51.8 10.1 %collective-permute-start.2 = (bf16[8,16,896]{2,1,0:T(8,128)(2,1)S(1)}, bf16[8,16,896]{2,1,0:T(8,128)(2,1)S(1)}, u32[]{:S(2)}, u32[]{:S(2)}) collective-permute-start(bf16[8,16,896]{2,1,0:T(8,128)(2,1)S(1)} %get-tuple-element.28.refs_0_), channel_id=1, source_target_pairs={{0,4},{1,5},{2,6},{3,7},{4,0},{5,1},{6,2},{7,3},{8,12},{9,13},{10,... | collective-permute-start | bytes 688136 | tf_op jit(solution)/shard_map/ppermute | solution.py:267
  52.8 10.2 %collective-permute-start.3 = (bf16[8,16,896]{2,1,0:T(8,128)(2,1)S(1)}, bf16[8,16,896]{2,1,0:T(8,128)(2,1)S(1)}, u32[]{:S(2)}, u32[]{:S(2)}) collective-permute-start(bf16[8,16,896]{2,1,0:T(8,128)(2,1)S(1)} %get-tuple-element.28.refs_0_), channel_id=1, source_target_pairs={{0,1},{1,0},{2,3},{3,2},{4,5},{5,4},{6,7},{7,6},{8,9},{9,8},{10,11... | collective-permute-start | bytes 688136 | tf_op jit(solution)/shard_map/ppermute | solution.py:271
  57.8 7.3 %collective-permute-start.4 = (bf16[8,16,896]{2,1,0:T(8,128)(2,1)S(1)}, bf16[8,16,896]{2,1,0:T(8,128)(2,1)S(1)}, u32[]{:S(2)}, u32[]{:S(2)}) collective-permute-start(bf16[8,16,896]{2,1,0:T(8,128)(2,1)S(1)} %collective-permute-done.refs_1_), channel_id=1, source_target_pairs={{0,1},{1,0},{2,3},{3,2},{4,5},{5,4},{6,7},{7,6},{8,9},{9,8},{10,11... | collective-permute-start | bytes 688136 | tf_op jit(solution)/shard_map/ppermute | solution.py:271
  59.0 7.1 %collective-permute-start.5 = (bf16[8,16,896]{2,1,0:T(8,128)(2,1)S(1)}, bf16[8,16,896]{2,1,0:T(8,128)(2,1)S(1)}, u32[]{:S(2)}, u32[]{:S(2)}) collective-permute-start(bf16[8,16,896]{2,1,0:T(8,128)(2,1)S(1)} %collective-permute-done.1.refs_2_), channel_id=1, source_target_pairs={{0,1},{1,0},{2,3},{3,2},{4,5},{5,4},{6,7},{7,6},{8,9},{9,8},{10,11... | collective-permute-start | bytes 688136 | tf_op jit(solution)/shard_map/ppermute | solution.py:271
  61.9 4.2 %collective-permute-start.6 = (bf16[8,16,896]{2,1,0:T(8,128)(2,1)S(1)}, bf16[8,16,896]{2,1,0:T(8,128)(2,1)S(1)}, u32[]{:S(2)}, u32[]{:S(2)}) collective-permute-start(bf16[8,16,896]{2,1,0:T(8,128)(2,1)S(1)} %collective-permute-done.2.refs_3_), channel_id=1, source_target_pairs={{0,1},{1,0},{2,3},{3,2},{4,5},{5,4},{6,7},{7,6},{8,9},{9,8},{10,11... | collective-permute-start | bytes 688136 | tf_op jit(solution)/shard_map/ppermute | solution.py:271
  61.9 13.1 %collective-permute-start.11 = (bf16[8,16,896]{2,1,0:T(8,128)(2,1)S(1)}, bf16[8,16,896]{2,1,0:T(8,128)(2,1)S(1)}, u32[]{:S(2)}, u32[]{:S(2)}) collective-permute-start(bf16[8,16,896]{2,1,0:T(8,128)(2,1)S(1)} %get-tuple-element.34.refs_0_), channel_id=1, source_target_pairs={{0,2},{1,3},{2,4},{3,5},{4,6},{5,7},{6,0},{7,1},{8,10},{9,11},{10,... | collective-permute-start | bytes 688136 | tf_op jit(solution)/shard_map/ppermute | solution.py:267
  63.0 12.3 %collective-permute-start.12 = (bf16[8,16,896]{2,1,0:T(8,128)(2,1)S(1)}, bf16[8,16,896]{2,1,0:T(8,128)(2,1)S(1)}, u32[]{:S(2)}, u32[]{:S(2)}) collective-permute-start(bf16[8,16,896]{2,1,0:T(8,128)(2,1)S(1)} %get-tuple-element.34.refs_0_), channel_id=1, source_target_pairs={{0,6},{1,7},{2,0},{3,1},{4,2},{5,3},{6,4},{7,5},{8,14},{9,15},{10,... | collective-permute-start | bytes 688136 | tf_op jit(solution)/shard_map/ppermute | solution.py:267
  65.1 11.7 %collective-permute-start.13 = (bf16[8,16,896]{2,1,0:T(8,128)(2,1)S(1)}, bf16[8,16,896]{2,1,0:T(8,128)(2,1)S(1)}, u32[]{:S(2)}, u32[]{:S(2)}) collective-permute-start(bf16[8,16,896]{2,1,0:T(8,128)(2,1)S(1)} %get-tuple-element.34.refs_0_), channel_id=1, source_target_pairs={{0,4},{1,5},{2,6},{3,7},{4,0},{5,1},{6,2},{7,3},{8,12},{9,13},{10,... | collective-permute-start | bytes 688136 | tf_op jit(solution)/shard_map/ppermute | solution.py:267
  76.8 24.4 %all-to-all-start.3 = ((bf16[16,64,512]{2,1,0:T(8,128)(2,1)}), bf16[16,64,512]{2,1,0:T(8,128)(2,1)S(1)}, u32[]{:S(2)}, u32[]{:S(2)}) async-start(bf16[16,64,512]{2,1,0:T(8,128)(2,1)} %get-tuple-element.47), calls=%async_computation.3 | async-start | bytes 2097152 | tf_op jit(solution)/shard_map/all_to_all | solution.py:280
  84.0 1.8 %collective-permute-start.15 = (bf16[8,16,896]{2,1,0:T(8,128)(2,1)S(1)}, bf16[8,16,896]{2,1,0:T(8,128)(2,1)S(1)}, u32[]{:S(2)}, u32[]{:S(2)}) collective-permute-start(bf16[8,16,896]{2,1,0:T(8,128)(2,1)S(1)} %collective-permute-done.11.refs_1_), channel_id=1, source_target_pairs={{0,1},{1,0},{2,3},{3,2},{4,5},{5,4},{6,7},{7,6},{8,9},{9,8},{10,11... | collective-permute-start | bytes 688136 | tf_op jit(solution)/shard_map/ppermute | solution.py:271
  84.6 1.9 %collective-permute-start.17 = (bf16[8,16,896]{2,1,0:T(8,128)(2,1)S(1)}, bf16[8,16,896]{2,1,0:T(8,128)(2,1)S(1)}, u32[]{:S(2)}, u32[]{:S(2)}) collective-permute-start(bf16[8,16,896]{2,1,0:T(8,128)(2,1)S(1)} %collective-permute-done.13.refs_3_), channel_id=1, source_target_pairs={{0,1},{1,0},{2,3},{3,2},{4,5},{5,4},{6,7},{7,6},{8,9},{9,8},{10,11... | collective-permute-start | bytes 688136 | tf_op jit(solution)/shard_map/ppermute | solution.py:271
  102.2 41.3 %all-to-all-start.4 = ((bf16[16,176,512]{2,1,0:T(8,128)(2,1)}), bf16[16,176,512]{2,1,0:T(8,128)(2,1)S(1)}, u32[]{:S(2)}, u32[]{:S(2)}) async-start(bf16[16,176,512]{2,1,0:T(8,128)(2,1)} %get-tuple-element.48), calls=%async_computation.4 | async-start | bytes 5767168 | tf_op jit(solution)/shard_map/all_to_all | solution.py:280
  107.2 2.0 %collective-permute-start.18 = (bf16[4,128,512]{2,1,0:T(8,128)(2,1)S(1)}, bf16[4,128,512]{2,1,0:T(8,128)(2,1)S(1)}, u32[]{:S(2)}, u32[]{:S(2)}) collective-permute-start(bf16[4,128,512]{2,1,0:T(8,128)(2,1)S(1)} %pad_maximum_fusion.1), channel_id=1, source_target_pairs={{0,1},{1,0},{2,3},{3,2},{4,5},{5,4},{6,7},{7,6},{8,9},{9,8},{10,11... | collective-permute-start | bytes 1572872 | tf_op jit(solution)/shard_map/ppermute | solution.py:271
  110.3 7.9 %collective-permute-start.21 = (bf16[128,512]{1,0:T(8,128)(2,1)S(1)}, bf16[128,512]{1,0:T(8,128)(2,1)S(1)}, u32[]{:S(2)}, u32[]{:S(2)}) collective-permute-start(bf16[128,512]{1,0:T(8,128)(2,1)S(1)} %get-tuple-element.54), channel_id=1, source_target_pairs={{0,4},{1,5},{2,6},{3,7},{4,0},{5,1},{6,2},{7,3},{8,12},{9,13},{10,... | collective-permute-start | bytes 393224 | tf_op jit(solution)/shard_map/ppermute | solution.py:267
  111.2 7.1 %collective-permute-start.20 = (bf16[128,512]{1,0:T(8,128)(2,1)S(1)}, bf16[128,512]{1,0:T(8,128)(2,1)S(1)}, u32[]{:S(2)}, u32[]{:S(2)}) collective-permute-start(bf16[128,512]{1,0:T(8,128)(2,1)S(1)} %get-tuple-element.55), channel_id=1, source_target_pairs={{0,6},{1,7},{2,0},{3,1},{4,2},{5,3},{6,4},{7,5},{8,14},{9,15},{10,... | collective-permute-start | bytes 393224 | tf_op jit(solution)/shard_map/ppermute | solution.py:267
  113.7 6.7 %collective-permute-start.19 = (bf16[128,512]{1,0:T(8,128)(2,1)S(1)}, bf16[128,512]{1,0:T(8,128)(2,1)S(1)}, u32[]{:S(2)}, u32[]{:S(2)}) collective-permute-start(bf16[128,512]{1,0:T(8,128)(2,1)S(1)} %get-tuple-element.53), channel_id=1, source_target_pairs={{0,2},{1,3},{2,4},{3,5},{4,6},{5,7},{6,0},{7,1},{8,10},{9,11},{10,... | collective-permute-start | bytes 393224 | tf_op jit(solution)/shard_map/ppermute | solution.py:267
  (30 other events, 246.7 us)

commit v6 on v5

v6 whole, which is shorter than its diff:
```python
import functools
import math

import jax
import jax.numpy as jnp
from jax import lax
from jax.experimental import pallas as pl
from jax.experimental.pallas import tpu as pltpu
from jax.sharding import PartitionSpec as P

HD = 128
BF = jnp.bfloat16
F32 = jnp.float32
VMEM_LIMIT = 60 * 1024 * 1024
SMALL_LIMIT = 8 * 1024 * 1024


def mm(a, b, ca, cb):
    return lax.dot_general(a, b, (((ca,), (cb,)), ((), ())), preferred_element_type=F32)


def params():
    return pltpu.CompilerParams(vmem_limit_bytes=VMEM_LIMIT)


ANY = pl.BlockSpec(memory_space=pl.ANY)
HBM = pl.BlockSpec(memory_space=pltpu.HBM)
VM = pl.BlockSpec(memory_space=pltpu.VMEM)
SM = pl.BlockSpec(memory_space=pltpu.SMEM)


def pick_kernel(rows_ref, src_ref, *rest, row_of, count):
    *outs, held, load_sem, store_sem = rest
    places = [out.at[n] for out in outs for n in range(out.shape[0])]
    loads = [
        pltpu.make_async_copy(src_ref.at[row_of(rows_ref, k)], held.at[k], load_sem.at[k])
        for k in range(count)
    ]
    stores = [pltpu.make_async_copy(held.at[k], places[k], store_sem.at[k]) for k in range(count)]
    for load in loads:
        load.start()
    for load, store in zip(loads, stores):
        load.wait()
        store.start()
    for store in stores:
        store.wait()


def pick(rows, row_of, src, counts, place, limit):
    item = src.shape[1:]
    total = sum(counts)
    return pl.pallas_call(
        functools.partial(pick_kernel, row_of=row_of, count=total),
        out_shape=[jax.ShapeDtypeStruct((n, *item), src.dtype) for n in counts],
        in_specs=[SM, place],
        out_specs=[ANY] * len(counts),
        scratch_shapes=[
            pltpu.VMEM((total, *item), src.dtype),
            pltpu.SemaphoreType.DMA((total,)),
            pltpu.SemaphoreType.DMA((total,)),
        ],
        compiler_params=pltpu.CompilerParams(vmem_limit_bytes=limit),
    )(rows, src)


def start_loads(pairs, sem, first=0):
    loads = [pltpu.make_async_copy(src, dst, sem.at[first + k]) for k, (src, dst) in enumerate(pairs)]
    for load in loads:
        load.start()
    return loads


def wait_all(copies):
    for copy in copies:
        copy.wait()


def row_blocks(src, dst, count):
    step = src.shape[0] // count
    return [(src.at[pl.ds(k * step, step)], dst.at[pl.ds(k * step, step)]) for k in range(count)]


def back_kernel(a_in, w_in, out_in, a_ref, w_ref, out_ref, sem):
    loads = start_loads([(a_in, a_ref), *row_blocks(w_in, w_ref, 4)], sem)
    wait_all(loads)
    back_project(a_ref, w_ref, out_ref)
    wait_all(start_loads([(out_ref, out_in)], sem, len(loads)))


def back_project(a_ref, w_ref, out_ref):
    groups = out_ref.shape[0]
    part = a_ref.shape[0] // groups
    for h in range(a_ref.shape[1] // HD):
        cols = slice(h * HD, (h + 1) * HD)
        value = mm(a_ref[:, cols], w_ref[:, cols], 1, 1).astype(BF)
        for c in range(groups):
            out_ref[c, h * part : (h + 1) * part] = value[c * part : (c + 1) * part]


def back(a, w, groups):
    tall = (groups, a.shape[1] // HD * a.shape[0] // groups, w.shape[0])
    return pl.pallas_call(
        back_kernel,
        out_shape=jax.ShapeDtypeStruct(tall, BF),
        in_specs=[HBM, HBM],
        out_specs=HBM,
        scratch_shapes=[pltpu.VMEM(shape, BF) for shape in (a.shape, w.shape, tall)]
        + [pltpu.SemaphoreType.DMA((6,))],
        compiler_params=params(),
        cost_estimate=pl.CostEstimate(flops=120_000_000, bytes_accessed=2_000_000, transcendentals=0),
    )(a, w)


def prep_kernel(at_ref, near_in, far_in, wo_in, wv_in, dm_out, dt_out, gc_out, *refs):
    near_ref, far_ref, wo_ref, wv_ref, dm_ref, dt_ref, gc_ref, sem = refs
    chips, rows, width = near_ref.shape
    cuts = gc_ref.shape[0] // (2 * chips)
    piece = width // cuts
    share = gc_ref.shape[1]
    own = pl.ds(pl.multiple_of((at_ref[0] * 2 + at_ref[1]) * share, share), share)
    first = start_loads([(near_in, near_ref), (far_in, far_ref)], sem)
    blocks = start_loads(row_blocks(wo_in, wo_ref, 8), sem, 2)
    late = start_loads([(wv_in, wv_ref)], sem, 10)
    wait_all(first)
    places = []
    for core, g_ref in enumerate((near_ref, far_ref)):
        for s in range(chips):
            j = lax.rem(at_ref[0] + chips - s, chips) * 2 + lax.rem(at_ref[1] + core, 2)
            places.append((g_ref, s, pl.ds(pl.multiple_of(j * width, width), width)))
            for p in range(cuts):
                gc_ref[j * cuts + p, :, :piece] = g_ref[s, own, p * piece : (p + 1) * piece]
                gc_ref[j * cuts + p, :, piece:] = jnp.zeros((share, width - piece), BF)
    stores = start_loads([(gc_ref, gc_out)], sem, 11)
    wait_all(blocks)
    acc = jnp.zeros((rows, width), F32)
    for g_ref, s, cols in places:
        acc += mm(g_ref[s], wo_ref[:, cols], 1, 1)
    dm_ref[...] = acc.astype(BF)
    wait_all(late)
    back_project(dm_ref, wv_ref, dt_ref)
    stores += start_loads([(dm_ref, dm_out), (dt_ref, dt_out)], sem, 12)
    wait_all(stores)


def prep(at, near, far, wo, wv, groups, db_count):
    chips, rows, width = near.shape
    tall = (groups, width // HD * rows // groups, wv.shape[0])
    made = [(rows, width), tall, (db_count, rows // (2 * chips), width)]
    operands = (near, far, wo, wv)
    return pl.pallas_call(
        prep_kernel,
        out_shape=[jax.ShapeDtypeStruct(shape, BF) for shape in made],
        in_specs=[SM] + [HBM] * 4,
        out_specs=[HBM] * 3,
        scratch_shapes=[pltpu.VMEM(shape, BF) for shape in (*(v.shape for v in operands), *made)]
        + [pltpu.SemaphoreType.DMA((14,))],
        compiler_params=params(),
        cost_estimate=pl.CostEstimate(flops=700_000_000, bytes_accessed=8_000_000, transcendentals=0),
    )(at, *operands)


def attn_kernel(count_ref, *refs, c, pieces, last):
    x_in, refs = refs[:pieces], refs[pieces:]
    more = 7 if last else 4
    ins, refs = refs[:more], refs[more:]
    outs = 2 if last else 3
    (send_ref, *keep_outs), refs = refs[:outs], refs[outs:]
    x_ref, mixed_ref, t_ref, u_ref, qt_ref, dt_ref, wv_ref, *refs = refs
    sem = refs[-1]
    slots, sub, enc = x_in[0].shape
    qt_in, dt_in, wv_in = ins[:3]
    part, width = mixed_ref.shape
    heads = width // HD
    db_count = send_ref.shape[0]
    used = 0

    def start(pairs):
        nonlocal used
        loads = start_loads(pairs, sem, used)
        used += len(pairs)
        return loads

    x_loads = start(
        [(qt_in.at[c], qt_ref)]
        + [(x_in[p], x_ref.at[pl.ds(p * slots, slots)]) for p in range(pieces)]
    )
    dt_loads = start([(dt_in.at[c], dt_ref)])
    wv_loads = start(row_blocks(wv_in, wv_ref, 2))
    if last:
        q_ref, dm_ref, t0_ref, u0_ref, gw_ref = refs[:5]
        last_loads = start(list(zip(ins[3:], (q_ref, dm_ref, t0_ref, u0_ref))))
    else:
        gs_ref = refs[0]
        gs_loads = start([(ins[3], gs_ref)])
    factor = 1.0 / math.sqrt(HD)
    wait_all(x_loads)
    x = x_ref[...].reshape(pieces * slots * sub, enc)
    keys = x.shape[0]
    s = mm(qt_ref[...], x, 1, 1) * factor
    slot = (lax.broadcasted_iota(jnp.int32, (1, keys), 1) // sub) % slots
    expo = jnp.where(slot < count_ref[c], jnp.exp(s), 0.0)
    probs = expo / jnp.sum(expo, axis=-1, keepdims=True)
    t_ref[...] = mm(probs.astype(BF), x, 1, 0).astype(BF)
    wait_all(wv_loads)
    for h in range(heads):
        cols = slice(h * HD, (h + 1) * HD)
        mixed_ref[:, cols] = mm(t_ref[h * part : (h + 1) * part], wv_ref[:, cols], 1, 0).astype(BF)
    stores = start([(mixed_ref, send_ref.at[i, pl.ds(0, part)]) for i in range(db_count)])
    if not last:
        wait_all(gs_loads)
        tail = pl.ds(part, gs_ref.shape[1])
        stores += start([(t_ref, keep_outs[1]), (gs_ref, send_ref.at[:, tail])])
    wait_all(dt_loads)
    d = mm(dt_ref[...], x, 1, 1)
    inner = jnp.sum(probs * d, axis=-1, keepdims=True)
    ds = (probs * (d - inner) * factor).astype(BF)
    u_ref[...] = mm(ds, x, 1, 0).astype(BF)
    stores += start([(u_ref, keep_outs[0])])
    if last:
        wait_all(last_loads)
        share = enc // db_count
        for h in range(heads):
            rows = slice(h * part, (h + 1) * part)
            cols = slice(h * HD, (h + 1) * HD)
            u_all = jnp.concatenate([u0_ref[rows], u_ref[rows]], axis=0)
            t_all = jnp.concatenate([t0_ref[rows], t_ref[rows]], axis=0)
            sums = (mm(u_all, q_ref[:, cols], 0, 0), mm(t_all, dm_ref[:, cols], 0, 0))
            for k, total in enumerate(sums):
                for i in range(db_count):
                    gw_ref[i, k * share : (k + 1) * share, cols] = total[
                        i * share : (i + 1) * share
                    ].astype(BF)
        stores += start([(gw_ref, send_ref.at[:, pl.ds(part, 2 * share)])])
    wait_all(stores)


def attn(count, xs, qt, dt, wv, c, db_count, extra, last):
    slots, sub, enc = xs[0].shape
    width = wv.shape[1]
    tall = qt.shape[1:]
    part = tall[0] * HD // width
    grown = 2 * enc // db_count if last else extra[0].shape[1]
    made = [(db_count, part + grown, width), tall]
    more = list(extra)
    held = [(len(xs) * slots, sub, enc), (part, width), tall, tall, tall, tall, wv.shape]
    held += [v.shape for v in more]
    copies = len(xs) + 8 + len(more) + db_count
    if last:
        held += [(db_count, grown, width)]
    else:
        made += [tall]
    return pl.pallas_call(
        functools.partial(attn_kernel, c=c, pieces=len(xs), last=last),
        out_shape=[jax.ShapeDtypeStruct(shape, BF) for shape in made],
        in_specs=[SM] + [HBM] * (len(xs) + 3 + len(more)),
        out_specs=[HBM] * len(made),
        scratch_shapes=[pltpu.VMEM(shape, BF) for shape in held] + [pltpu.SemaphoreType.DMA((copies,))],
        compiler_params=params(),
        cost_estimate=pl.CostEstimate(flops=3_000_000_000, bytes_accessed=8_000_000, transcendentals=262144),
    )(count, *xs, qt, dt, wv, *more)


def close_kernel(at_ref, *refs, groups):
    sends, us = refs[:groups], refs[groups : 2 * groups]
    wo_in, wk_in, keep_ref, give_ref, gq_ref, mixed_ref, u_ref, wo_ref, wk_ref, sem = refs[2 * groups :]
    chips, rows, width = keep_ref.shape
    part = rows // groups
    first = []
    for c in range(groups):
        pairs = [(sends[c].at[0, pl.ds(0, part)], mixed_ref.at[pl.ds(c * part, part)]), (us[c], u_ref.at[c])]
        first += start_loads(pairs, sem, 2 * c)
    first += start_loads([(wk_in, wk_ref)], sem, 2 * groups)
    loads = start_loads(row_blocks(wo_in, wo_ref, 8), sem, 2 * groups + 1)
    wait_all(first)
    for c in range(groups):
        for h in range(width // HD):
            cols = slice(h * HD, (h + 1) * HD)
            gq_ref[c * part : (c + 1) * part, cols] = mm(
                u_ref[c, h * part : (h + 1) * part], wk_ref[:, cols], 1, 0
            ).astype(BF)
    wait_all(loads)
    mixed = mixed_ref[...]
    for core, block_ref in enumerate((keep_ref, give_ref)):
        for step in range(chips):
            j = lax.rem(at_ref[0] + step, chips) * 2 + lax.rem(at_ref[1] + core, 2)
            cols = pl.ds(pl.multiple_of(j * width, width), width)
            block_ref[step] = mm(mixed, wo_ref[:, cols], 1, 0).astype(BF)


def close(at, sends, us, wo, wk, part, head_count):
    groups = len(us)
    width = wk.shape[1]
    rows = groups * part
    half = jax.ShapeDtypeStruct((head_count // 2, rows, width), BF)
    return pl.pallas_call(
        functools.partial(close_kernel, groups=groups),
        out_shape=[half, half, jax.ShapeDtypeStruct((rows, width), BF)],
        in_specs=[SM] + [HBM] * (2 * groups + 2),
        out_specs=[VM] * 3,
        scratch_shapes=[
            pltpu.VMEM((rows, width), BF),
            pltpu.VMEM((groups, *us[0].shape), BF),
            pltpu.VMEM(wo.shape, BF),
            pltpu.VMEM(wk.shape, BF),
            pltpu.SemaphoreType.DMA((2 * groups + 9,)),
        ],
        compiler_params=params(),
        cost_estimate=pl.CostEstimate(flops=700_000_000, bytes_accessed=8_000_000, transcendentals=0),
    )(at, *sends, *us, wo, wk)


def order_kernel(at_ref, near_ref, far_ref, out_ref):
    chips, _, share, _ = near_ref.shape
    for core, g_ref in enumerate((near_ref, far_ref)):
        for s in range(chips):
            j = lax.rem(at_ref[0] + chips - s, chips) * 2 + lax.rem(at_ref[1] + core, 2)
            out_ref[:, pl.ds(pl.multiple_of(j * share, share), share)] = g_ref[s]


def order(at, near, far):
    chips, db_count, share, piece = near.shape
    return pl.pallas_call(
        order_kernel,
        out_shape=jax.ShapeDtypeStruct((db_count, 2 * chips * share, piece), BF),
        in_specs=[SM, VM, VM],
        out_specs=VM,
        compiler_params=params(),
        cost_estimate=pl.CostEstimate(flops=0, bytes_accessed=2_000_000, transcendentals=0),
    )(at, near, far)


def chips_stack(x, steps, count):
    pieces = {0: x, **{s: along(x, s, count) for s in steps}}
    return jnp.stack([pieces[s] for s in range(count // 2)])


def along(v, step, count):
    chips = count // 2
    return lax.ppermute(v, "head", [(i, ((i // 2 + step) % chips) * 2 + i % 2) for i in range(count)])


def swap(v, count):
    return lax.ppermute(v, "head", [(i, i ^ 1) for i in range(count)])


def ring_steps(count):
    chips = count // 2
    return sorted(range(1, chips), key=lambda s: min(s, chips - s))


def exchange(x, axis):
    return lax.all_to_all(x, axis, split_axis=0, concat_axis=0, tiled=True)


def after(x, *others):
    return lax.optimization_barrier((x, *others))[0]


def shards(queries, w_key, w_value, w_out, encodings, nbr_row, nbr_owner, nbr_count, grad_out):
    db_count = lax.axis_size("db")
    head_count = lax.axis_size("head")
    groups, slot_count = nbr_row.shape
    tok_rows, width = queries.shape
    part = tok_rows // groups
    enc = encodings.shape[2]
    head_at = lax.axis_index("head")
    at = jnp.stack([head_at // 2, head_at % 2]).astype(jnp.int32)
    owner_ids = lax.broadcasted_iota(jnp.int32, (db_count, 1, 1, 1), 0)
    wanted = jnp.sum(jnp.where(nbr_owner[None, None] == owner_ids, nbr_row[None, None], 0), axis=3)
    incoming = exchange(wanted, "db")
    steps = ring_steps(head_count)
    (table,) = pick(
        incoming,
        lambda ref, k: ref[k // groups, 0, k % groups],
        encodings,
        (db_count * groups,),
        HBM,
        VMEM_LIMIT,
    )
    qt = back(after(queries, table), w_key, groups)
    received = after(exchange(table, "db"), qt)
    mine = pick(
        nbr_owner,
        lambda ref, k: ref[k // slot_count, k % slot_count] * groups + k // slot_count,
        received,
        (slot_count,) * groups,
        ANY,
        SMALL_LIMIT,
    )
    token = mine[0]
    near = chips_stack(after(grad_out, table), steps, head_count)
    far = swap(near, head_count)
    dm, dt, grad_cols = prep(at, near, far, w_out, w_value, groups, db_count)
    ring = []
    for c in range(groups):
        held = mine[c] if c == 0 else after(mine[c], *ring[-1])
        came = [along(held, s, head_count) for s in steps]
        if c == 0:
            came = lax.optimization_barrier((*came, dm))[:-1]
        ring.append([held, *came])
    spread = []
    for pieces in ring:
        spread.append([*pieces, *(swap(v, head_count) for v in pieces)])
    sent, sends, us = [], [], []
    extra = (grad_cols,)
    for c in range(groups):
        m, u, *t = attn(nbr_count, spread[c], qt, dt, w_value, c, db_count, extra, c == groups - 1)
        us.append(u)
        sends.append(m)
        sent.append(exchange(after(m, *(ring[-1] if c == 0 else sent)), "db"))
        extra = (queries, dm, *t, u)
    share = tok_rows // head_count
    piece = width * head_count // db_count
    rows_near = chips_stack(sent[0][:, part : part + share, :piece], steps, head_count)
    grad_tok = order(at, rows_near, swap(rows_near, head_count))
    keep, give, grad_q = close(at, sends, us, w_out, w_key, part, head_count)
    other = swap(give, head_count)
    pair = (keep.astype(F32) + other.astype(F32)).astype(BF)
    terms = [pair[0]] + [along(pair[s], s, head_count) for s in steps]
    attended = sum(t.astype(F32) for t in terms).astype(BF)
    share = enc // db_count
    grad_tok = grad_tok.reshape(db_count, groups, part, -1)
    grad_wo = None
    for c in range(groups):
        term = lax.dot_general(
            sent[c][:, :part], grad_tok[:, c], (((0, 1), (0, 1)), ((), ())), preferred_element_type=F32
        )
        grad_wo = term if grad_wo is None else grad_wo + term
        if c < groups - 1:
            sent[-1], grad_wo = lax.optimization_barrier((sent[-1], grad_wo))
    grad_w = [
        jnp.sum(sent[-1][:, part + k * share : part + (k + 1) * share].astype(F32), axis=0)
        for k in range(2)
    ]
    return (attended, grad_q, *grad_w, grad_wo)


def solution(mesh):
    placed = (
        P("db", "head"),
        P(None, "head"),
        P(None, "head"),
        P("head", None),
        P("db", "head", None),
        P("db", None),
        P("db", None),
        P("db"),
        P("db", "head"),
    )
    return jax.shard_map(
        shards,
        mesh=mesh,
        in_specs=placed,
        out_specs=(
            P("db", "head"),
            P("db", "head"),
            P("db", "head"),
            P("db", "head"),
            P("head", "db"),
        ),
        check_vma=False,
    )
```

time: 148 us -> 143 us (0.966)
  waiting for transfers between devices: 52.9 us -> 38.4 us
  Pallas kernels: 29.4 us -> 36.8 us
  local copies, waits for them, and re-layouts: 3.41 us -> 5.55 us
  other arithmetic: 6.02 us -> 4.41 us
  starting transfers between devices: 35.9 us -> 37.4 us
    all_to_all x4 -> x3, waiting for transfers between devices: 28.4 us -> 12.3 us  [exchange(): return lax.all_to_all(x, axis, split_axis=0, concat_axis=0, tiled=True)]
    pallas_call x1 -> x4, Pallas kernels: 6.71 us -> 16.4 us  [the longest x1 6.23 us: prep(): pl.pallas_call(prep_kernel, out_shape=[jax.ShapeDtypeStruct(shape, BF) fo...]
    ppermute x12 -> x15, waiting for transfers between devices: 19.9 us -> 24.6 us  [along(): lax.ppermute(v, 'head', [(i, (i // 2 + step) % chips * 2 + i % 2) for i i...]
    ppermute x12 -> x15, starting transfers between devices: 16.6 us -> 20.8 us  [along(): lax.ppermute(v, 'head', [(i, (i // 2 + step) % chips * 2 + i % 2) for i i...]
    all_to_all x4 -> x3, starting transfers between devices: 17.9 us -> 14.6 us  [exchange(): return lax.all_to_all(x, axis, split_axis=0, concat_axis=0, tiled=True)]
    ppermute x10 -> x11, waiting for transfers between devices: 4.64 us -> 1.46 us  [swap(): return lax.ppermute(v, 'head', [(i, i ^ 1) for i in range(count)])]
    pallas_call x2, Pallas kernels: 16.9 us -> 14.4 us  [attn(): pl.pallas_call(functools.partial(attn_kernel, c=c, pieces=len(xs), last=l...]
    concatenate x2 -> x0, other arithmetic: 1.81 us -> none  [the longest x1 1.14 us: shards(): other = swap(jnp.concatenate(give, axis=1), head_count)]
  transfers between devices with their start and end apart: 26 -> 29, of which waited for: 19 -> 19; matrix products, arithmetic and copies ran while one was open for 3% -> 4% of each run, Pallas kernels for 16% -> 23%
where the time goes in v6:
time: 143 us; the launch traced here: 142 us
  waiting for transfers between devices  38.4 us (27%)
  starting transfers between devices  37.4 us (26%)
  Pallas kernels  36.8 us (26%)
  blocking collectives  15.4 us (11%)
  local copies, waits for them, and re-layouts  5.55 us (4%)
  other arithmetic  4.41 us (3%)
  matrix products  3.1 us (2%)
    ppermute x15, waiting for transfers between devices, along(): lax.ppermute(v, 'head', [(i, (i // 2 + step) % chips * 2 + i % 2) for i i...  24.6 us
    ppermute x15, starting transfers between devices, along(): lax.ppermute(v, 'head', [(i, (i // 2 + step) % chips * 2 + i % 2) for i i...  20.8 us
    all_to_all x1, blocking collectives, exchange(): return lax.all_to_all(x, axis, split_axis=0, concat_axis=0, tiled=True)  15.4 us
    all_to_all x3, starting transfers between devices, exchange(): return lax.all_to_all(x, axis, split_axis=0, concat_axis=0, tiled=True)  14.6 us
    pallas_call x2, Pallas kernels, attn(): pl.pallas_call(functools.partial(attn_kernel, c=c, pieces=len(xs), last=l...  14.4 us
    all_to_all x3, waiting for transfers between devices, exchange(): return lax.all_to_all(x, axis, split_axis=0, concat_axis=0, tiled=True)  12.3 us
    pallas_call x1, Pallas kernels, prep(): pl.pallas_call(prep_kernel, out_shape=[jax.ShapeDtypeStruct(shape, BF) fo...  6.23 us
    pallas_call x2, Pallas kernels, pick(): pl.pallas_call(functools.partial(pick_kernel, row_of=row_of, count=total)...  5.93 us
  transfers between devices with their start and end apart: 29, of which 19 were waited for; matrix products, arithmetic and copies ran while one was open for 4% of the time, Pallas kernels for 23%

profile of v6, /device:TPU:0, one launch (start us, length us, event | category | flops | bytes accessed | tf_op | source)
XLA Modules:
  0.0 142.0 jit_solution(6191546811770783054)
XLA Ops:
  1.5 15.4 %all_to_all.20.rows_ref = s32[16,1,2]{2,1,0:T(1,128)} all-to-all(s32[16,1,2]{2,1,0:T(1,128)S(1)} %copy.17), channel_id=1, replica_groups=mesh['db'=16,'head'=8] {'db'}, dimensions={0} | all-to-all | bytes 256 | tf_op jit(solution)/shard_map/all_to_all | solution.py:352
  16.9 3.8 %shard_map.128 = bf16[32,16,896]{2,1,0:T(8,128)(2,1)} custom-call(s32[16,1,2]{2,1,0:T(1,128)} %all_to_all.20.rows_ref, bf16[64,16,896]{2,1,0:T(8,128)(2,1)} %src_ref.1), custom_call_target="tpu_custom_call" | custom-call | tf_op jit(solution)/shard_map/pallas_call | solution.py:52
  20.7 3.6 %all-to-all-start.1 = ((bf16[32,16,896]{2,1,0:T(8,128)(2,1)}), bf16[32,16,896]{2,1,0:T(8,128)(2,1)S(1)}, u32[]{:S(2)}, u32[]{:S(2)}) async-start(bf16[32,16,896]{2,1,0:T(8,128)(2,1)} %shard_map.128), calls=%async_computation.1 | async-start | bytes 1835008 | tf_op jit(solution)/shard_map/all_to_all | solution.py:352
  24.4 3.1 %collective-permute-start.5 = (bf16[128,512]{1,0:T(8,128)(2,1)S(1)}, bf16[128,512]{1,0:T(8,128)(2,1)S(1)}, u32[]{:S(2)}, u32[]{:S(2)}) collective-permute-start(bf16[128,512]{1,0:T(8,128)(2,1)S(1)} %copy-done.9), channel_id=1, source_target_pairs={{0,6},{1,7},{2,0},{3,1},{4,2},{5,3},{6,4},{7,5},{8,14},{9,15},{10,... | collective-permute-start | bytes 393224 | tf_op jit(solution)/shard_map/ppermute | solution.py:339
  29.1 2.6 %collective-permute-done.5 = bf16[128,512]{1,0:T(8,128)(2,1)S(1)} collective-permute-done((bf16[128,512]{1,0:T(8,128)(2,1)S(1)}, bf16[128,512]{1,0:T(8,128)(2,1)S(1)}, u32[]{:S(2)}, u32[]{:S(2)}) %collective-permute-start.5) | collective-permute-done | bytes 131104 | tf_op jit(solution)/shard_map/ppermute | solution.py:339
  31.6 2.4 %collective-permute-done.4 = bf16[128,512]{1,0:T(8,128)(2,1)S(1)} collective-permute-done((bf16[128,512]{1,0:T(8,128)(2,1)S(1)}, bf16[128,512]{1,0:T(8,128)(2,1)S(1)}, u32[]{:S(2)}, u32[]{:S(2)}) %collective-permute-start.4) | collective-permute-done | bytes 131104 | tf_op jit(solution)/shard_map/ppermute | solution.py:339
  35.5 2.8 %shard_map.129.refs_8_ = bf16[2,256,896]{2,1,0:T(8,128)(2,1)} custom-call(bf16[128,512]{1,0:T(8,128)(2,1)} %refs_11_.1, bf16[896,512]{1,0:T(8,128)(2,1)} %refs_5_.1), custom_call_target="tpu_custom_call" | custom-call | flops 120000000 | bytes 2000000 | tf_op jit(solution)/shard_map/pallas_call | solution.py:102
  38.7 2.2 %shard_map.130 = (bf16[8,16,896]{2,1,0:T(8,128)(2,1)S(1)}, bf16[8,16,896]{2,1,0:T(8,128)(2,1)S(1)}) custom-call(s32[2,8]{1,0:T(2,128)S(1)} %copy-done, bf16[32,16,896]{2,1,0:T(8,128)(2,1)S(1)} %all-to-all-done.1.src_ref), custom_call_target="tpu_custom_call" | custom-call | tf_op jit(solution)/shard_map/pallas_call | solution.py:52
  44.2 2.0 %collective-permute-start.2 = (bf16[8,16,896]{2,1,0:T(8,128)(2,1)S(1)}, bf16[8,16,896]{2,1,0:T(8,128)(2,1)S(1)}, u32[]{:S(2)}, u32[]{:S(2)}) collective-permute-start(bf16[8,16,896]{2,1,0:T(8,128)(2,1)S(1)} %get-tuple-element.31.refs_0_), channel_id=1, source_target_pairs={{0,4},{1,5},{2,6},{3,7},{4,0},{5,1},{6,2},{7,3},{8,12},{9,13},{10,... | collective-permute-start | bytes 688136 | tf_op jit(solution)/shard_map/ppermute | solution.py:339
  47.7 6.2 %shard_map.131 = (bf16[128,512]{1,0:T(8,128)(2,1)}, bf16[2,256,896]{2,1,0:T(8,128)(2,1)}, bf16[16,16,512]{2,1,0:T(8,128)(2,1)}) custom-call(s32[2]{0:T(128)} %pad_add_fusion.at_ref, bf16[4,128,512]{2,1,0:T(8,128)(2,1)} %copy-done.3, bf16[4,128,512]{2,1,0:T(8,128)(2,1)} %copy-done.7, bf16[512,4096]{1,0:T(8,128)(2,1)} %refs_4_.1, bf16[896,512]{1,0:T(8,128)(2,1)} %refs_10_.3), custom_call_target="tpu_custom_call" | custom-call | flops 700000000 | bytes 8000000 | tf_op jit(solution)/shard_map/pallas_call | solution.py:150
  56.1 2.6 %collective-permute-start.12 = (bf16[8,16,896]{2,1,0:T(8,128)(2,1)S(1)}, bf16[8,16,896]{2,1,0:T(8,128)(2,1)S(1)}, u32[]{:S(2)}, u32[]{:S(2)}) collective-permute-start(bf16[8,16,896]{2,1,0:T(8,128)(2,1)S(1)} %get-tuple-element.41.refs_0_), channel_id=1, source_target_pairs={{0,6},{1,7},{2,0},{3,1},{4,2},{5,3},{6,4},{7,5},{8,14},{9,15},{10,... | collective-permute-start | bytes 688136 | tf_op jit(solution)/shard_map/ppermute | solution.py:339
  60.7 6.6 %shard_map.132 = (bf16[16,80,512]{2,1,0:T(8,128)(2,1)}, bf16[256,896]{1,0:T(8,128)(2,1)}, bf16[256,896]{1,0:T(8,128)(2,1)}) custom-call(s32[2]{0:T(128)} %count_ref.3, bf16[8,16,896]{2,1,0:T(8,128)(2,1)} %copy-done.2, bf16[8,16,896]{2,1,0:T(8,128)(2,1)} %copy-done.10, bf16[8,16,896]{2,1,0:T(8,128)(2,1)} %copy-done.11, bf16[8,16,896]{2,1,0:T(8,128)(2,1)} %copy-done.12, ...), custom_call_target="tpu_custom_call" | custom-call | flops 3000000000 | bytes 8000000 | tf_op jit(solution)/shard_map/pallas_call | solution.py:252
  70.6 7.2 %all-to-all-start.2 = ((bf16[16,80,512]{2,1,0:T(8,128)(2,1)}), bf16[16,80,512]{2,1,0:T(8,128)(2,1)S(1)}, u32[]{:S(2)}, u32[]{:S(2)}) async-start(bf16[16,80,512]{2,1,0:T(8,128)(2,1)} %get-tuple-element.49.refs_0_), calls=%async_computation.2 | async-start | bytes 2621440 | tf_op jit(solution)/shard_map/all_to_all | solution.py:352
  81.0 7.8 %shard_map.133 = (bf16[16,176,512]{2,1,0:T(8,128)(2,1)}, bf16[256,896]{1,0:T(8,128)(2,1)}) custom-call(s32[2]{0:T(128)} %count_ref.3, bf16[8,16,896]{2,1,0:T(8,128)(2,1)} %copy-done.1, bf16[8,16,896]{2,1,0:T(8,128)(2,1)} %copy-done.13, bf16[8,16,896]{2,1,0:T(8,128)(2,1)} %copy-done.14, bf16[8,16,896]{2,1,0:T(8,128)(2,1)} %copy-done.15, ...), custom_call_target="tpu_custom_call" | custom-call | flops 3000000000 | bytes 8000000 | tf_op jit(solution)/shard_map/pallas_call | solution.py:252
  88.8 9.6 %all-to-all-done.2 = bf16[16,80,512]{2,1,0:T(8,128)(2,1)S(1)} async-done(((bf16[16,80,512]{2,1,0:T(8,128)(2,1)}), bf16[16,80,512]{2,1,0:T(8,128)(2,1)S(1)}, u32[]{:S(2)}, u32[]{:S(2)}) %all-to-all-start.2) | async-done | bytes 1310752 | tf_op jit(solution)/shard_map/all_to_all | solution.py:352
  99.5 3.7 %all-to-all-start.3 = ((bf16[16,176,512]{2,1,0:T(8,128)(2,1)}), bf16[16,176,512]{2,1,0:T(8,128)(2,1)S(1)}, u32[]{:S(2)}, u32[]{:S(2)}) async-start(bf16[16,176,512]{2,1,0:T(8,128)(2,1)} %get-tuple-element.50.refs_1_), calls=%async_computation.3 | async-start | bytes 5767168 | tf_op jit(solution)/shard_map/all_to_all | solution.py:352
  103.2 5.1 %shard_map.134 = (bf16[4,128,512]{2,1,0:T(8,128)(2,1)}, bf16[4,128,512]{2,1,0:T(8,128)(2,1)}, bf16[128,512]{1,0:T(8,128)(2,1)}) custom-call(s32[2]{0:T(128)} %pad_add_fusion.at_ref, bf16[16,80,512]{2,1,0:T(8,128)(2,1)} %get-tuple-element.49.refs_0_, bf16[16,176,512]{2,1,0:T(8,128)(2,1)} %get-tuple-element.50.refs_1_, ...), custom_call_target="tpu_custom_call" | custom-call | flops 700000000 | bytes 8000000 | tf_op jit(solution)/shard_map/pallas_call | solution.py:295
  113.4 2.3 %collective-permute-done.24 = bf16[16,16,256]{2,1,0:T(8,128)(2,1)S(1)} collective-permute-done((bf16[16,16,256]{2,1,0:T(8,128)(2,1)S(1)}, bf16[16,16,256]{2,1,0:T(8,128)(2,1)S(1)}, u32[]{:S(2)}, u32[]{:S(2)}) %collective-permute-start.24) | collective-permute-done | bytes 131104 | tf_op jit(solution)/shard_map/ppermute | solution.py:339
  115.7 3.0 %collective-permute-done.23 = bf16[16,16,256]{2,1,0:T(8,128)(2,1)S(1)} collective-permute-done((bf16[16,16,256]{2,1,0:T(8,128)(2,1)S(1)}, bf16[16,16,256]{2,1,0:T(8,128)(2,1)S(1)}, u32[]{:S(2)}, u32[]{:S(2)}) %collective-permute-start.23) | collective-permute-done | bytes 131104 | tf_op jit(solution)/shard_map/ppermute | solution.py:339
  118.8 2.1 %collective-permute-done.22 = bf16[16,16,256]{2,1,0:T(8,128)(2,1)S(1)} collective-permute-done((bf16[16,16,256]{2,1,0:T(8,128)(2,1)S(1)}, bf16[16,16,256]{2,1,0:T(8,128)(2,1)S(1)}, u32[]{:S(2)}, u32[]{:S(2)}) %collective-permute-start.22) | collective-permute-done | bytes 131104 | tf_op jit(solution)/shard_map/ppermute | solution.py:339
  124.5 4.5 %collective-permute-done.21 = bf16[128,512]{1,0:T(8,128)(2,1)S(1)} collective-permute-done((bf16[128,512]{1,0:T(8,128)(2,1)S(1)}, bf16[128,512]{1,0:T(8,128)(2,1)S(1)}, u32[]{:S(2)}, u32[]{:S(2)}) %collective-permute-start.21) | collective-permute-done | bytes 131104 | tf_op jit(solution)/shard_map/ppermute | solution.py:339
  129.2 2.1 %collective-permute-done.19 = bf16[128,512]{1,0:T(8,128)(2,1)S(1)} collective-permute-done((bf16[128,512]{1,0:T(8,128)(2,1)S(1)}, bf16[128,512]{1,0:T(8,128)(2,1)S(1)}, u32[]{:S(2)}, u32[]{:S(2)}) %collective-permute-start.19) | collective-permute-done | bytes 131104 | tf_op jit(solution)/shard_map/ppermute | solution.py:339
  132.9 2.3 %shard_map.135 = bf16[16,128,256]{2,1,0:T(8,128)(2,1)} custom-call(s32[2]{0:T(128)} %pad_add_fusion.at_ref, bf16[4,16,16,256]{3,2,1,0:T(8,128)(2,1)} %copy-done.4, bf16[4,16,16,256]{3,2,1,0:T(8,128)(2,1)} %copy-done.8), custom_call_target="tpu_custom_call" | custom-call | bytes 2000000 | tf_op jit(solution)/shard_map/pallas_call | solution.py:322
  137.0 2.4 %all-to-all-done.3 = bf16[16,176,512]{2,1,0:T(8,128)(2,1)S(1)} async-done(((bf16[16,176,512]{2,1,0:T(8,128)(2,1)}), bf16[16,176,512]{2,1,0:T(8,128)(2,1)S(1)}, u32[]{:S(2)}, u32[]{:S(2)}) %all-to-all-start.3) | async-done | bytes 2883616 | tf_op jit(solution)/shard_map/all_to_all | solution.py:352
  (103 shorter events, 35.7 us)
Async XLA Ops:
  20.7 18.0 %all-to-all-start.1 = ((bf16[32,16,896]{2,1,0:T(8,128)(2,1)}), bf16[32,16,896]{2,1,0:T(8,128)(2,1)S(1)}, u32[]{:S(2)}, u32[]{:S(2)}) async-start(bf16[32,16,896]{2,1,0:T(8,128)(2,1)} %shard_map.128), calls=%async_computation.1 | async-start | bytes 1835008 | tf_op jit(solution)/shard_map/all_to_all | solution.py:352
  24.4 7.3 %collective-permute-start.5 = (bf16[128,512]{1,0:T(8,128)(2,1)S(1)}, bf16[128,512]{1,0:T(8,128)(2,1)S(1)}, u32[]{:S(2)}, u32[]{:S(2)}) collective-permute-start(bf16[128,512]{1,0:T(8,128)(2,1)S(1)} %copy-done.9), channel_id=1, source_target_pairs={{0,6},{1,7},{2,0},{3,1},{4,2},{5,3},{6,4},{7,5},{8,14},{9,15},{10,... | collective-permute-start | bytes 393224 | tf_op jit(solution)/shard_map/ppermute | solution.py:339
  27.5 6.6 %collective-permute-start.4 = (bf16[128,512]{1,0:T(8,128)(2,1)S(1)}, bf16[128,512]{1,0:T(8,128)(2,1)S(1)}, u32[]{:S(2)}, u32[]{:S(2)}) collective-permute-start(bf16[128,512]{1,0:T(8,128)(2,1)S(1)} %copy-done.9), channel_id=1, source_target_pairs={{0,4},{1,5},{2,6},{3,7},{4,0},{5,1},{6,2},{7,3},{8,12},{9,13},{10,... | collective-permute-start | bytes 393224 | tf_op jit(solution)/shard_map/ppermute | solution.py:339
  28.1 7.2 %collective-permute-start.3 = (bf16[128,512]{1,0:T(8,128)(2,1)S(1)}, bf16[128,512]{1,0:T(8,128)(2,1)S(1)}, u32[]{:S(2)}, u32[]{:S(2)}) collective-permute-start(bf16[128,512]{1,0:T(8,128)(2,1)S(1)} %copy-done.9), channel_id=1, source_target_pairs={{0,2},{1,3},{2,4},{3,5},{4,6},{5,7},{6,0},{7,1},{8,10},{9,11},{10,... | collective-permute-start | bytes 393224 | tf_op jit(solution)/shard_map/ppermute | solution.py:339
  35.4 11.4 %collective-permute-start.6 = (bf16[4,128,512]{2,1,0:T(8,128)(2,1)S(1)}, bf16[4,128,512]{2,1,0:T(8,128)(2,1)S(1)}, u32[]{:S(2)}, u32[]{:S(2)}) collective-permute-start(bf16[4,128,512]{2,1,0:T(8,128)(2,1)S(1)} %pad_maximum_fusion.near_in), channel_id=1, source_target_pairs={{0,1},{1,0},{2,3},{3,2},{4,5},{5,4},{6,7},{7,6},{8,9},{9,8},{10,11... | collective-permute-start | bytes 1572872 | tf_op jit(solution)/shard_map/ppermute | solution.py:343
  40.9 13.8 %collective-permute-start = (bf16[8,16,896]{2,1,0:T(8,128)(2,1)S(1)}, bf16[8,16,896]{2,1,0:T(8,128)(2,1)S(1)}, u32[]{:S(2)}, u32[]{:S(2)}) collective-permute-start(bf16[8,16,896]{2,1,0:T(8,128)(2,1)S(1)} %get-tuple-element.31.refs_0_), channel_id=1, source_target_pairs={{0,2},{1,3},{2,4},{3,5},{4,6},{5,7},{6,0},{7,1},{8,10},{9,11},{10,... | collective-permute-start | bytes 688136 | tf_op jit(solution)/shard_map/ppermute | solution.py:339
  42.5 12.1 %collective-permute-start.1 = (bf16[8,16,896]{2,1,0:T(8,128)(2,1)S(1)}, bf16[8,16,896]{2,1,0:T(8,128)(2,1)S(1)}, u32[]{:S(2)}, u32[]{:S(2)}) collective-permute-start(bf16[8,16,896]{2,1,0:T(8,128)(2,1)S(1)} %get-tuple-element.31.refs_0_), channel_id=1, source_target_pairs={{0,6},{1,7},{2,0},{3,1},{4,2},{5,3},{6,4},{7,5},{8,14},{9,15},{10,... | collective-permute-start | bytes 688136 | tf_op jit(solution)/shard_map/ppermute | solution.py:339
  44.2 10.5 %collective-permute-start.2 = (bf16[8,16,896]{2,1,0:T(8,128)(2,1)S(1)}, bf16[8,16,896]{2,1,0:T(8,128)(2,1)S(1)}, u32[]{:S(2)}, u32[]{:S(2)}) collective-permute-start(bf16[8,16,896]{2,1,0:T(8,128)(2,1)S(1)} %get-tuple-element.31.refs_0_), channel_id=1, source_target_pairs={{0,4},{1,5},{2,6},{3,7},{4,0},{5,1},{6,2},{7,3},{8,12},{9,13},{10,... | collective-permute-start | bytes 688136 | tf_op jit(solution)/shard_map/ppermute | solution.py:339
  54.7 3.9 %collective-permute-start.8 = (bf16[8,16,896]{2,1,0:T(8,128)(2,1)S(1)}, bf16[8,16,896]{2,1,0:T(8,128)(2,1)S(1)}, u32[]{:S(2)}, u32[]{:S(2)}) collective-permute-start(bf16[8,16,896]{2,1,0:T(8,128)(2,1)S(1)} %collective-permute-done.refs_1_), channel_id=1, source_target_pairs={{0,1},{1,0},{2,3},{3,2},{4,5},{5,4},{6,7},{7,6},{8,9},{9,8},{10,11... | collective-permute-start | bytes 688136 | tf_op jit(solution)/shard_map/ppermute | solution.py:343
  54.8 5.1 %collective-permute-start.9 = (bf16[8,16,896]{2,1,0:T(8,128)(2,1)S(1)}, bf16[8,16,896]{2,1,0:T(8,128)(2,1)S(1)}, u32[]{:S(2)}, u32[]{:S(2)}) collective-permute-start(bf16[8,16,896]{2,1,0:T(8,128)(2,1)S(1)} %collective-permute-done.1.refs_2_), channel_id=1, source_target_pairs={{0,1},{1,0},{2,3},{3,2},{4,5},{5,4},{6,7},{7,6},{8,9},{9,8},{10,11... | collective-permute-start | bytes 688136 | tf_op jit(solution)/shard_map/ppermute | solution.py:343
  55.3 4.6 %collective-permute-start.10 = (bf16[8,16,896]{2,1,0:T(8,128)(2,1)S(1)}, bf16[8,16,896]{2,1,0:T(8,128)(2,1)S(1)}, u32[]{:S(2)}, u32[]{:S(2)}) collective-permute-start(bf16[8,16,896]{2,1,0:T(8,128)(2,1)S(1)} %collective-permute-done.2.refs_3_), channel_id=1, source_target_pairs={{0,1},{1,0},{2,3},{3,2},{4,5},{5,4},{6,7},{7,6},{8,9},{9,8},{10,11... | collective-permute-start | bytes 688136 | tf_op jit(solution)/shard_map/ppermute | solution.py:343
  55.4 11.9 %collective-permute-start.11 = (bf16[8,16,896]{2,1,0:T(8,128)(2,1)S(1)}, bf16[8,16,896]{2,1,0:T(8,128)(2,1)S(1)}, u32[]{:S(2)}, u32[]{:S(2)}) collective-permute-start(bf16[8,16,896]{2,1,0:T(8,128)(2,1)S(1)} %get-tuple-element.41.refs_0_), channel_id=1, source_target_pairs={{0,2},{1,3},{2,4},{3,5},{4,6},{5,7},{6,0},{7,1},{8,10},{9,11},{10,... | collective-permute-start | bytes 688136 | tf_op jit(solution)/shard_map/ppermute | solution.py:339
  56.1 12.7 %collective-permute-start.12 = (bf16[8,16,896]{2,1,0:T(8,128)(2,1)S(1)}, bf16[8,16,896]{2,1,0:T(8,128)(2,1)S(1)}, u32[]{:S(2)}, u32[]{:S(2)}) collective-permute-start(bf16[8,16,896]{2,1,0:T(8,128)(2,1)S(1)} %get-tuple-element.41.refs_0_), channel_id=1, source_target_pairs={{0,6},{1,7},{2,0},{3,1},{4,2},{5,3},{6,4},{7,5},{8,14},{9,15},{10,... | collective-permute-start | bytes 688136 | tf_op jit(solution)/shard_map/ppermute | solution.py:339
  58.6 12.0 %collective-permute-start.13 = (bf16[8,16,896]{2,1,0:T(8,128)(2,1)S(1)}, bf16[8,16,896]{2,1,0:T(8,128)(2,1)S(1)}, u32[]{:S(2)}, u32[]{:S(2)}) collective-permute-start(bf16[8,16,896]{2,1,0:T(8,128)(2,1)S(1)} %get-tuple-element.41.refs_0_), channel_id=1, source_target_pairs={{0,4},{1,5},{2,6},{3,7},{4,0},{5,1},{6,2},{7,3},{8,12},{9,13},{10,... | collective-permute-start | bytes 688136 | tf_op jit(solution)/shard_map/ppermute | solution.py:339
  70.6 27.8 %all-to-all-start.2 = ((bf16[16,80,512]{2,1,0:T(8,128)(2,1)}), bf16[16,80,512]{2,1,0:T(8,128)(2,1)S(1)}, u32[]{:S(2)}, u32[]{:S(2)}) async-start(bf16[16,80,512]{2,1,0:T(8,128)(2,1)} %get-tuple-element.49.refs_0_), calls=%async_computation.2 | async-start | bytes 2621440 | tf_op jit(solution)/shard_map/all_to_all | solution.py:352
  99.5 40.0 %all-to-all-start.3 = ((bf16[16,176,512]{2,1,0:T(8,128)(2,1)}), bf16[16,176,512]{2,1,0:T(8,128)(2,1)S(1)}, u32[]{:S(2)}, u32[]{:S(2)}) async-start(bf16[16,176,512]{2,1,0:T(8,128)(2,1)} %get-tuple-element.50.refs_1_), calls=%async_computation.3 | async-start | bytes 5767168 | tf_op jit(solution)/shard_map/all_to_all | solution.py:352
  108.3 3.9 %collective-permute-start.18 = (bf16[4,128,512]{2,1,0:T(8,128)(2,1)}, bf16[4,128,512]{2,1,0:T(8,128)(2,1)S(1)}, u32[]{:S(2)}, u32[]{:S(2)}) collective-permute-start(bf16[4,128,512]{2,1,0:T(8,128)(2,1)} %get-tuple-element.47), channel_id=1, source_target_pairs={{0,1},{1,0},{2,3},{3,2},{4,5},{5,4},{6,7},{7,6},{8,9},{9,8},{10,11... | collective-permute-start | bytes 1572872 | tf_op jit(solution)/shard_map/ppermute | solution.py:343
  109.3 6.4 %collective-permute-start.24 = (bf16[16,16,256]{2,1,0:T(8,128)(2,1)S(1)}, bf16[16,16,256]{2,1,0:T(8,128)(2,1)S(1)}, u32[]{:S(2)}, u32[]{:S(2)}) collective-permute-start(bf16[16,16,256]{2,1,0:T(8,128)(2,1)S(1)} %get-tuple-element.56), channel_id=1, source_target_pairs={{0,6},{1,7},{2,0},{3,1},{4,2},{5,3},{6,4},{7,5},{8,14},{9,15},{10,... | collective-permute-start | bytes 393224 | tf_op jit(solution)/shard_map/ppermute | solution.py:339
  110.9 7.8 %collective-permute-start.23 = (bf16[16,16,256]{2,1,0:T(8,128)(2,1)S(1)}, bf16[16,16,256]{2,1,0:T(8,128)(2,1)S(1)}, u32[]{:S(2)}, u32[]{:S(2)}) collective-permute-start(bf16[16,16,256]{2,1,0:T(8,128)(2,1)S(1)} %get-tuple-element.56), channel_id=1, source_target_pairs={{0,4},{1,5},{2,6},{3,7},{4,0},{5,1},{6,2},{7,3},{8,12},{9,13},{10,... | collective-permute-start | bytes 393224 | tf_op jit(solution)/shard_map/ppermute | solution.py:339
  112.2 8.6 %collective-permute-start.22 = (bf16[16,16,256]{2,1,0:T(8,128)(2,1)S(1)}, bf16[16,16,256]{2,1,0:T(8,128)(2,1)S(1)}, u32[]{:S(2)}, u32[]{:S(2)}) collective-permute-start(bf16[16,16,256]{2,1,0:T(8,128)(2,1)S(1)} %get-tuple-element.56), channel_id=1, source_target_pairs={{0,2},{1,3},{2,4},{3,5},{4,6},{5,7},{6,0},{7,1},{8,10},{9,11},{10,... | collective-permute-start | bytes 393224 | tf_op jit(solution)/shard_map/ppermute | solution.py:339
  120.9 11.1 %collective-permute-start.25 = (bf16[4,16,16,256]{3,2,1,0:T(8,128)(2,1)S(1)}, bf16[4,16,16,256]{3,2,1,0:T(8,128)(2,1)S(1)}, u32[]{:S(2)}, u32[]{:S(2)}) collective-permute-start(bf16[4,16,16,256]{3,2,1,0:T(8,128)(2,1)S(1)} %pad_maximum_fusion.1.near_ref), channel_id=1, source_target_pairs={{0,1},{1,0},{2,3},{3,2},{4,5},{5,4},{6,7},{7,6},{8,9},{9,8},{10,11... | collective-permute-start | bytes 1572872 | tf_op jit(solution)/shard_map/ppermute | solution.py:343
  121.1 7.9 %collective-permute-start.21 = (bf16[128,512]{1,0:T(8,128)(2,1)S(1)}, bf16[128,512]{1,0:T(8,128)(2,1)S(1)}, u32[]{:S(2)}, u32[]{:S(2)}) collective-permute-start(bf16[128,512]{1,0:T(8,128)(2,1)S(1)} %get-tuple-element.58), channel_id=1, source_target_pairs={{0,4},{1,5},{2,6},{3,7},{4,0},{5,1},{6,2},{7,3},{8,12},{9,13},{10,... | collective-permute-start | bytes 393224 | tf_op jit(solution)/shard_map/ppermute | solution.py:339
  122.4 6.8 %collective-permute-start.20 = (bf16[128,512]{1,0:T(8,128)(2,1)S(1)}, bf16[128,512]{1,0:T(8,128)(2,1)S(1)}, u32[]{:S(2)}, u32[]{:S(2)}) collective-permute-start(bf16[128,512]{1,0:T(8,128)(2,1)S(1)} %get-tuple-element.59), channel_id=1, source_target_pairs={{0,6},{1,7},{2,0},{3,1},{4,2},{5,3},{6,4},{7,5},{8,14},{9,15},{10,... | collective-permute-start | bytes 393224 | tf_op jit(solution)/shard_map/ppermute | solution.py:339
  123.6 7.7 %collective-permute-start.19 = (bf16[128,512]{1,0:T(8,128)(2,1)S(1)}, bf16[128,512]{1,0:T(8,128)(2,1)S(1)}, u32[]{:S(2)}, u32[]{:S(2)}) collective-permute-start(bf16[128,512]{1,0:T(8,128)(2,1)S(1)} %get-tuple-element.57), channel_id=1, source_target_pairs={{0,2},{1,3},{2,4},{3,5},{4,6},{5,7},{6,0},{7,1},{8,10},{9,11},{10,... | collective-permute-start | bytes 393224 | tf_op jit(solution)/shard_map/ppermute | solution.py:339
  (29 other events, 167.3 us)

commit v7 on v6

--- a/solution.py
+++ b/solution.py
@@ -31,17 +31,20 @@
 
 def pick_kernel(rows_ref, src_ref, *rest, row_of, count):
     *outs, held, load_sem, store_sem = rest
-    places = [out.at[n] for out in outs for n in range(out.shape[0])]
     loads = [
         pltpu.make_async_copy(src_ref.at[row_of(rows_ref, k)], held.at[k], load_sem.at[k])
         for k in range(count)
     ]
-    stores = [pltpu.make_async_copy(held.at[k], places[k], store_sem.at[k]) for k in range(count)]
     for load in loads:
         load.start()
-    for load, store in zip(loads, stores):
-        load.wait()
-        store.start()
+    stores, first = [], 0
+    for n, out in enumerate(outs):
+        size = out.shape[0]
+        for load in loads[first : first + size]:
+            load.wait()
+        stores.append(pltpu.make_async_copy(held.at[pl.ds(first, size)], out, store_sem.at[n]))
+        stores[-1].start()
+        first += size
     for store in stores:
         store.wait()
 
@@ -57,7 +60,7 @@
         scratch_shapes=[
             pltpu.VMEM((total, *item), src.dtype),
             pltpu.SemaphoreType.DMA((total,)),
-            pltpu.SemaphoreType.DMA((total,)),
+            pltpu.SemaphoreType.DMA((len(counts),)),
         ],
         compiler_params=pltpu.CompilerParams(vmem_limit_bytes=limit),
     )(rows, src)
@@ -119,8 +122,9 @@
     share = gc_ref.shape[1]
     own = pl.ds(pl.multiple_of((at_ref[0] * 2 + at_ref[1]) * share, share), share)
     first = start_loads([(near_in, near_ref), (far_in, far_ref)], sem)
-    blocks = start_loads(row_blocks(wo_in, wo_ref, 8), sem, 2)
-    late = start_loads([(wv_in, wv_ref)], sem, 10)
+    heads = width // HD
+    blocks = start_loads(row_blocks(wo_in, wo_ref, heads), sem, 2)
+    late = start_loads([(wv_in, wv_ref)], sem, 2 + heads)
     wait_all(first)
     places = []
     for core, g_ref in enumerate((near_ref, far_ref)):
@@ -130,15 +134,23 @@
             for p in range(cuts):
                 gc_ref[j * cuts + p, :, :piece] = g_ref[s, own, p * piece : (p + 1) * piece]
                 gc_ref[j * cuts + p, :, piece:] = jnp.zeros((share, width - piece), BF)
-    stores = start_loads([(gc_ref, gc_out)], sem, 11)
-    wait_all(blocks)
-    acc = jnp.zeros((rows, width), F32)
-    for g_ref, s, cols in places:
-        acc += mm(g_ref[s], wo_ref[:, cols], 1, 1)
-    dm_ref[...] = acc.astype(BF)
-    wait_all(late)
-    back_project(dm_ref, wv_ref, dt_ref)
-    stores += start_loads([(dm_ref, dm_out), (dt_ref, dt_out)], sem, 12)
+    stores = start_loads([(gc_ref, gc_out)], sem, 3 + heads)
+    groups = dt_ref.shape[0]
+    part = rows // groups
+    for h in range(heads):
+        hd = slice(h * HD, (h + 1) * HD)
+        blocks[h].wait()
+        acc = jnp.zeros((rows, HD), F32)
+        for g_ref, s, cols in places:
+            acc += mm(g_ref[s], wo_ref[hd, cols], 1, 1)
+        dm = acc.astype(BF)
+        dm_ref[:, hd] = dm
+        if h == 0:
+            wait_all(late)
+        value = mm(dm, wv_ref[:, hd], 1, 1).astype(BF)
+        for c in range(groups):
+            dt_ref[c, h * part : (h + 1) * part] = value[c * part : (c + 1) * part]
+    stores += start_loads([(dm_ref, dm_out), (dt_ref, dt_out)], sem, 4 + heads)
     wait_all(stores)
 
 
@@ -153,7 +165,7 @@
         in_specs=[SM] + [HBM] * 4,
         out_specs=[HBM] * 3,
         scratch_shapes=[pltpu.VMEM(shape, BF) for shape in (*(v.shape for v in operands), *made)]
-        + [pltpu.SemaphoreType.DMA((14,))],
+        + [pltpu.SemaphoreType.DMA((6 + width // HD,))],
         compiler_params=params(),
         cost_estimate=pl.CostEstimate(flops=700_000_000, bytes_accessed=8_000_000, transcendentals=0),
     )(at, *operands)
@@ -184,8 +196,9 @@
         [(qt_in.at[c], qt_ref)]
         + [(x_in[p], x_ref.at[pl.ds(p * slots, slots)]) for p in range(pieces)]
     )
+    wait_all(x_loads)
+    wv_loads = start(row_blocks(wv_in, wv_ref, 2))
     dt_loads = start([(dt_in.at[c], dt_ref)])
-    wv_loads = start(row_blocks(wv_in, wv_ref, 2))
     if last:
         q_ref, dm_ref, t0_ref, u0_ref, gw_ref = refs[:5]
         last_loads = start(list(zip(ins[3:], (q_ref, dm_ref, t0_ref, u0_ref))))
@@ -193,7 +206,6 @@
         gs_ref = refs[0]
         gs_loads = start([(ins[3], gs_ref)])
     factor = 1.0 / math.sqrt(HD)
-    wait_all(x_loads)
     x = x_ref[...].reshape(pieces * slots * sub, enc)
     keys = x.shape[0]
     s = mm(qt_ref[...], x, 1, 1) * factor
@@ -230,7 +242,9 @@
                     gw_ref[i, k * share : (k + 1) * share, cols] = total[
                         i * share : (i + 1) * share
                     ].astype(BF)
-        stores += start([(gw_ref, send_ref.at[:, pl.ds(part, 2 * share)])])
+            stores += start(
+                [(gw_ref.at[:, :, pl.ds(h * HD, HD)], send_ref.at[:, pl.ds(part, 2 * share), pl.ds(h * HD, HD)])]
+            )
     wait_all(stores)
 
 
@@ -244,7 +258,7 @@
     more = list(extra)
     held = [(len(xs) * slots, sub, enc), (part, width), tall, tall, tall, tall, wv.shape]
     held += [v.shape for v in more]
-    copies = len(xs) + 8 + len(more) + db_count
+    copies = len(xs) + 8 + len(more) + db_count + width // HD
     if last:
         held += [(db_count, grown, width)]
     else:
@@ -309,24 +323,34 @@
     )(at, *sends, *us, wo, wk)
 
 
-def order_kernel(at_ref, near_ref, far_ref, out_ref):
-    chips, _, share, _ = near_ref.shape
+def order_kernel(at_ref, near_ref, far_ref, sent_in, out_ref, wo_ref, mixed_ref, sem):
+    chips, db_count, share, piece = near_ref.shape
+    part, width = mixed_ref.shape[1:]
+    loads = start_loads([(sent_in.at[:, pl.ds(0, part)], mixed_ref)], sem)
     for core, g_ref in enumerate((near_ref, far_ref)):
         for s in range(chips):
             j = lax.rem(at_ref[0] + chips - s, chips) * 2 + lax.rem(at_ref[1] + core, 2)
             out_ref[:, pl.ds(pl.multiple_of(j * share, share), share)] = g_ref[s]
-
-
-def order(at, near, far):
+    wait_all(loads)
+    mixed = mixed_ref[...].reshape(db_count * part, width)
+    wo_ref[...] = mm(mixed, out_ref[:, :part].reshape(db_count * part, piece), 0, 0)
+
+
+def order(at, near, far, sent, part):
     chips, db_count, share, piece = near.shape
+    width = sent.shape[2]
     return pl.pallas_call(
         order_kernel,
-        out_shape=jax.ShapeDtypeStruct((db_count, 2 * chips * share, piece), BF),
-        in_specs=[SM, VM, VM],
-        out_specs=VM,
+        out_shape=[
+            jax.ShapeDtypeStruct((db_count, 2 * chips * share, piece), BF),
+            jax.ShapeDtypeStruct((width, piece), F32),
+        ],
+        in_specs=[SM, VM, VM, HBM],
+        out_specs=[VM, VM],
+        scratch_shapes=[pltpu.VMEM((db_count, part, width), BF), pltpu.SemaphoreType.DMA((1,))],
         compiler_params=params(),
-        cost_estimate=pl.CostEstimate(flops=0, bytes_accessed=2_000_000, transcendentals=0),
-    )(at, near, far)
+        cost_estimate=pl.CostEstimate(flops=300_000_000, bytes_accessed=4_000_000, transcendentals=0),
+    )(at, near, far, sent)
 
 
 def chips_stack(x, steps, count):
@@ -367,7 +391,8 @@
     at = jnp.stack([head_at // 2, head_at % 2]).astype(jnp.int32)
     owner_ids = lax.broadcasted_iota(jnp.int32, (db_count, 1, 1, 1), 0)
     wanted = jnp.sum(jnp.where(nbr_owner[None, None] == owner_ids, nbr_row[None, None], 0), axis=3)
-    incoming = exchange(wanted, "db")
+    qt = back(queries, w_key, groups)
+    incoming = after(exchange(wanted, "db"), qt)
     steps = ring_steps(head_count)
     (table,) = pick(
         incoming,
@@ -377,8 +402,7 @@
         HBM,
         VMEM_LIMIT,
     )
-    qt = back(after(queries, table), w_key, groups)
-    received = after(exchange(table, "db"), qt)
+    received = exchange(table, "db")
     mine = pick(
         nbr_owner,
         lambda ref, k: ref[k // slot_count, k % slot_count] * groups + k // slot_count,
@@ -412,7 +436,7 @@
     share = tok_rows // head_count
     piece = width * head_count // db_count
     rows_near = chips_stack(sent[0][:, part : part + share, :piece], steps, head_count)
-    grad_tok = order(at, rows_near, swap(rows_near, head_count))
+    grad_tok, grad_wo = order(at, rows_near, swap(rows_near, head_count), sent[0], part)
     keep, give, grad_q = close(at, sends, us, w_out, w_key, part, head_count)
     other = swap(give, head_count)
     pair = (keep.astype(F32) + other.astype(F32)).astype(BF)
@@ -420,14 +444,11 @@
     attended = sum(t.astype(F32) for t in terms).astype(BF)
     share = enc // db_count
     grad_tok = grad_tok.reshape(db_count, groups, part, -1)
-    grad_wo = None
-    for c in range(groups):
-        term = lax.dot_general(
+    sent[-1], grad_wo = lax.optimization_barrier((sent[-1], grad_wo))
+    for c in range(1, groups):
+        grad_wo = grad_wo + lax.dot_general(
             sent[c][:, :part], grad_tok[:, c], (((0, 1), (0, 1)), ((), ())), preferred_element_type=F32
         )
-        grad_wo = term if grad_wo is None else grad_wo + term
-        if c < groups - 1:
-            sent[-1], grad_wo = lax.optimization_barrier((sent[-1], grad_wo))
     grad_w = [
         jnp.sum(sent[-1][:, part + k * share : part + (k + 1) * share].astype(F32), axis=0)
         for k in range(2)

time: 143 us -> 142 us (level)
  blocking collectives: 15.4 us -> 0 us
  waiting for transfers between devices: 38.4 us -> 44.6 us
  starting transfers between devices: 37.4 us -> 42.8 us
  Pallas kernels: 36.8 us -> 39.1 us
  matrix products: 3.1 us -> 1.51 us
    all_to_all x1 -> x0, blocking collectives: 15.4 us -> none  [exchange(): return lax.all_to_all(x, axis, split_axis=0, concat_axis=0, tiled=True)]
    all_to_all x3 -> x4, waiting for transfers between devices: 12.3 us -> 20.6 us  [exchange(): return lax.all_to_all(x, axis, split_axis=0, concat_axis=0, tiled=True)]
    all_to_all x3 -> x4, starting transfers between devices: 14.6 us -> 20 us  [exchange(): return lax.all_to_all(x, axis, split_axis=0, concat_axis=0, tiled=True)]
    ppermute x15, waiting for transfers between devices: 24.6 us -> 22.5 us  [along(): lax.ppermute(v, 'head', [(i, (i // 2 + step) % chips * 2 + i % 2) for i i...]
    dot_general x2 -> x1, matrix products: 3.1 us -> 1.51 us  [shards(): lax.dot_general(sent[c][:, :part], grad_tok[:, c], (((0, 1), (0, 1)), (()...]
    pallas_call x1, Pallas kernels: 2.29 us -> 3.74 us  [order(): pl.pallas_call(order_kernel, out_shape=[jax.ShapeDtypeStruct((db_count, 2...]
    unnamed x48 -> x50, local copies, waits for them, and re-layouts: 4.51 us -> 4.73 us
  transfers between devices with their start and end apart: 29 -> 30, of which waited for: 19 -> 18; matrix products, arithmetic and copies ran while one was open for 4% -> 3% of each run, Pallas kernels for 23% -> 25%
where the time goes in v7:
time: 142 us; the launch traced here: 141 us
  waiting for transfers between devices  44.6 us (31%)
  starting transfers between devices  42.8 us (30%)
  Pallas kernels  39.1 us (28%)
  local copies, waits for them, and re-layouts  6.38 us (4%)
  other arithmetic  5.27 us (4%)
  matrix products  1.51 us (1%)
    ppermute x15, waiting for transfers between devices, along(): lax.ppermute(v, 'head', [(i, (i // 2 + step) % chips * 2 + i % 2) for i i...  22.5 us
    all_to_all x4, waiting for transfers between devices, exchange(): return lax.all_to_all(x, axis, split_axis=0, concat_axis=0, tiled=True)  20.6 us
    ppermute x15, starting transfers between devices, along(): lax.ppermute(v, 'head', [(i, (i // 2 + step) % chips * 2 + i % 2) for i i...  20.3 us
    all_to_all x4, starting transfers between devices, exchange(): return lax.all_to_all(x, axis, split_axis=0, concat_axis=0, tiled=True)  20 us
    pallas_call x2, Pallas kernels, attn(): pl.pallas_call(functools.partial(attn_kernel, c=c, pieces=len(xs), last=l...  14.6 us
    pallas_call x1, Pallas kernels, prep(): pl.pallas_call(prep_kernel, out_shape=[jax.ShapeDtypeStruct(shape, BF) fo...  7.5 us
    pallas_call x2, Pallas kernels, pick(): pl.pallas_call(functools.partial(pick_kernel, row_of=row_of, count=total)...  5.4 us
    pallas_call x1, Pallas kernels, close(): pl.pallas_call(functools.partial(close_kernel, groups=groups), out_shape=...  5.08 us
  transfers between devices with their start and end apart: 30, of which 18 were waited for; matrix products, arithmetic and copies ran while one was open for 3% of the time, Pallas kernels for 25%

profile of v7, /device:TPU:0, one launch (start us, length us, event | category | flops | bytes accessed | tf_op | source)
XLA Modules:
  0.0 140.7 jit_solution(2769579969544289866)
XLA Ops:
  2.1 8.0 %all-to-all-start = ((s32[16,1,2]{2,1,0:T(1,128)}), s32[16,1,2]{2,1,0:T(1,128)S(1)}, u32[]{:S(2)}, u32[]{:S(2)}) async-start(s32[16,1,2]{2,1,0:T(1,128)} %copy.16), calls=%async_computation | async-start | bytes 16384 | tf_op jit(solution)/shard_map/all_to_all | solution.py:376
  10.1 2.8 %shard_map.128.refs_8_ = bf16[2,256,896]{2,1,0:T(8,128)(2,1)} custom-call(bf16[128,512]{1,0:T(8,128)(2,1)} %refs_11_.1, bf16[896,512]{1,0:T(8,128)(2,1)} %refs_5_.1), custom_call_target="tpu_custom_call" | custom-call | flops 120000000 | bytes 2000000 | tf_op jit(solution)/shard_map/pallas_call | solution.py:105
  12.9 4.7 %all-to-all-done.rows_ref = s32[16,1,2]{2,1,0:T(1,128)S(1)} async-done(((s32[16,1,2]{2,1,0:T(1,128)}), s32[16,1,2]{2,1,0:T(1,128)S(1)}, u32[]{:S(2)}, u32[]{:S(2)}) %all-to-all-start) | async-done | bytes 160 | tf_op jit(solution)/shard_map/all_to_all | solution.py:376
  18.1 3.4 %shard_map.129 = bf16[32,16,896]{2,1,0:T(8,128)(2,1)} custom-call(s32[16,1,2]{2,1,0:T(1,128)} %copy-done.10, bf16[64,16,896]{2,1,0:T(8,128)(2,1)} %src_ref.1), custom_call_target="tpu_custom_call" | custom-call | tf_op jit(solution)/shard_map/pallas_call | solution.py:55
  21.6 3.6 %all-to-all-start.1 = ((bf16[32,16,896]{2,1,0:T(8,128)(2,1)}), bf16[32,16,896]{2,1,0:T(8,128)(2,1)S(1)}, u32[]{:S(2)}, u32[]{:S(2)}) async-start(bf16[32,16,896]{2,1,0:T(8,128)(2,1)} %shard_map.129), calls=%async_computation.1 | async-start | bytes 1835008 | tf_op jit(solution)/shard_map/all_to_all | solution.py:376
  25.2 3.1 %collective-permute-start.5 = (bf16[128,512]{1,0:T(8,128)(2,1)S(1)}, bf16[128,512]{1,0:T(8,128)(2,1)S(1)}, u32[]{:S(2)}, u32[]{:S(2)}) collective-permute-start(bf16[128,512]{1,0:T(8,128)(2,1)S(1)} %copy-done.9), channel_id=1, source_target_pairs={{0,6},{1,7},{2,0},{3,1},{4,2},{5,3},{6,4},{7,5},{8,14},{9,15},{10,... | collective-permute-start | bytes 393224 | tf_op jit(solution)/shard_map/ppermute | solution.py:363
  29.9 2.7 %collective-permute-done.5 = bf16[128,512]{1,0:T(8,128)(2,1)S(1)} collective-permute-done((bf16[128,512]{1,0:T(8,128)(2,1)S(1)}, bf16[128,512]{1,0:T(8,128)(2,1)S(1)}, u32[]{:S(2)}, u32[]{:S(2)}) %collective-permute-start.5) | collective-permute-done | bytes 131104 | tf_op jit(solution)/shard_map/ppermute | solution.py:363
  32.6 2.3 %collective-permute-done.4 = bf16[128,512]{1,0:T(8,128)(2,1)S(1)} collective-permute-done((bf16[128,512]{1,0:T(8,128)(2,1)S(1)}, bf16[128,512]{1,0:T(8,128)(2,1)S(1)}, u32[]{:S(2)}, u32[]{:S(2)}) %collective-permute-start.4) | collective-permute-done | bytes 131104 | tf_op jit(solution)/shard_map/ppermute | solution.py:363
  36.4 3.4 %all-to-all-done.1.src_ref = bf16[32,16,896]{2,1,0:T(8,128)(2,1)S(1)} async-done(((bf16[32,16,896]{2,1,0:T(8,128)(2,1)}), bf16[32,16,896]{2,1,0:T(8,128)(2,1)S(1)}, u32[]{:S(2)}, u32[]{:S(2)}) %all-to-all-start.1) | async-done | bytes 917536 | tf_op jit(solution)/shard_map/all_to_all | solution.py:376
  48.5 7.5 %shard_map.131 = (bf16[128,512]{1,0:T(8,128)(2,1)}, bf16[2,256,896]{2,1,0:T(8,128)(2,1)}, bf16[16,16,512]{2,1,0:T(8,128)(2,1)}) custom-call(s32[2]{0:T(128)} %pad_add_fusion.at_ref, bf16[4,128,512]{2,1,0:T(8,128)(2,1)} %copy-done.4, bf16[4,128,512]{2,1,0:T(8,128)(2,1)} %copy-done.6, bf16[512,4096]{1,0:T(8,128)(2,1)} %refs_4_.1, bf16[896,512]{1,0:T(8,128)(2,1)} %refs_10_.3), custom_call_target="tpu_custom_call" | custom-call | flops 700000000 | bytes 8000000 | tf_op jit(solution)/shard_map/pallas_call | solution.py:162
  58.0 2.6 %collective-permute-start.12 = (bf16[8,16,896]{2,1,0:T(8,128)(2,1)S(1)}, bf16[8,16,896]{2,1,0:T(8,128)(2,1)S(1)}, u32[]{:S(2)}, u32[]{:S(2)}) collective-permute-start(bf16[8,16,896]{2,1,0:T(8,128)(2,1)S(1)} %get-tuple-element.41.refs_0_), channel_id=1, source_target_pairs={{0,6},{1,7},{2,0},{3,1},{4,2},{5,3},{6,4},{7,5},{8,14},{9,15},{10,... | collective-permute-start | bytes 688136 | tf_op jit(solution)/shard_map/ppermute | solution.py:363
  61.6 6.6 %shard_map.132 = (bf16[16,80,512]{2,1,0:T(8,128)(2,1)}, bf16[256,896]{1,0:T(8,128)(2,1)}, bf16[256,896]{1,0:T(8,128)(2,1)}) custom-call(s32[2]{0:T(128)} %count_ref.3, bf16[8,16,896]{2,1,0:T(8,128)(2,1)} %copy-done.2, bf16[8,16,896]{2,1,0:T(8,128)(2,1)} %copy-done.11, bf16[8,16,896]{2,1,0:T(8,128)(2,1)} %copy-done.12, bf16[8,16,896]{2,1,0:T(8,128)(2,1)} %copy-done.13, ...), custom_call_target="tpu_custom_call" | custom-call | flops 3000000000 | bytes 8000000 | tf_op jit(solution)/shard_map/pallas_call | solution.py:266
  68.3 2.7 %collective-permute-done.11.refs_1_ = bf16[8,16,896]{2,1,0:T(8,128)(2,1)S(1)} collective-permute-done((bf16[8,16,896]{2,1,0:T(8,128)(2,1)S(1)}, bf16[8,16,896]{2,1,0:T(8,128)(2,1)S(1)}, u32[]{:S(2)}, u32[]{:S(2)}) %collective-permute-start.11) | collective-permute-done | bytes 229408 | tf_op jit(solution)/shard_map/ppermute | solution.py:363
  71.0 4.7 %all-to-all-start.2 = ((bf16[16,80,512]{2,1,0:T(8,128)(2,1)}), bf16[16,80,512]{2,1,0:T(8,128)(2,1)S(1)}, u32[]{:S(2)}, u32[]{:S(2)}) async-start(bf16[16,80,512]{2,1,0:T(8,128)(2,1)} %get-tuple-element.49.refs_0_), calls=%async_computation.2 | async-start | bytes 2621440 | tf_op jit(solution)/shard_map/all_to_all | solution.py:376
  78.9 8.0 %shard_map.133 = (bf16[16,176,512]{2,1,0:T(8,128)(2,1)}, bf16[256,896]{1,0:T(8,128)(2,1)}) custom-call(s32[2]{0:T(128)} %count_ref.3, bf16[8,16,896]{2,1,0:T(8,128)(2,1)} %copy-done.1, bf16[8,16,896]{2,1,0:T(8,128)(2,1)} %copy-done.14, bf16[8,16,896]{2,1,0:T(8,128)(2,1)} %copy-done.15, bf16[8,16,896]{2,1,0:T(8,128)(2,1)} %copy-done.16, ...), custom_call_target="tpu_custom_call" | custom-call | flops 3000000000 | bytes 8000000 | tf_op jit(solution)/shard_map/pallas_call | solution.py:266
  86.9 9.4 %all-to-all-done.2.sent_in = bf16[16,80,512]{2,1,0:T(8,128)(2,1)S(1)} async-done(((bf16[16,80,512]{2,1,0:T(8,128)(2,1)}), bf16[16,80,512]{2,1,0:T(8,128)(2,1)S(1)}, u32[]{:S(2)}, u32[]{:S(2)}) %all-to-all-start.2) | async-done | bytes 1310752 | tf_op jit(solution)/shard_map/all_to_all | solution.py:376
  97.4 3.7 %all-to-all-start.3 = ((bf16[16,176,512]{2,1,0:T(8,128)(2,1)}), bf16[16,176,512]{2,1,0:T(8,128)(2,1)S(1)}, u32[]{:S(2)}, u32[]{:S(2)}) async-start(bf16[16,176,512]{2,1,0:T(8,128)(2,1)} %get-tuple-element.50.refs_1_), calls=%async_computation.3 | async-start | bytes 5767168 | tf_op jit(solution)/shard_map/all_to_all | solution.py:376
  101.1 5.1 %shard_map.134 = (bf16[4,128,512]{2,1,0:T(8,128)(2,1)}, bf16[4,128,512]{2,1,0:T(8,128)(2,1)}, bf16[128,512]{1,0:T(8,128)(2,1)}) custom-call(s32[2]{0:T(128)} %pad_add_fusion.at_ref, bf16[16,80,512]{2,1,0:T(8,128)(2,1)} %get-tuple-element.49.refs_0_, bf16[16,176,512]{2,1,0:T(8,128)(2,1)} %get-tuple-element.50.refs_1_, ...), custom_call_target="tpu_custom_call" | custom-call | flops 700000000 | bytes 8000000 | tf_op jit(solution)/shard_map/pallas_call | solution.py:309
  111.3 2.3 %collective-permute-done.24 = bf16[16,16,256]{2,1,0:T(8,128)(2,1)S(1)} collective-permute-done((bf16[16,16,256]{2,1,0:T(8,128)(2,1)S(1)}, bf16[16,16,256]{2,1,0:T(8,128)(2,1)S(1)}, u32[]{:S(2)}, u32[]{:S(2)}) %collective-permute-start.24) | collective-permute-done | bytes 131104 | tf_op jit(solution)/shard_map/ppermute | solution.py:363
  113.6 2.6 %collective-permute-done.23 = bf16[16,16,256]{2,1,0:T(8,128)(2,1)S(1)} collective-permute-done((bf16[16,16,256]{2,1,0:T(8,128)(2,1)S(1)}, bf16[16,16,256]{2,1,0:T(8,128)(2,1)S(1)}, u32[]{:S(2)}, u32[]{:S(2)}) %collective-permute-start.23) | collective-permute-done | bytes 131104 | tf_op jit(solution)/shard_map/ppermute | solution.py:363
  122.4 4.0 %collective-permute-done.21 = bf16[128,512]{1,0:T(8,128)(2,1)S(1)} collective-permute-done((bf16[128,512]{1,0:T(8,128)(2,1)S(1)}, bf16[128,512]{1,0:T(8,128)(2,1)S(1)}, u32[]{:S(2)}, u32[]{:S(2)}) %collective-permute-start.21) | collective-permute-done | bytes 131104 | tf_op jit(solution)/shard_map/ppermute | solution.py:363
  126.7 2.1 %collective-permute-done.19 = bf16[128,512]{1,0:T(8,128)(2,1)S(1)} collective-permute-done((bf16[128,512]{1,0:T(8,128)(2,1)S(1)}, bf16[128,512]{1,0:T(8,128)(2,1)S(1)}, u32[]{:S(2)}, u32[]{:S(2)}) %collective-permute-start.19) | collective-permute-done | bytes 131104 | tf_op jit(solution)/shard_map/ppermute | solution.py:363
  130.3 3.7 %shard_map.135 = (bf16[16,128,256]{2,1,0:T(8,128)(2,1)}, f32[512,256]{1,0:T(8,128)}) custom-call(s32[2]{0:T(128)} %pad_add_fusion.at_ref, bf16[4,16,16,256]{3,2,1,0:T(8,128)(2,1)} %copy-done.5, bf16[4,16,16,256]{3,2,1,0:T(8,128)(2,1)} %copy-done.7, bf16[16,80,512]{2,1,0:T(8,128)(2,1)} %copy-done.3), custom_call_target="tpu_custom_call" | custom-call | flops 300000000 | bytes 4000000 | tf_op jit(solution)/shard_map/pallas_call | solution.py:342
  134.1 3.2 %all-to-all-done.3 = bf16[16,176,512]{2,1,0:T(8,128)(2,1)S(1)} async-done(((bf16[16,176,512]{2,1,0:T(8,128)(2,1)}), bf16[16,176,512]{2,1,0:T(8,128)(2,1)S(1)}, u32[]{:S(2)}, u32[]{:S(2)}) %all-to-all-start.3) | async-done | bytes 2883616 | tf_op jit(solution)/shard_map/all_to_all | solution.py:376
  (106 shorter events, 37.4 us)
Async XLA Ops:
  2.1 15.5 %all-to-all-start = ((s32[16,1,2]{2,1,0:T(1,128)}), s32[16,1,2]{2,1,0:T(1,128)S(1)}, u32[]{:S(2)}, u32[]{:S(2)}) async-start(s32[16,1,2]{2,1,0:T(1,128)} %copy.16), calls=%async_computation | async-start | bytes 16384 | tf_op jit(solution)/shard_map/all_to_all | solution.py:376
  21.6 18.2 %all-to-all-start.1 = ((bf16[32,16,896]{2,1,0:T(8,128)(2,1)}), bf16[32,16,896]{2,1,0:T(8,128)(2,1)S(1)}, u32[]{:S(2)}, u32[]{:S(2)}) async-start(bf16[32,16,896]{2,1,0:T(8,128)(2,1)} %shard_map.129), calls=%async_computation.1 | async-start | bytes 1835008 | tf_op jit(solution)/shard_map/all_to_all | solution.py:376
  25.2 7.4 %collective-permute-start.5 = (bf16[128,512]{1,0:T(8,128)(2,1)S(1)}, bf16[128,512]{1,0:T(8,128)(2,1)S(1)}, u32[]{:S(2)}, u32[]{:S(2)}) collective-permute-start(bf16[128,512]{1,0:T(8,128)(2,1)S(1)} %copy-done.9), channel_id=1, source_target_pairs={{0,6},{1,7},{2,0},{3,1},{4,2},{5,3},{6,4},{7,5},{8,14},{9,15},{10,... | collective-permute-start | bytes 393224 | tf_op jit(solution)/shard_map/ppermute | solution.py:363
  28.3 6.6 %collective-permute-start.4 = (bf16[128,512]{1,0:T(8,128)(2,1)S(1)}, bf16[128,512]{1,0:T(8,128)(2,1)S(1)}, u32[]{:S(2)}, u32[]{:S(2)}) collective-permute-start(bf16[128,512]{1,0:T(8,128)(2,1)S(1)} %copy-done.9), channel_id=1, source_target_pairs={{0,4},{1,5},{2,6},{3,7},{4,0},{5,1},{6,2},{7,3},{8,12},{9,13},{10,... | collective-permute-start | bytes 393224 | tf_op jit(solution)/shard_map/ppermute | solution.py:363
  28.9 7.2 %collective-permute-start.3 = (bf16[128,512]{1,0:T(8,128)(2,1)S(1)}, bf16[128,512]{1,0:T(8,128)(2,1)S(1)}, u32[]{:S(2)}, u32[]{:S(2)}) collective-permute-start(bf16[128,512]{1,0:T(8,128)(2,1)S(1)} %copy-done.9), channel_id=1, source_target_pairs={{0,2},{1,3},{2,4},{3,5},{4,6},{5,7},{6,0},{7,1},{8,10},{9,11},{10,... | collective-permute-start | bytes 393224 | tf_op jit(solution)/shard_map/ppermute | solution.py:363
  36.3 11.4 %collective-permute-start.6 = (bf16[4,128,512]{2,1,0:T(8,128)(2,1)S(1)}, bf16[4,128,512]{2,1,0:T(8,128)(2,1)S(1)}, u32[]{:S(2)}, u32[]{:S(2)}) collective-permute-start(bf16[4,128,512]{2,1,0:T(8,128)(2,1)S(1)} %pad_maximum_fusion.near_in), channel_id=1, source_target_pairs={{0,1},{1,0},{2,3},{3,2},{4,5},{5,4},{6,7},{7,6},{8,9},{9,8},{10,11... | collective-permute-start | bytes 1572872 | tf_op jit(solution)/shard_map/ppermute | solution.py:367
  41.8 14.4 %collective-permute-start = (bf16[8,16,896]{2,1,0:T(8,128)(2,1)S(1)}, bf16[8,16,896]{2,1,0:T(8,128)(2,1)S(1)}, u32[]{:S(2)}, u32[]{:S(2)}) collective-permute-start(bf16[8,16,896]{2,1,0:T(8,128)(2,1)S(1)} %get-tuple-element.31.refs_0_), channel_id=1, source_target_pairs={{0,2},{1,3},{2,4},{3,5},{4,6},{5,7},{6,0},{7,1},{8,10},{9,11},{10,... | collective-permute-start | bytes 688136 | tf_op jit(solution)/shard_map/ppermute | solution.py:363
  43.4 12.8 %collective-permute-start.1 = (bf16[8,16,896]{2,1,0:T(8,128)(2,1)S(1)}, bf16[8,16,896]{2,1,0:T(8,128)(2,1)S(1)}, u32[]{:S(2)}, u32[]{:S(2)}) collective-permute-start(bf16[8,16,896]{2,1,0:T(8,128)(2,1)S(1)} %get-tuple-element.31.refs_0_), channel_id=1, source_target_pairs={{0,6},{1,7},{2,0},{3,1},{4,2},{5,3},{6,4},{7,5},{8,14},{9,15},{10,... | collective-permute-start | bytes 688136 | tf_op jit(solution)/shard_map/ppermute | solution.py:363
  45.1 11.1 %collective-permute-start.2 = (bf16[8,16,896]{2,1,0:T(8,128)(2,1)S(1)}, bf16[8,16,896]{2,1,0:T(8,128)(2,1)S(1)}, u32[]{:S(2)}, u32[]{:S(2)}) collective-permute-start(bf16[8,16,896]{2,1,0:T(8,128)(2,1)S(1)} %get-tuple-element.31.refs_0_), channel_id=1, source_target_pairs={{0,4},{1,5},{2,6},{3,7},{4,0},{5,1},{6,2},{7,3},{8,12},{9,13},{10,... | collective-permute-start | bytes 688136 | tf_op jit(solution)/shard_map/ppermute | solution.py:363
  56.2 4.3 %collective-permute-start.8 = (bf16[8,16,896]{2,1,0:T(8,128)(2,1)S(1)}, bf16[8,16,896]{2,1,0:T(8,128)(2,1)S(1)}, u32[]{:S(2)}, u32[]{:S(2)}) collective-permute-start(bf16[8,16,896]{2,1,0:T(8,128)(2,1)S(1)} %collective-permute-done.refs_1_), channel_id=1, source_target_pairs={{0,1},{1,0},{2,3},{3,2},{4,5},{5,4},{6,7},{7,6},{8,9},{9,8},{10,11... | collective-permute-start | bytes 688136 | tf_op jit(solution)/shard_map/ppermute | solution.py:367
  56.8 4.1 %collective-permute-start.9 = (bf16[8,16,896]{2,1,0:T(8,128)(2,1)S(1)}, bf16[8,16,896]{2,1,0:T(8,128)(2,1)S(1)}, u32[]{:S(2)}, u32[]{:S(2)}) collective-permute-start(bf16[8,16,896]{2,1,0:T(8,128)(2,1)S(1)} %collective-permute-done.1.refs_2_), channel_id=1, source_target_pairs={{0,1},{1,0},{2,3},{3,2},{4,5},{5,4},{6,7},{7,6},{8,9},{9,8},{10,11... | collective-permute-start | bytes 688136 | tf_op jit(solution)/shard_map/ppermute | solution.py:367
  56.9 4.0 %collective-permute-start.10 = (bf16[8,16,896]{2,1,0:T(8,128)(2,1)S(1)}, bf16[8,16,896]{2,1,0:T(8,128)(2,1)S(1)}, u32[]{:S(2)}, u32[]{:S(2)}) collective-permute-start(bf16[8,16,896]{2,1,0:T(8,128)(2,1)S(1)} %collective-permute-done.2.refs_3_), channel_id=1, source_target_pairs={{0,1},{1,0},{2,3},{3,2},{4,5},{5,4},{6,7},{7,6},{8,9},{9,8},{10,11... | collective-permute-start | bytes 688136 | tf_op jit(solution)/shard_map/ppermute | solution.py:367
  57.3 13.7 %collective-permute-start.11 = (bf16[8,16,896]{2,1,0:T(8,128)(2,1)S(1)}, bf16[8,16,896]{2,1,0:T(8,128)(2,1)S(1)}, u32[]{:S(2)}, u32[]{:S(2)}) collective-permute-start(bf16[8,16,896]{2,1,0:T(8,128)(2,1)S(1)} %get-tuple-element.41.refs_0_), channel_id=1, source_target_pairs={{0,2},{1,3},{2,4},{3,5},{4,6},{5,7},{6,0},{7,1},{8,10},{9,11},{10,... | collective-permute-start | bytes 688136 | tf_op jit(solution)/shard_map/ppermute | solution.py:363
  58.0 13.1 %collective-permute-start.12 = (bf16[8,16,896]{2,1,0:T(8,128)(2,1)S(1)}, bf16[8,16,896]{2,1,0:T(8,128)(2,1)S(1)}, u32[]{:S(2)}, u32[]{:S(2)}) collective-permute-start(bf16[8,16,896]{2,1,0:T(8,128)(2,1)S(1)} %get-tuple-element.41.refs_0_), channel_id=1, source_target_pairs={{0,6},{1,7},{2,0},{3,1},{4,2},{5,3},{6,4},{7,5},{8,14},{9,15},{10,... | collective-permute-start | bytes 688136 | tf_op jit(solution)/shard_map/ppermute | solution.py:363
  60.5 10.5 %collective-permute-start.13 = (bf16[8,16,896]{2,1,0:T(8,128)(2,1)S(1)}, bf16[8,16,896]{2,1,0:T(8,128)(2,1)S(1)}, u32[]{:S(2)}, u32[]{:S(2)}) collective-permute-start(bf16[8,16,896]{2,1,0:T(8,128)(2,1)S(1)} %get-tuple-element.41.refs_0_), channel_id=1, source_target_pairs={{0,4},{1,5},{2,6},{3,7},{4,0},{5,1},{6,2},{7,3},{8,12},{9,13},{10,... | collective-permute-start | bytes 688136 | tf_op jit(solution)/shard_map/ppermute | solution.py:363
  71.0 25.3 %all-to-all-start.2 = ((bf16[16,80,512]{2,1,0:T(8,128)(2,1)}), bf16[16,80,512]{2,1,0:T(8,128)(2,1)S(1)}, u32[]{:S(2)}, u32[]{:S(2)}) async-start(bf16[16,80,512]{2,1,0:T(8,128)(2,1)} %get-tuple-element.49.refs_0_), calls=%async_computation.2 | async-start | bytes 2621440 | tf_op jit(solution)/shard_map/all_to_all | solution.py:376
  97.4 40.0 %all-to-all-start.3 = ((bf16[16,176,512]{2,1,0:T(8,128)(2,1)}), bf16[16,176,512]{2,1,0:T(8,128)(2,1)S(1)}, u32[]{:S(2)}, u32[]{:S(2)}) async-start(bf16[16,176,512]{2,1,0:T(8,128)(2,1)} %get-tuple-element.50.refs_1_), calls=%async_computation.3 | async-start | bytes 5767168 | tf_op jit(solution)/shard_map/all_to_all | solution.py:376
  107.2 6.4 %collective-permute-start.24 = (bf16[16,16,256]{2,1,0:T(8,128)(2,1)S(1)}, bf16[16,16,256]{2,1,0:T(8,128)(2,1)S(1)}, u32[]{:S(2)}, u32[]{:S(2)}) collective-permute-start(bf16[16,16,256]{2,1,0:T(8,128)(2,1)S(1)} %get-tuple-element.58), channel_id=1, source_target_pairs={{0,6},{1,7},{2,0},{3,1},{4,2},{5,3},{6,4},{7,5},{8,14},{9,15},{10,... | collective-permute-start | bytes 393224 | tf_op jit(solution)/shard_map/ppermute | solution.py:363
  108.4 7.8 %collective-permute-start.23 = (bf16[16,16,256]{2,1,0:T(8,128)(2,1)S(1)}, bf16[16,16,256]{2,1,0:T(8,128)(2,1)S(1)}, u32[]{:S(2)}, u32[]{:S(2)}) collective-permute-start(bf16[16,16,256]{2,1,0:T(8,128)(2,1)S(1)} %get-tuple-element.58), channel_id=1, source_target_pairs={{0,4},{1,5},{2,6},{3,7},{4,0},{5,1},{6,2},{7,3},{8,12},{9,13},{10,... | collective-permute-start | bytes 393224 | tf_op jit(solution)/shard_map/ppermute | solution.py:363
  110.1 8.2 %collective-permute-start.22 = (bf16[16,16,256]{2,1,0:T(8,128)(2,1)S(1)}, bf16[16,16,256]{2,1,0:T(8,128)(2,1)S(1)}, u32[]{:S(2)}, u32[]{:S(2)}) collective-permute-start(bf16[16,16,256]{2,1,0:T(8,128)(2,1)S(1)} %get-tuple-element.58), channel_id=1, source_target_pairs={{0,2},{1,3},{2,4},{3,5},{4,6},{5,7},{6,0},{7,1},{8,10},{9,11},{10,... | collective-permute-start | bytes 393224 | tf_op jit(solution)/shard_map/ppermute | solution.py:363
  118.4 11.1 %collective-permute-start.25 = (bf16[4,16,16,256]{3,2,1,0:T(8,128)(2,1)S(1)}, bf16[4,16,16,256]{3,2,1,0:T(8,128)(2,1)S(1)}, u32[]{:S(2)}, u32[]{:S(2)}) collective-permute-start(bf16[4,16,16,256]{3,2,1,0:T(8,128)(2,1)S(1)} %pad_maximum_fusion.1.near_ref), channel_id=1, source_target_pairs={{0,1},{1,0},{2,3},{3,2},{4,5},{5,4},{6,7},{7,6},{8,9},{9,8},{10,11... | collective-permute-start | bytes 1572872 | tf_op jit(solution)/shard_map/ppermute | solution.py:367
  118.5 7.9 %collective-permute-start.21 = (bf16[128,512]{1,0:T(8,128)(2,1)S(1)}, bf16[128,512]{1,0:T(8,128)(2,1)S(1)}, u32[]{:S(2)}, u32[]{:S(2)}) collective-permute-start(bf16[128,512]{1,0:T(8,128)(2,1)S(1)} %get-tuple-element.60), channel_id=1, source_target_pairs={{0,4},{1,5},{2,6},{3,7},{4,0},{5,1},{6,2},{7,3},{8,12},{9,13},{10,... | collective-permute-start | bytes 393224 | tf_op jit(solution)/shard_map/ppermute | solution.py:363
  120.3 6.4 %collective-permute-start.20 = (bf16[128,512]{1,0:T(8,128)(2,1)S(1)}, bf16[128,512]{1,0:T(8,128)(2,1)S(1)}, u32[]{:S(2)}, u32[]{:S(2)}) collective-permute-start(bf16[128,512]{1,0:T(8,128)(2,1)S(1)} %get-tuple-element.61), channel_id=1, source_target_pairs={{0,6},{1,7},{2,0},{3,1},{4,2},{5,3},{6,4},{7,5},{8,14},{9,15},{10,... | collective-permute-start | bytes 393224 | tf_op jit(solution)/shard_map/ppermute | solution.py:363
  121.5 7.3 %collective-permute-start.19 = (bf16[128,512]{1,0:T(8,128)(2,1)S(1)}, bf16[128,512]{1,0:T(8,128)(2,1)S(1)}, u32[]{:S(2)}, u32[]{:S(2)}) collective-permute-start(bf16[128,512]{1,0:T(8,128)(2,1)S(1)} %get-tuple-element.59), channel_id=1, source_target_pairs={{0,2},{1,3},{2,4},{3,5},{4,6},{5,7},{6,0},{7,1},{8,10},{9,11},{10,... | collective-permute-start | bytes 393224 | tf_op jit(solution)/shard_map/ppermute | solution.py:363
  (31 other events, 175.4 us)

commit v8 on v6

--- a/solution.py
+++ b/solution.py
@@ -31,17 +31,20 @@
 
 def pick_kernel(rows_ref, src_ref, *rest, row_of, count):
     *outs, held, load_sem, store_sem = rest
-    places = [out.at[n] for out in outs for n in range(out.shape[0])]
     loads = [
         pltpu.make_async_copy(src_ref.at[row_of(rows_ref, k)], held.at[k], load_sem.at[k])
         for k in range(count)
     ]
-    stores = [pltpu.make_async_copy(held.at[k], places[k], store_sem.at[k]) for k in range(count)]
     for load in loads:
         load.start()
-    for load, store in zip(loads, stores):
-        load.wait()
-        store.start()
+    stores, first = [], 0
+    for n, out in enumerate(outs):
+        size = out.shape[0]
+        for load in loads[first : first + size]:
+            load.wait()
+        stores.append(pltpu.make_async_copy(held.at[pl.ds(first, size)], out, store_sem.at[n]))
+        stores[-1].start()
+        first += size
     for store in stores:
         store.wait()
 
@@ -57,7 +60,7 @@
         scratch_shapes=[
             pltpu.VMEM((total, *item), src.dtype),
             pltpu.SemaphoreType.DMA((total,)),
-            pltpu.SemaphoreType.DMA((total,)),
+            pltpu.SemaphoreType.DMA((len(counts),)),
         ],
         compiler_params=pltpu.CompilerParams(vmem_limit_bytes=limit),
     )(rows, src)
@@ -119,26 +122,35 @@
     share = gc_ref.shape[1]
     own = pl.ds(pl.multiple_of((at_ref[0] * 2 + at_ref[1]) * share, share), share)
     first = start_loads([(near_in, near_ref), (far_in, far_ref)], sem)
-    blocks = start_loads(row_blocks(wo_in, wo_ref, 8), sem, 2)
-    late = start_loads([(wv_in, wv_ref)], sem, 10)
-    wait_all(first)
     places = []
     for core, g_ref in enumerate((near_ref, far_ref)):
         for s in range(chips):
             j = lax.rem(at_ref[0] + chips - s, chips) * 2 + lax.rem(at_ref[1] + core, 2)
-            places.append((g_ref, s, pl.ds(pl.multiple_of(j * width, width), width)))
-            for p in range(cuts):
-                gc_ref[j * cuts + p, :, :piece] = g_ref[s, own, p * piece : (p + 1) * piece]
-                gc_ref[j * cuts + p, :, piece:] = jnp.zeros((share, width - piece), BF)
-    stores = start_loads([(gc_ref, gc_out)], sem, 11)
-    wait_all(blocks)
+            places.append((g_ref, s, j))
+    blocks = start_loads(
+        [
+            (wo_in.at[:, pl.ds(pl.multiple_of(j * width, width), width)], wo_ref.at[k])
+            for k, (_, _, j) in enumerate(places)
+        ],
+        sem,
+        2,
+    )
+    used = 2 + len(places)
+    late = start_loads([(wv_in, wv_ref)], sem, used)
+    wait_all(first)
+    for g_ref, s, j in places:
+        for p in range(cuts):
+            gc_ref[j * cuts + p, :, :piece] = g_ref[s, own, p * piece : (p + 1) * piece]
+            gc_ref[j * cuts + p, :, piece:] = jnp.zeros((share, width - piece), BF)
+    stores = start_loads([(gc_ref, gc_out)], sem, used + 1)
     acc = jnp.zeros((rows, width), F32)
-    for g_ref, s, cols in places:
-        acc += mm(g_ref[s], wo_ref[:, cols], 1, 1)
+    for k, (g_ref, s, _) in enumerate(places):
+        blocks[k].wait()
+        acc += mm(g_ref[s], wo_ref[k], 1, 1)
     dm_ref[...] = acc.astype(BF)
     wait_all(late)
     back_project(dm_ref, wv_ref, dt_ref)
-    stores += start_loads([(dm_ref, dm_out), (dt_ref, dt_out)], sem, 12)
+    stores += start_loads([(dm_ref, dm_out), (dt_ref, dt_out)], sem, used + 2)
     wait_all(stores)
 
 
@@ -152,8 +164,11 @@
         out_shape=[jax.ShapeDtypeStruct(shape, BF) for shape in made],
         in_specs=[SM] + [HBM] * 4,
         out_specs=[HBM] * 3,
-        scratch_shapes=[pltpu.VMEM(shape, BF) for shape in (*(v.shape for v in operands), *made)]
-        + [pltpu.SemaphoreType.DMA((14,))],
+        scratch_shapes=[
+            pltpu.VMEM(shape, BF)
+            for shape in (near.shape, far.shape, (2 * chips, width, width), wv.shape, *made)
+        ]
+        + [pltpu.SemaphoreType.DMA((6 + 2 * chips,))],
         compiler_params=params(),
         cost_estimate=pl.CostEstimate(flops=700_000_000, bytes_accessed=8_000_000, transcendentals=0),
     )(at, *operands)
@@ -184,8 +199,9 @@
         [(qt_in.at[c], qt_ref)]
         + [(x_in[p], x_ref.at[pl.ds(p * slots, slots)]) for p in range(pieces)]
     )
+    wait_all(x_loads)
+    wv_loads = start(row_blocks(wv_in, wv_ref, 2))
     dt_loads = start([(dt_in.at[c], dt_ref)])
-    wv_loads = start(row_blocks(wv_in, wv_ref, 2))
     if last:
         q_ref, dm_ref, t0_ref, u0_ref, gw_ref = refs[:5]
         last_loads = start(list(zip(ins[3:], (q_ref, dm_ref, t0_ref, u0_ref))))
@@ -193,7 +209,6 @@
         gs_ref = refs[0]
         gs_loads = start([(ins[3], gs_ref)])
     factor = 1.0 / math.sqrt(HD)
-    wait_all(x_loads)
     x = x_ref[...].reshape(pieces * slots * sub, enc)
     keys = x.shape[0]
     s = mm(qt_ref[...], x, 1, 1) * factor
@@ -230,7 +245,9 @@
                     gw_ref[i, k * share : (k + 1) * share, cols] = total[
                         i * share : (i + 1) * share
                     ].astype(BF)
-        stores += start([(gw_ref, send_ref.at[:, pl.ds(part, 2 * share)])])
+            stores += start(
+                [(gw_ref.at[:, :, pl.ds(h * HD, HD)], send_ref.at[:, pl.ds(part, 2 * share), pl.ds(h * HD, HD)])]
+            )
     wait_all(stores)
 
 
@@ -244,7 +261,7 @@
     more = list(extra)
     held = [(len(xs) * slots, sub, enc), (part, width), tall, tall, tall, tall, wv.shape]
     held += [v.shape for v in more]
-    copies = len(xs) + 8 + len(more) + db_count
+    copies = len(xs) + 8 + len(more) + db_count + width // HD
     if last:
         held += [(db_count, grown, width)]
     else:
@@ -367,7 +384,8 @@
     at = jnp.stack([head_at // 2, head_at % 2]).astype(jnp.int32)
     owner_ids = lax.broadcasted_iota(jnp.int32, (db_count, 1, 1, 1), 0)
     wanted = jnp.sum(jnp.where(nbr_owner[None, None] == owner_ids, nbr_row[None, None], 0), axis=3)
-    incoming = exchange(wanted, "db")
+    qt = back(queries, w_key, groups)
+    incoming = after(exchange(wanted, "db"), qt)
     steps = ring_steps(head_count)
     (table,) = pick(
         incoming,
@@ -377,8 +395,7 @@
         HBM,
         VMEM_LIMIT,
     )
-    qt = back(after(queries, table), w_key, groups)
-    received = after(exchange(table, "db"), qt)
+    received = exchange(table, "db")
     mine = pick(
         nbr_owner,
         lambda ref, k: ref[k // slot_count, k % slot_count] * groups + k // slot_count,
@@ -390,6 +407,8 @@
     token = mine[0]
     near = chips_stack(after(grad_out, table), steps, head_count)
     far = swap(near, head_count)
+    crossed = [swap(v, head_count) for v in mine]
+    near = after(near, crossed[0])
     dm, dt, grad_cols = prep(at, near, far, w_out, w_value, groups, db_count)
     ring = []
     for c in range(groups):
@@ -399,8 +418,8 @@
             came = lax.optimization_barrier((*came, dm))[:-1]
         ring.append([held, *came])
     spread = []
-    for pieces in ring:
-        spread.append([*pieces, *(swap(v, head_count) for v in pieces)])
+    for c, pieces in enumerate(ring):
+        spread.append([*pieces, crossed[c], *(swap(v, head_count) for v in pieces[1:])])
     sent, sends, us = [], [], []
     extra = (grad_cols,)
     for c in range(groups):

time: 143 us -> 141 us (0.986)
  blocking collectives: 15.4 us -> 0 us
  waiting for transfers between devices: 38.4 us -> 49.2 us
  starting transfers between devices: 37.4 us -> 40.6 us
    all_to_all x1 -> x0, blocking collectives: 15.4 us -> none  [exchange(): return lax.all_to_all(x, axis, split_axis=0, concat_axis=0, tiled=True)]
    all_to_all x3 -> x4, waiting for transfers between devices: 12.3 us -> 20.1 us  [exchange(): return lax.all_to_all(x, axis, split_axis=0, concat_axis=0, tiled=True)]
    all_to_all x3 -> x4, starting transfers between devices: 14.6 us -> 19.1 us  [exchange(): return lax.all_to_all(x, axis, split_axis=0, concat_axis=0, tiled=True)]
    ppermute x15, waiting for transfers between devices: 24.6 us -> 27.6 us  [along(): lax.ppermute(v, 'head', [(i, (i // 2 + step) % chips * 2 + i % 2) for i i...]
    unnamed x48 -> x50, local copies, waits for them, and re-layouts: 4.51 us -> 5.18 us
  transfers between devices with their start and end apart: 29 -> 30, of which waited for: 19 -> 20; matrix products, arithmetic and copies ran while one was open for 4% -> 4% of each run, Pallas kernels for 23% -> 23%
where the time goes in v8:
time: 141 us
  waiting for transfers between devices  49.2 us (35%)
  starting transfers between devices  40.6 us (29%)
  Pallas kernels  35.6 us (25%)
  local copies, waits for them, and re-layouts  6.82 us (5%)
  other arithmetic  4.34 us (3%)
  matrix products  3.1 us (2%)
    ppermute x15, waiting for transfers between devices, along(): lax.ppermute(v, 'head', [(i, (i // 2 + step) % chips * 2 + i % 2) for i i...  27.6 us
    all_to_all x4, waiting for transfers between devices, exchange(): return lax.all_to_all(x, axis, split_axis=0, concat_axis=0, tiled=True)  20.1 us
    ppermute x15, starting transfers between devices, along(): lax.ppermute(v, 'head', [(i, (i // 2 + step) % chips * 2 + i % 2) for i i...  19.5 us
    all_to_all x4, starting transfers between devices, exchange(): return lax.all_to_all(x, axis, split_axis=0, concat_axis=0, tiled=True)  19.1 us
    pallas_call x2, Pallas kernels, attn(): pl.pallas_call(functools.partial(attn_kernel, c=c, pieces=len(xs), last=l...  14.6 us
    pallas_call x2, Pallas kernels, pick(): pl.pallas_call(functools.partial(pick_kernel, row_of=row_of, count=total)...  5.43 us
    pallas_call x1, Pallas kernels, prep(): pl.pallas_call(prep_kernel, out_shape=[jax.ShapeDtypeStruct(shape, BF) fo...  5.4 us
    unnamed x50, local copies, waits for them, and re-layouts  5.18 us
  transfers between devices with their start and end apart: 30, of which 20 were waited for; matrix products, arithmetic and copies ran while one was open for 4% of the time, Pallas kernels for 23%

profile of v8, /device:TPU:0, one launch (start us, length us, event | category | flops | bytes accessed | tf_op | source)
XLA Modules:
  0.0 140.6 jit_solution(13714364380442572211)
XLA Ops:
  2.1 8.0 %all-to-all-start = ((s32[16,1,2]{2,1,0:T(1,128)}), s32[16,1,2]{2,1,0:T(1,128)S(1)}, u32[]{:S(2)}, u32[]{:S(2)}) async-start(s32[16,1,2]{2,1,0:T(1,128)} %copy.17), calls=%async_computation | async-start | bytes 16384 | tf_op jit(solution)/shard_map/all_to_all | solution.py:369
  10.1 2.8 %shard_map.128.refs_8_ = bf16[2,256,896]{2,1,0:T(8,128)(2,1)} custom-call(bf16[128,512]{1,0:T(8,128)(2,1)} %refs_11_.1, bf16[896,512]{1,0:T(8,128)(2,1)} %refs_5_.1), custom_call_target="tpu_custom_call" | custom-call | flops 120000000 | bytes 2000000 | tf_op jit(solution)/shard_map/pallas_call | solution.py:105
  12.8 4.7 %all-to-all-done.rows_ref = s32[16,1,2]{2,1,0:T(1,128)S(1)} async-done(((s32[16,1,2]{2,1,0:T(1,128)}), s32[16,1,2]{2,1,0:T(1,128)S(1)}, u32[]{:S(2)}, u32[]{:S(2)}) %all-to-all-start) | async-done | bytes 160 | tf_op jit(solution)/shard_map/all_to_all | solution.py:369
  18.1 3.4 %shard_map.129 = bf16[32,16,896]{2,1,0:T(8,128)(2,1)} custom-call(s32[16,1,2]{2,1,0:T(1,128)} %copy-done.10, bf16[64,16,896]{2,1,0:T(8,128)(2,1)} %src_ref.1), custom_call_target="tpu_custom_call" | custom-call | tf_op jit(solution)/shard_map/pallas_call | solution.py:55
  21.6 3.6 %all-to-all-start.1 = ((bf16[32,16,896]{2,1,0:T(8,128)(2,1)}), bf16[32,16,896]{2,1,0:T(8,128)(2,1)S(1)}, u32[]{:S(2)}, u32[]{:S(2)}) async-start(bf16[32,16,896]{2,1,0:T(8,128)(2,1)} %shard_map.129), calls=%async_computation.1 | async-start | bytes 1835008 | tf_op jit(solution)/shard_map/all_to_all | solution.py:369
  25.3 3.1 %collective-permute-start.5 = (bf16[128,512]{1,0:T(8,128)(2,1)S(1)}, bf16[128,512]{1,0:T(8,128)(2,1)S(1)}, u32[]{:S(2)}, u32[]{:S(2)}) collective-permute-start(bf16[128,512]{1,0:T(8,128)(2,1)S(1)} %copy-done.9), channel_id=1, source_target_pairs={{0,6},{1,7},{2,0},{3,1},{4,2},{5,3},{6,4},{7,5},{8,14},{9,15},{10,... | collective-permute-start | bytes 393224 | tf_op jit(solution)/shard_map/ppermute | solution.py:356
  30.0 2.7 %collective-permute-done.5 = bf16[128,512]{1,0:T(8,128)(2,1)S(1)} collective-permute-done((bf16[128,512]{1,0:T(8,128)(2,1)S(1)}, bf16[128,512]{1,0:T(8,128)(2,1)S(1)}, u32[]{:S(2)}, u32[]{:S(2)}) %collective-permute-start.5) | collective-permute-done | bytes 131104 | tf_op jit(solution)/shard_map/ppermute | solution.py:356
  32.7 2.3 %collective-permute-done.4 = bf16[128,512]{1,0:T(8,128)(2,1)S(1)} collective-permute-done((bf16[128,512]{1,0:T(8,128)(2,1)S(1)}, bf16[128,512]{1,0:T(8,128)(2,1)S(1)}, u32[]{:S(2)}, u32[]{:S(2)}) %collective-permute-start.4) | collective-permute-done | bytes 131104 | tf_op jit(solution)/shard_map/ppermute | solution.py:356
  36.4 3.4 %all-to-all-done.1.src_ref = bf16[32,16,896]{2,1,0:T(8,128)(2,1)S(1)} async-done(((bf16[32,16,896]{2,1,0:T(8,128)(2,1)}), bf16[32,16,896]{2,1,0:T(8,128)(2,1)S(1)}, u32[]{:S(2)}, u32[]{:S(2)}) %all-to-all-start.1) | async-done | bytes 917536 | tf_op jit(solution)/shard_map/all_to_all | solution.py:369
  48.7 5.4 %shard_map.131 = (bf16[128,512]{1,0:T(8,128)(2,1)}, bf16[2,256,896]{2,1,0:T(8,128)(2,1)}, bf16[16,16,512]{2,1,0:T(8,128)(2,1)}) custom-call(s32[2]{0:T(128)} %pad_add_fusion.at_ref, bf16[4,128,512]{2,1,0:T(8,128)(2,1)} %copy-done.3, bf16[4,128,512]{2,1,0:T(8,128)(2,1)} %copy-done.7, bf16[512,4096]{1,0:T(8,128)(2,1)} %refs_4_.1, bf16[896,512]{1,0:T(8,128)(2,1)} %refs_10_.3), custom_call_target="tpu_custom_call" | custom-call | flops 700000000 | bytes 8000000 | tf_op jit(solution)/shard_map/pallas_call | solution.py:162
  54.1 3.2 %collective-permute-done.2.refs_3_ = bf16[8,16,896]{2,1,0:T(8,128)(2,1)S(1)} collective-permute-done((bf16[8,16,896]{2,1,0:T(8,128)(2,1)S(1)}, bf16[8,16,896]{2,1,0:T(8,128)(2,1)S(1)}, u32[]{:S(2)}, u32[]{:S(2)}) %collective-permute-start.2) | collective-permute-done | bytes 229408 | tf_op jit(solution)/shard_map/ppermute | solution.py:356
  58.9 2.1 %collective-permute-start.12 = (bf16[8,16,896]{2,1,0:T(8,128)(2,1)S(1)}, bf16[8,16,896]{2,1,0:T(8,128)(2,1)S(1)}, u32[]{:S(2)}, u32[]{:S(2)}) collective-permute-start(bf16[8,16,896]{2,1,0:T(8,128)(2,1)S(1)} %get-tuple-element.41.refs_0_), channel_id=1, source_target_pairs={{0,6},{1,7},{2,0},{3,1},{4,2},{5,3},{6,4},{7,5},{8,14},{9,15},{10,... | collective-permute-start | bytes 688136 | tf_op jit(solution)/shard_map/ppermute | solution.py:356
  62.1 6.6 %shard_map.132 = (bf16[16,80,512]{2,1,0:T(8,128)(2,1)}, bf16[256,896]{1,0:T(8,128)(2,1)}, bf16[256,896]{1,0:T(8,128)(2,1)}) custom-call(s32[2]{0:T(128)} %count_ref.3, bf16[8,16,896]{2,1,0:T(8,128)(2,1)} %copy-done.2, bf16[8,16,896]{2,1,0:T(8,128)(2,1)} %copy-done.12, bf16[8,16,896]{2,1,0:T(8,128)(2,1)} %copy-done.13, bf16[8,16,896]{2,1,0:T(8,128)(2,1)} %copy-done.14, ...), custom_call_target="tpu_custom_call" | custom-call | flops 3000000000 | bytes 8000000 | tf_op jit(solution)/shard_map/pallas_call | solution.py:269
  68.7 2.5 %collective-permute-done.12.refs_2_ = bf16[8,16,896]{2,1,0:T(8,128)(2,1)S(1)} collective-permute-done((bf16[8,16,896]{2,1,0:T(8,128)(2,1)S(1)}, bf16[8,16,896]{2,1,0:T(8,128)(2,1)S(1)}, u32[]{:S(2)}, u32[]{:S(2)}) %collective-permute-start.12) | collective-permute-done | bytes 229408 | tf_op jit(solution)/shard_map/ppermute | solution.py:356
  72.0 3.8 %all-to-all-start.2 = ((bf16[16,80,512]{2,1,0:T(8,128)(2,1)}), bf16[16,80,512]{2,1,0:T(8,128)(2,1)S(1)}, u32[]{:S(2)}, u32[]{:S(2)}) async-start(bf16[16,80,512]{2,1,0:T(8,128)(2,1)} %get-tuple-element.49.refs_0_), calls=%async_computation.2 | async-start | bytes 2621440 | tf_op jit(solution)/shard_map/all_to_all | solution.py:369
  79.1 8.0 %shard_map.133 = (bf16[16,176,512]{2,1,0:T(8,128)(2,1)}, bf16[256,896]{1,0:T(8,128)(2,1)}) custom-call(s32[2]{0:T(128)} %count_ref.3, bf16[8,16,896]{2,1,0:T(8,128)(2,1)} %copy-done.1, bf16[8,16,896]{2,1,0:T(8,128)(2,1)} %copy-done.15, bf16[8,16,896]{2,1,0:T(8,128)(2,1)} %copy-done.16, bf16[8,16,896]{2,1,0:T(8,128)(2,1)} %copy-done.17, ...), custom_call_target="tpu_custom_call" | custom-call | flops 3000000000 | bytes 8000000 | tf_op jit(solution)/shard_map/pallas_call | solution.py:269
  87.1 9.5 %all-to-all-done.2 = bf16[16,80,512]{2,1,0:T(8,128)(2,1)S(1)} async-done(((bf16[16,80,512]{2,1,0:T(8,128)(2,1)}), bf16[16,80,512]{2,1,0:T(8,128)(2,1)S(1)}, u32[]{:S(2)}, u32[]{:S(2)}) %all-to-all-start.2) | async-done | bytes 1310752 | tf_op jit(solution)/shard_map/all_to_all | solution.py:369
  97.7 3.7 %all-to-all-start.3 = ((bf16[16,176,512]{2,1,0:T(8,128)(2,1)}), bf16[16,176,512]{2,1,0:T(8,128)(2,1)S(1)}, u32[]{:S(2)}, u32[]{:S(2)}) async-start(bf16[16,176,512]{2,1,0:T(8,128)(2,1)} %get-tuple-element.50.refs_1_), calls=%async_computation.3 | async-start | bytes 5767168 | tf_op jit(solution)/shard_map/all_to_all | solution.py:369
  101.4 5.1 %shard_map.134 = (bf16[4,128,512]{2,1,0:T(8,128)(2,1)}, bf16[4,128,512]{2,1,0:T(8,128)(2,1)}, bf16[128,512]{1,0:T(8,128)(2,1)}) custom-call(s32[2]{0:T(128)} %pad_add_fusion.at_ref, bf16[16,80,512]{2,1,0:T(8,128)(2,1)} %get-tuple-element.49.refs_0_, bf16[16,176,512]{2,1,0:T(8,128)(2,1)} %get-tuple-element.50.refs_1_, ...), custom_call_target="tpu_custom_call" | custom-call | flops 700000000 | bytes 8000000 | tf_op jit(solution)/shard_map/pallas_call | solution.py:312
  111.7 4.0 %collective-permute-done.24 = bf16[16,16,256]{2,1,0:T(8,128)(2,1)S(1)} collective-permute-done((bf16[16,16,256]{2,1,0:T(8,128)(2,1)S(1)}, bf16[16,16,256]{2,1,0:T(8,128)(2,1)S(1)}, u32[]{:S(2)}, u32[]{:S(2)}) %collective-permute-start.24) | collective-permute-done | bytes 131104 | tf_op jit(solution)/shard_map/ppermute | solution.py:356
  122.7 4.8 %collective-permute-done.21 = bf16[128,512]{1,0:T(8,128)(2,1)S(1)} collective-permute-done((bf16[128,512]{1,0:T(8,128)(2,1)S(1)}, bf16[128,512]{1,0:T(8,128)(2,1)S(1)}, u32[]{:S(2)}, u32[]{:S(2)}) %collective-permute-start.21) | collective-permute-done | bytes 131104 | tf_op jit(solution)/shard_map/ppermute | solution.py:356
  127.8 2.1 %collective-permute-done.19 = bf16[128,512]{1,0:T(8,128)(2,1)S(1)} collective-permute-done((bf16[128,512]{1,0:T(8,128)(2,1)S(1)}, bf16[128,512]{1,0:T(8,128)(2,1)S(1)}, u32[]{:S(2)}, u32[]{:S(2)}) %collective-permute-start.19) | collective-permute-done | bytes 131104 | tf_op jit(solution)/shard_map/ppermute | solution.py:356
  131.4 2.3 %shard_map.135 = bf16[16,128,256]{2,1,0:T(8,128)(2,1)} custom-call(s32[2]{0:T(128)} %pad_add_fusion.at_ref, bf16[4,16,16,256]{3,2,1,0:T(8,128)(2,1)} %copy-done.4, bf16[4,16,16,256]{3,2,1,0:T(8,128)(2,1)} %copy-done.8), custom_call_target="tpu_custom_call" | custom-call | bytes 2000000 | tf_op jit(solution)/shard_map/pallas_call | solution.py:339
  135.5 2.5 %all-to-all-done.3 = bf16[16,176,512]{2,1,0:T(8,128)(2,1)S(1)} async-done(((bf16[16,176,512]{2,1,0:T(8,128)(2,1)}), bf16[16,176,512]{2,1,0:T(8,128)(2,1)S(1)}, u32[]{:S(2)}, u32[]{:S(2)}) %all-to-all-start.3) | async-done | bytes 2883616 | tf_op jit(solution)/shard_map/all_to_all | solution.py:369
  (106 shorter events, 40.1 us)
Async XLA Ops:
  2.1 15.5 %all-to-all-start = ((s32[16,1,2]{2,1,0:T(1,128)}), s32[16,1,2]{2,1,0:T(1,128)S(1)}, u32[]{:S(2)}, u32[]{:S(2)}) async-start(s32[16,1,2]{2,1,0:T(1,128)} %copy.17), calls=%async_computation | async-start | bytes 16384 | tf_op jit(solution)/shard_map/all_to_all | solution.py:369
  21.6 18.2 %all-to-all-start.1 = ((bf16[32,16,896]{2,1,0:T(8,128)(2,1)}), bf16[32,16,896]{2,1,0:T(8,128)(2,1)S(1)}, u32[]{:S(2)}, u32[]{:S(2)}) async-start(bf16[32,16,896]{2,1,0:T(8,128)(2,1)} %shard_map.129), calls=%async_computation.1 | async-start | bytes 1835008 | tf_op jit(solution)/shard_map/all_to_all | solution.py:369
  25.3 7.4 %collective-permute-start.5 = (bf16[128,512]{1,0:T(8,128)(2,1)S(1)}, bf16[128,512]{1,0:T(8,128)(2,1)S(1)}, u32[]{:S(2)}, u32[]{:S(2)}) collective-permute-start(bf16[128,512]{1,0:T(8,128)(2,1)S(1)} %copy-done.9), channel_id=1, source_target_pairs={{0,6},{1,7},{2,0},{3,1},{4,2},{5,3},{6,4},{7,5},{8,14},{9,15},{10,... | collective-permute-start | bytes 393224 | tf_op jit(solution)/shard_map/ppermute | solution.py:356
  28.4 6.6 %collective-permute-start.4 = (bf16[128,512]{1,0:T(8,128)(2,1)S(1)}, bf16[128,512]{1,0:T(8,128)(2,1)S(1)}, u32[]{:S(2)}, u32[]{:S(2)}) collective-permute-start(bf16[128,512]{1,0:T(8,128)(2,1)S(1)} %copy-done.9), channel_id=1, source_target_pairs={{0,4},{1,5},{2,6},{3,7},{4,0},{5,1},{6,2},{7,3},{8,12},{9,13},{10,... | collective-permute-start | bytes 393224 | tf_op jit(solution)/shard_map/ppermute | solution.py:356
  29.0 7.2 %collective-permute-start.3 = (bf16[128,512]{1,0:T(8,128)(2,1)S(1)}, bf16[128,512]{1,0:T(8,128)(2,1)S(1)}, u32[]{:S(2)}, u32[]{:S(2)}) collective-permute-start(bf16[128,512]{1,0:T(8,128)(2,1)S(1)} %copy-done.9), channel_id=1, source_target_pairs={{0,2},{1,3},{2,4},{3,5},{4,6},{5,7},{6,0},{7,1},{8,10},{9,11},{10,... | collective-permute-start | bytes 393224 | tf_op jit(solution)/shard_map/ppermute | solution.py:356
  36.3 11.5 %collective-permute-start.7 = (bf16[4,128,512]{2,1,0:T(8,128)(2,1)S(1)}, bf16[4,128,512]{2,1,0:T(8,128)(2,1)S(1)}, u32[]{:S(2)}, u32[]{:S(2)}) collective-permute-start(bf16[4,128,512]{2,1,0:T(8,128)(2,1)S(1)} %pad_maximum_fusion.near_in), channel_id=1, source_target_pairs={{0,1},{1,0},{2,3},{3,2},{4,5},{5,4},{6,7},{7,6},{8,9},{9,8},{10,11... | collective-permute-start | bytes 1572872 | tf_op jit(solution)/shard_map/ppermute | solution.py:360
  41.8 6.0 %collective-permute-start.6 = (bf16[8,16,896]{2,1,0:T(8,128)(2,1)S(1)}, bf16[8,16,896]{2,1,0:T(8,128)(2,1)S(1)}, u32[]{:S(2)}, u32[]{:S(2)}) collective-permute-start(bf16[8,16,896]{2,1,0:T(8,128)(2,1)S(1)} %get-tuple-element.30.refs_0_), channel_id=1, source_target_pairs={{0,1},{1,0},{2,3},{3,2},{4,5},{5,4},{6,7},{7,6},{8,9},{9,8},{10,11... | collective-permute-start | bytes 688136 | tf_op jit(solution)/shard_map/ppermute | solution.py:360
  41.9 12.2 %collective-permute-start = (bf16[8,16,896]{2,1,0:T(8,128)(2,1)S(1)}, bf16[8,16,896]{2,1,0:T(8,128)(2,1)S(1)}, u32[]{:S(2)}, u32[]{:S(2)}) collective-permute-start(bf16[8,16,896]{2,1,0:T(8,128)(2,1)S(1)} %get-tuple-element.30.refs_0_), channel_id=1, source_target_pairs={{0,2},{1,3},{2,4},{3,5},{4,6},{5,7},{6,0},{7,1},{8,10},{9,11},{10,... | collective-permute-start | bytes 688136 | tf_op jit(solution)/shard_map/ppermute | solution.py:356
  43.5 10.6 %collective-permute-start.1 = (bf16[8,16,896]{2,1,0:T(8,128)(2,1)S(1)}, bf16[8,16,896]{2,1,0:T(8,128)(2,1)S(1)}, u32[]{:S(2)}, u32[]{:S(2)}) collective-permute-start(bf16[8,16,896]{2,1,0:T(8,128)(2,1)S(1)} %get-tuple-element.30.refs_0_), channel_id=1, source_target_pairs={{0,6},{1,7},{2,0},{3,1},{4,2},{5,3},{6,4},{7,5},{8,14},{9,15},{10,... | collective-permute-start | bytes 688136 | tf_op jit(solution)/shard_map/ppermute | solution.py:356
  45.2 12.1 %collective-permute-start.2 = (bf16[8,16,896]{2,1,0:T(8,128)(2,1)S(1)}, bf16[8,16,896]{2,1,0:T(8,128)(2,1)S(1)}, u32[]{:S(2)}, u32[]{:S(2)}) collective-permute-start(bf16[8,16,896]{2,1,0:T(8,128)(2,1)S(1)} %get-tuple-element.30.refs_0_), channel_id=1, source_target_pairs={{0,4},{1,5},{2,6},{3,7},{4,0},{5,1},{6,2},{7,3},{8,12},{9,13},{10,... | collective-permute-start | bytes 688136 | tf_op jit(solution)/shard_map/ppermute | solution.py:356
  57.3 4.0 %collective-permute-start.9 = (bf16[8,16,896]{2,1,0:T(8,128)(2,1)S(1)}, bf16[8,16,896]{2,1,0:T(8,128)(2,1)S(1)}, u32[]{:S(2)}, u32[]{:S(2)}) collective-permute-start(bf16[8,16,896]{2,1,0:T(8,128)(2,1)S(1)} %collective-permute-done.1.refs_2_), channel_id=1, source_target_pairs={{0,1},{1,0},{2,3},{3,2},{4,5},{5,4},{6,7},{7,6},{8,9},{9,8},{10,11... | collective-permute-start | bytes 688136 | tf_op jit(solution)/shard_map/ppermute | solution.py:360
  57.8 10.9 %collective-permute-start.11 = (bf16[8,16,896]{2,1,0:T(8,128)(2,1)S(1)}, bf16[8,16,896]{2,1,0:T(8,128)(2,1)S(1)}, u32[]{:S(2)}, u32[]{:S(2)}) collective-permute-start(bf16[8,16,896]{2,1,0:T(8,128)(2,1)S(1)} %get-tuple-element.41.refs_0_), channel_id=1, source_target_pairs={{0,2},{1,3},{2,4},{3,5},{4,6},{5,7},{6,0},{7,1},{8,10},{9,11},{10,... | collective-permute-start | bytes 688136 | tf_op jit(solution)/shard_map/ppermute | solution.py:356
  58.9 12.3 %collective-permute-start.12 = (bf16[8,16,896]{2,1,0:T(8,128)(2,1)S(1)}, bf16[8,16,896]{2,1,0:T(8,128)(2,1)S(1)}, u32[]{:S(2)}, u32[]{:S(2)}) collective-permute-start(bf16[8,16,896]{2,1,0:T(8,128)(2,1)S(1)} %get-tuple-element.41.refs_0_), channel_id=1, source_target_pairs={{0,6},{1,7},{2,0},{3,1},{4,2},{5,3},{6,4},{7,5},{8,14},{9,15},{10,... | collective-permute-start | bytes 688136 | tf_op jit(solution)/shard_map/ppermute | solution.py:356
  61.0 11.0 %collective-permute-start.13 = (bf16[8,16,896]{2,1,0:T(8,128)(2,1)S(1)}, bf16[8,16,896]{2,1,0:T(8,128)(2,1)S(1)}, u32[]{:S(2)}, u32[]{:S(2)}) collective-permute-start(bf16[8,16,896]{2,1,0:T(8,128)(2,1)S(1)} %get-tuple-element.41.refs_0_), channel_id=1, source_target_pairs={{0,4},{1,5},{2,6},{3,7},{4,0},{5,1},{6,2},{7,3},{8,12},{9,13},{10,... | collective-permute-start | bytes 688136 | tf_op jit(solution)/shard_map/ppermute | solution.py:356
  72.0 24.5 %all-to-all-start.2 = ((bf16[16,80,512]{2,1,0:T(8,128)(2,1)}), bf16[16,80,512]{2,1,0:T(8,128)(2,1)S(1)}, u32[]{:S(2)}, u32[]{:S(2)}) async-start(bf16[16,80,512]{2,1,0:T(8,128)(2,1)} %get-tuple-element.49.refs_0_), calls=%async_computation.2 | async-start | bytes 2621440 | tf_op jit(solution)/shard_map/all_to_all | solution.py:369
  97.7 40.3 %all-to-all-start.3 = ((bf16[16,176,512]{2,1,0:T(8,128)(2,1)}), bf16[16,176,512]{2,1,0:T(8,128)(2,1)S(1)}, u32[]{:S(2)}, u32[]{:S(2)}) async-start(bf16[16,176,512]{2,1,0:T(8,128)(2,1)} %get-tuple-element.50.refs_1_), calls=%async_computation.3 | async-start | bytes 5767168 | tf_op jit(solution)/shard_map/all_to_all | solution.py:369
  106.5 4.0 %collective-permute-start.18 = (bf16[4,128,512]{2,1,0:T(8,128)(2,1)}, bf16[4,128,512]{2,1,0:T(8,128)(2,1)S(1)}, u32[]{:S(2)}, u32[]{:S(2)}) collective-permute-start(bf16[4,128,512]{2,1,0:T(8,128)(2,1)} %get-tuple-element.47), channel_id=1, source_target_pairs={{0,1},{1,0},{2,3},{3,2},{4,5},{5,4},{6,7},{7,6},{8,9},{9,8},{10,11... | collective-permute-start | bytes 1572872 | tf_op jit(solution)/shard_map/ppermute | solution.py:360
  107.5 8.2 %collective-permute-start.24 = (bf16[16,16,256]{2,1,0:T(8,128)(2,1)S(1)}, bf16[16,16,256]{2,1,0:T(8,128)(2,1)S(1)}, u32[]{:S(2)}, u32[]{:S(2)}) collective-permute-start(bf16[16,16,256]{2,1,0:T(8,128)(2,1)S(1)} %get-tuple-element.56), channel_id=1, source_target_pairs={{0,6},{1,7},{2,0},{3,1},{4,2},{5,3},{6,4},{7,5},{8,14},{9,15},{10,... | collective-permute-start | bytes 393224 | tf_op jit(solution)/shard_map/ppermute | solution.py:356
  109.4 7.9 %collective-permute-start.23 = (bf16[16,16,256]{2,1,0:T(8,128)(2,1)S(1)}, bf16[16,16,256]{2,1,0:T(8,128)(2,1)S(1)}, u32[]{:S(2)}, u32[]{:S(2)}) collective-permute-start(bf16[16,16,256]{2,1,0:T(8,128)(2,1)S(1)} %get-tuple-element.56), channel_id=1, source_target_pairs={{0,4},{1,5},{2,6},{3,7},{4,0},{5,1},{6,2},{7,3},{8,12},{9,13},{10,... | collective-permute-start | bytes 393224 | tf_op jit(solution)/shard_map/ppermute | solution.py:356
  110.4 8.9 %collective-permute-start.22 = (bf16[16,16,256]{2,1,0:T(8,128)(2,1)S(1)}, bf16[16,16,256]{2,1,0:T(8,128)(2,1)S(1)}, u32[]{:S(2)}, u32[]{:S(2)}) collective-permute-start(bf16[16,16,256]{2,1,0:T(8,128)(2,1)S(1)} %get-tuple-element.56), channel_id=1, source_target_pairs={{0,2},{1,3},{2,4},{3,5},{4,6},{5,7},{6,0},{7,1},{8,10},{9,11},{10,... | collective-permute-start | bytes 393224 | tf_op jit(solution)/shard_map/ppermute | solution.py:356
  119.5 11.1 %collective-permute-start.25 = (bf16[4,16,16,256]{3,2,1,0:T(8,128)(2,1)S(1)}, bf16[4,16,16,256]{3,2,1,0:T(8,128)(2,1)S(1)}, u32[]{:S(2)}, u32[]{:S(2)}) collective-permute-start(bf16[4,16,16,256]{3,2,1,0:T(8,128)(2,1)S(1)} %pad_maximum_fusion.1.near_ref), channel_id=1, source_target_pairs={{0,1},{1,0},{2,3},{3,2},{4,5},{5,4},{6,7},{7,6},{8,9},{9,8},{10,11... | collective-permute-start | bytes 1572872 | tf_op jit(solution)/shard_map/ppermute | solution.py:360
  119.6 7.9 %collective-permute-start.21 = (bf16[128,512]{1,0:T(8,128)(2,1)S(1)}, bf16[128,512]{1,0:T(8,128)(2,1)S(1)}, u32[]{:S(2)}, u32[]{:S(2)}) collective-permute-start(bf16[128,512]{1,0:T(8,128)(2,1)S(1)} %get-tuple-element.58), channel_id=1, source_target_pairs={{0,4},{1,5},{2,6},{3,7},{4,0},{5,1},{6,2},{7,3},{8,12},{9,13},{10,... | collective-permute-start | bytes 393224 | tf_op jit(solution)/shard_map/ppermute | solution.py:356
  120.7 7.1 %collective-permute-start.20 = (bf16[128,512]{1,0:T(8,128)(2,1)S(1)}, bf16[128,512]{1,0:T(8,128)(2,1)S(1)}, u32[]{:S(2)}, u32[]{:S(2)}) collective-permute-start(bf16[128,512]{1,0:T(8,128)(2,1)S(1)} %get-tuple-element.59), channel_id=1, source_target_pairs={{0,6},{1,7},{2,0},{3,1},{4,2},{5,3},{6,4},{7,5},{8,14},{9,15},{10,... | collective-permute-start | bytes 393224 | tf_op jit(solution)/shard_map/ppermute | solution.py:356
  121.8 8.0 %collective-permute-start.19 = (bf16[128,512]{1,0:T(8,128)(2,1)S(1)}, bf16[128,512]{1,0:T(8,128)(2,1)S(1)}, u32[]{:S(2)}, u32[]{:S(2)}) collective-permute-start(bf16[128,512]{1,0:T(8,128)(2,1)S(1)} %get-tuple-element.57), channel_id=1, source_target_pairs={{0,2},{1,3},{2,4},{3,5},{4,6},{5,7},{6,0},{7,1},{8,10},{9,11},{10,... | collective-permute-start | bytes 393224 | tf_op jit(solution)/shard_map/ppermute | solution.py:356
  (31 other events, 178.9 us)

commit v9 on v8

--- a/solution.py
+++ b/solution.py
@@ -174,19 +174,20 @@
     )(at, *operands)
 
 
-def attn_kernel(count_ref, *refs, c, pieces, last):
+def attn_kernel(count_ref, *refs, c, pieces, front, rear):
     x_in, refs = refs[:pieces], refs[pieces:]
-    more = 7 if last else 4
+    last = front and rear
+    more = 7 if last else 4 if front else 3
     ins, refs = refs[:more], refs[more:]
-    outs = 2 if last else 3
-    (send_ref, *keep_outs), refs = refs[:outs], refs[outs:]
+    outs = 1 if rear and not front else 2
+    results, refs = refs[:outs], refs[outs:]
     x_ref, mixed_ref, t_ref, u_ref, qt_ref, dt_ref, wv_ref, *refs = refs
     sem = refs[-1]
+    send_ref = results[0]
     slots, sub, enc = x_in[0].shape
     qt_in, dt_in, wv_in = ins[:3]
     part, width = mixed_ref.shape
     heads = width // HD
-    db_count = send_ref.shape[0]
     used = 0
 
     def start(pairs):
@@ -200,12 +201,14 @@
         + [(x_in[p], x_ref.at[pl.ds(p * slots, slots)]) for p in range(pieces)]
     )
     wait_all(x_loads)
-    wv_loads = start(row_blocks(wv_in, wv_ref, 2))
-    dt_loads = start([(dt_in.at[c], dt_ref)])
+    if front:
+        wv_loads = start(row_blocks(wv_in, wv_ref, 2))
+    if rear:
+        dt_loads = start([(dt_in.at[c], dt_ref)])
     if last:
         q_ref, dm_ref, t0_ref, u0_ref, gw_ref = refs[:5]
         last_loads = start(list(zip(ins[3:], (q_ref, dm_ref, t0_ref, u0_ref))))
-    else:
+    elif front:
         gs_ref = refs[0]
         gs_loads = start([(ins[3], gs_ref)])
     factor = 1.0 / math.sqrt(HD)
@@ -215,22 +218,26 @@
     slot = (lax.broadcasted_iota(jnp.int32, (1, keys), 1) // sub) % slots
     expo = jnp.where(slot < count_ref[c], jnp.exp(s), 0.0)
     probs = expo / jnp.sum(expo, axis=-1, keepdims=True)
-    t_ref[...] = mm(probs.astype(BF), x, 1, 0).astype(BF)
-    wait_all(wv_loads)
-    for h in range(heads):
-        cols = slice(h * HD, (h + 1) * HD)
-        mixed_ref[:, cols] = mm(t_ref[h * part : (h + 1) * part], wv_ref[:, cols], 1, 0).astype(BF)
-    stores = start([(mixed_ref, send_ref.at[i, pl.ds(0, part)]) for i in range(db_count)])
-    if not last:
+    stores = []
+    if front:
+        db_count = send_ref.shape[0]
+        t_ref[...] = mm(probs.astype(BF), x, 1, 0).astype(BF)
+        wait_all(wv_loads)
+        for h in range(heads):
+            cols = slice(h * HD, (h + 1) * HD)
+            mixed_ref[:, cols] = mm(t_ref[h * part : (h + 1) * part], wv_ref[:, cols], 1, 0).astype(BF)
+        stores = start([(mixed_ref, send_ref.at[i, pl.ds(0, part)]) for i in range(db_count)])
+    if front and not rear:
         wait_all(gs_loads)
         tail = pl.ds(part, gs_ref.shape[1])
-        stores += start([(t_ref, keep_outs[1]), (gs_ref, send_ref.at[:, tail])])
-    wait_all(dt_loads)
-    d = mm(dt_ref[...], x, 1, 1)
-    inner = jnp.sum(probs * d, axis=-1, keepdims=True)
-    ds = (probs * (d - inner) * factor).astype(BF)
-    u_ref[...] = mm(ds, x, 1, 0).astype(BF)
-    stores += start([(u_ref, keep_outs[0])])
+        stores += start([(t_ref, results[1]), (gs_ref, send_ref.at[:, tail])])
+    if rear:
+        wait_all(dt_loads)
+        d = mm(dt_ref[...], x, 1, 1)
+        inner = jnp.sum(probs * d, axis=-1, keepdims=True)
+        ds = (probs * (d - inner) * factor).astype(BF)
+        u_ref[...] = mm(ds, x, 1, 0).astype(BF)
+        stores += start([(u_ref, results[-1])])
     if last:
         wait_all(last_loads)
         share = enc // db_count
@@ -251,29 +258,28 @@
     wait_all(stores)
 
 
-def attn(count, xs, qt, dt, wv, c, db_count, extra, last):
+def attn(count, xs, qt, dt, wv, c, db_count, extra, front=True, rear=True):
     slots, sub, enc = xs[0].shape
     width = wv.shape[1]
     tall = qt.shape[1:]
     part = tall[0] * HD // width
-    grown = 2 * enc // db_count if last else extra[0].shape[1]
-    made = [(db_count, part + grown, width), tall]
+    last = front and rear
     more = list(extra)
+    grown = 2 * enc // db_count if last else more[0].shape[1] if front else 0
+    made = [(db_count, part + grown, width), tall] if front else [tall]
     held = [(len(xs) * slots, sub, enc), (part, width), tall, tall, tall, tall, wv.shape]
     held += [v.shape for v in more]
     copies = len(xs) + 8 + len(more) + db_count + width // HD
     if last:
         held += [(db_count, grown, width)]
-    else:
-        made += [tall]
-    return pl.pallas_call(
-        functools.partial(attn_kernel, c=c, pieces=len(xs), last=last),
+    return pl.pallas_call(
+        functools.partial(attn_kernel, c=c, pieces=len(xs), front=front, rear=rear),
         out_shape=[jax.ShapeDtypeStruct(shape, BF) for shape in made],
         in_specs=[SM] + [HBM] * (len(xs) + 3 + len(more)),
         out_specs=[HBM] * len(made),
         scratch_shapes=[pltpu.VMEM(shape, BF) for shape in held] + [pltpu.SemaphoreType.DMA((copies,))],
         compiler_params=params(),
-        cost_estimate=pl.CostEstimate(flops=3_000_000_000, bytes_accessed=8_000_000, transcendentals=262144),
+        cost_estimate=pl.CostEstimate(flops=100_000, bytes_accessed=100_000, transcendentals=0),
     )(count, *xs, qt, dt, wv, *more)
 
 
@@ -412,22 +418,29 @@
     dm, dt, grad_cols = prep(at, near, far, w_out, w_value, groups, db_count)
     ring = []
     for c in range(groups):
-        held = mine[c] if c == 0 else after(mine[c], *ring[-1])
+        held = mine[c] if c == 0 else after(mine[c], *ring[-1][1:-1])
         came = [along(held, s, head_count) for s in steps]
         if c == 0:
-            came = lax.optimization_barrier((*came, dm))[:-1]
+            came = [after(v, dm) for v in came]
         ring.append([held, *came])
     spread = []
     for c, pieces in enumerate(ring):
         spread.append([*pieces, crossed[c], *(swap(v, head_count) for v in pieces[1:])])
     sent, sends, us = [], [], []
-    extra = (grad_cols,)
+    extra = ()
     for c in range(groups):
-        m, u, *t = attn(nbr_count, spread[c], qt, dt, w_value, c, db_count, extra, c == groups - 1)
+        if c == groups - 1:
+            m, u = attn(nbr_count, spread[c], qt, dt, w_value, c, db_count, extra)
+            m = after(m, *sent)
+        else:
+            m, t = attn(nbr_count, spread[c], qt, dt, w_value, c, db_count, (grad_cols,), rear=False)
+            m = after(m, *ring[c + 1])
+            held = lax.optimization_barrier((*spread[c], m))[:-1]
+            (u,) = attn(nbr_count, held, qt, dt, w_value, c, db_count, (), front=False)
+            extra = (queries, dm, t, u)
         us.append(u)
         sends.append(m)
-        sent.append(exchange(after(m, *(ring[-1] if c == 0 else sent)), "db"))
-        extra = (queries, dm, *t, u)
+        sent.append(exchange(m, "db"))
     share = tok_rows // head_count
     piece = width * head_count // db_count
     rows_near = chips_stack(sent[0][:, part : part + share, :piece], steps, head_count)

time: 141 us -> 144 us (1.021)
  waiting for transfers between devices: 49.2 us -> 36.6 us
  starting transfers between devices: 40.6 us -> 48.9 us
  Pallas kernels: 35.6 us -> 40.6 us
    ppermute x15, waiting for transfers between devices: 27.6 us -> 19 us  [along(): lax.ppermute(v, 'head', [(i, (i // 2 + step) % chips * 2 + i % 2) for i i...]
    ppermute x15, starting transfers between devices: 19.5 us -> 27.7 us  [along(): lax.ppermute(v, 'head', [(i, (i // 2 + step) % chips * 2 + i % 2) for i i...]
    pallas_call x2 -> x3, Pallas kernels: 14.6 us -> 19.4 us  [attn(): pl.pallas_call(functools.partial(attn_kernel, c=c, pieces=len(xs), front=...]
    all_to_all x4, waiting for transfers between devices: 20.1 us -> 17.5 us  [exchange(): return lax.all_to_all(x, axis, split_axis=0, concat_axis=0, tiled=True)]
  transfers between devices with their start and end apart: 30 -> 30, of which waited for: 20 -> 14; matrix products, arithmetic and copies ran while one was open for 4% -> 5% of each run, Pallas kernels for 23% -> 26%
where the time goes in v9:
time: 144 us; the launch traced here: 143 us
  starting transfers between devices  48.9 us (34%)
  Pallas kernels  40.6 us (28%)
  waiting for transfers between devices  36.6 us (25%)
  local copies, waits for them, and re-layouts  7.7 us (5%)
  other arithmetic  5.46 us (4%)
  matrix products  3.1 us (2%)
    ppermute x15, starting transfers between devices, along(): lax.ppermute(v, 'head', [(i, (i // 2 + step) % chips * 2 + i % 2) for i i...  27.7 us
    pallas_call x3, Pallas kernels, attn(): pl.pallas_call(functools.partial(attn_kernel, c=c, pieces=len(xs), front=...  19.4 us
    all_to_all x4, starting transfers between devices, exchange(): return lax.all_to_all(x, axis, split_axis=0, concat_axis=0, tiled=True)  19.2 us
    ppermute x15, waiting for transfers between devices, along(): lax.ppermute(v, 'head', [(i, (i // 2 + step) % chips * 2 + i % 2) for i i...  19 us
    all_to_all x4, waiting for transfers between devices, exchange(): return lax.all_to_all(x, axis, split_axis=0, concat_axis=0, tiled=True)  17.5 us
    pallas_call x2, Pallas kernels, pick(): pl.pallas_call(functools.partial(pick_kernel, row_of=row_of, count=total)...  5.62 us
    pallas_call x1, Pallas kernels, prep(): pl.pallas_call(prep_kernel, out_shape=[jax.ShapeDtypeStruct(shape, BF) fo...  5.39 us
    unnamed x50, local copies, waits for them, and re-layouts  5.34 us
  transfers between devices with their start and end apart: 30, of which 14 were waited for; matrix products, arithmetic and copies ran while one was open for 5% of the time, Pallas kernels for 26%

profile of v9, /device:TPU:0, one launch (start us, length us, event | category | flops | bytes accessed | tf_op | source)
XLA Modules:
  0.0 143.4 jit_solution(2614384458235619699)
XLA Ops:
  2.1 8.0 %all-to-all-start = ((s32[16,1,2]{2,1,0:T(1,128)}), s32[16,1,2]{2,1,0:T(1,128)S(1)}, u32[]{:S(2)}, u32[]{:S(2)}) async-start(s32[16,1,2]{2,1,0:T(1,128)} %copy.17), calls=%async_computation | async-start | bytes 16384 | tf_op jit(solution)/shard_map/all_to_all | solution.py:375
  10.1 2.8 %shard_map.128.refs_8_ = bf16[2,256,896]{2,1,0:T(8,128)(2,1)} custom-call(bf16[128,512]{1,0:T(8,128)(2,1)} %refs_11_.1, bf16[896,512]{1,0:T(8,128)(2,1)} %refs_5_.1), custom_call_target="tpu_custom_call" | custom-call | flops 120000000 | bytes 2000000 | tf_op jit(solution)/shard_map/pallas_call | solution.py:105
  12.8 4.7 %all-to-all-done.rows_ref = s32[16,1,2]{2,1,0:T(1,128)S(1)} async-done(((s32[16,1,2]{2,1,0:T(1,128)}), s32[16,1,2]{2,1,0:T(1,128)S(1)}, u32[]{:S(2)}, u32[]{:S(2)}) %all-to-all-start) | async-done | bytes 160 | tf_op jit(solution)/shard_map/all_to_all | solution.py:375
  18.1 3.6 %shard_map.129 = bf16[32,16,896]{2,1,0:T(8,128)(2,1)} custom-call(s32[16,1,2]{2,1,0:T(1,128)} %copy-done.24, bf16[64,16,896]{2,1,0:T(8,128)(2,1)} %src_ref.1), custom_call_target="tpu_custom_call" | custom-call | tf_op jit(solution)/shard_map/pallas_call | solution.py:55
  21.8 3.6 %all-to-all-start.1 = ((bf16[32,16,896]{2,1,0:T(8,128)(2,1)}), bf16[32,16,896]{2,1,0:T(8,128)(2,1)S(1)}, u32[]{:S(2)}, u32[]{:S(2)}) async-start(bf16[32,16,896]{2,1,0:T(8,128)(2,1)} %shard_map.129), calls=%async_computation.1 | async-start | bytes 1835008 | tf_op jit(solution)/shard_map/all_to_all | solution.py:375
  25.5 3.1 %collective-permute-start.3 = (bf16[128,512]{1,0:T(8,128)(2,1)S(1)}, bf16[128,512]{1,0:T(8,128)(2,1)S(1)}, u32[]{:S(2)}, u32[]{:S(2)}) collective-permute-start(bf16[128,512]{1,0:T(8,128)(2,1)S(1)} %copy-done.23), channel_id=1, source_target_pairs={{0,6},{1,7},{2,0},{3,1},{4,2},{5,3},{6,4},{7,5},{8,14},{9,15},{10,... | collective-permute-start | bytes 393224 | tf_op jit(solution)/shard_map/ppermute | solution.py:362
  30.1 2.7 %collective-permute-done.3 = bf16[128,512]{1,0:T(8,128)(2,1)S(1)} collective-permute-done((bf16[128,512]{1,0:T(8,128)(2,1)S(1)}, bf16[128,512]{1,0:T(8,128)(2,1)S(1)}, u32[]{:S(2)}, u32[]{:S(2)}) %collective-permute-start.3) | collective-permute-done | bytes 131104 | tf_op jit(solution)/shard_map/ppermute | solution.py:362
  36.6 3.4 %all-to-all-done.1.src_ref = bf16[32,16,896]{2,1,0:T(8,128)(2,1)S(1)} async-done(((bf16[32,16,896]{2,1,0:T(8,128)(2,1)}), bf16[32,16,896]{2,1,0:T(8,128)(2,1)S(1)}, u32[]{:S(2)}, u32[]{:S(2)}) %all-to-all-start.1) | async-done | bytes 917536 | tf_op jit(solution)/shard_map/all_to_all | solution.py:375
  44.4 2.9 %collective-permute-start.7 = (bf16[8,16,896]{2,1,0:T(8,128)(2,1)S(1)}, bf16[8,16,896]{2,1,0:T(8,128)(2,1)S(1)}, u32[]{:S(2)}, u32[]{:S(2)}) collective-permute-start(bf16[8,16,896]{2,1,0:T(8,128)(2,1)S(1)} %get-tuple-element.51.refs_0_), channel_id=1, source_target_pairs={{0,4},{1,5},{2,6},{3,7},{4,0},{5,1},{6,2},{7,3},{8,12},{9,13},{10,... | collective-permute-start | bytes 688136 | tf_op jit(solution)/shard_map/ppermute | solution.py:362
  49.5 5.4 %shard_map.131 = (bf16[128,512]{1,0:T(8,128)(2,1)}, bf16[2,256,896]{2,1,0:T(8,128)(2,1)}, bf16[16,16,512]{2,1,0:T(8,128)(2,1)}) custom-call(s32[2]{0:T(128)} %pad_add_fusion.at_ref, bf16[4,128,512]{2,1,0:T(8,128)(2,1)} %copy-done.3, bf16[4,128,512]{2,1,0:T(8,128)(2,1)} %copy-done.14, bf16[512,4096]{1,0:T(8,128)(2,1)} %refs_4_.1, bf16[896,512]{1,0:T(8,128)(2,1)} %refs_10_.5), custom_call_target="tpu_custom_call" | custom-call | flops 700000000 | bytes 8000000 | tf_op jit(solution)/shard_map/pallas_call | solution.py:162
  58.1 3.2 %collective-permute-start.13 = (bf16[8,16,896]{2,1,0:T(8,128)(2,1)S(1)}, bf16[8,16,896]{2,1,0:T(8,128)(2,1)S(1)}, u32[]{:S(2)}, u32[]{:S(2)}) collective-permute-start(bf16[8,16,896]{2,1,0:T(8,128)(2,1)S(1)} %get-tuple-element.48.refs_0_), channel_id=1, source_target_pairs={{0,4},{1,5},{2,6},{3,7},{4,0},{5,1},{6,2},{7,3},{8,12},{9,13},{10,... | collective-permute-start | bytes 688136 | tf_op jit(solution)/shard_map/ppermute | solution.py:362
  64.0 5.6 %shard_map.132 = (bf16[16,80,512]{2,1,0:T(8,128)(2,1)}, bf16[256,896]{1,0:T(8,128)(2,1)}) custom-call(s32[2]{0:T(128)} %count_ref.5, bf16[8,16,896]{2,1,0:T(8,128)(2,1)} %copy-done, bf16[8,16,896]{2,1,0:T(8,128)(2,1)} %copy-done.8, bf16[8,16,896]{2,1,0:T(8,128)(2,1)} %copy-done.10, bf16[8,16,896]{2,1,0:T(8,128)(2,1)} %copy-done.9, ...), custom_call_target="tpu_custom_call" | custom-call | flops 100000 | bytes 100000 | tf_op jit(solution)/shard_map/pallas_call | solution.py:275
  72.8 3.9 %all-to-all-start.2 = ((bf16[16,80,512]{2,1,0:T(8,128)(2,1)}), bf16[16,80,512]{2,1,0:T(8,128)(2,1)S(1)}, u32[]{:S(2)}, u32[]{:S(2)}) async-start(bf16[16,80,512]{2,1,0:T(8,128)(2,1)} %get-tuple-element.49.refs_0_), calls=%async_computation.2 | async-start | bytes 2621440 | tf_op jit(solution)/shard_map/all_to_all | solution.py:375
  77.8 5.9 %shard_map.133.refs_14_.refs_2_ = bf16[256,896]{1,0:T(8,128)(2,1)} custom-call(s32[2]{0:T(128)} %count_ref.5, bf16[8,16,896]{2,1,0:T(8,128)(2,1)} %copy-done, bf16[8,16,896]{2,1,0:T(8,128)(2,1)} %copy-done.8, bf16[8,16,896]{2,1,0:T(8,128)(2,1)} %copy-done.10, bf16[8,16,896]{2,1,0:T(8,128)(2,1)} %copy-done.9, bf16[8,16,896]{2,1,0:T(8,128)(2,1)} %copy-done.7, ...), custom_call_target="tpu_custom_call" | custom-call | flops 100000 | bytes 100000 | tf_op jit(solution)/shard_map/pallas_call | solution.py:275
  84.7 8.0 %shard_map.134 = (bf16[16,176,512]{2,1,0:T(8,128)(2,1)}, bf16[256,896]{1,0:T(8,128)(2,1)}) custom-call(s32[2]{0:T(128)} %count_ref.5, bf16[8,16,896]{2,1,0:T(8,128)(2,1)} %copy-done.1, bf16[8,16,896]{2,1,0:T(8,128)(2,1)} %copy-done.17, bf16[8,16,896]{2,1,0:T(8,128)(2,1)} %copy-done.16, bf16[8,16,896]{2,1,0:T(8,128)(2,1)} %copy-done.15, ...), custom_call_target="tpu_custom_call" | custom-call | flops 100000 | bytes 100000 | tf_op jit(solution)/shard_map/pallas_call | solution.py:275
  92.7 4.7 %all-to-all-done.2 = bf16[16,80,512]{2,1,0:T(8,128)(2,1)S(1)} async-done(((bf16[16,80,512]{2,1,0:T(8,128)(2,1)}), bf16[16,80,512]{2,1,0:T(8,128)(2,1)S(1)}, u32[]{:S(2)}, u32[]{:S(2)}) %all-to-all-start.2) | async-done | bytes 1310752 | tf_op jit(solution)/shard_map/all_to_all | solution.py:375
  98.5 3.7 %all-to-all-start.3 = ((bf16[16,176,512]{2,1,0:T(8,128)(2,1)}), bf16[16,176,512]{2,1,0:T(8,128)(2,1)S(1)}, u32[]{:S(2)}, u32[]{:S(2)}) async-start(bf16[16,176,512]{2,1,0:T(8,128)(2,1)} %get-tuple-element.60.refs_1_), calls=%async_computation.3 | async-start | bytes 5767168 | tf_op jit(solution)/shard_map/all_to_all | solution.py:375
  102.2 5.1 %shard_map.135 = (bf16[4,128,512]{2,1,0:T(8,128)(2,1)}, bf16[4,128,512]{2,1,0:T(8,128)(2,1)}, bf16[128,512]{1,0:T(8,128)(2,1)}) custom-call(s32[2]{0:T(128)} %pad_add_fusion.at_ref, bf16[16,80,512]{2,1,0:T(8,128)(2,1)} %get-tuple-element.49.refs_0_, bf16[16,176,512]{2,1,0:T(8,128)(2,1)} %get-tuple-element.60.refs_1_, ...), custom_call_target="tpu_custom_call" | custom-call | flops 700000000 | bytes 8000000 | tf_op jit(solution)/shard_map/pallas_call | solution.py:318
  108.4 3.7 %collective-permute-start.23 = (bf16[16,16,256]{2,1,0:T(8,128)(2,1)S(1)}, bf16[16,16,256]{2,1,0:T(8,128)(2,1)S(1)}, u32[]{:S(2)}, u32[]{:S(2)}) collective-permute-start(bf16[16,16,256]{2,1,0:T(8,128)(2,1)S(1)} %get-tuple-element.70), channel_id=1, source_target_pairs={{0,4},{1,5},{2,6},{3,7},{4,0},{5,1},{6,2},{7,3},{8,12},{9,13},{10,... | collective-permute-start | bytes 393224 | tf_op jit(solution)/shard_map/ppermute | solution.py:362
  112.3 2.9 %collective-permute-start.24 = (bf16[16,16,256]{2,1,0:T(8,128)(2,1)S(1)}, bf16[16,16,256]{2,1,0:T(8,128)(2,1)S(1)}, u32[]{:S(2)}, u32[]{:S(2)}) collective-permute-start(bf16[16,16,256]{2,1,0:T(8,128)(2,1)S(1)} %get-tuple-element.70), channel_id=1, source_target_pairs={{0,6},{1,7},{2,0},{3,1},{4,2},{5,3},{6,4},{7,5},{8,14},{9,15},{10,... | collective-permute-start | bytes 393224 | tf_op jit(solution)/shard_map/ppermute | solution.py:362
  116.4 2.6 %collective-permute-done.22 = bf16[16,16,256]{2,1,0:T(8,128)(2,1)S(1)} collective-permute-done((bf16[16,16,256]{2,1,0:T(8,128)(2,1)S(1)}, bf16[16,16,256]{2,1,0:T(8,128)(2,1)S(1)}, u32[]{:S(2)}, u32[]{:S(2)}) %collective-permute-start.22) | collective-permute-done | bytes 131104 | tf_op jit(solution)/shard_map/ppermute | solution.py:362
  123.0 2.6 %collective-permute-start.21 = (bf16[128,512]{1,0:T(8,128)(2,1)}, bf16[128,512]{1,0:T(8,128)(2,1)}, u32[]{:S(2)}, u32[]{:S(2)}) collective-permute-start(bf16[128,512]{1,0:T(8,128)(2,1)} %get-tuple-element.72), channel_id=1, source_target_pairs={{0,4},{1,5},{2,6},{3,7},{4,0},{5,1},{6,2},{7,3},{8,12},{9,13},{10,... | collective-permute-start | bytes 393224 | tf_op jit(solution)/shard_map/ppermute | solution.py:362
  128.5 4.0 %collective-permute-done.21 = bf16[128,512]{1,0:T(8,128)(2,1)} collective-permute-done((bf16[128,512]{1,0:T(8,128)(2,1)}, bf16[128,512]{1,0:T(8,128)(2,1)}, u32[]{:S(2)}, u32[]{:S(2)}) %collective-permute-start.21) | collective-permute-done | bytes 131104 | tf_op jit(solution)/shard_map/ppermute | solution.py:362
  136.1 4.8 %all-to-all-done.3 = bf16[16,176,512]{2,1,0:T(8,128)(2,1)S(1)} async-done(((bf16[16,176,512]{2,1,0:T(8,128)(2,1)}), bf16[16,176,512]{2,1,0:T(8,128)(2,1)S(1)}, u32[]{:S(2)}, u32[]{:S(2)}) %all-to-all-start.3) | async-done | bytes 2883616 | tf_op jit(solution)/shard_map/all_to_all | solution.py:375
  (107 shorter events, 41.6 us)
Async XLA Ops:
  2.1 15.5 %all-to-all-start = ((s32[16,1,2]{2,1,0:T(1,128)}), s32[16,1,2]{2,1,0:T(1,128)S(1)}, u32[]{:S(2)}, u32[]{:S(2)}) async-start(s32[16,1,2]{2,1,0:T(1,128)} %copy.17), calls=%async_computation | async-start | bytes 16384 | tf_op jit(solution)/shard_map/all_to_all | solution.py:375
  21.8 18.2 %all-to-all-start.1 = ((bf16[32,16,896]{2,1,0:T(8,128)(2,1)}), bf16[32,16,896]{2,1,0:T(8,128)(2,1)S(1)}, u32[]{:S(2)}, u32[]{:S(2)}) async-start(bf16[32,16,896]{2,1,0:T(8,128)(2,1)} %shard_map.129), calls=%async_computation.1 | async-start | bytes 1835008 | tf_op jit(solution)/shard_map/all_to_all | solution.py:375
  25.5 7.4 %collective-permute-start.3 = (bf16[128,512]{1,0:T(8,128)(2,1)S(1)}, bf16[128,512]{1,0:T(8,128)(2,1)S(1)}, u32[]{:S(2)}, u32[]{:S(2)}) collective-permute-start(bf16[128,512]{1,0:T(8,128)(2,1)S(1)} %copy-done.23), channel_id=1, source_target_pairs={{0,6},{1,7},{2,0},{3,1},{4,2},{5,3},{6,4},{7,5},{8,14},{9,15},{10,... | collective-permute-start | bytes 393224 | tf_op jit(solution)/shard_map/ppermute | solution.py:362
  29.2 7.2 %collective-permute-start.1 = (bf16[128,512]{1,0:T(8,128)(2,1)S(1)}, bf16[128,512]{1,0:T(8,128)(2,1)S(1)}, u32[]{:S(2)}, u32[]{:S(2)}) collective-permute-start(bf16[128,512]{1,0:T(8,128)(2,1)S(1)} %copy-done.23), channel_id=1, source_target_pairs={{0,2},{1,3},{2,4},{3,5},{4,6},{5,7},{6,0},{7,1},{8,10},{9,11},{10,... | collective-permute-start | bytes 393224 | tf_op jit(solution)/shard_map/ppermute | solution.py:362
  36.5 12.1 %collective-permute-start.5 = (bf16[4,128,512]{2,1,0:T(8,128)(2,1)S(1)}, bf16[4,128,512]{2,1,0:T(8,128)(2,1)S(1)}, u32[]{:S(2)}, u32[]{:S(2)}) collective-permute-start(bf16[4,128,512]{2,1,0:T(8,128)(2,1)S(1)} %pad_maximum_fusion.near_in), channel_id=1, source_target_pairs={{0,1},{1,0},{2,3},{3,2},{4,5},{5,4},{6,7},{7,6},{8,9},{9,8},{10,11... | collective-permute-start | bytes 1572872 | tf_op jit(solution)/shard_map/ppermute | solution.py:366
  42.1 12.9 %collective-permute-start = (bf16[8,16,896]{2,1,0:T(8,128)(2,1)S(1)}, bf16[8,16,896]{2,1,0:T(8,128)(2,1)S(1)}, u32[]{:S(2)}, u32[]{:S(2)}) collective-permute-start(bf16[8,16,896]{2,1,0:T(8,128)(2,1)S(1)} %get-tuple-element.51.refs_0_), channel_id=1, source_target_pairs={{0,2},{1,3},{2,4},{3,5},{4,6},{5,7},{6,0},{7,1},{8,10},{9,11},{10,... | collective-permute-start | bytes 688136 | tf_op jit(solution)/shard_map/ppermute | solution.py:362
  44.4 13.1 %collective-permute-start.7 = (bf16[8,16,896]{2,1,0:T(8,128)(2,1)S(1)}, bf16[8,16,896]{2,1,0:T(8,128)(2,1)S(1)}, u32[]{:S(2)}, u32[]{:S(2)}) collective-permute-start(bf16[8,16,896]{2,1,0:T(8,128)(2,1)S(1)} %get-tuple-element.51.refs_0_), channel_id=1, source_target_pairs={{0,4},{1,5},{2,6},{3,7},{4,0},{5,1},{6,2},{7,3},{8,12},{9,13},{10,... | collective-permute-start | bytes 688136 | tf_op jit(solution)/shard_map/ppermute | solution.py:362
  47.3 10.3 %collective-permute-start.6 = (bf16[8,16,896]{2,1,0:T(8,128)(2,1)S(1)}, bf16[8,16,896]{2,1,0:T(8,128)(2,1)S(1)}, u32[]{:S(2)}, u32[]{:S(2)}) collective-permute-start(bf16[8,16,896]{2,1,0:T(8,128)(2,1)S(1)} %get-tuple-element.51.refs_0_), channel_id=1, source_target_pairs={{0,6},{1,7},{2,0},{3,1},{4,2},{5,3},{6,4},{7,5},{8,14},{9,15},{10,... | collective-permute-start | bytes 688136 | tf_op jit(solution)/shard_map/ppermute | solution.py:362
  55.0 7.5 %collective-permute-start.8 = (bf16[8,16,896]{2,1,0:T(8,128)(2,1)S(1)}, bf16[8,16,896]{2,1,0:T(8,128)(2,1)S(1)}, u32[]{:S(2)}, u32[]{:S(2)}) collective-permute-start(bf16[8,16,896]{2,1,0:T(8,128)(2,1)S(1)} %collective-permute-done.refs_1_), channel_id=1, source_target_pairs={{0,1},{1,0},{2,3},{3,2},{4,5},{5,4},{6,7},{7,6},{8,9},{9,8},{10,11... | collective-permute-start | bytes 688136 | tf_op jit(solution)/shard_map/ppermute | solution.py:366
  58.1 11.5 %collective-permute-start.13 = (bf16[8,16,896]{2,1,0:T(8,128)(2,1)S(1)}, bf16[8,16,896]{2,1,0:T(8,128)(2,1)S(1)}, u32[]{:S(2)}, u32[]{:S(2)}) collective-permute-start(bf16[8,16,896]{2,1,0:T(8,128)(2,1)S(1)} %get-tuple-element.48.refs_0_), channel_id=1, source_target_pairs={{0,4},{1,5},{2,6},{3,7},{4,0},{5,1},{6,2},{7,3},{8,12},{9,13},{10,... | collective-permute-start | bytes 688136 | tf_op jit(solution)/shard_map/ppermute | solution.py:362
  61.2 10.8 %collective-permute-start.12 = (bf16[8,16,896]{2,1,0:T(8,128)(2,1)S(1)}, bf16[8,16,896]{2,1,0:T(8,128)(2,1)S(1)}, u32[]{:S(2)}, u32[]{:S(2)}) collective-permute-start(bf16[8,16,896]{2,1,0:T(8,128)(2,1)S(1)} %get-tuple-element.48.refs_0_), channel_id=1, source_target_pairs={{0,6},{1,7},{2,0},{3,1},{4,2},{5,3},{6,4},{7,5},{8,14},{9,15},{10,... | collective-permute-start | bytes 688136 | tf_op jit(solution)/shard_map/ppermute | solution.py:362
  62.5 9.6 %collective-permute-start.11 = (bf16[8,16,896]{2,1,0:T(8,128)(2,1)S(1)}, bf16[8,16,896]{2,1,0:T(8,128)(2,1)S(1)}, u32[]{:S(2)}, u32[]{:S(2)}) collective-permute-start(bf16[8,16,896]{2,1,0:T(8,128)(2,1)S(1)} %get-tuple-element.48.refs_0_), channel_id=1, source_target_pairs={{0,2},{1,3},{2,4},{3,5},{4,6},{5,7},{6,0},{7,1},{8,10},{9,11},{10,... | collective-permute-start | bytes 688136 | tf_op jit(solution)/shard_map/ppermute | solution.py:362
  72.8 24.6 %all-to-all-start.2 = ((bf16[16,80,512]{2,1,0:T(8,128)(2,1)}), bf16[16,80,512]{2,1,0:T(8,128)(2,1)S(1)}, u32[]{:S(2)}, u32[]{:S(2)}) async-start(bf16[16,80,512]{2,1,0:T(8,128)(2,1)} %get-tuple-element.49.refs_0_), calls=%async_computation.2 | async-start | bytes 2621440 | tf_op jit(solution)/shard_map/all_to_all | solution.py:375
  76.7 7.0 %collective-permute-start.14 = (bf16[8,16,896]{2,1,0:T(8,128)(2,1)S(1)}, bf16[8,16,896]{2,1,0:T(8,128)(2,1)S(1)}, u32[]{:S(2)}, u32[]{:S(2)}) collective-permute-start(bf16[8,16,896]{2,1,0:T(8,128)(2,1)S(1)} %get-tuple-element.48.refs_0_), channel_id=1, source_target_pairs={{0,1},{1,0},{2,3},{3,2},{4,5},{5,4},{6,7},{7,6},{8,9},{9,8},{10,11... | collective-permute-start | bytes 688136 | tf_op jit(solution)/shard_map/ppermute | solution.py:366
  76.8 6.9 %collective-permute-start.17 = (bf16[8,16,896]{2,1,0:T(8,128)(2,1)S(1)}, bf16[8,16,896]{2,1,0:T(8,128)(2,1)S(1)}, u32[]{:S(2)}, u32[]{:S(2)}) collective-permute-start(bf16[8,16,896]{2,1,0:T(8,128)(2,1)S(1)} %collective-permute-done.13.refs_3_), channel_id=1, source_target_pairs={{0,1},{1,0},{2,3},{3,2},{4,5},{5,4},{6,7},{7,6},{8,9},{9,8},{10,11... | collective-permute-start | bytes 688136 | tf_op jit(solution)/shard_map/ppermute | solution.py:366
  98.5 42.3 %all-to-all-start.3 = ((bf16[16,176,512]{2,1,0:T(8,128)(2,1)}), bf16[16,176,512]{2,1,0:T(8,128)(2,1)S(1)}, u32[]{:S(2)}, u32[]{:S(2)}) async-start(bf16[16,176,512]{2,1,0:T(8,128)(2,1)} %get-tuple-element.60.refs_1_), calls=%async_computation.3 | async-start | bytes 5767168 | tf_op jit(solution)/shard_map/all_to_all | solution.py:375
  107.3 11.9 %collective-permute-start.18 = (bf16[4,128,512]{2,1,0:T(8,128)(2,1)}, bf16[4,128,512]{2,1,0:T(8,128)(2,1)S(1)}, u32[]{:S(2)}, u32[]{:S(2)}) collective-permute-start(bf16[4,128,512]{2,1,0:T(8,128)(2,1)} %get-tuple-element.63), channel_id=1, source_target_pairs={{0,1},{1,0},{2,3},{3,2},{4,5},{5,4},{6,7},{7,6},{8,9},{9,8},{10,11... | collective-permute-start | bytes 1572872 | tf_op jit(solution)/shard_map/ppermute | solution.py:366
  108.4 8.0 %collective-permute-start.23 = (bf16[16,16,256]{2,1,0:T(8,128)(2,1)S(1)}, bf16[16,16,256]{2,1,0:T(8,128)(2,1)S(1)}, u32[]{:S(2)}, u32[]{:S(2)}) collective-permute-start(bf16[16,16,256]{2,1,0:T(8,128)(2,1)S(1)} %get-tuple-element.70), channel_id=1, source_target_pairs={{0,4},{1,5},{2,6},{3,7},{4,0},{5,1},{6,2},{7,3},{8,12},{9,13},{10,... | collective-permute-start | bytes 393224 | tf_op jit(solution)/shard_map/ppermute | solution.py:362
  112.0 7.0 %collective-permute-start.22 = (bf16[16,16,256]{2,1,0:T(8,128)(2,1)S(1)}, bf16[16,16,256]{2,1,0:T(8,128)(2,1)S(1)}, u32[]{:S(2)}, u32[]{:S(2)}) collective-permute-start(bf16[16,16,256]{2,1,0:T(8,128)(2,1)S(1)} %get-tuple-element.70), channel_id=1, source_target_pairs={{0,2},{1,3},{2,4},{3,5},{4,6},{5,7},{6,0},{7,1},{8,10},{9,11},{10,... | collective-permute-start | bytes 393224 | tf_op jit(solution)/shard_map/ppermute | solution.py:362
  112.3 6.7 %collective-permute-start.24 = (bf16[16,16,256]{2,1,0:T(8,128)(2,1)S(1)}, bf16[16,16,256]{2,1,0:T(8,128)(2,1)S(1)}, u32[]{:S(2)}, u32[]{:S(2)}) collective-permute-start(bf16[16,16,256]{2,1,0:T(8,128)(2,1)S(1)} %get-tuple-element.70), channel_id=1, source_target_pairs={{0,6},{1,7},{2,0},{3,1},{4,2},{5,3},{6,4},{7,5},{8,14},{9,15},{10,... | collective-permute-start | bytes 393224 | tf_op jit(solution)/shard_map/ppermute | solution.py:362
  119.1 7.1 %collective-permute-start.25 = (bf16[4,16,16,256]{3,2,1,0:T(8,128)(2,1)S(1)}, bf16[4,16,16,256]{3,2,1,0:T(8,128)(2,1)}, u32[]{:S(2)}, u32[]{:S(2)}) collective-permute-start(bf16[4,16,16,256]{3,2,1,0:T(8,128)(2,1)S(1)} %pad_maximum_fusion.1.near_ref), channel_id=1, source_target_pairs={{0,1},{1,0},{2,3},{3,2},{4,5},{5,4},{6,7},{7,6},{8,9},{9,8},{10,11... | collective-permute-start | bytes 1572872 | tf_op jit(solution)/shard_map/ppermute | solution.py:366
  121.2 7.3 %collective-permute-start.19 = (bf16[128,512]{1,0:T(8,128)(2,1)}, bf16[128,512]{1,0:T(8,128)(2,1)S(1)}, u32[]{:S(2)}, u32[]{:S(2)}) collective-permute-start(bf16[128,512]{1,0:T(8,128)(2,1)} %get-tuple-element.71), channel_id=1, source_target_pairs={{0,2},{1,3},{2,4},{3,5},{4,6},{5,7},{6,0},{7,1},{8,10},{9,11},{10,... | collective-permute-start | bytes 393224 | tf_op jit(solution)/shard_map/ppermute | solution.py:362
  123.0 9.6 %collective-permute-start.21 = (bf16[128,512]{1,0:T(8,128)(2,1)}, bf16[128,512]{1,0:T(8,128)(2,1)}, u32[]{:S(2)}, u32[]{:S(2)}) collective-permute-start(bf16[128,512]{1,0:T(8,128)(2,1)} %get-tuple-element.72), channel_id=1, source_target_pairs={{0,4},{1,5},{2,6},{3,7},{4,0},{5,1},{6,2},{7,3},{8,12},{9,13},{10,... | collective-permute-start | bytes 393224 | tf_op jit(solution)/shard_map/ppermute | solution.py:362
  125.6 6.9 %collective-permute-start.20 = (bf16[128,512]{1,0:T(8,128)(2,1)}, bf16[128,512]{1,0:T(8,128)(2,1)}, u32[]{:S(2)}, u32[]{:S(2)}) collective-permute-start(bf16[128,512]{1,0:T(8,128)(2,1)} %get-tuple-element.73), channel_id=1, source_target_pairs={{0,6},{1,7},{2,0},{3,1},{4,2},{5,3},{6,4},{7,5},{8,14},{9,15},{10,... | collective-permute-start | bytes 393224 | tf_op jit(solution)/shard_map/ppermute | solution.py:362
  (31 other events, 201.8 us)

commit v10 on v8

--- a/solution.py
+++ b/solution.py
@@ -119,7 +119,8 @@
     chips, rows, width = near_ref.shape
     cuts = gc_ref.shape[0] // (2 * chips)
     piece = width // cuts
-    share = gc_ref.shape[1]
+    half = gc_ref.shape[1]
+    share = 2 * half
     own = pl.ds(pl.multiple_of((at_ref[0] * 2 + at_ref[1]) * share, share), share)
     first = start_loads([(near_in, near_ref), (far_in, far_ref)], sem)
     places = []
@@ -140,8 +141,8 @@
     wait_all(first)
     for g_ref, s, j in places:
         for p in range(cuts):
-            gc_ref[j * cuts + p, :, :piece] = g_ref[s, own, p * piece : (p + 1) * piece]
-            gc_ref[j * cuts + p, :, piece:] = jnp.zeros((share, width - piece), BF)
+            rows_of = g_ref[s, own, p * piece : (p + 1) * piece]
+            gc_ref[j * cuts + p] = jnp.concatenate([rows_of[:half], rows_of[half:]], axis=1)
     stores = start_loads([(gc_ref, gc_out)], sem, used + 1)
     acc = jnp.zeros((rows, width), F32)
     for k, (g_ref, s, _) in enumerate(places):
@@ -157,7 +158,7 @@
 def prep(at, near, far, wo, wv, groups, db_count):
     chips, rows, width = near.shape
     tall = (groups, width // HD * rows // groups, wv.shape[0])
-    made = [(rows, width), tall, (db_count, rows // (2 * chips), width)]
+    made = [(rows, width), tall, (db_count, rows // (4 * chips), width)]
     operands = (near, far, wo, wv)
     return pl.pallas_call(
         prep_kernel,
@@ -206,7 +207,7 @@
         q_ref, dm_ref, t0_ref, u0_ref, gw_ref = refs[:5]
         last_loads = start(list(zip(ins[3:], (q_ref, dm_ref, t0_ref, u0_ref))))
     else:
-        gs_ref = refs[0]
+        gs_ref, whole_ref = refs[:2]
         gs_loads = start([(ins[3], gs_ref)])
     factor = 1.0 / math.sqrt(HD)
     x = x_ref[...].reshape(pieces * slots * sub, enc)
@@ -220,11 +221,15 @@
     for h in range(heads):
         cols = slice(h * HD, (h + 1) * HD)
         mixed_ref[:, cols] = mm(t_ref[h * part : (h + 1) * part], wv_ref[:, cols], 1, 0).astype(BF)
-    stores = start([(mixed_ref, send_ref.at[i, pl.ds(0, part)]) for i in range(db_count)])
-    if not last:
+    if last:
+        stores = start([(mixed_ref, send_ref.at[i, pl.ds(0, part)]) for i in range(db_count)])
+    else:
         wait_all(gs_loads)
-        tail = pl.ds(part, gs_ref.shape[1])
-        stores += start([(t_ref, keep_outs[1]), (gs_ref, send_ref.at[:, tail])])
+        mixed = mixed_ref[...]
+        for i in range(db_count):
+            whole_ref[i, :part] = mixed
+            whole_ref[i, part:] = gs_ref[i]
+        stores = start([(t_ref, keep_outs[1]), (whole_ref, send_ref)])
     wait_all(dt_loads)
     d = mm(dt_ref[...], x, 1, 1)
     inner = jnp.sum(probs * d, axis=-1, keepdims=True)
@@ -265,6 +270,7 @@
     if last:
         held += [(db_count, grown, width)]
     else:
+        held += [made[0]]
         made += [tall]
     return pl.pallas_call(
         functools.partial(attn_kernel, c=c, pieces=len(xs), last=last),
@@ -327,18 +333,20 @@
 
 
 def order_kernel(at_ref, near_ref, far_ref, out_ref):
-    chips, _, share, _ = near_ref.shape
+    chips, _, half, width = near_ref.shape
+    share, piece = 2 * half, width // 2
     for core, g_ref in enumerate((near_ref, far_ref)):
         for s in range(chips):
             j = lax.rem(at_ref[0] + chips - s, chips) * 2 + lax.rem(at_ref[1] + core, 2)
-            out_ref[:, pl.ds(pl.multiple_of(j * share, share), share)] = g_ref[s]
+            rows = jnp.concatenate([g_ref[s, :, :, :piece], g_ref[s, :, :, piece:]], axis=1)
+            out_ref[:, pl.ds(pl.multiple_of(j * share, share), share)] = rows
 
 
 def order(at, near, far):
-    chips, db_count, share, piece = near.shape
+    chips, db_count, half, width = near.shape
     return pl.pallas_call(
         order_kernel,
-        out_shape=jax.ShapeDtypeStruct((db_count, 2 * chips * share, piece), BF),
+        out_shape=jax.ShapeDtypeStruct((db_count, 4 * chips * half, width // 2), BF),
         in_specs=[SM, VM, VM],
         out_specs=VM,
         compiler_params=params(),
@@ -384,8 +392,7 @@
     at = jnp.stack([head_at // 2, head_at % 2]).astype(jnp.int32)
     owner_ids = lax.broadcasted_iota(jnp.int32, (db_count, 1, 1, 1), 0)
     wanted = jnp.sum(jnp.where(nbr_owner[None, None] == owner_ids, nbr_row[None, None], 0), axis=3)
-    qt = back(queries, w_key, groups)
-    incoming = after(exchange(wanted, "db"), qt)
+    incoming = exchange(wanted, "db")
     steps = ring_steps(head_count)
     (table,) = pick(
         incoming,
@@ -409,13 +416,14 @@
     far = swap(near, head_count)
     crossed = [swap(v, head_count) for v in mine]
     near = after(near, crossed[0])
+    qt = back(after(queries, crossed[0]), w_key, groups)
     dm, dt, grad_cols = prep(at, near, far, w_out, w_value, groups, db_count)
     ring = []
     for c in range(groups):
         held = mine[c] if c == 0 else after(mine[c], *ring[-1])
         came = [along(held, s, head_count) for s in steps]
         if c == 0:
-            came = lax.optimization_barrier((*came, dm))[:-1]
+            came = lax.optimization_barrier((*came, dm, qt))[:-2]
         ring.append([held, *came])
     spread = []
     for c, pieces in enumerate(ring):
@@ -428,9 +436,7 @@
         sends.append(m)
         sent.append(exchange(after(m, *(ring[-1] if c == 0 else sent)), "db"))
         extra = (queries, dm, *t, u)
-    share = tok_rows // head_count
-    piece = width * head_count // db_count
-    rows_near = chips_stack(sent[0][:, part : part + share, :piece], steps, head_count)
+    rows_near = chips_stack(sent[0][:, part:], steps, head_count)
     grad_tok = order(at, rows_near, swap(rows_near, head_count))
     keep, give, grad_q = close(at, sends, us, w_out, w_key, part, head_count)
     other = swap(give, head_count)

time: 141 us -> 138 us (0.979)
  blocking collectives: 0 us -> 15.4 us
  waiting for transfers between devices: 49.2 us -> 39.2 us
  starting transfers between devices: 40.6 us -> 32.8 us
    all_to_all x0 -> x1, blocking collectives: none -> 15.4 us  [exchange(): return lax.all_to_all(x, axis, split_axis=0, concat_axis=0, tiled=True)]
    all_to_all x4 -> x3, starting transfers between devices: 19.1 us -> 11.3 us  [exchange(): return lax.all_to_all(x, axis, split_axis=0, concat_axis=0, tiled=True)]
    all_to_all x4 -> x3, waiting for transfers between devices: 20.1 us -> 13.1 us  [exchange(): return lax.all_to_all(x, axis, split_axis=0, concat_axis=0, tiled=True)]
    ppermute x15, waiting for transfers between devices: 27.6 us -> 24.7 us  [along(): lax.ppermute(v, 'head', [(i, (i // 2 + step) % chips * 2 + i % 2) for i i...]
    unnamed x50 -> x48, local copies, waits for them, and re-layouts: 5.18 us -> 4.48 us
  transfers between devices with their start and end apart: 30 -> 29, of which waited for: 20 -> 19; matrix products, arithmetic and copies ran while one was open for 4% -> 4% of each run, Pallas kernels for 23% -> 24%
where the time goes in v10:
time: 138 us
  waiting for transfers between devices  39.2 us (28%)
  Pallas kernels  36 us (26%)
  starting transfers between devices  32.8 us (24%)
  blocking collectives  15.4 us (11%)
  local copies, waits for them, and re-layouts  5.51 us (4%)
  other arithmetic  4.41 us (3%)
  matrix products  3.1 us (2%)
    ppermute x15, waiting for transfers between devices, along(): lax.ppermute(v, 'head', [(i, (i // 2 + step) % chips * 2 + i % 2) for i i...  24.7 us
    ppermute x15, starting transfers between devices, along(): lax.ppermute(v, 'head', [(i, (i // 2 + step) % chips * 2 + i % 2) for i i...  19.5 us
    all_to_all x1, blocking collectives, exchange(): return lax.all_to_all(x, axis, split_axis=0, concat_axis=0, tiled=True)  15.4 us
    pallas_call x2, Pallas kernels, attn(): pl.pallas_call(functools.partial(attn_kernel, c=c, pieces=len(xs), last=l...  14.7 us
    all_to_all x3, waiting for transfers between devices, exchange(): return lax.all_to_all(x, axis, split_axis=0, concat_axis=0, tiled=True)  13.1 us
    all_to_all x3, starting transfers between devices, exchange(): return lax.all_to_all(x, axis, split_axis=0, concat_axis=0, tiled=True)  11.3 us
    pallas_call x2, Pallas kernels, pick(): pl.pallas_call(functools.partial(pick_kernel, row_of=row_of, count=total)...  5.7 us
    pallas_call x1, Pallas kernels, prep(): pl.pallas_call(prep_kernel, out_shape=[jax.ShapeDtypeStruct(shape, BF) fo...  5.39 us
  transfers between devices with their start and end apart: 29, of which 19 were waited for; matrix products, arithmetic and copies ran while one was open for 4% of the time, Pallas kernels for 24%

profile of v10, /device:TPU:0, one launch (start us, length us, event | category | flops | bytes accessed | tf_op | source)
XLA Modules:
  0.0 137.5 jit_solution(10104687152936125319)
XLA Ops:
  1.5 15.4 %all_to_all.20.rows_ref = s32[16,1,2]{2,1,0:T(1,128)} all-to-all(s32[16,1,2]{2,1,0:T(1,128)S(1)} %copy.17), channel_id=1, replica_groups=mesh['db'=16,'head'=8] {'db'}, dimensions={0} | all-to-all | bytes 256 | tf_op jit(solution)/shard_map/all_to_all | solution.py:377
  16.9 3.7 %shard_map.128 = bf16[32,16,896]{2,1,0:T(8,128)(2,1)} custom-call(s32[16,1,2]{2,1,0:T(1,128)} %all_to_all.20.rows_ref, bf16[64,16,896]{2,1,0:T(8,128)(2,1)} %src_ref.1), custom_call_target="tpu_custom_call" | custom-call | tf_op jit(solution)/shard_map/pallas_call | solution.py:55
  20.6 3.6 %all-to-all-start.1 = ((bf16[32,16,896]{2,1,0:T(8,128)(2,1)}), bf16[32,16,896]{2,1,0:T(8,128)(2,1)S(1)}, u32[]{:S(2)}, u32[]{:S(2)}) async-start(bf16[32,16,896]{2,1,0:T(8,128)(2,1)} %shard_map.128), calls=%async_computation.1 | async-start | bytes 1835008 | tf_op jit(solution)/shard_map/all_to_all | solution.py:377
  24.3 3.1 %collective-permute-start.5 = (bf16[128,512]{1,0:T(8,128)(2,1)S(1)}, bf16[128,512]{1,0:T(8,128)(2,1)S(1)}, u32[]{:S(2)}, u32[]{:S(2)}) collective-permute-start(bf16[128,512]{1,0:T(8,128)(2,1)S(1)} %copy-done.9), channel_id=1, source_target_pairs={{0,6},{1,7},{2,0},{3,1},{4,2},{5,3},{6,4},{7,5},{8,14},{9,15},{10,... | collective-permute-start | bytes 393224 | tf_op jit(solution)/shard_map/ppermute | solution.py:364
  29.0 2.6 %collective-permute-done.5 = bf16[128,512]{1,0:T(8,128)(2,1)S(1)} collective-permute-done((bf16[128,512]{1,0:T(8,128)(2,1)S(1)}, bf16[128,512]{1,0:T(8,128)(2,1)S(1)}, u32[]{:S(2)}, u32[]{:S(2)}) %collective-permute-start.5) | collective-permute-done | bytes 131104 | tf_op jit(solution)/shard_map/ppermute | solution.py:364
  31.6 2.4 %collective-permute-done.4 = bf16[128,512]{1,0:T(8,128)(2,1)S(1)} collective-permute-done((bf16[128,512]{1,0:T(8,128)(2,1)S(1)}, bf16[128,512]{1,0:T(8,128)(2,1)S(1)}, u32[]{:S(2)}, u32[]{:S(2)}) %collective-permute-start.4) | collective-permute-done | bytes 131104 | tf_op jit(solution)/shard_map/ppermute | solution.py:364
  35.4 3.2 %all-to-all-done.1.src_ref = bf16[32,16,896]{2,1,0:T(8,128)(2,1)S(1)} async-done(((bf16[32,16,896]{2,1,0:T(8,128)(2,1)}), bf16[32,16,896]{2,1,0:T(8,128)(2,1)S(1)}, u32[]{:S(2)}, u32[]{:S(2)}) %all-to-all-start.1) | async-done | bytes 917536 | tf_op jit(solution)/shard_map/all_to_all | solution.py:377
  38.7 2.0 %shard_map.129 = (bf16[8,16,896]{2,1,0:T(8,128)(2,1)S(1)}, bf16[8,16,896]{2,1,0:T(8,128)(2,1)S(1)}) custom-call(s32[2,8]{1,0:T(2,128)S(1)} %copy-done, bf16[32,16,896]{2,1,0:T(8,128)(2,1)S(1)} %all-to-all-done.1.src_ref), custom_call_target="tpu_custom_call" | custom-call | tf_op jit(solution)/shard_map/pallas_call | solution.py:55
  46.7 2.8 %shard_map.131.refs_8_ = bf16[2,256,896]{2,1,0:T(8,128)(2,1)} custom-call(bf16[128,512]{1,0:T(8,128)(2,1)} %refs_11_.1, bf16[896,512]{1,0:T(8,128)(2,1)} %refs_5_.1), custom_call_target="tpu_custom_call" | custom-call | flops 120000000 | bytes 2000000 | tf_op jit(solution)/shard_map/pallas_call | solution.py:105
  50.4 5.4 %shard_map.130 = (bf16[128,512]{1,0:T(8,128)(2,1)}, bf16[2,256,896]{2,1,0:T(8,128)(2,1)}, bf16[16,8,512]{2,1,0:T(8,128)(2,1)}) custom-call(s32[2]{0:T(128)} %pad_add_fusion.at_ref, bf16[4,128,512]{2,1,0:T(8,128)(2,1)} %copy-done.3, bf16[4,128,512]{2,1,0:T(8,128)(2,1)} %copy-done.7, bf16[512,4096]{1,0:T(8,128)(2,1)} %refs_4_.1, bf16[896,512]{1,0:T(8,128)(2,1)} %refs_10_.3), custom_call_target="tpu_custom_call" | custom-call | flops 700000000 | bytes 8000000 | tf_op jit(solution)/shard_map/pallas_call | solution.py:163
  57.8 2.1 %collective-permute-start.12 = (bf16[8,16,896]{2,1,0:T(8,128)(2,1)S(1)}, bf16[8,16,896]{2,1,0:T(8,128)(2,1)S(1)}, u32[]{:S(2)}, u32[]{:S(2)}) collective-permute-start(bf16[8,16,896]{2,1,0:T(8,128)(2,1)S(1)} %get-tuple-element.41.refs_0_), channel_id=1, source_target_pairs={{0,6},{1,7},{2,0},{3,1},{4,2},{5,3},{6,4},{7,5},{8,14},{9,15},{10,... | collective-permute-start | bytes 688136 | tf_op jit(solution)/shard_map/ppermute | solution.py:364
  60.9 6.7 %shard_map.132 = (bf16[16,72,512]{2,1,0:T(8,128)(2,1)}, bf16[256,896]{1,0:T(8,128)(2,1)}, bf16[256,896]{1,0:T(8,128)(2,1)}) custom-call(s32[2]{0:T(128)} %count_ref.3, bf16[8,16,896]{2,1,0:T(8,128)(2,1)} %copy-done.2, bf16[8,16,896]{2,1,0:T(8,128)(2,1)} %copy-done.11, bf16[8,16,896]{2,1,0:T(8,128)(2,1)} %copy-done.12, bf16[8,16,896]{2,1,0:T(8,128)(2,1)} %copy-done.13, ...), custom_call_target="tpu_custom_call" | custom-call | flops 3000000000 | bytes 8000000 | tf_op jit(solution)/shard_map/pallas_call | solution.py:275
  67.7 2.4 %collective-permute-done.12.refs_2_ = bf16[8,16,896]{2,1,0:T(8,128)(2,1)S(1)} collective-permute-done((bf16[8,16,896]{2,1,0:T(8,128)(2,1)S(1)}, bf16[8,16,896]{2,1,0:T(8,128)(2,1)S(1)}, u32[]{:S(2)}, u32[]{:S(2)}) %collective-permute-start.12) | collective-permute-done | bytes 229408 | tf_op jit(solution)/shard_map/ppermute | solution.py:364
  70.9 4.0 %all-to-all-start.2 = ((bf16[16,72,512]{2,1,0:T(8,128)(2,1)}), bf16[16,72,512]{2,1,0:T(8,128)(2,1)S(1)}, u32[]{:S(2)}, u32[]{:S(2)}) async-start(bf16[16,72,512]{2,1,0:T(8,128)(2,1)} %get-tuple-element.49.refs_0_), calls=%async_computation.2 | async-start | bytes 2359296 | tf_op jit(solution)/shard_map/all_to_all | solution.py:377
  78.1 8.0 %shard_map.133 = (bf16[16,176,512]{2,1,0:T(8,128)(2,1)}, bf16[256,896]{1,0:T(8,128)(2,1)}) custom-call(s32[2]{0:T(128)} %count_ref.3, bf16[8,16,896]{2,1,0:T(8,128)(2,1)} %copy-done.1, bf16[8,16,896]{2,1,0:T(8,128)(2,1)} %copy-done.14, bf16[8,16,896]{2,1,0:T(8,128)(2,1)} %copy-done.15, bf16[8,16,896]{2,1,0:T(8,128)(2,1)} %copy-done.16, ...), custom_call_target="tpu_custom_call" | custom-call | flops 3000000000 | bytes 8000000 | tf_op jit(solution)/shard_map/pallas_call | solution.py:275
  86.1 7.8 %all-to-all-done.2 = bf16[16,72,512]{2,1,0:T(8,128)(2,1)S(1)} async-done(((bf16[16,72,512]{2,1,0:T(8,128)(2,1)}), bf16[16,72,512]{2,1,0:T(8,128)(2,1)S(1)}, u32[]{:S(2)}, u32[]{:S(2)}) %all-to-all-start.2) | async-done | bytes 1179680 | tf_op jit(solution)/shard_map/all_to_all | solution.py:377
  94.9 3.7 %all-to-all-start.3 = ((bf16[16,176,512]{2,1,0:T(8,128)(2,1)}), bf16[16,176,512]{2,1,0:T(8,128)(2,1)S(1)}, u32[]{:S(2)}, u32[]{:S(2)}) async-start(bf16[16,176,512]{2,1,0:T(8,128)(2,1)} %get-tuple-element.50.refs_1_), calls=%async_computation.3 | async-start | bytes 5767168 | tf_op jit(solution)/shard_map/all_to_all | solution.py:377
  98.7 5.1 %shard_map.134 = (bf16[4,128,512]{2,1,0:T(8,128)(2,1)}, bf16[4,128,512]{2,1,0:T(8,128)(2,1)}, bf16[128,512]{1,0:T(8,128)(2,1)}) custom-call(s32[2]{0:T(128)} %pad_add_fusion.at_ref, bf16[16,72,512]{2,1,0:T(8,128)(2,1)} %get-tuple-element.49.refs_0_, bf16[16,176,512]{2,1,0:T(8,128)(2,1)} %get-tuple-element.50.refs_1_, ...), custom_call_target="tpu_custom_call" | custom-call | flops 700000000 | bytes 8000000 | tf_op jit(solution)/shard_map/pallas_call | solution.py:318
  109.0 3.9 %collective-permute-done.24 = bf16[16,8,512]{2,1,0:T(8,128)(2,1)S(1)} collective-permute-done((bf16[16,8,512]{2,1,0:T(8,128)(2,1)S(1)}, bf16[16,8,512]{2,1,0:T(8,128)(2,1)S(1)}, u32[]{:S(2)}, u32[]{:S(2)}) %collective-permute-start.24) | collective-permute-done | bytes 131104 | tf_op jit(solution)/shard_map/ppermute | solution.py:364
  114.5 2.1 %collective-permute-done.22 = bf16[16,8,512]{2,1,0:T(8,128)(2,1)S(1)} collective-permute-done((bf16[16,8,512]{2,1,0:T(8,128)(2,1)S(1)}, bf16[16,8,512]{2,1,0:T(8,128)(2,1)S(1)}, u32[]{:S(2)}, u32[]{:S(2)}) %collective-permute-start.22) | collective-permute-done | bytes 131104 | tf_op jit(solution)/shard_map/ppermute | solution.py:364
  119.8 4.8 %collective-permute-done.21 = bf16[128,512]{1,0:T(8,128)(2,1)S(1)} collective-permute-done((bf16[128,512]{1,0:T(8,128)(2,1)S(1)}, bf16[128,512]{1,0:T(8,128)(2,1)S(1)}, u32[]{:S(2)}, u32[]{:S(2)}) %collective-permute-start.21) | collective-permute-done | bytes 131104 | tf_op jit(solution)/shard_map/ppermute | solution.py:364
  125.0 2.1 %collective-permute-done.19 = bf16[128,512]{1,0:T(8,128)(2,1)S(1)} collective-permute-done((bf16[128,512]{1,0:T(8,128)(2,1)S(1)}, bf16[128,512]{1,0:T(8,128)(2,1)S(1)}, u32[]{:S(2)}, u32[]{:S(2)}) %collective-permute-start.19) | collective-permute-done | bytes 131104 | tf_op jit(solution)/shard_map/ppermute | solution.py:364
  128.6 2.4 %shard_map.135 = bf16[16,128,256]{2,1,0:T(8,128)(2,1)} custom-call(s32[2]{0:T(128)} %pad_add_fusion.at_ref, bf16[4,16,8,512]{3,2,1,0:T(8,128)(2,1)} %copy-done.4, bf16[4,16,8,512]{3,2,1,0:T(8,128)(2,1)} %copy-done.8), custom_call_target="tpu_custom_call" | custom-call | bytes 2000000 | tf_op jit(solution)/shard_map/pallas_call | solution.py:347
  132.8 2.1 %all-to-all-done.3 = bf16[16,176,512]{2,1,0:T(8,128)(2,1)S(1)} async-done(((bf16[16,176,512]{2,1,0:T(8,128)(2,1)}), bf16[16,176,512]{2,1,0:T(8,128)(2,1)S(1)}, u32[]{:S(2)}, u32[]{:S(2)}) %all-to-all-start.3) | async-done | bytes 2883616 | tf_op jit(solution)/shard_map/all_to_all | solution.py:377
  (103 shorter events, 35.1 us)
Async XLA Ops:
  20.6 18.0 %all-to-all-start.1 = ((bf16[32,16,896]{2,1,0:T(8,128)(2,1)}), bf16[32,16,896]{2,1,0:T(8,128)(2,1)S(1)}, u32[]{:S(2)}, u32[]{:S(2)}) async-start(bf16[32,16,896]{2,1,0:T(8,128)(2,1)} %shard_map.128), calls=%async_computation.1 | async-start | bytes 1835008 | tf_op jit(solution)/shard_map/all_to_all | solution.py:377
  24.3 7.3 %collective-permute-start.5 = (bf16[128,512]{1,0:T(8,128)(2,1)S(1)}, bf16[128,512]{1,0:T(8,128)(2,1)S(1)}, u32[]{:S(2)}, u32[]{:S(2)}) collective-permute-start(bf16[128,512]{1,0:T(8,128)(2,1)S(1)} %copy-done.9), channel_id=1, source_target_pairs={{0,6},{1,7},{2,0},{3,1},{4,2},{5,3},{6,4},{7,5},{8,14},{9,15},{10,... | collective-permute-start | bytes 393224 | tf_op jit(solution)/shard_map/ppermute | solution.py:364
  27.4 6.6 %collective-permute-start.4 = (bf16[128,512]{1,0:T(8,128)(2,1)S(1)}, bf16[128,512]{1,0:T(8,128)(2,1)S(1)}, u32[]{:S(2)}, u32[]{:S(2)}) collective-permute-start(bf16[128,512]{1,0:T(8,128)(2,1)S(1)} %copy-done.9), channel_id=1, source_target_pairs={{0,4},{1,5},{2,6},{3,7},{4,0},{5,1},{6,2},{7,3},{8,12},{9,13},{10,... | collective-permute-start | bytes 393224 | tf_op jit(solution)/shard_map/ppermute | solution.py:364
  28.0 7.2 %collective-permute-start.3 = (bf16[128,512]{1,0:T(8,128)(2,1)S(1)}, bf16[128,512]{1,0:T(8,128)(2,1)S(1)}, u32[]{:S(2)}, u32[]{:S(2)}) collective-permute-start(bf16[128,512]{1,0:T(8,128)(2,1)S(1)} %copy-done.9), channel_id=1, source_target_pairs={{0,2},{1,3},{2,4},{3,5},{4,6},{5,7},{6,0},{7,1},{8,10},{9,11},{10,... | collective-permute-start | bytes 393224 | tf_op jit(solution)/shard_map/ppermute | solution.py:364
  35.3 14.2 %collective-permute-start.7 = (bf16[4,128,512]{2,1,0:T(8,128)(2,1)S(1)}, bf16[4,128,512]{2,1,0:T(8,128)(2,1)S(1)}, u32[]{:S(2)}, u32[]{:S(2)}) collective-permute-start(bf16[4,128,512]{2,1,0:T(8,128)(2,1)S(1)} %pad_maximum_fusion.near_in), channel_id=1, source_target_pairs={{0,1},{1,0},{2,3},{3,2},{4,5},{5,4},{6,7},{7,6},{8,9},{9,8},{10,11... | collective-permute-start | bytes 1572872 | tf_op jit(solution)/shard_map/ppermute | solution.py:368
  40.7 6.1 %collective-permute-start.6 = (bf16[8,16,896]{2,1,0:T(8,128)(2,1)S(1)}, bf16[8,16,896]{2,1,0:T(8,128)(2,1)S(1)}, u32[]{:S(2)}, u32[]{:S(2)}) collective-permute-start(bf16[8,16,896]{2,1,0:T(8,128)(2,1)S(1)} %get-tuple-element.29.refs_0_), channel_id=1, source_target_pairs={{0,1},{1,0},{2,3},{3,2},{4,5},{5,4},{6,7},{7,6},{8,9},{9,8},{10,11... | collective-permute-start | bytes 688136 | tf_op jit(solution)/shard_map/ppermute | solution.py:368
  40.8 15.0 %collective-permute-start = (bf16[8,16,896]{2,1,0:T(8,128)(2,1)S(1)}, bf16[8,16,896]{2,1,0:T(8,128)(2,1)S(1)}, u32[]{:S(2)}, u32[]{:S(2)}) collective-permute-start(bf16[8,16,896]{2,1,0:T(8,128)(2,1)S(1)} %get-tuple-element.29.refs_0_), channel_id=1, source_target_pairs={{0,2},{1,3},{2,4},{3,5},{4,6},{5,7},{6,0},{7,1},{8,10},{9,11},{10,... | collective-permute-start | bytes 688136 | tf_op jit(solution)/shard_map/ppermute | solution.py:364
  42.4 13.4 %collective-permute-start.1 = (bf16[8,16,896]{2,1,0:T(8,128)(2,1)S(1)}, bf16[8,16,896]{2,1,0:T(8,128)(2,1)S(1)}, u32[]{:S(2)}, u32[]{:S(2)}) collective-permute-start(bf16[8,16,896]{2,1,0:T(8,128)(2,1)S(1)} %get-tuple-element.29.refs_0_), channel_id=1, source_target_pairs={{0,6},{1,7},{2,0},{3,1},{4,2},{5,3},{6,4},{7,5},{8,14},{9,15},{10,... | collective-permute-start | bytes 688136 | tf_op jit(solution)/shard_map/ppermute | solution.py:364
  44.1 12.1 %collective-permute-start.2 = (bf16[8,16,896]{2,1,0:T(8,128)(2,1)S(1)}, bf16[8,16,896]{2,1,0:T(8,128)(2,1)S(1)}, u32[]{:S(2)}, u32[]{:S(2)}) collective-permute-start(bf16[8,16,896]{2,1,0:T(8,128)(2,1)S(1)} %get-tuple-element.29.refs_0_), channel_id=1, source_target_pairs={{0,4},{1,5},{2,6},{3,7},{4,0},{5,1},{6,2},{7,3},{8,12},{9,13},{10,... | collective-permute-start | bytes 688136 | tf_op jit(solution)/shard_map/ppermute | solution.py:364
  56.2 3.8 %collective-permute-start.8 = (bf16[8,16,896]{2,1,0:T(8,128)(2,1)S(1)}, bf16[8,16,896]{2,1,0:T(8,128)(2,1)S(1)}, u32[]{:S(2)}, u32[]{:S(2)}) collective-permute-start(bf16[8,16,896]{2,1,0:T(8,128)(2,1)S(1)} %collective-permute-done.refs_1_), channel_id=1, source_target_pairs={{0,1},{1,0},{2,3},{3,2},{4,5},{5,4},{6,7},{7,6},{8,9},{9,8},{10,11... | collective-permute-start | bytes 688136 | tf_op jit(solution)/shard_map/ppermute | solution.py:368
  56.2 4.0 %collective-permute-start.9 = (bf16[8,16,896]{2,1,0:T(8,128)(2,1)S(1)}, bf16[8,16,896]{2,1,0:T(8,128)(2,1)S(1)}, u32[]{:S(2)}, u32[]{:S(2)}) collective-permute-start(bf16[8,16,896]{2,1,0:T(8,128)(2,1)S(1)} %collective-permute-done.1.refs_2_), channel_id=1, source_target_pairs={{0,1},{1,0},{2,3},{3,2},{4,5},{5,4},{6,7},{7,6},{8,9},{9,8},{10,11... | collective-permute-start | bytes 688136 | tf_op jit(solution)/shard_map/ppermute | solution.py:368
  56.7 11.0 %collective-permute-start.11 = (bf16[8,16,896]{2,1,0:T(8,128)(2,1)S(1)}, bf16[8,16,896]{2,1,0:T(8,128)(2,1)S(1)}, u32[]{:S(2)}, u32[]{:S(2)}) collective-permute-start(bf16[8,16,896]{2,1,0:T(8,128)(2,1)S(1)} %get-tuple-element.41.refs_0_), channel_id=1, source_target_pairs={{0,2},{1,3},{2,4},{3,5},{4,6},{5,7},{6,0},{7,1},{8,10},{9,11},{10,... | collective-permute-start | bytes 688136 | tf_op jit(solution)/shard_map/ppermute | solution.py:364
  57.8 12.3 %collective-permute-start.12 = (bf16[8,16,896]{2,1,0:T(8,128)(2,1)S(1)}, bf16[8,16,896]{2,1,0:T(8,128)(2,1)S(1)}, u32[]{:S(2)}, u32[]{:S(2)}) collective-permute-start(bf16[8,16,896]{2,1,0:T(8,128)(2,1)S(1)} %get-tuple-element.41.refs_0_), channel_id=1, source_target_pairs={{0,6},{1,7},{2,0},{3,1},{4,2},{5,3},{6,4},{7,5},{8,14},{9,15},{10,... | collective-permute-start | bytes 688136 | tf_op jit(solution)/shard_map/ppermute | solution.py:364
  59.9 11.0 %collective-permute-start.13 = (bf16[8,16,896]{2,1,0:T(8,128)(2,1)S(1)}, bf16[8,16,896]{2,1,0:T(8,128)(2,1)S(1)}, u32[]{:S(2)}, u32[]{:S(2)}) collective-permute-start(bf16[8,16,896]{2,1,0:T(8,128)(2,1)S(1)} %get-tuple-element.41.refs_0_), channel_id=1, source_target_pairs={{0,4},{1,5},{2,6},{3,7},{4,0},{5,1},{6,2},{7,3},{8,12},{9,13},{10,... | collective-permute-start | bytes 688136 | tf_op jit(solution)/shard_map/ppermute | solution.py:364
  70.9 23.0 %all-to-all-start.2 = ((bf16[16,72,512]{2,1,0:T(8,128)(2,1)}), bf16[16,72,512]{2,1,0:T(8,128)(2,1)S(1)}, u32[]{:S(2)}, u32[]{:S(2)}) async-start(bf16[16,72,512]{2,1,0:T(8,128)(2,1)} %get-tuple-element.49.refs_0_), calls=%async_computation.2 | async-start | bytes 2359296 | tf_op jit(solution)/shard_map/all_to_all | solution.py:377
  94.9 40.0 %all-to-all-start.3 = ((bf16[16,176,512]{2,1,0:T(8,128)(2,1)}), bf16[16,176,512]{2,1,0:T(8,128)(2,1)S(1)}, u32[]{:S(2)}, u32[]{:S(2)}) async-start(bf16[16,176,512]{2,1,0:T(8,128)(2,1)} %get-tuple-element.50.refs_1_), calls=%async_computation.3 | async-start | bytes 5767168 | tf_op jit(solution)/shard_map/all_to_all | solution.py:377
  103.8 4.0 %collective-permute-start.18 = (bf16[4,128,512]{2,1,0:T(8,128)(2,1)}, bf16[4,128,512]{2,1,0:T(8,128)(2,1)S(1)}, u32[]{:S(2)}, u32[]{:S(2)}) collective-permute-start(bf16[4,128,512]{2,1,0:T(8,128)(2,1)} %get-tuple-element.47), channel_id=1, source_target_pairs={{0,1},{1,0},{2,3},{3,2},{4,5},{5,4},{6,7},{7,6},{8,9},{9,8},{10,11... | collective-permute-start | bytes 1572872 | tf_op jit(solution)/shard_map/ppermute | solution.py:368
  104.8 8.1 %collective-permute-start.24 = (bf16[16,8,512]{2,1,0:T(8,128)(2,1)S(1)}, bf16[16,8,512]{2,1,0:T(8,128)(2,1)S(1)}, u32[]{:S(2)}, u32[]{:S(2)}) collective-permute-start(bf16[16,8,512]{2,1,0:T(8,128)(2,1)S(1)} %get-tuple-element.56), channel_id=1, source_target_pairs={{0,6},{1,7},{2,0},{3,1},{4,2},{5,3},{6,4},{7,5},{8,14},{9,15},{10,... | collective-permute-start | bytes 393224 | tf_op jit(solution)/shard_map/ppermute | solution.py:364
  106.6 7.9 %collective-permute-start.23 = (bf16[16,8,512]{2,1,0:T(8,128)(2,1)S(1)}, bf16[16,8,512]{2,1,0:T(8,128)(2,1)S(1)}, u32[]{:S(2)}, u32[]{:S(2)}) collective-permute-start(bf16[16,8,512]{2,1,0:T(8,128)(2,1)S(1)} %get-tuple-element.56), channel_id=1, source_target_pairs={{0,4},{1,5},{2,6},{3,7},{4,0},{5,1},{6,2},{7,3},{8,12},{9,13},{10,... | collective-permute-start | bytes 393224 | tf_op jit(solution)/shard_map/ppermute | solution.py:364
  107.6 9.0 %collective-permute-start.22 = (bf16[16,8,512]{2,1,0:T(8,128)(2,1)S(1)}, bf16[16,8,512]{2,1,0:T(8,128)(2,1)S(1)}, u32[]{:S(2)}, u32[]{:S(2)}) collective-permute-start(bf16[16,8,512]{2,1,0:T(8,128)(2,1)S(1)} %get-tuple-element.56), channel_id=1, source_target_pairs={{0,2},{1,3},{2,4},{3,5},{4,6},{5,7},{6,0},{7,1},{8,10},{9,11},{10,... | collective-permute-start | bytes 393224 | tf_op jit(solution)/shard_map/ppermute | solution.py:364
  116.7 11.1 %collective-permute-start.25 = (bf16[4,16,8,512]{3,2,1,0:T(8,128)(2,1)S(1)}, bf16[4,16,8,512]{3,2,1,0:T(8,128)(2,1)S(1)}, u32[]{:S(2)}, u32[]{:S(2)}) collective-permute-start(bf16[4,16,8,512]{3,2,1,0:T(8,128)(2,1)S(1)} %pad_maximum_fusion.1.near_ref), channel_id=1, source_target_pairs={{0,1},{1,0},{2,3},{3,2},{4,5},{5,4},{6,7},{7,6},{8,9},{9,8},{10,11... | collective-permute-start | bytes 1572872 | tf_op jit(solution)/shard_map/ppermute | solution.py:368
  116.8 7.9 %collective-permute-start.21 = (bf16[128,512]{1,0:T(8,128)(2,1)S(1)}, bf16[128,512]{1,0:T(8,128)(2,1)S(1)}, u32[]{:S(2)}, u32[]{:S(2)}) collective-permute-start(bf16[128,512]{1,0:T(8,128)(2,1)S(1)} %get-tuple-element.58), channel_id=1, source_target_pairs={{0,4},{1,5},{2,6},{3,7},{4,0},{5,1},{6,2},{7,3},{8,12},{9,13},{10,... | collective-permute-start | bytes 393224 | tf_op jit(solution)/shard_map/ppermute | solution.py:364
  117.8 7.2 %collective-permute-start.20 = (bf16[128,512]{1,0:T(8,128)(2,1)S(1)}, bf16[128,512]{1,0:T(8,128)(2,1)S(1)}, u32[]{:S(2)}, u32[]{:S(2)}) collective-permute-start(bf16[128,512]{1,0:T(8,128)(2,1)S(1)} %get-tuple-element.59), channel_id=1, source_target_pairs={{0,6},{1,7},{2,0},{3,1},{4,2},{5,3},{6,4},{7,5},{8,14},{9,15},{10,... | collective-permute-start | bytes 393224 | tf_op jit(solution)/shard_map/ppermute | solution.py:364
  119.0 8.1 %collective-permute-start.19 = (bf16[128,512]{1,0:T(8,128)(2,1)S(1)}, bf16[128,512]{1,0:T(8,128)(2,1)S(1)}, u32[]{:S(2)}, u32[]{:S(2)}) collective-permute-start(bf16[128,512]{1,0:T(8,128)(2,1)S(1)} %get-tuple-element.57), channel_id=1, source_target_pairs={{0,2},{1,3},{2,4},{3,5},{4,6},{5,7},{6,0},{7,1},{8,10},{9,11},{10,... | collective-permute-start | bytes 393224 | tf_op jit(solution)/shard_map/ppermute | solution.py:364
  (29 other events, 165.1 us)

commit v11 on v10

--- a/solution.py
+++ b/solution.py
@@ -83,13 +83,6 @@
     return [(src.at[pl.ds(k * step, step)], dst.at[pl.ds(k * step, step)]) for k in range(count)]
 
 
-def back_kernel(a_in, w_in, out_in, a_ref, w_ref, out_ref, sem):
-    loads = start_loads([(a_in, a_ref), *row_blocks(w_in, w_ref, 4)], sem)
-    wait_all(loads)
-    back_project(a_ref, w_ref, out_ref)
-    wait_all(start_loads([(out_ref, out_in)], sem, len(loads)))
-
-
 def back_project(a_ref, w_ref, out_ref):
     groups = out_ref.shape[0]
     part = a_ref.shape[0] // groups
@@ -100,29 +93,17 @@
             out_ref[c, h * part : (h + 1) * part] = value[c * part : (c + 1) * part]
 
 
-def back(a, w, groups):
-    tall = (groups, a.shape[1] // HD * a.shape[0] // groups, w.shape[0])
-    return pl.pallas_call(
-        back_kernel,
-        out_shape=jax.ShapeDtypeStruct(tall, BF),
-        in_specs=[HBM, HBM],
-        out_specs=HBM,
-        scratch_shapes=[pltpu.VMEM(shape, BF) for shape in (a.shape, w.shape, tall)]
-        + [pltpu.SemaphoreType.DMA((6,))],
-        compiler_params=params(),
-        cost_estimate=pl.CostEstimate(flops=120_000_000, bytes_accessed=2_000_000, transcendentals=0),
-    )(a, w)
-
-
-def prep_kernel(at_ref, near_in, far_in, wo_in, wv_in, dm_out, dt_out, gc_out, *refs):
-    near_ref, far_ref, wo_ref, wv_ref, dm_ref, dt_ref, gc_ref, sem = refs
+def prep_kernel(at_ref, *refs):
+    q_in, wk_in, near_in, far_in, wo_in, wv_in, qt_out, dm_out, dt_out, gc_out = refs[:10]
+    q_ref, wk_ref, near_ref, far_ref, wo_ref, wv_ref, qt_ref, dm_ref, dt_ref, gc_ref, sem = refs[10:]
     chips, rows, width = near_ref.shape
     cuts = gc_ref.shape[0] // (2 * chips)
     piece = width // cuts
     half = gc_ref.shape[1]
     share = 2 * half
     own = pl.ds(pl.multiple_of((at_ref[0] * 2 + at_ref[1]) * share, share), share)
-    first = start_loads([(near_in, near_ref), (far_in, far_ref)], sem)
+    ahead = start_loads([(q_in, q_ref), (wk_in, wk_ref)], sem)
+    first = start_loads([(near_in, near_ref), (far_in, far_ref)], sem, 2)
     places = []
     for core, g_ref in enumerate((near_ref, far_ref)):
         for s in range(chips):
@@ -134,16 +115,19 @@
             for k, (_, _, j) in enumerate(places)
         ],
         sem,
-        2,
-    )
-    used = 2 + len(places)
+        4,
+    )
+    used = 4 + len(places)
     late = start_loads([(wv_in, wv_ref)], sem, used)
+    wait_all(ahead)
+    back_project(q_ref, wk_ref, qt_ref)
+    stores = start_loads([(qt_ref, qt_out)], sem, used + 1)
     wait_all(first)
     for g_ref, s, j in places:
         for p in range(cuts):
             rows_of = g_ref[s, own, p * piece : (p + 1) * piece]
             gc_ref[j * cuts + p] = jnp.concatenate([rows_of[:half], rows_of[half:]], axis=1)
-    stores = start_loads([(gc_ref, gc_out)], sem, used + 1)
+    stores += start_loads([(gc_ref, gc_out)], sem, used + 2)
     acc = jnp.zeros((rows, width), F32)
     for k, (g_ref, s, _) in enumerate(places):
         blocks[k].wait()
@@ -151,25 +135,25 @@
     dm_ref[...] = acc.astype(BF)
     wait_all(late)
     back_project(dm_ref, wv_ref, dt_ref)
-    stores += start_loads([(dm_ref, dm_out), (dt_ref, dt_out)], sem, used + 2)
+    stores += start_loads([(dm_ref, dm_out), (dt_ref, dt_out)], sem, used + 3)
     wait_all(stores)
 
 
-def prep(at, near, far, wo, wv, groups, db_count):
+def prep(at, q, wk, near, far, wo, wv, groups, db_count):
     chips, rows, width = near.shape
     tall = (groups, width // HD * rows // groups, wv.shape[0])
-    made = [(rows, width), tall, (db_count, rows // (4 * chips), width)]
-    operands = (near, far, wo, wv)
+    made = [tall, (rows, width), tall, (db_count, rows // (4 * chips), width)]
+    operands = (q, wk, near, far, wo, wv)
     return pl.pallas_call(
         prep_kernel,
         out_shape=[jax.ShapeDtypeStruct(shape, BF) for shape in made],
-        in_specs=[SM] + [HBM] * 4,
-        out_specs=[HBM] * 3,
+        in_specs=[SM] + [HBM] * 6,
+        out_specs=[HBM] * 4,
         scratch_shapes=[
             pltpu.VMEM(shape, BF)
-            for shape in (near.shape, far.shape, (2 * chips, width, width), wv.shape, *made)
+            for shape in (q.shape, wk.shape, near.shape, far.shape, (2 * chips, width, width), wv.shape, *made)
         ]
-        + [pltpu.SemaphoreType.DMA((6 + 2 * chips,))],
+        + [pltpu.SemaphoreType.DMA((10 + 2 * chips,))],
         compiler_params=params(),
         cost_estimate=pl.CostEstimate(flops=700_000_000, bytes_accessed=8_000_000, transcendentals=0),
     )(at, *operands)
@@ -415,9 +399,7 @@
     near = chips_stack(after(grad_out, table), steps, head_count)
     far = swap(near, head_count)
     crossed = [swap(v, head_count) for v in mine]
-    near = after(near, crossed[0])
-    qt = back(after(queries, crossed[0]), w_key, groups)
-    dm, dt, grad_cols = prep(at, near, far, w_out, w_value, groups, db_count)
+    qt, dm, dt, grad_cols = prep(at, queries, w_key, near, far, w_out, w_value, groups, db_count)
     ring = []
     for c in range(groups):
         held = mine[c] if c == 0 else after(mine[c], *ring[-1])

time: 138 us -> 138 us (level)
  starting transfers between devices: 32.8 us -> 36.2 us
  Pallas kernels: 36 us -> 33.4 us
    pallas_call x1 -> x0, Pallas kernels: 2.81 us -> none  [back(): pl.pallas_call(back_kernel, out_shape=jax.ShapeDtypeStruct(tall, BF), in_...]
    all_to_all x3, starting transfers between devices: 11.3 us -> 13.9 us  [exchange(): return lax.all_to_all(x, axis, split_axis=0, concat_axis=0, tiled=True)]
    ppermute x15, waiting for transfers between devices: 24.7 us -> 23.2 us  [along(): lax.ppermute(v, 'head', [(i, (i // 2 + step) % chips * 2 + i % 2) for i i...]
  transfers between devices with their start and end apart: 29 -> 29, of which waited for: 19 -> 17; matrix products, arithmetic and copies ran while one was open for 4% -> 4% of each run, Pallas kernels for 24% -> 22%
where the time goes in v11:
time: 138 us; the launch traced here: 137 us
  waiting for transfers between devices  38.1 us (28%)
  starting transfers between devices  36.2 us (26%)
  Pallas kernels  33.4 us (24%)
  blocking collectives  15.4 us (11%)
  local copies, waits for them, and re-layouts  5.51 us (4%)
  other arithmetic  4.41 us (3%)
  matrix products  3.1 us (2%)
    ppermute x15, waiting for transfers between devices, along(): lax.ppermute(v, 'head', [(i, (i // 2 + step) % chips * 2 + i % 2) for i i...  23.2 us
    ppermute x15, starting transfers between devices, along(): lax.ppermute(v, 'head', [(i, (i // 2 + step) % chips * 2 + i % 2) for i i...  19.8 us
    all_to_all x1, blocking collectives, exchange(): return lax.all_to_all(x, axis, split_axis=0, concat_axis=0, tiled=True)  15.4 us
    pallas_call x2, Pallas kernels, attn(): pl.pallas_call(functools.partial(attn_kernel, c=c, pieces=len(xs), last=l...  14.7 us
    all_to_all x3, starting transfers between devices, exchange(): return lax.all_to_all(x, axis, split_axis=0, concat_axis=0, tiled=True)  13.9 us
    all_to_all x3, waiting for transfers between devices, exchange(): return lax.all_to_all(x, axis, split_axis=0, concat_axis=0, tiled=True)  13.4 us
    pallas_call x1, Pallas kernels, prep(): pl.pallas_call(prep_kernel, out_shape=[jax.ShapeDtypeStruct(shape, BF) fo...  5.78 us
    pallas_call x2, Pallas kernels, pick(): pl.pallas_call(functools.partial(pick_kernel, row_of=row_of, count=total)...  5.48 us
  transfers between devices with their start and end apart: 29, of which 17 were waited for; matrix products, arithmetic and copies ran while one was open for 4% of the time, Pallas kernels for 22%

profile of v11, /device:TPU:0, one launch (start us, length us, event | category | flops | bytes accessed | tf_op | source)
XLA Modules:
  0.0 137.2 jit_solution(17755094226001746017)
XLA Ops:
  1.5 15.4 %all_to_all.20.rows_ref = s32[16,1,2]{2,1,0:T(1,128)} all-to-all(s32[16,1,2]{2,1,0:T(1,128)S(1)} %copy.17), channel_id=1, replica_groups=mesh['db'=16,'head'=8] {'db'}, dimensions={0} | all-to-all | bytes 256 | tf_op jit(solution)/shard_map/all_to_all | solution.py:361
  16.9 3.5 %shard_map.128 = bf16[32,16,896]{2,1,0:T(8,128)(2,1)} custom-call(s32[16,1,2]{2,1,0:T(1,128)} %all_to_all.20.rows_ref, bf16[64,16,896]{2,1,0:T(8,128)(2,1)} %src_ref.1), custom_call_target="tpu_custom_call" | custom-call | tf_op jit(solution)/shard_map/pallas_call | solution.py:55
  20.4 3.6 %all-to-all-start.1 = ((bf16[32,16,896]{2,1,0:T(8,128)(2,1)}), bf16[32,16,896]{2,1,0:T(8,128)(2,1)S(1)}, u32[]{:S(2)}, u32[]{:S(2)}) async-start(bf16[32,16,896]{2,1,0:T(8,128)(2,1)} %shard_map.128), calls=%async_computation.1 | async-start | bytes 1835008 | tf_op jit(solution)/shard_map/all_to_all | solution.py:361
  24.1 3.1 %collective-permute-start.5 = (bf16[128,512]{1,0:T(8,128)(2,1)S(1)}, bf16[128,512]{1,0:T(8,128)(2,1)S(1)}, u32[]{:S(2)}, u32[]{:S(2)}) collective-permute-start(bf16[128,512]{1,0:T(8,128)(2,1)S(1)} %copy-done.9), channel_id=1, source_target_pairs={{0,6},{1,7},{2,0},{3,1},{4,2},{5,3},{6,4},{7,5},{8,14},{9,15},{10,... | collective-permute-start | bytes 393224 | tf_op jit(solution)/shard_map/ppermute | solution.py:348
  28.8 2.6 %collective-permute-done.5 = bf16[128,512]{1,0:T(8,128)(2,1)S(1)} collective-permute-done((bf16[128,512]{1,0:T(8,128)(2,1)S(1)}, bf16[128,512]{1,0:T(8,128)(2,1)S(1)}, u32[]{:S(2)}, u32[]{:S(2)}) %collective-permute-start.5) | collective-permute-done | bytes 131104 | tf_op jit(solution)/shard_map/ppermute | solution.py:348
  31.4 2.4 %collective-permute-done.4 = bf16[128,512]{1,0:T(8,128)(2,1)S(1)} collective-permute-done((bf16[128,512]{1,0:T(8,128)(2,1)S(1)}, bf16[128,512]{1,0:T(8,128)(2,1)S(1)}, u32[]{:S(2)}, u32[]{:S(2)}) %collective-permute-start.4) | collective-permute-done | bytes 131104 | tf_op jit(solution)/shard_map/ppermute | solution.py:348
  35.2 3.2 %all-to-all-done.1.src_ref = bf16[32,16,896]{2,1,0:T(8,128)(2,1)S(1)} async-done(((bf16[32,16,896]{2,1,0:T(8,128)(2,1)}), bf16[32,16,896]{2,1,0:T(8,128)(2,1)S(1)}, u32[]{:S(2)}, u32[]{:S(2)}) %all-to-all-start.1) | async-done | bytes 917536 | tf_op jit(solution)/shard_map/all_to_all | solution.py:361
  38.4 2.0 %shard_map.129 = (bf16[8,16,896]{2,1,0:T(8,128)(2,1)S(1)}, bf16[8,16,896]{2,1,0:T(8,128)(2,1)S(1)}) custom-call(s32[2,8]{1,0:T(2,128)S(1)} %copy-done, bf16[32,16,896]{2,1,0:T(8,128)(2,1)S(1)} %all-to-all-done.1.src_ref), custom_call_target="tpu_custom_call" | custom-call | tf_op jit(solution)/shard_map/pallas_call | solution.py:55
  47.2 5.8 %shard_map.130 = (bf16[2,256,896]{2,1,0:T(8,128)(2,1)}, bf16[128,512]{1,0:T(8,128)(2,1)}, bf16[2,256,896]{2,1,0:T(8,128)(2,1)}, bf16[16,8,512]{2,1,0:T(8,128)(2,1)}) custom-call(s32[2]{0:T(128)} %pad_add_fusion.at_ref, bf16[128,512]{1,0:T(8,128)(2,1)} %refs_11_.1, bf16[896,512]{1,0:T(8,128)(2,1)} %refs_5_.3, bf16[4,128,512]{2,1,0:T(8,128)(2,1)} %copy-done.3, ...), custom_call_target="tpu_custom_call" | custom-call | flops 700000000 | bytes 8000000 | tf_op jit(solution)/shard_map/pallas_call | solution.py:147
  54.9 2.6 %collective-permute-start.12 = (bf16[8,16,896]{2,1,0:T(8,128)(2,1)S(1)}, bf16[8,16,896]{2,1,0:T(8,128)(2,1)S(1)}, u32[]{:S(2)}, u32[]{:S(2)}) collective-permute-start(bf16[8,16,896]{2,1,0:T(8,128)(2,1)S(1)} %get-tuple-element.39.refs_0_), channel_id=1, source_target_pairs={{0,6},{1,7},{2,0},{3,1},{4,2},{5,3},{6,4},{7,5},{8,14},{9,15},{10,... | collective-permute-start | bytes 688136 | tf_op jit(solution)/shard_map/ppermute | solution.py:348
  58.6 6.7 %shard_map.131 = (bf16[16,72,512]{2,1,0:T(8,128)(2,1)}, bf16[256,896]{1,0:T(8,128)(2,1)}, bf16[256,896]{1,0:T(8,128)(2,1)}) custom-call(s32[2]{0:T(128)} %count_ref.3, bf16[8,16,896]{2,1,0:T(8,128)(2,1)} %copy-done.2, bf16[8,16,896]{2,1,0:T(8,128)(2,1)} %copy-done.10, bf16[8,16,896]{2,1,0:T(8,128)(2,1)} %copy-done.11, bf16[8,16,896]{2,1,0:T(8,128)(2,1)} %copy-done.12, ...), custom_call_target="tpu_custom_call" | custom-call | flops 3000000000 | bytes 8000000 | tf_op jit(solution)/shard_map/pallas_call | solution.py:259
  65.3 2.6 %collective-permute-done.11.refs_1_ = bf16[8,16,896]{2,1,0:T(8,128)(2,1)S(1)} collective-permute-done((bf16[8,16,896]{2,1,0:T(8,128)(2,1)S(1)}, bf16[8,16,896]{2,1,0:T(8,128)(2,1)S(1)}, u32[]{:S(2)}, u32[]{:S(2)}) %collective-permute-start.11) | collective-permute-done | bytes 229408 | tf_op jit(solution)/shard_map/ppermute | solution.py:348
  68.0 6.6 %all-to-all-start.2 = ((bf16[16,72,512]{2,1,0:T(8,128)(2,1)}), bf16[16,72,512]{2,1,0:T(8,128)(2,1)S(1)}, u32[]{:S(2)}, u32[]{:S(2)}) async-start(bf16[16,72,512]{2,1,0:T(8,128)(2,1)} %get-tuple-element.47.refs_0_), calls=%async_computation.2 | async-start | bytes 2359296 | tf_op jit(solution)/shard_map/all_to_all | solution.py:361
  77.8 8.0 %shard_map.132 = (bf16[16,176,512]{2,1,0:T(8,128)(2,1)}, bf16[256,896]{1,0:T(8,128)(2,1)}) custom-call(s32[2]{0:T(128)} %count_ref.3, bf16[8,16,896]{2,1,0:T(8,128)(2,1)} %copy-done.1, bf16[8,16,896]{2,1,0:T(8,128)(2,1)} %copy-done.13, bf16[8,16,896]{2,1,0:T(8,128)(2,1)} %copy-done.14, bf16[8,16,896]{2,1,0:T(8,128)(2,1)} %copy-done.15, ...), custom_call_target="tpu_custom_call" | custom-call | flops 3000000000 | bytes 8000000 | tf_op jit(solution)/shard_map/pallas_call | solution.py:259
  85.8 7.8 %all-to-all-done.2 = bf16[16,72,512]{2,1,0:T(8,128)(2,1)S(1)} async-done(((bf16[16,72,512]{2,1,0:T(8,128)(2,1)}), bf16[16,72,512]{2,1,0:T(8,128)(2,1)S(1)}, u32[]{:S(2)}, u32[]{:S(2)}) %all-to-all-start.2) | async-done | bytes 1179680 | tf_op jit(solution)/shard_map/all_to_all | solution.py:361
  94.6 3.7 %all-to-all-start.3 = ((bf16[16,176,512]{2,1,0:T(8,128)(2,1)}), bf16[16,176,512]{2,1,0:T(8,128)(2,1)S(1)}, u32[]{:S(2)}, u32[]{:S(2)}) async-start(bf16[16,176,512]{2,1,0:T(8,128)(2,1)} %get-tuple-element.48.refs_1_), calls=%async_computation.3 | async-start | bytes 5767168 | tf_op jit(solution)/shard_map/all_to_all | solution.py:361
  98.3 5.1 %shard_map.133 = (bf16[4,128,512]{2,1,0:T(8,128)(2,1)}, bf16[4,128,512]{2,1,0:T(8,128)(2,1)}, bf16[128,512]{1,0:T(8,128)(2,1)}) custom-call(s32[2]{0:T(128)} %pad_add_fusion.at_ref, bf16[16,72,512]{2,1,0:T(8,128)(2,1)} %get-tuple-element.47.refs_0_, bf16[16,176,512]{2,1,0:T(8,128)(2,1)} %get-tuple-element.48.refs_1_, ...), custom_call_target="tpu_custom_call" | custom-call | flops 700000000 | bytes 8000000 | tf_op jit(solution)/shard_map/pallas_call | solution.py:302
  108.5 2.3 %collective-permute-done.24 = bf16[16,8,512]{2,1,0:T(8,128)(2,1)S(1)} collective-permute-done((bf16[16,8,512]{2,1,0:T(8,128)(2,1)S(1)}, bf16[16,8,512]{2,1,0:T(8,128)(2,1)S(1)}, u32[]{:S(2)}, u32[]{:S(2)}) %collective-permute-start.24) | collective-permute-done | bytes 131104 | tf_op jit(solution)/shard_map/ppermute | solution.py:348
  110.8 3.0 %collective-permute-done.23 = bf16[16,8,512]{2,1,0:T(8,128)(2,1)S(1)} collective-permute-done((bf16[16,8,512]{2,1,0:T(8,128)(2,1)S(1)}, bf16[16,8,512]{2,1,0:T(8,128)(2,1)S(1)}, u32[]{:S(2)}, u32[]{:S(2)}) %collective-permute-start.23) | collective-permute-done | bytes 131104 | tf_op jit(solution)/shard_map/ppermute | solution.py:348
  113.8 2.1 %collective-permute-done.22 = bf16[16,8,512]{2,1,0:T(8,128)(2,1)S(1)} collective-permute-done((bf16[16,8,512]{2,1,0:T(8,128)(2,1)S(1)}, bf16[16,8,512]{2,1,0:T(8,128)(2,1)S(1)}, u32[]{:S(2)}, u32[]{:S(2)}) %collective-permute-start.22) | collective-permute-done | bytes 131104 | tf_op jit(solution)/shard_map/ppermute | solution.py:348
  119.5 4.5 %collective-permute-done.21 = bf16[128,512]{1,0:T(8,128)(2,1)S(1)} collective-permute-done((bf16[128,512]{1,0:T(8,128)(2,1)S(1)}, bf16[128,512]{1,0:T(8,128)(2,1)S(1)}, u32[]{:S(2)}, u32[]{:S(2)}) %collective-permute-start.21) | collective-permute-done | bytes 131104 | tf_op jit(solution)/shard_map/ppermute | solution.py:348
  124.3 2.1 %collective-permute-done.19 = bf16[128,512]{1,0:T(8,128)(2,1)S(1)} collective-permute-done((bf16[128,512]{1,0:T(8,128)(2,1)S(1)}, bf16[128,512]{1,0:T(8,128)(2,1)S(1)}, u32[]{:S(2)}, u32[]{:S(2)}) %collective-permute-start.19) | collective-permute-done | bytes 131104 | tf_op jit(solution)/shard_map/ppermute | solution.py:348
  128.0 2.4 %shard_map.134 = bf16[16,128,256]{2,1,0:T(8,128)(2,1)} custom-call(s32[2]{0:T(128)} %pad_add_fusion.at_ref, bf16[4,16,8,512]{3,2,1,0:T(8,128)(2,1)} %copy-done.4, bf16[4,16,8,512]{3,2,1,0:T(8,128)(2,1)} %copy-done.8), custom_call_target="tpu_custom_call" | custom-call | bytes 2000000 | tf_op jit(solution)/shard_map/pallas_call | solution.py:331
  132.2 2.5 %all-to-all-done.3 = bf16[16,176,512]{2,1,0:T(8,128)(2,1)S(1)} async-done(((bf16[16,176,512]{2,1,0:T(8,128)(2,1)}), bf16[16,176,512]{2,1,0:T(8,128)(2,1)S(1)}, u32[]{:S(2)}, u32[]{:S(2)}) %all-to-all-start.3) | async-done | bytes 2883616 | tf_op jit(solution)/shard_map/all_to_all | solution.py:361
  (102 shorter events, 32.7 us)
Async XLA Ops:
  20.4 18.0 %all-to-all-start.1 = ((bf16[32,16,896]{2,1,0:T(8,128)(2,1)}), bf16[32,16,896]{2,1,0:T(8,128)(2,1)S(1)}, u32[]{:S(2)}, u32[]{:S(2)}) async-start(bf16[32,16,896]{2,1,0:T(8,128)(2,1)} %shard_map.128), calls=%async_computation.1 | async-start | bytes 1835008 | tf_op jit(solution)/shard_map/all_to_all | solution.py:361
  24.1 7.3 %collective-permute-start.5 = (bf16[128,512]{1,0:T(8,128)(2,1)S(1)}, bf16[128,512]{1,0:T(8,128)(2,1)S(1)}, u32[]{:S(2)}, u32[]{:S(2)}) collective-permute-start(bf16[128,512]{1,0:T(8,128)(2,1)S(1)} %copy-done.9), channel_id=1, source_target_pairs={{0,6},{1,7},{2,0},{3,1},{4,2},{5,3},{6,4},{7,5},{8,14},{9,15},{10,... | collective-permute-start | bytes 393224 | tf_op jit(solution)/shard_map/ppermute | solution.py:348
  27.2 6.6 %collective-permute-start.4 = (bf16[128,512]{1,0:T(8,128)(2,1)S(1)}, bf16[128,512]{1,0:T(8,128)(2,1)S(1)}, u32[]{:S(2)}, u32[]{:S(2)}) collective-permute-start(bf16[128,512]{1,0:T(8,128)(2,1)S(1)} %copy-done.9), channel_id=1, source_target_pairs={{0,4},{1,5},{2,6},{3,7},{4,0},{5,1},{6,2},{7,3},{8,12},{9,13},{10,... | collective-permute-start | bytes 393224 | tf_op jit(solution)/shard_map/ppermute | solution.py:348
  27.8 7.2 %collective-permute-start.3 = (bf16[128,512]{1,0:T(8,128)(2,1)S(1)}, bf16[128,512]{1,0:T(8,128)(2,1)S(1)}, u32[]{:S(2)}, u32[]{:S(2)}) collective-permute-start(bf16[128,512]{1,0:T(8,128)(2,1)S(1)} %copy-done.9), channel_id=1, source_target_pairs={{0,2},{1,3},{2,4},{3,5},{4,6},{5,7},{6,0},{7,1},{8,10},{9,11},{10,... | collective-permute-start | bytes 393224 | tf_op jit(solution)/shard_map/ppermute | solution.py:348
  35.1 11.3 %collective-permute-start.6 = (bf16[4,128,512]{2,1,0:T(8,128)(2,1)S(1)}, bf16[4,128,512]{2,1,0:T(8,128)(2,1)S(1)}, u32[]{:S(2)}, u32[]{:S(2)}) collective-permute-start(bf16[4,128,512]{2,1,0:T(8,128)(2,1)S(1)} %pad_maximum_fusion.refs_2_), channel_id=1, source_target_pairs={{0,1},{1,0},{2,3},{3,2},{4,5},{5,4},{6,7},{7,6},{8,9},{9,8},{10,11... | collective-permute-start | bytes 1572872 | tf_op jit(solution)/shard_map/ppermute | solution.py:352
  40.5 12.6 %collective-permute-start = (bf16[8,16,896]{2,1,0:T(8,128)(2,1)S(1)}, bf16[8,16,896]{2,1,0:T(8,128)(2,1)S(1)}, u32[]{:S(2)}, u32[]{:S(2)}) collective-permute-start(bf16[8,16,896]{2,1,0:T(8,128)(2,1)S(1)} %get-tuple-element.28.refs_0_), channel_id=1, source_target_pairs={{0,2},{1,3},{2,4},{3,5},{4,6},{5,7},{6,0},{7,1},{8,10},{9,11},{10,... | collective-permute-start | bytes 688136 | tf_op jit(solution)/shard_map/ppermute | solution.py:348
  42.1 11.0 %collective-permute-start.1 = (bf16[8,16,896]{2,1,0:T(8,128)(2,1)S(1)}, bf16[8,16,896]{2,1,0:T(8,128)(2,1)S(1)}, u32[]{:S(2)}, u32[]{:S(2)}) collective-permute-start(bf16[8,16,896]{2,1,0:T(8,128)(2,1)S(1)} %get-tuple-element.28.refs_0_), channel_id=1, source_target_pairs={{0,6},{1,7},{2,0},{3,1},{4,2},{5,3},{6,4},{7,5},{8,14},{9,15},{10,... | collective-permute-start | bytes 688136 | tf_op jit(solution)/shard_map/ppermute | solution.py:348
  43.8 9.4 %collective-permute-start.2 = (bf16[8,16,896]{2,1,0:T(8,128)(2,1)S(1)}, bf16[8,16,896]{2,1,0:T(8,128)(2,1)S(1)}, u32[]{:S(2)}, u32[]{:S(2)}) collective-permute-start(bf16[8,16,896]{2,1,0:T(8,128)(2,1)S(1)} %get-tuple-element.28.refs_0_), channel_id=1, source_target_pairs={{0,4},{1,5},{2,6},{3,7},{4,0},{5,1},{6,2},{7,3},{8,12},{9,13},{10,... | collective-permute-start | bytes 688136 | tf_op jit(solution)/shard_map/ppermute | solution.py:348
  53.2 4.3 %collective-permute-start.8 = (bf16[8,16,896]{2,1,0:T(8,128)(2,1)S(1)}, bf16[8,16,896]{2,1,0:T(8,128)(2,1)S(1)}, u32[]{:S(2)}, u32[]{:S(2)}) collective-permute-start(bf16[8,16,896]{2,1,0:T(8,128)(2,1)S(1)} %collective-permute-done.refs_1_), channel_id=1, source_target_pairs={{0,1},{1,0},{2,3},{3,2},{4,5},{5,4},{6,7},{7,6},{8,9},{9,8},{10,11... | collective-permute-start | bytes 688136 | tf_op jit(solution)/shard_map/ppermute | solution.py:352
  53.7 4.1 %collective-permute-start.9 = (bf16[8,16,896]{2,1,0:T(8,128)(2,1)S(1)}, bf16[8,16,896]{2,1,0:T(8,128)(2,1)S(1)}, u32[]{:S(2)}, u32[]{:S(2)}) collective-permute-start(bf16[8,16,896]{2,1,0:T(8,128)(2,1)S(1)} %collective-permute-done.1.refs_2_), channel_id=1, source_target_pairs={{0,1},{1,0},{2,3},{3,2},{4,5},{5,4},{6,7},{7,6},{8,9},{9,8},{10,11... | collective-permute-start | bytes 688136 | tf_op jit(solution)/shard_map/ppermute | solution.py:352
  53.8 4.0 %collective-permute-start.10 = (bf16[8,16,896]{2,1,0:T(8,128)(2,1)S(1)}, bf16[8,16,896]{2,1,0:T(8,128)(2,1)S(1)}, u32[]{:S(2)}, u32[]{:S(2)}) collective-permute-start(bf16[8,16,896]{2,1,0:T(8,128)(2,1)S(1)} %collective-permute-done.2.refs_3_), channel_id=1, source_target_pairs={{0,1},{1,0},{2,3},{3,2},{4,5},{5,4},{6,7},{7,6},{8,9},{9,8},{10,11... | collective-permute-start | bytes 688136 | tf_op jit(solution)/shard_map/ppermute | solution.py:352
  54.2 13.7 %collective-permute-start.11 = (bf16[8,16,896]{2,1,0:T(8,128)(2,1)S(1)}, bf16[8,16,896]{2,1,0:T(8,128)(2,1)S(1)}, u32[]{:S(2)}, u32[]{:S(2)}) collective-permute-start(bf16[8,16,896]{2,1,0:T(8,128)(2,1)S(1)} %get-tuple-element.39.refs_0_), channel_id=1, source_target_pairs={{0,2},{1,3},{2,4},{3,5},{4,6},{5,7},{6,0},{7,1},{8,10},{9,11},{10,... | collective-permute-start | bytes 688136 | tf_op jit(solution)/shard_map/ppermute | solution.py:348
  54.9 13.1 %collective-permute-start.12 = (bf16[8,16,896]{2,1,0:T(8,128)(2,1)S(1)}, bf16[8,16,896]{2,1,0:T(8,128)(2,1)S(1)}, u32[]{:S(2)}, u32[]{:S(2)}) collective-permute-start(bf16[8,16,896]{2,1,0:T(8,128)(2,1)S(1)} %get-tuple-element.39.refs_0_), channel_id=1, source_target_pairs={{0,6},{1,7},{2,0},{3,1},{4,2},{5,3},{6,4},{7,5},{8,14},{9,15},{10,... | collective-permute-start | bytes 688136 | tf_op jit(solution)/shard_map/ppermute | solution.py:348
  57.5 10.5 %collective-permute-start.13 = (bf16[8,16,896]{2,1,0:T(8,128)(2,1)S(1)}, bf16[8,16,896]{2,1,0:T(8,128)(2,1)S(1)}, u32[]{:S(2)}, u32[]{:S(2)}) collective-permute-start(bf16[8,16,896]{2,1,0:T(8,128)(2,1)S(1)} %get-tuple-element.39.refs_0_), channel_id=1, source_target_pairs={{0,4},{1,5},{2,6},{3,7},{4,0},{5,1},{6,2},{7,3},{8,12},{9,13},{10,... | collective-permute-start | bytes 688136 | tf_op jit(solution)/shard_map/ppermute | solution.py:348
  68.0 25.6 %all-to-all-start.2 = ((bf16[16,72,512]{2,1,0:T(8,128)(2,1)}), bf16[16,72,512]{2,1,0:T(8,128)(2,1)S(1)}, u32[]{:S(2)}, u32[]{:S(2)}) async-start(bf16[16,72,512]{2,1,0:T(8,128)(2,1)} %get-tuple-element.47.refs_0_), calls=%async_computation.2 | async-start | bytes 2359296 | tf_op jit(solution)/shard_map/all_to_all | solution.py:361
  94.6 40.0 %all-to-all-start.3 = ((bf16[16,176,512]{2,1,0:T(8,128)(2,1)}), bf16[16,176,512]{2,1,0:T(8,128)(2,1)S(1)}, u32[]{:S(2)}, u32[]{:S(2)}) async-start(bf16[16,176,512]{2,1,0:T(8,128)(2,1)} %get-tuple-element.48.refs_1_), calls=%async_computation.3 | async-start | bytes 5767168 | tf_op jit(solution)/shard_map/all_to_all | solution.py:361
  103.4 3.9 %collective-permute-start.18 = (bf16[4,128,512]{2,1,0:T(8,128)(2,1)}, bf16[4,128,512]{2,1,0:T(8,128)(2,1)S(1)}, u32[]{:S(2)}, u32[]{:S(2)}) collective-permute-start(bf16[4,128,512]{2,1,0:T(8,128)(2,1)} %get-tuple-element.45), channel_id=1, source_target_pairs={{0,1},{1,0},{2,3},{3,2},{4,5},{5,4},{6,7},{7,6},{8,9},{9,8},{10,11... | collective-permute-start | bytes 1572872 | tf_op jit(solution)/shard_map/ppermute | solution.py:352
  104.5 6.4 %collective-permute-start.24 = (bf16[16,8,512]{2,1,0:T(8,128)(2,1)S(1)}, bf16[16,8,512]{2,1,0:T(8,128)(2,1)S(1)}, u32[]{:S(2)}, u32[]{:S(2)}) collective-permute-start(bf16[16,8,512]{2,1,0:T(8,128)(2,1)S(1)} %get-tuple-element.54), channel_id=1, source_target_pairs={{0,6},{1,7},{2,0},{3,1},{4,2},{5,3},{6,4},{7,5},{8,14},{9,15},{10,... | collective-permute-start | bytes 393224 | tf_op jit(solution)/shard_map/ppermute | solution.py:348
  106.0 7.8 %collective-permute-start.23 = (bf16[16,8,512]{2,1,0:T(8,128)(2,1)S(1)}, bf16[16,8,512]{2,1,0:T(8,128)(2,1)S(1)}, u32[]{:S(2)}, u32[]{:S(2)}) collective-permute-start(bf16[16,8,512]{2,1,0:T(8,128)(2,1)S(1)} %get-tuple-element.54), channel_id=1, source_target_pairs={{0,4},{1,5},{2,6},{3,7},{4,0},{5,1},{6,2},{7,3},{8,12},{9,13},{10,... | collective-permute-start | bytes 393224 | tf_op jit(solution)/shard_map/ppermute | solution.py:348
  107.3 8.6 %collective-permute-start.22 = (bf16[16,8,512]{2,1,0:T(8,128)(2,1)S(1)}, bf16[16,8,512]{2,1,0:T(8,128)(2,1)S(1)}, u32[]{:S(2)}, u32[]{:S(2)}) collective-permute-start(bf16[16,8,512]{2,1,0:T(8,128)(2,1)S(1)} %get-tuple-element.54), channel_id=1, source_target_pairs={{0,2},{1,3},{2,4},{3,5},{4,6},{5,7},{6,0},{7,1},{8,10},{9,11},{10,... | collective-permute-start | bytes 393224 | tf_op jit(solution)/shard_map/ppermute | solution.py:348
  116.0 11.1 %collective-permute-start.25 = (bf16[4,16,8,512]{3,2,1,0:T(8,128)(2,1)S(1)}, bf16[4,16,8,512]{3,2,1,0:T(8,128)(2,1)S(1)}, u32[]{:S(2)}, u32[]{:S(2)}) collective-permute-start(bf16[4,16,8,512]{3,2,1,0:T(8,128)(2,1)S(1)} %pad_maximum_fusion.1.near_ref), channel_id=1, source_target_pairs={{0,1},{1,0},{2,3},{3,2},{4,5},{5,4},{6,7},{7,6},{8,9},{9,8},{10,11... | collective-permute-start | bytes 1572872 | tf_op jit(solution)/shard_map/ppermute | solution.py:352
  116.1 7.9 %collective-permute-start.21 = (bf16[128,512]{1,0:T(8,128)(2,1)S(1)}, bf16[128,512]{1,0:T(8,128)(2,1)S(1)}, u32[]{:S(2)}, u32[]{:S(2)}) collective-permute-start(bf16[128,512]{1,0:T(8,128)(2,1)S(1)} %get-tuple-element.56), channel_id=1, source_target_pairs={{0,4},{1,5},{2,6},{3,7},{4,0},{5,1},{6,2},{7,3},{8,12},{9,13},{10,... | collective-permute-start | bytes 393224 | tf_op jit(solution)/shard_map/ppermute | solution.py:348
  117.5 6.8 %collective-permute-start.20 = (bf16[128,512]{1,0:T(8,128)(2,1)S(1)}, bf16[128,512]{1,0:T(8,128)(2,1)S(1)}, u32[]{:S(2)}, u32[]{:S(2)}) collective-permute-start(bf16[128,512]{1,0:T(8,128)(2,1)S(1)} %get-tuple-element.57), channel_id=1, source_target_pairs={{0,6},{1,7},{2,0},{3,1},{4,2},{5,3},{6,4},{7,5},{8,14},{9,15},{10,... | collective-permute-start | bytes 393224 | tf_op jit(solution)/shard_map/ppermute | solution.py:348
  118.7 7.7 %collective-permute-start.19 = (bf16[128,512]{1,0:T(8,128)(2,1)S(1)}, bf16[128,512]{1,0:T(8,128)(2,1)S(1)}, u32[]{:S(2)}, u32[]{:S(2)}) collective-permute-start(bf16[128,512]{1,0:T(8,128)(2,1)S(1)} %get-tuple-element.55), channel_id=1, source_target_pairs={{0,2},{1,3},{2,4},{3,5},{4,6},{5,7},{6,0},{7,1},{8,10},{9,11},{10,... | collective-permute-start | bytes 393224 | tf_op jit(solution)/shard_map/ppermute | solution.py:348
  (29 other events, 156.9 us)

commit v12 on v11

--- a/solution.py
+++ b/solution.py
@@ -47,6 +47,30 @@
         first += size
     for store in stores:
         store.wait()
+
+
+def select_kernel(rows_ref, src_ref, *rest, row_of, count):
+    *outs, sem = rest
+    places = [out.at[n] for out in outs for n in range(out.shape[0])]
+    copies = [
+        pltpu.make_async_copy(src_ref.at[row_of(rows_ref, k)], places[k], sem.at[k]) for k in range(count)
+    ]
+    for copy in copies:
+        copy.start()
+    for copy in copies:
+        copy.wait()
+
+
+def select(rows, row_of, src, counts):
+    total = sum(counts)
+    return pl.pallas_call(
+        functools.partial(select_kernel, row_of=row_of, count=total),
+        out_shape=[jax.ShapeDtypeStruct((n, *src.shape[1:]), src.dtype) for n in counts],
+        in_specs=[SM, ANY],
+        out_specs=[VM] * len(counts),
+        scratch_shapes=[pltpu.SemaphoreType.DMA((total,))],
+        compiler_params=pltpu.CompilerParams(vmem_limit_bytes=SMALL_LIMIT),
+    )(rows, src)
 
 
 def pick(rows, row_of, src, counts, place, limit):
@@ -354,7 +378,7 @@
 
 def ring_steps(count):
     chips = count // 2
-    return sorted(range(1, chips), key=lambda s: min(s, chips - s))
+    return sorted(range(1, chips), key=lambda s: -min(s, chips - s))
 
 
 def exchange(x, axis):
@@ -387,15 +411,12 @@
         VMEM_LIMIT,
     )
     received = exchange(table, "db")
-    mine = pick(
+    mine = select(
         nbr_owner,
         lambda ref, k: ref[k // slot_count, k % slot_count] * groups + k // slot_count,
         received,
         (slot_count,) * groups,
-        ANY,
-        SMALL_LIMIT,
-    )
-    token = mine[0]
+    )
     near = chips_stack(after(grad_out, table), steps, head_count)
     far = swap(near, head_count)
     crossed = [swap(v, head_count) for v in mine]

time: 138 us -> 139 us (level)
  waiting for transfers between devices: 38.1 us -> 41.3 us
  starting transfers between devices: 36.2 us -> 34.1 us
    all_to_all x3, waiting for transfers between devices: 13.4 us -> 15.6 us  [exchange(): return lax.all_to_all(x, axis, split_axis=0, concat_axis=0, tiled=True)]
    all_to_all x3, starting transfers between devices: 13.9 us -> 11.9 us  [exchange(): return lax.all_to_all(x, axis, split_axis=0, concat_axis=0, tiled=True)]
    pallas_call x2 -> x1, Pallas kernels: 5.48 us -> 3.68 us  [pick(): pl.pallas_call(functools.partial(pick_kernel, row_of=row_of, count=total)...]
  transfers between devices with their start and end apart: 29 -> 29, of which waited for: 17 -> 17; matrix products, arithmetic and copies ran while one was open for 4% -> 4% of each run, Pallas kernels for 22% -> 21%
where the time goes in v12:
time: 139 us; the launch traced here: 138 us
  waiting for transfers between devices  41.3 us (30%)
  starting transfers between devices  34.1 us (25%)
  Pallas kernels  32.9 us (24%)
  blocking collectives  15.4 us (11%)
  local copies, waits for them, and re-layouts  5.51 us (4%)
  other arithmetic  4.41 us (3%)
  matrix products  3.1 us (2%)
    ppermute x15, waiting for transfers between devices, along(): lax.ppermute(v, 'head', [(i, (i // 2 + step) % chips * 2 + i % 2) for i i...  23.9 us
    ppermute x15, starting transfers between devices, along(): lax.ppermute(v, 'head', [(i, (i // 2 + step) % chips * 2 + i % 2) for i i...  19.7 us
    all_to_all x3, waiting for transfers between devices, exchange(): return lax.all_to_all(x, axis, split_axis=0, concat_axis=0, tiled=True)  15.6 us
    all_to_all x1, blocking collectives, exchange(): return lax.all_to_all(x, axis, split_axis=0, concat_axis=0, tiled=True)  15.4 us
    pallas_call x2, Pallas kernels, attn(): pl.pallas_call(functools.partial(attn_kernel, c=c, pieces=len(xs), last=l...  14.7 us
    all_to_all x3, starting transfers between devices, exchange(): return lax.all_to_all(x, axis, split_axis=0, concat_axis=0, tiled=True)  11.9 us
    pallas_call x1, Pallas kernels, prep(): pl.pallas_call(prep_kernel, out_shape=[jax.ShapeDtypeStruct(shape, BF) fo...  5.78 us
    pallas_call x1, Pallas kernels, close(): pl.pallas_call(functools.partial(close_kernel, groups=groups), out_shape=...  5.09 us
  transfers between devices with their start and end apart: 29, of which 17 were waited for; matrix products, arithmetic and copies ran while one was open for 4% of the time, Pallas kernels for 21%

profile of v12, /device:TPU:0, one launch (start us, length us, event | category | flops | bytes accessed | tf_op | source)
XLA Modules:
  0.0 137.7 jit_solution(1384893080410431541)
XLA Ops:
  1.5 15.4 %all_to_all.20.rows_ref = s32[16,1,2]{2,1,0:T(1,128)} all-to-all(s32[16,1,2]{2,1,0:T(1,128)S(1)} %copy.17), channel_id=1, replica_groups=mesh['db'=16,'head'=8] {'db'}, dimensions={0} | all-to-all | bytes 256 | tf_op jit(solution)/shard_map/all_to_all | solution.py:385
  16.9 3.7 %shard_map.128 = bf16[32,16,896]{2,1,0:T(8,128)(2,1)} custom-call(s32[16,1,2]{2,1,0:T(1,128)} %all_to_all.20.rows_ref, bf16[64,16,896]{2,1,0:T(8,128)(2,1)} %src_ref.1), custom_call_target="tpu_custom_call" | custom-call | tf_op jit(solution)/shard_map/pallas_call | solution.py:79
  20.6 3.6 %all-to-all-start.1 = ((bf16[32,16,896]{2,1,0:T(8,128)(2,1)}), bf16[32,16,896]{2,1,0:T(8,128)(2,1)S(1)}, u32[]{:S(2)}, u32[]{:S(2)}) async-start(bf16[32,16,896]{2,1,0:T(8,128)(2,1)} %shard_map.128), calls=%async_computation.1 | async-start | bytes 1835008 | tf_op jit(solution)/shard_map/all_to_all | solution.py:385
  24.3 3.1 %collective-permute-start.5 = (bf16[128,512]{1,0:T(8,128)(2,1)S(1)}, bf16[128,512]{1,0:T(8,128)(2,1)S(1)}, u32[]{:S(2)}, u32[]{:S(2)}) collective-permute-start(bf16[128,512]{1,0:T(8,128)(2,1)S(1)} %copy-done.9), channel_id=1, source_target_pairs={{0,6},{1,7},{2,0},{3,1},{4,2},{5,3},{6,4},{7,5},{8,14},{9,15},{10,... | collective-permute-start | bytes 393224 | tf_op jit(solution)/shard_map/ppermute | solution.py:372
  29.0 2.6 %collective-permute-done.5 = bf16[128,512]{1,0:T(8,128)(2,1)S(1)} collective-permute-done((bf16[128,512]{1,0:T(8,128)(2,1)S(1)}, bf16[128,512]{1,0:T(8,128)(2,1)S(1)}, u32[]{:S(2)}, u32[]{:S(2)}) %collective-permute-start.5) | collective-permute-done | bytes 131104 | tf_op jit(solution)/shard_map/ppermute | solution.py:372
  31.6 2.4 %collective-permute-done.4 = bf16[128,512]{1,0:T(8,128)(2,1)S(1)} collective-permute-done((bf16[128,512]{1,0:T(8,128)(2,1)S(1)}, bf16[128,512]{1,0:T(8,128)(2,1)S(1)}, u32[]{:S(2)}, u32[]{:S(2)}) %collective-permute-start.4) | collective-permute-done | bytes 131104 | tf_op jit(solution)/shard_map/ppermute | solution.py:372
  35.4 3.2 %all-to-all-done.1.src_ref = bf16[32,16,896]{2,1,0:T(8,128)(2,1)S(1)} async-done(((bf16[32,16,896]{2,1,0:T(8,128)(2,1)}), bf16[32,16,896]{2,1,0:T(8,128)(2,1)S(1)}, u32[]{:S(2)}, u32[]{:S(2)}) %all-to-all-start.1) | async-done | bytes 917536 | tf_op jit(solution)/shard_map/all_to_all | solution.py:385
  40.0 3.3 %collective-permute-start = (bf16[8,16,896]{2,1,0:T(8,128)(2,1)S(1)}, bf16[8,16,896]{2,1,0:T(8,128)(2,1)S(1)}, u32[]{:S(2)}, u32[]{:S(2)}) collective-permute-start(bf16[8,16,896]{2,1,0:T(8,128)(2,1)S(1)} %get-tuple-element.28.refs_0_), channel_id=1, source_target_pairs={{0,4},{1,5},{2,6},{3,7},{4,0},{5,1},{6,2},{7,3},{8,12},{9,13},{10,... | collective-permute-start | bytes 688136 | tf_op jit(solution)/shard_map/ppermute | solution.py:372
  44.0 2.6 %collective-permute-start.2 = (bf16[8,16,896]{2,1,0:T(8,128)(2,1)S(1)}, bf16[8,16,896]{2,1,0:T(8,128)(2,1)S(1)}, u32[]{:S(2)}, u32[]{:S(2)}) collective-permute-start(bf16[8,16,896]{2,1,0:T(8,128)(2,1)S(1)} %get-tuple-element.28.refs_0_), channel_id=1, source_target_pairs={{0,6},{1,7},{2,0},{3,1},{4,2},{5,3},{6,4},{7,5},{8,14},{9,15},{10,... | collective-permute-start | bytes 688136 | tf_op jit(solution)/shard_map/ppermute | solution.py:372
  48.0 5.8 %shard_map.130 = (bf16[2,256,896]{2,1,0:T(8,128)(2,1)}, bf16[128,512]{1,0:T(8,128)(2,1)}, bf16[2,256,896]{2,1,0:T(8,128)(2,1)}, bf16[16,8,512]{2,1,0:T(8,128)(2,1)}) custom-call(s32[2]{0:T(128)} %pad_add_fusion.at_ref, bf16[128,512]{1,0:T(8,128)(2,1)} %refs_11_.1, bf16[896,512]{1,0:T(8,128)(2,1)} %refs_5_.3, bf16[4,128,512]{2,1,0:T(8,128)(2,1)} %copy-done.3, ...), custom_call_target="tpu_custom_call" | custom-call | flops 700000000 | bytes 8000000 | tf_op jit(solution)/shard_map/pallas_call | solution.py:171
  55.9 2.7 %collective-permute-start.13 = (bf16[8,16,896]{2,1,0:T(8,128)(2,1)S(1)}, bf16[8,16,896]{2,1,0:T(8,128)(2,1)S(1)}, u32[]{:S(2)}, u32[]{:S(2)}) collective-permute-start(bf16[8,16,896]{2,1,0:T(8,128)(2,1)S(1)} %get-tuple-element.39.refs_0_), channel_id=1, source_target_pairs={{0,6},{1,7},{2,0},{3,1},{4,2},{5,3},{6,4},{7,5},{8,14},{9,15},{10,... | collective-permute-start | bytes 688136 | tf_op jit(solution)/shard_map/ppermute | solution.py:372
  59.4 6.7 %shard_map.131 = (bf16[16,72,512]{2,1,0:T(8,128)(2,1)}, bf16[256,896]{1,0:T(8,128)(2,1)}, bf16[256,896]{1,0:T(8,128)(2,1)}) custom-call(s32[2]{0:T(128)} %count_ref.3, bf16[8,16,896]{2,1,0:T(8,128)(2,1)} %copy-done.2, bf16[8,16,896]{2,1,0:T(8,128)(2,1)} %copy-done.10, bf16[8,16,896]{2,1,0:T(8,128)(2,1)} %copy-done.11, bf16[8,16,896]{2,1,0:T(8,128)(2,1)} %copy-done.12, ...), custom_call_target="tpu_custom_call" | custom-call | flops 3000000000 | bytes 8000000 | tf_op jit(solution)/shard_map/pallas_call | solution.py:283
  66.1 2.9 %collective-permute-done.12.refs_2_ = bf16[8,16,896]{2,1,0:T(8,128)(2,1)S(1)} collective-permute-done((bf16[8,16,896]{2,1,0:T(8,128)(2,1)S(1)}, bf16[8,16,896]{2,1,0:T(8,128)(2,1)S(1)}, u32[]{:S(2)}, u32[]{:S(2)}) %collective-permute-start.12) | collective-permute-done | bytes 229408 | tf_op jit(solution)/shard_map/ppermute | solution.py:372
  69.0 4.5 %all-to-all-start.2 = ((bf16[16,72,512]{2,1,0:T(8,128)(2,1)}), bf16[16,72,512]{2,1,0:T(8,128)(2,1)S(1)}, u32[]{:S(2)}, u32[]{:S(2)}) async-start(bf16[16,72,512]{2,1,0:T(8,128)(2,1)} %get-tuple-element.47.refs_0_), calls=%async_computation.2 | async-start | bytes 2359296 | tf_op jit(solution)/shard_map/all_to_all | solution.py:385
  76.8 8.0 %shard_map.132 = (bf16[16,176,512]{2,1,0:T(8,128)(2,1)}, bf16[256,896]{1,0:T(8,128)(2,1)}) custom-call(s32[2]{0:T(128)} %count_ref.3, bf16[8,16,896]{2,1,0:T(8,128)(2,1)} %copy-done.1, bf16[8,16,896]{2,1,0:T(8,128)(2,1)} %copy-done.13, bf16[8,16,896]{2,1,0:T(8,128)(2,1)} %copy-done.14, bf16[8,16,896]{2,1,0:T(8,128)(2,1)} %copy-done.15, ...), custom_call_target="tpu_custom_call" | custom-call | flops 3000000000 | bytes 8000000 | tf_op jit(solution)/shard_map/pallas_call | solution.py:283
  84.8 8.3 %all-to-all-done.2 = bf16[16,72,512]{2,1,0:T(8,128)(2,1)S(1)} async-done(((bf16[16,72,512]{2,1,0:T(8,128)(2,1)}), bf16[16,72,512]{2,1,0:T(8,128)(2,1)S(1)}, u32[]{:S(2)}, u32[]{:S(2)}) %all-to-all-start.2) | async-done | bytes 1179680 | tf_op jit(solution)/shard_map/all_to_all | solution.py:385
  94.1 3.7 %all-to-all-start.3 = ((bf16[16,176,512]{2,1,0:T(8,128)(2,1)}), bf16[16,176,512]{2,1,0:T(8,128)(2,1)S(1)}, u32[]{:S(2)}, u32[]{:S(2)}) async-start(bf16[16,176,512]{2,1,0:T(8,128)(2,1)} %get-tuple-element.48.refs_1_), calls=%async_computation.3 | async-start | bytes 5767168 | tf_op jit(solution)/shard_map/all_to_all | solution.py:385
  97.8 5.1 %shard_map.133 = (bf16[4,128,512]{2,1,0:T(8,128)(2,1)}, bf16[4,128,512]{2,1,0:T(8,128)(2,1)}, bf16[128,512]{1,0:T(8,128)(2,1)}) custom-call(s32[2]{0:T(128)} %pad_add_fusion.at_ref, bf16[16,72,512]{2,1,0:T(8,128)(2,1)} %get-tuple-element.47.refs_0_, bf16[16,176,512]{2,1,0:T(8,128)(2,1)} %get-tuple-element.48.refs_1_, ...), custom_call_target="tpu_custom_call" | custom-call | flops 700000000 | bytes 8000000 | tf_op jit(solution)/shard_map/pallas_call | solution.py:326
  107.4 2.9 %collective-permute-done.24 = bf16[16,8,512]{2,1,0:T(8,128)(2,1)S(1)} collective-permute-done((bf16[16,8,512]{2,1,0:T(8,128)(2,1)S(1)}, bf16[16,8,512]{2,1,0:T(8,128)(2,1)S(1)}, u32[]{:S(2)}, u32[]{:S(2)}) %collective-permute-start.24) | collective-permute-done | bytes 131104 | tf_op jit(solution)/shard_map/ppermute | solution.py:372
  110.3 2.1 %collective-permute-done.23 = bf16[16,8,512]{2,1,0:T(8,128)(2,1)S(1)} collective-permute-done((bf16[16,8,512]{2,1,0:T(8,128)(2,1)S(1)}, bf16[16,8,512]{2,1,0:T(8,128)(2,1)S(1)}, u32[]{:S(2)}, u32[]{:S(2)}) %collective-permute-start.23) | collective-permute-done | bytes 131104 | tf_op jit(solution)/shard_map/ppermute | solution.py:372
  117.6 3.4 %collective-permute-done.21 = bf16[128,512]{1,0:T(8,128)(2,1)S(1)} collective-permute-done((bf16[128,512]{1,0:T(8,128)(2,1)S(1)}, bf16[128,512]{1,0:T(8,128)(2,1)S(1)}, u32[]{:S(2)}, u32[]{:S(2)}) %collective-permute-start.21) | collective-permute-done | bytes 131104 | tf_op jit(solution)/shard_map/ppermute | solution.py:372
  121.0 4.3 %collective-permute-done.20 = bf16[128,512]{1,0:T(8,128)(2,1)S(1)} collective-permute-done((bf16[128,512]{1,0:T(8,128)(2,1)S(1)}, bf16[128,512]{1,0:T(8,128)(2,1)S(1)}, u32[]{:S(2)}, u32[]{:S(2)}) %collective-permute-start.20) | collective-permute-done | bytes 131104 | tf_op jit(solution)/shard_map/ppermute | solution.py:372
  126.8 2.4 %shard_map.134 = bf16[16,128,256]{2,1,0:T(8,128)(2,1)} custom-call(s32[2]{0:T(128)} %pad_add_fusion.at_ref, bf16[4,16,8,512]{3,2,1,0:T(8,128)(2,1)} %copy-done.4, bf16[4,16,8,512]{3,2,1,0:T(8,128)(2,1)} %copy-done.8), custom_call_target="tpu_custom_call" | custom-call | bytes 2000000 | tf_op jit(solution)/shard_map/pallas_call | solution.py:355
  131.0 4.1 %all-to-all-done.3 = bf16[16,176,512]{2,1,0:T(8,128)(2,1)S(1)} async-done(((bf16[16,176,512]{2,1,0:T(8,128)(2,1)}), bf16[16,176,512]{2,1,0:T(8,128)(2,1)S(1)}, u32[]{:S(2)}, u32[]{:S(2)}) %all-to-all-start.3) | async-done | bytes 2883616 | tf_op jit(solution)/shard_map/all_to_all | solution.py:385
  (102 shorter events, 30.2 us)
Async XLA Ops:
  20.6 18.0 %all-to-all-start.1 = ((bf16[32,16,896]{2,1,0:T(8,128)(2,1)}), bf16[32,16,896]{2,1,0:T(8,128)(2,1)S(1)}, u32[]{:S(2)}, u32[]{:S(2)}) async-start(bf16[32,16,896]{2,1,0:T(8,128)(2,1)} %shard_map.128), calls=%async_computation.1 | async-start | bytes 1835008 | tf_op jit(solution)/shard_map/all_to_all | solution.py:385
  24.3 7.3 %collective-permute-start.5 = (bf16[128,512]{1,0:T(8,128)(2,1)S(1)}, bf16[128,512]{1,0:T(8,128)(2,1)S(1)}, u32[]{:S(2)}, u32[]{:S(2)}) collective-permute-start(bf16[128,512]{1,0:T(8,128)(2,1)S(1)} %copy-done.9), channel_id=1, source_target_pairs={{0,6},{1,7},{2,0},{3,1},{4,2},{5,3},{6,4},{7,5},{8,14},{9,15},{10,... | collective-permute-start | bytes 393224 | tf_op jit(solution)/shard_map/ppermute | solution.py:372
  27.4 6.6 %collective-permute-start.4 = (bf16[128,512]{1,0:T(8,128)(2,1)S(1)}, bf16[128,512]{1,0:T(8,128)(2,1)S(1)}, u32[]{:S(2)}, u32[]{:S(2)}) collective-permute-start(bf16[128,512]{1,0:T(8,128)(2,1)S(1)} %copy-done.9), channel_id=1, source_target_pairs={{0,4},{1,5},{2,6},{3,7},{4,0},{5,1},{6,2},{7,3},{8,12},{9,13},{10,... | collective-permute-start | bytes 393224 | tf_op jit(solution)/shard_map/ppermute | solution.py:372
  28.0 7.2 %collective-permute-start.3 = (bf16[128,512]{1,0:T(8,128)(2,1)S(1)}, bf16[128,512]{1,0:T(8,128)(2,1)S(1)}, u32[]{:S(2)}, u32[]{:S(2)}) collective-permute-start(bf16[128,512]{1,0:T(8,128)(2,1)S(1)} %copy-done.9), channel_id=1, source_target_pairs={{0,2},{1,3},{2,4},{3,5},{4,6},{5,7},{6,0},{7,1},{8,10},{9,11},{10,... | collective-permute-start | bytes 393224 | tf_op jit(solution)/shard_map/ppermute | solution.py:372
  35.3 11.9 %collective-permute-start.6 = (bf16[4,128,512]{2,1,0:T(8,128)(2,1)S(1)}, bf16[4,128,512]{2,1,0:T(8,128)(2,1)S(1)}, u32[]{:S(2)}, u32[]{:S(2)}) collective-permute-start(bf16[4,128,512]{2,1,0:T(8,128)(2,1)S(1)} %pad_maximum_fusion.refs_2_), channel_id=1, source_target_pairs={{0,1},{1,0},{2,3},{3,2},{4,5},{5,4},{6,7},{7,6},{8,9},{9,8},{10,11... | collective-permute-start | bytes 1572872 | tf_op jit(solution)/shard_map/ppermute | solution.py:376
  40.0 13.9 %collective-permute-start = (bf16[8,16,896]{2,1,0:T(8,128)(2,1)S(1)}, bf16[8,16,896]{2,1,0:T(8,128)(2,1)S(1)}, u32[]{:S(2)}, u32[]{:S(2)}) collective-permute-start(bf16[8,16,896]{2,1,0:T(8,128)(2,1)S(1)} %get-tuple-element.28.refs_0_), channel_id=1, source_target_pairs={{0,4},{1,5},{2,6},{3,7},{4,0},{5,1},{6,2},{7,3},{8,12},{9,13},{10,... | collective-permute-start | bytes 688136 | tf_op jit(solution)/shard_map/ppermute | solution.py:372
  43.3 10.6 %collective-permute-start.1 = (bf16[8,16,896]{2,1,0:T(8,128)(2,1)S(1)}, bf16[8,16,896]{2,1,0:T(8,128)(2,1)S(1)}, u32[]{:S(2)}, u32[]{:S(2)}) collective-permute-start(bf16[8,16,896]{2,1,0:T(8,128)(2,1)S(1)} %get-tuple-element.28.refs_0_), channel_id=1, source_target_pairs={{0,2},{1,3},{2,4},{3,5},{4,6},{5,7},{6,0},{7,1},{8,10},{9,11},{10,... | collective-permute-start | bytes 688136 | tf_op jit(solution)/shard_map/ppermute | solution.py:372
  44.0 10.0 %collective-permute-start.2 = (bf16[8,16,896]{2,1,0:T(8,128)(2,1)S(1)}, bf16[8,16,896]{2,1,0:T(8,128)(2,1)S(1)}, u32[]{:S(2)}, u32[]{:S(2)}) collective-permute-start(bf16[8,16,896]{2,1,0:T(8,128)(2,1)S(1)} %get-tuple-element.28.refs_0_), channel_id=1, source_target_pairs={{0,6},{1,7},{2,0},{3,1},{4,2},{5,3},{6,4},{7,5},{8,14},{9,15},{10,... | collective-permute-start | bytes 688136 | tf_op jit(solution)/shard_map/ppermute | solution.py:372
  53.9 2.0 %collective-permute-start.8 = (bf16[8,16,896]{2,1,0:T(8,128)(2,1)S(1)}, bf16[8,16,896]{2,1,0:T(8,128)(2,1)S(1)}, u32[]{:S(2)}, u32[]{:S(2)}) collective-permute-start(bf16[8,16,896]{2,1,0:T(8,128)(2,1)S(1)} %collective-permute-done.refs_1_), channel_id=1, source_target_pairs={{0,1},{1,0},{2,3},{3,2},{4,5},{5,4},{6,7},{7,6},{8,9},{9,8},{10,11... | collective-permute-start | bytes 688136 | tf_op jit(solution)/shard_map/ppermute | solution.py:376
  54.5 4.1 %collective-permute-start.9 = (bf16[8,16,896]{2,1,0:T(8,128)(2,1)S(1)}, bf16[8,16,896]{2,1,0:T(8,128)(2,1)S(1)}, u32[]{:S(2)}, u32[]{:S(2)}) collective-permute-start(bf16[8,16,896]{2,1,0:T(8,128)(2,1)S(1)} %collective-permute-done.1.refs_2_), channel_id=1, source_target_pairs={{0,1},{1,0},{2,3},{3,2},{4,5},{5,4},{6,7},{7,6},{8,9},{9,8},{10,11... | collective-permute-start | bytes 688136 | tf_op jit(solution)/shard_map/ppermute | solution.py:376
  54.6 4.0 %collective-permute-start.10 = (bf16[8,16,896]{2,1,0:T(8,128)(2,1)S(1)}, bf16[8,16,896]{2,1,0:T(8,128)(2,1)S(1)}, u32[]{:S(2)}, u32[]{:S(2)}) collective-permute-start(bf16[8,16,896]{2,1,0:T(8,128)(2,1)S(1)} %collective-permute-done.2.refs_3_), channel_id=1, source_target_pairs={{0,1},{1,0},{2,3},{3,2},{4,5},{5,4},{6,7},{7,6},{8,9},{9,8},{10,11... | collective-permute-start | bytes 688136 | tf_op jit(solution)/shard_map/ppermute | solution.py:376
  55.0 11.1 %collective-permute-start.11 = (bf16[8,16,896]{2,1,0:T(8,128)(2,1)S(1)}, bf16[8,16,896]{2,1,0:T(8,128)(2,1)S(1)}, u32[]{:S(2)}, u32[]{:S(2)}) collective-permute-start(bf16[8,16,896]{2,1,0:T(8,128)(2,1)S(1)} %get-tuple-element.39.refs_0_), channel_id=1, source_target_pairs={{0,4},{1,5},{2,6},{3,7},{4,0},{5,1},{6,2},{7,3},{8,12},{9,13},{10,... | collective-permute-start | bytes 688136 | tf_op jit(solution)/shard_map/ppermute | solution.py:372
  55.4 13.7 %collective-permute-start.12 = (bf16[8,16,896]{2,1,0:T(8,128)(2,1)S(1)}, bf16[8,16,896]{2,1,0:T(8,128)(2,1)S(1)}, u32[]{:S(2)}, u32[]{:S(2)}) collective-permute-start(bf16[8,16,896]{2,1,0:T(8,128)(2,1)S(1)} %get-tuple-element.39.refs_0_), channel_id=1, source_target_pairs={{0,2},{1,3},{2,4},{3,5},{4,6},{5,7},{6,0},{7,1},{8,10},{9,11},{10,... | collective-permute-start | bytes 688136 | tf_op jit(solution)/shard_map/ppermute | solution.py:372
  55.9 13.1 %collective-permute-start.13 = (bf16[8,16,896]{2,1,0:T(8,128)(2,1)S(1)}, bf16[8,16,896]{2,1,0:T(8,128)(2,1)S(1)}, u32[]{:S(2)}, u32[]{:S(2)}) collective-permute-start(bf16[8,16,896]{2,1,0:T(8,128)(2,1)S(1)} %get-tuple-element.39.refs_0_), channel_id=1, source_target_pairs={{0,6},{1,7},{2,0},{3,1},{4,2},{5,3},{6,4},{7,5},{8,14},{9,15},{10,... | collective-permute-start | bytes 688136 | tf_op jit(solution)/shard_map/ppermute | solution.py:372
  69.0 24.0 %all-to-all-start.2 = ((bf16[16,72,512]{2,1,0:T(8,128)(2,1)}), bf16[16,72,512]{2,1,0:T(8,128)(2,1)S(1)}, u32[]{:S(2)}, u32[]{:S(2)}) async-start(bf16[16,72,512]{2,1,0:T(8,128)(2,1)} %get-tuple-element.47.refs_0_), calls=%async_computation.2 | async-start | bytes 2359296 | tf_op jit(solution)/shard_map/all_to_all | solution.py:385
  94.1 41.1 %all-to-all-start.3 = ((bf16[16,176,512]{2,1,0:T(8,128)(2,1)}), bf16[16,176,512]{2,1,0:T(8,128)(2,1)S(1)}, u32[]{:S(2)}, u32[]{:S(2)}) async-start(bf16[16,176,512]{2,1,0:T(8,128)(2,1)} %get-tuple-element.48.refs_1_), calls=%async_computation.3 | async-start | bytes 5767168 | tf_op jit(solution)/shard_map/all_to_all | solution.py:385
  102.9 3.3 %collective-permute-start.18 = (bf16[4,128,512]{2,1,0:T(8,128)(2,1)}, bf16[4,128,512]{2,1,0:T(8,128)(2,1)S(1)}, u32[]{:S(2)}, u32[]{:S(2)}) collective-permute-start(bf16[4,128,512]{2,1,0:T(8,128)(2,1)} %get-tuple-element.45), channel_id=1, source_target_pairs={{0,1},{1,0},{2,3},{3,2},{4,5},{5,4},{6,7},{7,6},{8,9},{9,8},{10,11... | collective-permute-start | bytes 1572872 | tf_op jit(solution)/shard_map/ppermute | solution.py:376
  103.9 6.4 %collective-permute-start.24 = (bf16[16,8,512]{2,1,0:T(8,128)(2,1)S(1)}, bf16[16,8,512]{2,1,0:T(8,128)(2,1)S(1)}, u32[]{:S(2)}, u32[]{:S(2)}) collective-permute-start(bf16[16,8,512]{2,1,0:T(8,128)(2,1)S(1)} %get-tuple-element.54), channel_id=1, source_target_pairs={{0,6},{1,7},{2,0},{3,1},{4,2},{5,3},{6,4},{7,5},{8,14},{9,15},{10,... | collective-permute-start | bytes 393224 | tf_op jit(solution)/shard_map/ppermute | solution.py:372
  104.6 7.8 %collective-permute-start.23 = (bf16[16,8,512]{2,1,0:T(8,128)(2,1)S(1)}, bf16[16,8,512]{2,1,0:T(8,128)(2,1)S(1)}, u32[]{:S(2)}, u32[]{:S(2)}) collective-permute-start(bf16[16,8,512]{2,1,0:T(8,128)(2,1)S(1)} %get-tuple-element.54), channel_id=1, source_target_pairs={{0,4},{1,5},{2,6},{3,7},{4,0},{5,1},{6,2},{7,3},{8,12},{9,13},{10,... | collective-permute-start | bytes 393224 | tf_op jit(solution)/shard_map/ppermute | solution.py:372
  105.4 9.1 %collective-permute-start.22 = (bf16[16,8,512]{2,1,0:T(8,128)(2,1)S(1)}, bf16[16,8,512]{2,1,0:T(8,128)(2,1)S(1)}, u32[]{:S(2)}, u32[]{:S(2)}) collective-permute-start(bf16[16,8,512]{2,1,0:T(8,128)(2,1)S(1)} %get-tuple-element.54), channel_id=1, source_target_pairs={{0,2},{1,3},{2,4},{3,5},{4,6},{5,7},{6,0},{7,1},{8,10},{9,11},{10,... | collective-permute-start | bytes 393224 | tf_op jit(solution)/shard_map/ppermute | solution.py:372
  114.6 11.4 %collective-permute-start.25 = (bf16[4,16,8,512]{3,2,1,0:T(8,128)(2,1)S(1)}, bf16[4,16,8,512]{3,2,1,0:T(8,128)(2,1)S(1)}, u32[]{:S(2)}, u32[]{:S(2)}) collective-permute-start(bf16[4,16,8,512]{3,2,1,0:T(8,128)(2,1)S(1)} %pad_maximum_fusion.1.near_ref), channel_id=1, source_target_pairs={{0,1},{1,0},{2,3},{3,2},{4,5},{5,4},{6,7},{7,6},{8,9},{9,8},{10,11... | collective-permute-start | bytes 1572872 | tf_op jit(solution)/shard_map/ppermute | solution.py:376
  114.7 6.3 %collective-permute-start.21 = (bf16[128,512]{1,0:T(8,128)(2,1)S(1)}, bf16[128,512]{1,0:T(8,128)(2,1)S(1)}, u32[]{:S(2)}, u32[]{:S(2)}) collective-permute-start(bf16[128,512]{1,0:T(8,128)(2,1)S(1)} %get-tuple-element.56), channel_id=1, source_target_pairs={{0,6},{1,7},{2,0},{3,1},{4,2},{5,3},{6,4},{7,5},{8,14},{9,15},{10,... | collective-permute-start | bytes 393224 | tf_op jit(solution)/shard_map/ppermute | solution.py:372
  115.7 9.6 %collective-permute-start.20 = (bf16[128,512]{1,0:T(8,128)(2,1)S(1)}, bf16[128,512]{1,0:T(8,128)(2,1)S(1)}, u32[]{:S(2)}, u32[]{:S(2)}) collective-permute-start(bf16[128,512]{1,0:T(8,128)(2,1)S(1)} %get-tuple-element.57), channel_id=1, source_target_pairs={{0,2},{1,3},{2,4},{3,5},{4,6},{5,7},{6,0},{7,1},{8,10},{9,11},{10,... | collective-permute-start | bytes 393224 | tf_op jit(solution)/shard_map/ppermute | solution.py:372
  116.8 8.5 %collective-permute-start.19 = (bf16[128,512]{1,0:T(8,128)(2,1)S(1)}, bf16[128,512]{1,0:T(8,128)(2,1)S(1)}, u32[]{:S(2)}, u32[]{:S(2)}) collective-permute-start(bf16[128,512]{1,0:T(8,128)(2,1)S(1)} %get-tuple-element.55), channel_id=1, source_target_pairs={{0,4},{1,5},{2,6},{3,7},{4,0},{5,1},{6,2},{7,3},{8,12},{9,13},{10,... | collective-permute-start | bytes 393224 | tf_op jit(solution)/shard_map/ppermute | solution.py:372
  (29 other events, 157.4 us)

commit v13 on v12

--- a/solution.py
+++ b/solution.py
@@ -12,6 +12,7 @@
 BF = jnp.bfloat16
 F32 = jnp.float32
 VMEM_LIMIT = 60 * 1024 * 1024
+PARTS = 4
 SMALL_LIMIT = 8 * 1024 * 1024
 
 
@@ -40,11 +41,16 @@
     stores, first = [], 0
     for n, out in enumerate(outs):
         size = out.shape[0]
-        for load in loads[first : first + size]:
-            load.wait()
-        stores.append(pltpu.make_async_copy(held.at[pl.ds(first, size)], out, store_sem.at[n]))
-        stores[-1].start()
-        first += size
+        step = size // PARTS
+        for p in range(PARTS):
+            for load in loads[first : first + step]:
+                load.wait()
+            part = out.at[pl.ds(p * step, step)]
+            stores.append(
+                pltpu.make_async_copy(held.at[pl.ds(first, step)], part, store_sem.at[n * PARTS + p])
+            )
+            stores[-1].start()
+            first += step
     for store in stores:
         store.wait()
 
@@ -84,7 +90,7 @@
         scratch_shapes=[
             pltpu.VMEM((total, *item), src.dtype),
             pltpu.SemaphoreType.DMA((total,)),
-            pltpu.SemaphoreType.DMA((len(counts),)),
+            pltpu.SemaphoreType.DMA((len(counts) * PARTS,)),
         ],
         compiler_params=pltpu.CompilerParams(vmem_limit_bytes=limit),
     )(rows, src)

time: 139 us -> 138 us (level)
  no operation moved by 1% of the time
where the time goes in v13:
time: 138 us
  waiting for transfers between devices  41.3 us (30%)
  starting transfers between devices  34.1 us (25%)
  Pallas kernels  32.9 us (24%)
  blocking collectives  15.4 us (11%)
  local copies, waits for them, and re-layouts  5.51 us (4%)
  other arithmetic  4.41 us (3%)
  matrix products  3.1 us (2%)
    ppermute x15, waiting for transfers between devices, along(): lax.ppermute(v, 'head', [(i, (i // 2 + step) % chips * 2 + i % 2) for i i...  23.9 us
    ppermute x15, starting transfers between devices, along(): lax.ppermute(v, 'head', [(i, (i // 2 + step) % chips * 2 + i % 2) for i i...  19.7 us
    all_to_all x3, waiting for transfers between devices, exchange(): return lax.all_to_all(x, axis, split_axis=0, concat_axis=0, tiled=True)  15.6 us
    all_to_all x1, blocking collectives, exchange(): return lax.all_to_all(x, axis, split_axis=0, concat_axis=0, tiled=True)  15.4 us
    pallas_call x2, Pallas kernels, attn(): pl.pallas_call(functools.partial(attn_kernel, c=c, pieces=len(xs), last=l...  14.7 us
    all_to_all x3, starting transfers between devices, exchange(): return lax.all_to_all(x, axis, split_axis=0, concat_axis=0, tiled=True)  11.9 us
    pallas_call x1, Pallas kernels, prep(): pl.pallas_call(prep_kernel, out_shape=[jax.ShapeDtypeStruct(shape, BF) fo...  5.78 us
    pallas_call x1, Pallas kernels, close(): pl.pallas_call(functools.partial(close_kernel, groups=groups), out_shape=...  5.08 us
  transfers between devices with their start and end apart: 29, of which 17 were waited for; matrix products, arithmetic and copies ran while one was open for 4% of the time, Pallas kernels for 21%

profile of v13, /device:TPU:0, one launch (start us, length us, event | category | flops | bytes accessed | tf_op | source)
XLA Modules:
  0.0 137.7 jit_solution(2726884533340054676)
XLA Ops:
  1.5 15.4 %all_to_all.20.rows_ref = s32[16,1,2]{2,1,0:T(1,128)} all-to-all(s32[16,1,2]{2,1,0:T(1,128)S(1)} %copy.17), channel_id=1, replica_groups=mesh['db'=16,'head'=8] {'db'}, dimensions={0} | all-to-all | bytes 256 | tf_op jit(solution)/shard_map/all_to_all | solution.py:391
  16.9 3.7 %shard_map.128 = bf16[32,16,896]{2,1,0:T(8,128)(2,1)} custom-call(s32[16,1,2]{2,1,0:T(1,128)} %all_to_all.20.rows_ref, bf16[64,16,896]{2,1,0:T(8,128)(2,1)} %src_ref.1), custom_call_target="tpu_custom_call" | custom-call | tf_op jit(solution)/shard_map/pallas_call | solution.py:85
  20.6 3.6 %all-to-all-start.1 = ((bf16[32,16,896]{2,1,0:T(8,128)(2,1)}), bf16[32,16,896]{2,1,0:T(8,128)(2,1)S(1)}, u32[]{:S(2)}, u32[]{:S(2)}) async-start(bf16[32,16,896]{2,1,0:T(8,128)(2,1)} %shard_map.128), calls=%async_computation.1 | async-start | bytes 1835008 | tf_op jit(solution)/shard_map/all_to_all | solution.py:391
  24.3 3.1 %collective-permute-start.5 = (bf16[128,512]{1,0:T(8,128)(2,1)S(1)}, bf16[128,512]{1,0:T(8,128)(2,1)S(1)}, u32[]{:S(2)}, u32[]{:S(2)}) collective-permute-start(bf16[128,512]{1,0:T(8,128)(2,1)S(1)} %copy-done.9), channel_id=1, source_target_pairs={{0,6},{1,7},{2,0},{3,1},{4,2},{5,3},{6,4},{7,5},{8,14},{9,15},{10,... | collective-permute-start | bytes 393224 | tf_op jit(solution)/shard_map/ppermute | solution.py:378
  29.0 2.6 %collective-permute-done.5 = bf16[128,512]{1,0:T(8,128)(2,1)S(1)} collective-permute-done((bf16[128,512]{1,0:T(8,128)(2,1)S(1)}, bf16[128,512]{1,0:T(8,128)(2,1)S(1)}, u32[]{:S(2)}, u32[]{:S(2)}) %collective-permute-start.5) | collective-permute-done | bytes 131104 | tf_op jit(solution)/shard_map/ppermute | solution.py:378
  31.5 2.4 %collective-permute-done.4 = bf16[128,512]{1,0:T(8,128)(2,1)S(1)} collective-permute-done((bf16[128,512]{1,0:T(8,128)(2,1)S(1)}, bf16[128,512]{1,0:T(8,128)(2,1)S(1)}, u32[]{:S(2)}, u32[]{:S(2)}) %collective-permute-start.4) | collective-permute-done | bytes 131104 | tf_op jit(solution)/shard_map/ppermute | solution.py:378
  35.4 3.2 %all-to-all-done.1.src_ref = bf16[32,16,896]{2,1,0:T(8,128)(2,1)S(1)} async-done(((bf16[32,16,896]{2,1,0:T(8,128)(2,1)}), bf16[32,16,896]{2,1,0:T(8,128)(2,1)S(1)}, u32[]{:S(2)}, u32[]{:S(2)}) %all-to-all-start.1) | async-done | bytes 917536 | tf_op jit(solution)/shard_map/all_to_all | solution.py:391
  40.0 3.3 %collective-permute-start = (bf16[8,16,896]{2,1,0:T(8,128)(2,1)S(1)}, bf16[8,16,896]{2,1,0:T(8,128)(2,1)S(1)}, u32[]{:S(2)}, u32[]{:S(2)}) collective-permute-start(bf16[8,16,896]{2,1,0:T(8,128)(2,1)S(1)} %get-tuple-element.28.refs_0_), channel_id=1, source_target_pairs={{0,4},{1,5},{2,6},{3,7},{4,0},{5,1},{6,2},{7,3},{8,12},{9,13},{10,... | collective-permute-start | bytes 688136 | tf_op jit(solution)/shard_map/ppermute | solution.py:378
  43.9 2.6 %collective-permute-start.2 = (bf16[8,16,896]{2,1,0:T(8,128)(2,1)S(1)}, bf16[8,16,896]{2,1,0:T(8,128)(2,1)S(1)}, u32[]{:S(2)}, u32[]{:S(2)}) collective-permute-start(bf16[8,16,896]{2,1,0:T(8,128)(2,1)S(1)} %get-tuple-element.28.refs_0_), channel_id=1, source_target_pairs={{0,6},{1,7},{2,0},{3,1},{4,2},{5,3},{6,4},{7,5},{8,14},{9,15},{10,... | collective-permute-start | bytes 688136 | tf_op jit(solution)/shard_map/ppermute | solution.py:378
  48.0 5.8 %shard_map.130 = (bf16[2,256,896]{2,1,0:T(8,128)(2,1)}, bf16[128,512]{1,0:T(8,128)(2,1)}, bf16[2,256,896]{2,1,0:T(8,128)(2,1)}, bf16[16,8,512]{2,1,0:T(8,128)(2,1)}) custom-call(s32[2]{0:T(128)} %pad_add_fusion.at_ref, bf16[128,512]{1,0:T(8,128)(2,1)} %refs_11_.1, bf16[896,512]{1,0:T(8,128)(2,1)} %refs_5_.3, bf16[4,128,512]{2,1,0:T(8,128)(2,1)} %copy-done.3, ...), custom_call_target="tpu_custom_call" | custom-call | flops 700000000 | bytes 8000000 | tf_op jit(solution)/shard_map/pallas_call | solution.py:177
  55.9 2.7 %collective-permute-start.13 = (bf16[8,16,896]{2,1,0:T(8,128)(2,1)S(1)}, bf16[8,16,896]{2,1,0:T(8,128)(2,1)S(1)}, u32[]{:S(2)}, u32[]{:S(2)}) collective-permute-start(bf16[8,16,896]{2,1,0:T(8,128)(2,1)S(1)} %get-tuple-element.39.refs_0_), channel_id=1, source_target_pairs={{0,6},{1,7},{2,0},{3,1},{4,2},{5,3},{6,4},{7,5},{8,14},{9,15},{10,... | collective-permute-start | bytes 688136 | tf_op jit(solution)/shard_map/ppermute | solution.py:378
  59.4 6.7 %shard_map.131 = (bf16[16,72,512]{2,1,0:T(8,128)(2,1)}, bf16[256,896]{1,0:T(8,128)(2,1)}, bf16[256,896]{1,0:T(8,128)(2,1)}) custom-call(s32[2]{0:T(128)} %count_ref.3, bf16[8,16,896]{2,1,0:T(8,128)(2,1)} %copy-done.2, bf16[8,16,896]{2,1,0:T(8,128)(2,1)} %copy-done.10, bf16[8,16,896]{2,1,0:T(8,128)(2,1)} %copy-done.11, bf16[8,16,896]{2,1,0:T(8,128)(2,1)} %copy-done.12, ...), custom_call_target="tpu_custom_call" | custom-call | flops 3000000000 | bytes 8000000 | tf_op jit(solution)/shard_map/pallas_call | solution.py:289
  66.1 2.9 %collective-permute-done.12.refs_2_ = bf16[8,16,896]{2,1,0:T(8,128)(2,1)S(1)} collective-permute-done((bf16[8,16,896]{2,1,0:T(8,128)(2,1)S(1)}, bf16[8,16,896]{2,1,0:T(8,128)(2,1)S(1)}, u32[]{:S(2)}, u32[]{:S(2)}) %collective-permute-start.12) | collective-permute-done | bytes 229408 | tf_op jit(solution)/shard_map/ppermute | solution.py:378
  69.0 4.5 %all-to-all-start.2 = ((bf16[16,72,512]{2,1,0:T(8,128)(2,1)}), bf16[16,72,512]{2,1,0:T(8,128)(2,1)S(1)}, u32[]{:S(2)}, u32[]{:S(2)}) async-start(bf16[16,72,512]{2,1,0:T(8,128)(2,1)} %get-tuple-element.47.refs_0_), calls=%async_computation.2 | async-start | bytes 2359296 | tf_op jit(solution)/shard_map/all_to_all | solution.py:391
  76.8 8.0 %shard_map.132 = (bf16[16,176,512]{2,1,0:T(8,128)(2,1)}, bf16[256,896]{1,0:T(8,128)(2,1)}) custom-call(s32[2]{0:T(128)} %count_ref.3, bf16[8,16,896]{2,1,0:T(8,128)(2,1)} %copy-done.1, bf16[8,16,896]{2,1,0:T(8,128)(2,1)} %copy-done.13, bf16[8,16,896]{2,1,0:T(8,128)(2,1)} %copy-done.14, bf16[8,16,896]{2,1,0:T(8,128)(2,1)} %copy-done.15, ...), custom_call_target="tpu_custom_call" | custom-call | flops 3000000000 | bytes 8000000 | tf_op jit(solution)/shard_map/pallas_call | solution.py:289
  84.8 8.3 %all-to-all-done.2 = bf16[16,72,512]{2,1,0:T(8,128)(2,1)S(1)} async-done(((bf16[16,72,512]{2,1,0:T(8,128)(2,1)}), bf16[16,72,512]{2,1,0:T(8,128)(2,1)S(1)}, u32[]{:S(2)}, u32[]{:S(2)}) %all-to-all-start.2) | async-done | bytes 1179680 | tf_op jit(solution)/shard_map/all_to_all | solution.py:391
  94.0 3.7 %all-to-all-start.3 = ((bf16[16,176,512]{2,1,0:T(8,128)(2,1)}), bf16[16,176,512]{2,1,0:T(8,128)(2,1)S(1)}, u32[]{:S(2)}, u32[]{:S(2)}) async-start(bf16[16,176,512]{2,1,0:T(8,128)(2,1)} %get-tuple-element.48.refs_1_), calls=%async_computation.3 | async-start | bytes 5767168 | tf_op jit(solution)/shard_map/all_to_all | solution.py:391
  97.8 5.1 %shard_map.133 = (bf16[4,128,512]{2,1,0:T(8,128)(2,1)}, bf16[4,128,512]{2,1,0:T(8,128)(2,1)}, bf16[128,512]{1,0:T(8,128)(2,1)}) custom-call(s32[2]{0:T(128)} %pad_add_fusion.at_ref, bf16[16,72,512]{2,1,0:T(8,128)(2,1)} %get-tuple-element.47.refs_0_, bf16[16,176,512]{2,1,0:T(8,128)(2,1)} %get-tuple-element.48.refs_1_, ...), custom_call_target="tpu_custom_call" | custom-call | flops 700000000 | bytes 8000000 | tf_op jit(solution)/shard_map/pallas_call | solution.py:332
  107.4 2.8 %collective-permute-done.24 = bf16[16,8,512]{2,1,0:T(8,128)(2,1)S(1)} collective-permute-done((bf16[16,8,512]{2,1,0:T(8,128)(2,1)S(1)}, bf16[16,8,512]{2,1,0:T(8,128)(2,1)S(1)}, u32[]{:S(2)}, u32[]{:S(2)}) %collective-permute-start.24) | collective-permute-done | bytes 131104 | tf_op jit(solution)/shard_map/ppermute | solution.py:378
  110.3 2.1 %collective-permute-done.23 = bf16[16,8,512]{2,1,0:T(8,128)(2,1)S(1)} collective-permute-done((bf16[16,8,512]{2,1,0:T(8,128)(2,1)S(1)}, bf16[16,8,512]{2,1,0:T(8,128)(2,1)S(1)}, u32[]{:S(2)}, u32[]{:S(2)}) %collective-permute-start.23) | collective-permute-done | bytes 131104 | tf_op jit(solution)/shard_map/ppermute | solution.py:378
  117.6 3.4 %collective-permute-done.21 = bf16[128,512]{1,0:T(8,128)(2,1)S(1)} collective-permute-done((bf16[128,512]{1,0:T(8,128)(2,1)S(1)}, bf16[128,512]{1,0:T(8,128)(2,1)S(1)}, u32[]{:S(2)}, u32[]{:S(2)}) %collective-permute-start.21) | collective-permute-done | bytes 131104 | tf_op jit(solution)/shard_map/ppermute | solution.py:378
  121.0 4.3 %collective-permute-done.20 = bf16[128,512]{1,0:T(8,128)(2,1)S(1)} collective-permute-done((bf16[128,512]{1,0:T(8,128)(2,1)S(1)}, bf16[128,512]{1,0:T(8,128)(2,1)S(1)}, u32[]{:S(2)}, u32[]{:S(2)}) %collective-permute-start.20) | collective-permute-done | bytes 131104 | tf_op jit(solution)/shard_map/ppermute | solution.py:378
  126.8 2.4 %shard_map.134 = bf16[16,128,256]{2,1,0:T(8,128)(2,1)} custom-call(s32[2]{0:T(128)} %pad_add_fusion.at_ref, bf16[4,16,8,512]{3,2,1,0:T(8,128)(2,1)} %copy-done.4, bf16[4,16,8,512]{3,2,1,0:T(8,128)(2,1)} %copy-done.8), custom_call_target="tpu_custom_call" | custom-call | bytes 2000000 | tf_op jit(solution)/shard_map/pallas_call | solution.py:361
  131.0 4.1 %all-to-all-done.3 = bf16[16,176,512]{2,1,0:T(8,128)(2,1)S(1)} async-done(((bf16[16,176,512]{2,1,0:T(8,128)(2,1)}), bf16[16,176,512]{2,1,0:T(8,128)(2,1)S(1)}, u32[]{:S(2)}, u32[]{:S(2)}) %all-to-all-start.3) | async-done | bytes 2883616 | tf_op jit(solution)/shard_map/all_to_all | solution.py:391
  (102 shorter events, 30.2 us)
Async XLA Ops:
  20.6 18.0 %all-to-all-start.1 = ((bf16[32,16,896]{2,1,0:T(8,128)(2,1)}), bf16[32,16,896]{2,1,0:T(8,128)(2,1)S(1)}, u32[]{:S(2)}, u32[]{:S(2)}) async-start(bf16[32,16,896]{2,1,0:T(8,128)(2,1)} %shard_map.128), calls=%async_computation.1 | async-start | bytes 1835008 | tf_op jit(solution)/shard_map/all_to_all | solution.py:391
  24.3 7.3 %collective-permute-start.5 = (bf16[128,512]{1,0:T(8,128)(2,1)S(1)}, bf16[128,512]{1,0:T(8,128)(2,1)S(1)}, u32[]{:S(2)}, u32[]{:S(2)}) collective-permute-start(bf16[128,512]{1,0:T(8,128)(2,1)S(1)} %copy-done.9), channel_id=1, source_target_pairs={{0,6},{1,7},{2,0},{3,1},{4,2},{5,3},{6,4},{7,5},{8,14},{9,15},{10,... | collective-permute-start | bytes 393224 | tf_op jit(solution)/shard_map/ppermute | solution.py:378
  27.4 6.6 %collective-permute-start.4 = (bf16[128,512]{1,0:T(8,128)(2,1)S(1)}, bf16[128,512]{1,0:T(8,128)(2,1)S(1)}, u32[]{:S(2)}, u32[]{:S(2)}) collective-permute-start(bf16[128,512]{1,0:T(8,128)(2,1)S(1)} %copy-done.9), channel_id=1, source_target_pairs={{0,4},{1,5},{2,6},{3,7},{4,0},{5,1},{6,2},{7,3},{8,12},{9,13},{10,... | collective-permute-start | bytes 393224 | tf_op jit(solution)/shard_map/ppermute | solution.py:378
  28.0 7.2 %collective-permute-start.3 = (bf16[128,512]{1,0:T(8,128)(2,1)S(1)}, bf16[128,512]{1,0:T(8,128)(2,1)S(1)}, u32[]{:S(2)}, u32[]{:S(2)}) collective-permute-start(bf16[128,512]{1,0:T(8,128)(2,1)S(1)} %copy-done.9), channel_id=1, source_target_pairs={{0,2},{1,3},{2,4},{3,5},{4,6},{5,7},{6,0},{7,1},{8,10},{9,11},{10,... | collective-permute-start | bytes 393224 | tf_op jit(solution)/shard_map/ppermute | solution.py:378
  35.3 11.9 %collective-permute-start.6 = (bf16[4,128,512]{2,1,0:T(8,128)(2,1)S(1)}, bf16[4,128,512]{2,1,0:T(8,128)(2,1)S(1)}, u32[]{:S(2)}, u32[]{:S(2)}) collective-permute-start(bf16[4,128,512]{2,1,0:T(8,128)(2,1)S(1)} %pad_maximum_fusion.refs_2_), channel_id=1, source_target_pairs={{0,1},{1,0},{2,3},{3,2},{4,5},{5,4},{6,7},{7,6},{8,9},{9,8},{10,11... | collective-permute-start | bytes 1572872 | tf_op jit(solution)/shard_map/ppermute | solution.py:382
  40.0 13.9 %collective-permute-start = (bf16[8,16,896]{2,1,0:T(8,128)(2,1)S(1)}, bf16[8,16,896]{2,1,0:T(8,128)(2,1)S(1)}, u32[]{:S(2)}, u32[]{:S(2)}) collective-permute-start(bf16[8,16,896]{2,1,0:T(8,128)(2,1)S(1)} %get-tuple-element.28.refs_0_), channel_id=1, source_target_pairs={{0,4},{1,5},{2,6},{3,7},{4,0},{5,1},{6,2},{7,3},{8,12},{9,13},{10,... | collective-permute-start | bytes 688136 | tf_op jit(solution)/shard_map/ppermute | solution.py:378
  43.3 10.6 %collective-permute-start.1 = (bf16[8,16,896]{2,1,0:T(8,128)(2,1)S(1)}, bf16[8,16,896]{2,1,0:T(8,128)(2,1)S(1)}, u32[]{:S(2)}, u32[]{:S(2)}) collective-permute-start(bf16[8,16,896]{2,1,0:T(8,128)(2,1)S(1)} %get-tuple-element.28.refs_0_), channel_id=1, source_target_pairs={{0,2},{1,3},{2,4},{3,5},{4,6},{5,7},{6,0},{7,1},{8,10},{9,11},{10,... | collective-permute-start | bytes 688136 | tf_op jit(solution)/shard_map/ppermute | solution.py:378
  43.9 10.0 %collective-permute-start.2 = (bf16[8,16,896]{2,1,0:T(8,128)(2,1)S(1)}, bf16[8,16,896]{2,1,0:T(8,128)(2,1)S(1)}, u32[]{:S(2)}, u32[]{:S(2)}) collective-permute-start(bf16[8,16,896]{2,1,0:T(8,128)(2,1)S(1)} %get-tuple-element.28.refs_0_), channel_id=1, source_target_pairs={{0,6},{1,7},{2,0},{3,1},{4,2},{5,3},{6,4},{7,5},{8,14},{9,15},{10,... | collective-permute-start | bytes 688136 | tf_op jit(solution)/shard_map/ppermute | solution.py:378
  53.9 2.0 %collective-permute-start.8 = (bf16[8,16,896]{2,1,0:T(8,128)(2,1)S(1)}, bf16[8,16,896]{2,1,0:T(8,128)(2,1)S(1)}, u32[]{:S(2)}, u32[]{:S(2)}) collective-permute-start(bf16[8,16,896]{2,1,0:T(8,128)(2,1)S(1)} %collective-permute-done.refs_1_), channel_id=1, source_target_pairs={{0,1},{1,0},{2,3},{3,2},{4,5},{5,4},{6,7},{7,6},{8,9},{9,8},{10,11... | collective-permute-start | bytes 688136 | tf_op jit(solution)/shard_map/ppermute | solution.py:382
  54.5 4.1 %collective-permute-start.9 = (bf16[8,16,896]{2,1,0:T(8,128)(2,1)S(1)}, bf16[8,16,896]{2,1,0:T(8,128)(2,1)S(1)}, u32[]{:S(2)}, u32[]{:S(2)}) collective-permute-start(bf16[8,16,896]{2,1,0:T(8,128)(2,1)S(1)} %collective-permute-done.1.refs_2_), channel_id=1, source_target_pairs={{0,1},{1,0},{2,3},{3,2},{4,5},{5,4},{6,7},{7,6},{8,9},{9,8},{10,11... | collective-permute-start | bytes 688136 | tf_op jit(solution)/shard_map/ppermute | solution.py:382
  54.6 4.0 %collective-permute-start.10 = (bf16[8,16,896]{2,1,0:T(8,128)(2,1)S(1)}, bf16[8,16,896]{2,1,0:T(8,128)(2,1)S(1)}, u32[]{:S(2)}, u32[]{:S(2)}) collective-permute-start(bf16[8,16,896]{2,1,0:T(8,128)(2,1)S(1)} %collective-permute-done.2.refs_3_), channel_id=1, source_target_pairs={{0,1},{1,0},{2,3},{3,2},{4,5},{5,4},{6,7},{7,6},{8,9},{9,8},{10,11... | collective-permute-start | bytes 688136 | tf_op jit(solution)/shard_map/ppermute | solution.py:382
  55.0 11.1 %collective-permute-start.11 = (bf16[8,16,896]{2,1,0:T(8,128)(2,1)S(1)}, bf16[8,16,896]{2,1,0:T(8,128)(2,1)S(1)}, u32[]{:S(2)}, u32[]{:S(2)}) collective-permute-start(bf16[8,16,896]{2,1,0:T(8,128)(2,1)S(1)} %get-tuple-element.39.refs_0_), channel_id=1, source_target_pairs={{0,4},{1,5},{2,6},{3,7},{4,0},{5,1},{6,2},{7,3},{8,12},{9,13},{10,... | collective-permute-start | bytes 688136 | tf_op jit(solution)/shard_map/ppermute | solution.py:378
  55.3 13.7 %collective-permute-start.12 = (bf16[8,16,896]{2,1,0:T(8,128)(2,1)S(1)}, bf16[8,16,896]{2,1,0:T(8,128)(2,1)S(1)}, u32[]{:S(2)}, u32[]{:S(2)}) collective-permute-start(bf16[8,16,896]{2,1,0:T(8,128)(2,1)S(1)} %get-tuple-element.39.refs_0_), channel_id=1, source_target_pairs={{0,2},{1,3},{2,4},{3,5},{4,6},{5,7},{6,0},{7,1},{8,10},{9,11},{10,... | collective-permute-start | bytes 688136 | tf_op jit(solution)/shard_map/ppermute | solution.py:378
  55.9 13.1 %collective-permute-start.13 = (bf16[8,16,896]{2,1,0:T(8,128)(2,1)S(1)}, bf16[8,16,896]{2,1,0:T(8,128)(2,1)S(1)}, u32[]{:S(2)}, u32[]{:S(2)}) collective-permute-start(bf16[8,16,896]{2,1,0:T(8,128)(2,1)S(1)} %get-tuple-element.39.refs_0_), channel_id=1, source_target_pairs={{0,6},{1,7},{2,0},{3,1},{4,2},{5,3},{6,4},{7,5},{8,14},{9,15},{10,... | collective-permute-start | bytes 688136 | tf_op jit(solution)/shard_map/ppermute | solution.py:378
  69.0 24.0 %all-to-all-start.2 = ((bf16[16,72,512]{2,1,0:T(8,128)(2,1)}), bf16[16,72,512]{2,1,0:T(8,128)(2,1)S(1)}, u32[]{:S(2)}, u32[]{:S(2)}) async-start(bf16[16,72,512]{2,1,0:T(8,128)(2,1)} %get-tuple-element.47.refs_0_), calls=%async_computation.2 | async-start | bytes 2359296 | tf_op jit(solution)/shard_map/all_to_all | solution.py:391
  94.0 41.1 %all-to-all-start.3 = ((bf16[16,176,512]{2,1,0:T(8,128)(2,1)}), bf16[16,176,512]{2,1,0:T(8,128)(2,1)S(1)}, u32[]{:S(2)}, u32[]{:S(2)}) async-start(bf16[16,176,512]{2,1,0:T(8,128)(2,1)} %get-tuple-element.48.refs_1_), calls=%async_computation.3 | async-start | bytes 5767168 | tf_op jit(solution)/shard_map/all_to_all | solution.py:391
  102.9 3.4 %collective-permute-start.18 = (bf16[4,128,512]{2,1,0:T(8,128)(2,1)}, bf16[4,128,512]{2,1,0:T(8,128)(2,1)S(1)}, u32[]{:S(2)}, u32[]{:S(2)}) collective-permute-start(bf16[4,128,512]{2,1,0:T(8,128)(2,1)} %get-tuple-element.45), channel_id=1, source_target_pairs={{0,1},{1,0},{2,3},{3,2},{4,5},{5,4},{6,7},{7,6},{8,9},{9,8},{10,11... | collective-permute-start | bytes 1572872 | tf_op jit(solution)/shard_map/ppermute | solution.py:382
  103.9 6.4 %collective-permute-start.24 = (bf16[16,8,512]{2,1,0:T(8,128)(2,1)S(1)}, bf16[16,8,512]{2,1,0:T(8,128)(2,1)S(1)}, u32[]{:S(2)}, u32[]{:S(2)}) collective-permute-start(bf16[16,8,512]{2,1,0:T(8,128)(2,1)S(1)} %get-tuple-element.54), channel_id=1, source_target_pairs={{0,6},{1,7},{2,0},{3,1},{4,2},{5,3},{6,4},{7,5},{8,14},{9,15},{10,... | collective-permute-start | bytes 393224 | tf_op jit(solution)/shard_map/ppermute | solution.py:378
  104.5 7.8 %collective-permute-start.23 = (bf16[16,8,512]{2,1,0:T(8,128)(2,1)S(1)}, bf16[16,8,512]{2,1,0:T(8,128)(2,1)S(1)}, u32[]{:S(2)}, u32[]{:S(2)}) collective-permute-start(bf16[16,8,512]{2,1,0:T(8,128)(2,1)S(1)} %get-tuple-element.54), channel_id=1, source_target_pairs={{0,4},{1,5},{2,6},{3,7},{4,0},{5,1},{6,2},{7,3},{8,12},{9,13},{10,... | collective-permute-start | bytes 393224 | tf_op jit(solution)/shard_map/ppermute | solution.py:378
  105.4 9.1 %collective-permute-start.22 = (bf16[16,8,512]{2,1,0:T(8,128)(2,1)S(1)}, bf16[16,8,512]{2,1,0:T(8,128)(2,1)S(1)}, u32[]{:S(2)}, u32[]{:S(2)}) collective-permute-start(bf16[16,8,512]{2,1,0:T(8,128)(2,1)S(1)} %get-tuple-element.54), channel_id=1, source_target_pairs={{0,2},{1,3},{2,4},{3,5},{4,6},{5,7},{6,0},{7,1},{8,10},{9,11},{10,... | collective-permute-start | bytes 393224 | tf_op jit(solution)/shard_map/ppermute | solution.py:378
  114.6 11.4 %collective-permute-start.25 = (bf16[4,16,8,512]{3,2,1,0:T(8,128)(2,1)S(1)}, bf16[4,16,8,512]{3,2,1,0:T(8,128)(2,1)S(1)}, u32[]{:S(2)}, u32[]{:S(2)}) collective-permute-start(bf16[4,16,8,512]{3,2,1,0:T(8,128)(2,1)S(1)} %pad_maximum_fusion.1.near_ref), channel_id=1, source_target_pairs={{0,1},{1,0},{2,3},{3,2},{4,5},{5,4},{6,7},{7,6},{8,9},{9,8},{10,11... | collective-permute-start | bytes 1572872 | tf_op jit(solution)/shard_map/ppermute | solution.py:382
  114.7 6.3 %collective-permute-start.21 = (bf16[128,512]{1,0:T(8,128)(2,1)S(1)}, bf16[128,512]{1,0:T(8,128)(2,1)S(1)}, u32[]{:S(2)}, u32[]{:S(2)}) collective-permute-start(bf16[128,512]{1,0:T(8,128)(2,1)S(1)} %get-tuple-element.56), channel_id=1, source_target_pairs={{0,6},{1,7},{2,0},{3,1},{4,2},{5,3},{6,4},{7,5},{8,14},{9,15},{10,... | collective-permute-start | bytes 393224 | tf_op jit(solution)/shard_map/ppermute | solution.py:378
  115.6 9.6 %collective-permute-start.20 = (bf16[128,512]{1,0:T(8,128)(2,1)S(1)}, bf16[128,512]{1,0:T(8,128)(2,1)S(1)}, u32[]{:S(2)}, u32[]{:S(2)}) collective-permute-start(bf16[128,512]{1,0:T(8,128)(2,1)S(1)} %get-tuple-element.57), channel_id=1, source_target_pairs={{0,2},{1,3},{2,4},{3,5},{4,6},{5,7},{6,0},{7,1},{8,10},{9,11},{10,... | collective-permute-start | bytes 393224 | tf_op jit(solution)/shard_map/ppermute | solution.py:378
  116.8 8.5 %collective-permute-start.19 = (bf16[128,512]{1,0:T(8,128)(2,1)S(1)}, bf16[128,512]{1,0:T(8,128)(2,1)S(1)}, u32[]{:S(2)}, u32[]{:S(2)}) collective-permute-start(bf16[128,512]{1,0:T(8,128)(2,1)S(1)} %get-tuple-element.55), channel_id=1, source_target_pairs={{0,4},{1,5},{2,6},{3,7},{4,0},{5,1},{6,2},{7,3},{8,12},{9,13},{10,... | collective-permute-start | bytes 393224 | tf_op jit(solution)/shard_map/ppermute | solution.py:378
  (29 other events, 157.3 us)
